TPU v7x, 32 devices: a whole 2x2x4 slice. The times are simulated.
32 devices in a mesh: maps: 8 (over z, y), rows: 4 (over x, core).
Axes of the slice: x: 2, y: 2, z: 4, core: 2. Of those that a mesh axis runs over, the one named last changes fastest.
Arguments:
- block_input: bfloat16 [8, 48, 32, 512], P('maps', 'rows'), may hold values from -6 to 6
- conv_weights: bfloat16 [3, 9, 512, 512], replicated, may hold values from -0.09375 to 0.09375
- norm_params: float32 [2, 3, 512], replicated, may hold values from -1.1 to 3.6, as said below
- pool_index: int32 [8, 24, 16, 512], P('maps', 'rows'), may hold values from 0 to 3
- task_mask: int32 [8, 24, 16], P('maps'), may hold values 0 or 1
- map_kind: int32 [8], replicated, may hold values from 0 to 1
- map_domain: int32 [8], replicated, may hold values from 0 to 3, as said below
- out_grad: bfloat16 [8, 24, 16, 512], P('maps', None, None, 'rows'), may hold values from -6 to 6
- step: int32 [1], replicated, may hold values from 2 to 20
- conv_master: float32 [3, 9, 512, 512], P(None, None, 'maps', 'rows'), may hold values from -0.09375 to 0.09375
- conv_moment1: float32 [3, 9, 512, 512], P(None, None, 'maps', 'rows')
- conv_moment2: float32 [3, 9, 512, 512], P(None, None, 'maps', 'rows'), as said below
- norm_moment1: float32 [2, 3, 512], replicated
- norm_moment2: float32 [2, 3, 512], replicated, as said below
Outputs:
- pooled: bfloat16 [8, 24, 16, 512], P('maps', None, None, 'rows')
- input_grad: bfloat16 [8, 48, 32, 512], P('maps', 'rows')
- grad_norm: float32 [1], replicated
- conv_moment1_new: float32 [3, 9, 512, 512], P(None, None, 'maps', 'rows')
- conv_moment2_new: float32 [3, 9, 512, 512], P(None, None, 'maps', 'rows')
- conv_master_new: float32 [3, 9, 512, 512], P(None, None, 'maps', 'rows')
- norm_moment1_new: float32 [2, 3, 512], replicated
- norm_moment2_new: float32 [2, 3, 512], replicated
- norm_params_new: float32 [2, 3, 512], replicated
Inputs may be any that keep to these rules, and one draw needn't show every extreme that they name: `pool_index`: index of the window's maximum, 2 x row offset + column offset. `task_mask`: 1 where the pooled pixel carries a label. `map_kind`: kind 0: 42 x 32 valid pixels; kind 1: 48 x 26; the rest of the grid is padding. `map_domain`: each domain holds exactly 2 maps. `norm_params`: gains in row 0 are positive. `conv_moment2`: every entry positive. `norm_moment2`: every entry positive.
All inputs are finite; a program needn't handle non-finite values. No bound on the sum of `task_mask` on one device may be relied on, other than what follows from the above.
Results may differ from a plain program's by a relative error of at most 0.012.
Values may be sent and summed in bfloat16 or wider, within the bound.
No kernel may reach another device: no remote copies, remote signals or barrier semaphores. Data moves between devices by JAX's collectives and lax.ppermute only.
A program may use at most 128 MiB of HBM per device.

v0:
```python
import math

import jax
import jax.numpy as jnp
from jax import lax
from jax.sharding import PartitionSpec as P

DOMAINS = 4


norm_epsilon = 1e-05
clip_limit = 1.0
first_decay = 0.9
second_decay = 0.999
adam_epsilon = 1e-08
norm_rate = 0.5
weight_decay = 0.01
highest = lax.Precision.HIGHEST


def padded_2(block, sides, width):
    for axis, dim in sides:
        count = lax.axis_size(axis)
        forward = [(i, i + 1) for i in range(count - 1)]
        backward = [(target, source) for source, target in forward]
        low = lax.ppermute(
            lax.slice_in_dim(block, block.shape[dim] - width, None, axis=dim), axis, forward
        )
        high = lax.ppermute(lax.slice_in_dim(block, 0, width, axis=dim), axis, backward)
        block = jnp.concatenate([low, block, high], axis=dim)
    return block


def widen_forward(values):
    extended = padded_2(values, (("rows", 1),), 1)
    return jnp.pad(extended, ((0, 0), (0, 0), (1, 1), (0, 0)))


def widen_backward(values):
    extended = padded_2(values, (("rows", 1),), 1)
    return jnp.pad(extended, ((0, 0), (0, 0), (1, 1), (0, 0)))


def conv_taps(padded, kernel, band_rows, map_width):
    result = jnp.zeros((padded.shape[0], band_rows, map_width, kernel.shape[2]), jnp.float32)
    for tap_row in range(3):
        for tap_col in range(3):
            piece = padded[:, tap_row : tap_row + band_rows, tap_col : tap_col + map_width, :]
            result = result + jnp.einsum(
                "mhwc,cd->mhwd",
                piece,
                kernel[tap_row * 3 + tap_col],
                preferred_element_type=jnp.float32,
            )
    return result


def transpose_taps(padded, kernel, band_rows, map_width):
    result = jnp.zeros((padded.shape[0], band_rows, map_width, kernel.shape[1]), jnp.float32)
    for tap_row in range(3):
        for tap_col in range(3):
            piece = padded[
                :, 2 - tap_row : 2 - tap_row + band_rows, 2 - tap_col : 2 - tap_col + map_width, :
            ]
            result = result + jnp.einsum(
                "mhwd,cd->mhwc",
                piece,
                kernel[tap_row * 3 + tap_col],
                preferred_element_type=jnp.float32,
            )
    return result


def kernel_taps(padded, conv_grad, band_rows, map_width):
    return jnp.stack(
        [
            jnp.einsum(
                "mhwc,mhwd->cd",
                padded[
                    :,
                    tap_index // 3 : tap_index // 3 + band_rows,
                    tap_index % 3 : tap_index % 3 + map_width,
                    :,
                ],
                conv_grad,
                preferred_element_type=jnp.float32,
            )
            for tap_index in range(9)
        ]
    )


def domain_sums(member, first_term, second_term):
    return (
        jnp.dot(member.T, jnp.sum(first_term, axis=(1, 2)), precision=highest),
        jnp.dot(member.T, jnp.sum(second_term, axis=(1, 2)), precision=highest),
    )


def adamw_update(param, grad, first, second, rate, decay, scale, count):
    clipped = scale * grad
    first_new = first_decay * first + (1.0 - first_decay) * clipped
    second_new = second_decay * second + (1.0 - second_decay) * clipped * clipped
    first_fix = 1.0 - jnp.power(first_decay, count)
    second_fix = 1.0 - jnp.power(second_decay, count)
    update = first_new / first_fix / (jnp.sqrt(second_new / second_fix) + adam_epsilon)
    return (first_new, second_new, param - rate * (update + decay * param))


def local(
    block_input,
    conv_weights,
    norm_params,
    pool_index,
    task_mask,
    map_kind,
    map_domain,
    out_grad,
    step,
    conv_master,
    conv_moment1,
    conv_moment2,
    norm_moment1,
    norm_moment2,
):
    maps_here = block_input.shape[0]
    band_rows = block_input.shape[1]
    map_width = block_input.shape[2]
    channels = block_input.shape[3]
    conv_rate = 2.0 / math.sqrt(9.0 * channels)
    height = band_rows * lax.axis_size("rows")
    short_height = 2 * (height * 7 // 16)
    short_width = 2 * (map_width * 13 // 32)
    tall_all = map_kind == 1
    areas = jnp.where(tall_all, height * short_width, short_height * map_width).astype(jnp.float32)
    member_all = (map_domain[:, None] == jnp.arange(DOMAINS, dtype=jnp.int32)[None, :]).astype(
        jnp.float32
    )
    counts = jnp.dot(member_all.T, areas, precision=highest)
    first_map = lax.axis_index("maps") * maps_here
    kinds = lax.dynamic_slice_in_dim(map_kind, first_map, maps_here, 0)
    member = lax.dynamic_slice_in_dim(member_all, first_map, maps_here, 0)
    heights = jnp.where(kinds == 1, height, short_height).astype(jnp.int32)
    widths = jnp.where(kinds == 1, short_width, map_width).astype(jnp.int32)
    row_pos = lax.axis_index("rows") * band_rows + jnp.arange(band_rows, dtype=jnp.int32)
    col_pos = jnp.arange(map_width, dtype=jnp.int32)
    valid = (
        (row_pos[None, :, None] < heights[:, None, None])
        & (col_pos[None, None, :] < widths[:, None, None])
    ).astype(jnp.float32)
    mask = valid[..., None]
    values = block_input
    kept_inputs = []
    kept_convs = []
    kept_means = []
    kept_inverses = []
    for layer_index in range(3):
        padded = widen_forward(values)
        conv_out = conv_taps(padded, conv_weights[layer_index], band_rows, map_width)
        masked = conv_out * mask
        sums, squares = domain_sums(member, masked, masked * conv_out)
        sums, squares = lax.psum((sums, squares), ("maps", "rows"))
        mean = sums / counts[:, None]
        inverse = lax.rsqrt(squares / counts[:, None] - mean * mean + norm_epsilon)
        map_mean = jnp.dot(member, mean, precision=highest)
        map_inverse = jnp.dot(member, inverse, precision=highest)
        normed = (conv_out - map_mean[:, None, None, :]) * map_inverse[:, None, None, :]
        shifted = norm_params[0, layer_index] * normed + norm_params[1, layer_index]
        values = (jax.nn.silu(shifted) * mask).astype(jnp.bfloat16)
        kept_inputs.append(padded)
        kept_convs.append(conv_out)
        kept_means.append(map_mean)
        kept_inverses.append(map_inverse)
    pooled_local = jnp.zeros(pool_index.shape, jnp.bfloat16)
    for corner in range(4):
        pooled_local = jnp.where(
            pool_index == corner, values[:, corner // 2 :: 2, corner % 2 :: 2, :], pooled_local
        )
    pooled = lax.all_to_all(pooled_local, "rows", split_axis=3, concat_axis=1, tiled=True)
    labelled = out_grad * task_mask[..., None].astype(jnp.bfloat16)
    returned = lax.all_to_all(labelled, "rows", split_axis=1, concat_axis=3, tiled=True)
    zeros_back = jnp.zeros_like(returned)
    row_pairs = []
    for row_off in range(2):
        columns = [
            jnp.where(pool_index == row_off * 2 + col_off, returned, zeros_back)
            for col_off in range(2)
        ]
        row_pairs.append(
            jnp.stack(columns, axis=3).reshape(maps_here, band_rows // 2, map_width, channels)
        )
    upstream_grad = (
        jnp.stack(row_pairs, axis=2)
        .reshape(maps_here, band_rows, map_width, channels)
        .astype(jnp.float32)
    )
    kernel_grads = [None, None, None]
    gain_grads = [None, None, None]
    shift_grads = [None, None, None]
    for layer_index in (2, 1, 0):
        conv_out = kept_convs[layer_index]
        map_inverse = kept_inverses[layer_index]
        normed = (conv_out - kept_means[layer_index][:, None, None, :]) * map_inverse[
            :, None, None, :
        ]
        gain = norm_params[0, layer_index]
        shifted = gain * normed + norm_params[1, layer_index]
        sigmoid_val = jax.nn.sigmoid(shifted)
        out_side = upstream_grad * (sigmoid_val * (1.0 + shifted * (1.0 - sigmoid_val))) * mask
        first_sum, second_sum = domain_sums(member, out_side, out_side * normed)
        first_sum, second_sum = lax.psum((first_sum, second_sum), ("maps", "rows"))
        shift_grads[layer_index] = jnp.sum(first_sum, axis=0)
        gain_grads[layer_index] = jnp.sum(second_sum, axis=0)
        mean_one = jnp.dot(member, first_sum / counts[:, None], precision=highest)
        mean_two = jnp.dot(member, second_sum / counts[:, None], precision=highest)
        conv_grad = (
            gain
            * map_inverse[:, None, None, :]
            * (out_side - mean_one[:, None, None, :] - normed * mean_two[:, None, None, :])
            * mask
        ).astype(jnp.bfloat16)
        kernel_grads[layer_index] = kernel_taps(
            kept_inputs[layer_index], conv_grad, band_rows, map_width
        )
        grad_padded = widen_backward(conv_grad)
        upstream_grad = transpose_taps(grad_padded, conv_weights[layer_index], band_rows, map_width)
    input_grad = upstream_grad.astype(jnp.bfloat16)
    kernel_grad = jnp.stack(kernel_grads)
    norm_grad = jnp.stack([jnp.stack(gain_grads), jnp.stack(shift_grads)])
    partial_grad = lax.psum_scatter(kernel_grad, "maps", scatter_dimension=2, tiled=True)
    shard_grad = lax.psum_scatter(
        partial_grad.astype(jnp.bfloat16), "rows", scatter_dimension=3, tiled=True
    ).astype(jnp.float32)
    shard_squares = lax.psum(jnp.sum(shard_grad * shard_grad), ("maps", "rows"))
    total = jnp.sqrt(shard_squares + jnp.sum(norm_grad * norm_grad))
    scale = jnp.minimum(1.0, clip_limit / total)
    count = step[0].astype(jnp.float32)
    conv_first, conv_second, conv_new = adamw_update(
        conv_master, shard_grad, conv_moment1, conv_moment2, conv_rate, weight_decay, scale, count
    )
    norm_first, norm_second, norm_new = adamw_update(
        norm_params, norm_grad, norm_moment1, norm_moment2, norm_rate, 0.0, scale, count
    )
    return (
        pooled,
        input_grad,
        total.reshape(1),
        conv_first,
        conv_second,
        conv_new,
        norm_first,
        norm_second,
        norm_new,
    )


def solution(mesh):
    return jax.shard_map(
        local,
        mesh=mesh,
        in_specs=(
            P("maps", "rows", None, None),
            P(),
            P(),
            P("maps", "rows", None, None),
            P("maps", None, None),
            P(),
            P(),
            P("maps", None, None, "rows"),
            P(),
            P(None, None, "maps", "rows"),
            P(None, None, "maps", "rows"),
            P(None, None, "maps", "rows"),
            P(),
            P(),
        ),
        out_specs=(
            P("maps", None, None, "rows"),
            P("maps", "rows", None, None),
            P(),
            P(None, None, "maps", "rows"),
            P(None, None, "maps", "rows"),
            P(None, None, "maps", "rows"),
            P(),
            P(),
            P(),
        ),
        check_vma=False,
    )
```

profile of v0, /device:TPU:0, one launch (start us, length us, event | category | flops | bytes accessed | tf_op | source)
XLA Modules:
  0.0 991.6 jit_solution(9270450920264189992)
XLA Ops:
  8.0 2.3 collective-permute-start
  21.4 1.6 convolution_add_fusion.41
  30.1 1.5 multiply_reduce_fusion.2
  31.7 44.0 %all-reduce.11 = (f32[4,512]{1,0:T(4,128)S(1)}, f32[4,512]{1,0:T(4,128)S(1)}) all-reduce(f32[4,512]{1,0:T(4,128)S(1)} %get-tuple-element.113, f32[4,512]{1,0:T(4,128)S(1)} %get-tuple-element.112), channel_id=1, replica_groups=mesh['maps'=8,'rows'=4] {'maps','rows'}, use_global_device_ids=true, to_apply=%region_3.4 | all-reduce | flops 4096 | bytes 32768 | tf_op jit(solution)/shard_map/psum | solution.py:162
  79.9 6.5 all-to-all-start.1
  94.4 1.6 convolution_add_fusion.31
  98.8 1.5 multiply_reduce_fusion.1
  101.2 40.9 %all-reduce.10 = (f32[4,512]{1,0:T(4,128)}, f32[4,512]{1,0:T(4,128)}) all-reduce(f32[4,512]{1,0:T(4,128)} %get-tuple-element.111, f32[4,512]{1,0:T(4,128)S(1)} %get-tuple-element.110), channel_id=1, replica_groups=mesh['maps'=8,'rows'=4] {'maps','rows'}, use_global_device_ids=true, to_apply=%region_7.8 | all-reduce | flops 4096 | bytes 32768 | tf_op jit(solution)/shard_map/psum | solution.py:162
  148.1 2.1 collective-permute-start.4
  151.7 1.6 copy.94
  153.3 1.6 all_to_all.33
  154.9 1.8 select_bitcast_fusion.3
  158.2 1.7 stack_reshape.6
  159.9 1.8 copy.63
  161.7 1.7 stack_reshape.7
  169.6 1.6 convolution_add_fusion.27
  174.1 1.6 convolution_add_fusion.24
  178.5 2.4 multiply_reduce_fusion
  181.0 42.8 %all-reduce.9 = (f32[4,512]{1,0:T(4,128)S(1)}, f32[4,512]{1,0:T(4,128)S(1)}) all-reduce(f32[4,512]{1,0:T(4,128)S(1)} %get-tuple-element.109, f32[4,512]{1,0:T(4,128)S(1)} %get-tuple-element.108), channel_id=1, replica_groups=mesh['maps'=8,'rows'=4] {'maps','rows'}, use_global_device_ids=true, to_apply=%region_11.12 | all-reduce | flops 4096 | bytes 32768 | tf_op jit(solution)/shard_map/psum | solution.py:162
  224.2 2.9 fusion.302
  227.2 39.8 %all-reduce.8 = (f32[4,512]{1,0:T(4,128)S(1)}, f32[4,512]{1,0:T(4,128)S(1)}) all-reduce(f32[4,512]{1,0:T(4,128)S(1)} %get-tuple-element.107, f32[4,512]{1,0:T(4,128)S(1)} %get-tuple-element.106), channel_id=1, replica_groups=mesh['maps'=8,'rows'=4] {'maps','rows'}, use_global_device_ids=true, to_apply=%region_15.16 | all-reduce | flops 4096 | bytes 32768 | tf_op jit(solution)/shard_map/psum | solution.py:211
  267.3 1.6 multiply_convert_fusion.2
  270.9 1.5 collective-permute-start.7
  278.1 3.6 copy-done.1
  287.8 1.5 convolution_add_fusion.18
  293.7 2.6 fusion.301
  297.0 43.8 %all-reduce.7 = (f32[4,512]{1,0:T(4,128)}, f32[4,512]{1,0:T(4,128)}) all-reduce(f32[4,512]{1,0:T(4,128)} %get-tuple-element.105, f32[4,512]{1,0:T(4,128)S(1)} %get-tuple-element.104), channel_id=1, replica_groups=mesh['maps'=8,'rows'=4] {'maps','rows'}, use_global_device_ids=true, to_apply=%region_19.20 | all-reduce | flops 4096 | bytes 32768 | tf_op jit(solution)/shard_map/psum | solution.py:211
  344.5 1.5 collective-permute-start.8
  346.0 1.5 collective-permute-start.9
  352.4 3.6 copy-done.2
  367.8 1.8 fusion.300
  369.7 43.0 %all-reduce.6 = (f32[4,512]{1,0:T(4,128)S(1)}, f32[4,512]{1,0:T(4,128)S(1)}) all-reduce(f32[4,512]{1,0:T(4,128)S(1)} %get-tuple-element.103, f32[4,512]{1,0:T(4,128)S(1)} %get-tuple-element.102), channel_id=1, replica_groups=mesh['maps'=8,'rows'=4] {'maps','rows'}, use_global_device_ids=true, to_apply=%region_23.24 | all-reduce | flops 4096 | bytes 32768 | tf_op jit(solution)/shard_map/psum | solution.py:211
  420.4 9.8 pad_maximum_fusion
  430.5 450.5 %reduce-scatter.5.cloned.1.call-done = f32[3,9,64,512]{3,2,1,0:T(8,128)} async-done(((f32[3,9,512,512]{3,2,1,0:T(8,128)}), f32[3,9,64,512]{3,2,1,0:T(8,128)}) %reduce-scatter.5.cloned.1.call-update) | async-done | bytes 3538960 | tf_op jit(solution)/shard_map/reduce_scatter | solution.py:230
  881.1 3.5 convert_element_type.110
  884.7 8.2 copy.75
  892.9 7.8 reshape.882
  903.5 1.5 reshape.884
  905.0 3.3 all-to-all-start
  908.4 2.4 collective-permute-start.10
  916.6 2.3 fusion.58
  921.9 1.5 convolution_add_fusion.4
  926.3 1.5 convolution_add_fusion.1
  927.8 2.0 reduce-scatter.7.cloned.1.call-done
  929.8 1.9 reshape.883
  933.9 2.4 fusion.38
  936.3 39.8 %psum.103 = f32[]{:T(128)} all-reduce(f32[]{:T(128)} %fusion.42), channel_id=1, replica_groups=mesh['maps'=8,'rows'=4] {'maps','rows'}, use_global_device_ids=true, to_apply=%region_27.28 | all-reduce | flops 1 | bytes 8 | tf_op jit(solution)/shard_map/psum | solution.py:234
  979.4 3.7 multiply_subtract_fusion
  (299 shorter events, 120.2 us)
Async XLA Ops:
  7.2 18.7 %copy-start = (bf16[1,12,32,512]{3,2,1,0:T(8,128)(2,1)S(1)}, bf16[1,12,32,512]{3,2,1,0:T(8,128)(2,1)}, u32[]{:S(2)}) copy-start(bf16[1,12,32,512]{3,2,1,0:T(8,128)(2,1)} %param.14) | copy-start | bytes 1179652
  8.0 9.4 collective-permute-start
  10.4 7.0 collective-permute-start.1
  13.2 62.8 %copy-start.56 = (f32[4]{0:T(128)}, f32[4]{0:T(128)S(1)}, u32[]{:S(2)}) copy-start(f32[4]{0:T(128)S(1)} %convolution_bitcast_fusion.27) | copy-start | bytes 52
  17.2 59.0 %copy-start.41 = (f32[1,1,512]{2,0,1:T(1,128)}, f32[1,1,512]{2,0,1:T(1,128)S(1)}, u32[]{:S(2)}) copy-start(f32[1,1,512]{2,0,1:T(1,128)S(1)} %get-tuple-element.98) | copy-start | bytes 6148
  17.2 69.2 %copy-start.34 = (f32[1,1,512]{2,0,1:T(1,128)}, f32[1,1,512]{2,0,1:T(1,128)S(1)}, u32[]{:S(2)}) copy-start(f32[1,1,512]{2,0,1:T(1,128)S(1)} %get-tuple-element.99) | copy-start | bytes 6148
  17.3 58.7 %copy-start.52 = (pred[1,4]{1,0:T(4,128)(4,1)}, pred[1,4]{1,0:T(4,128)(4,1)S(1)}, u32[]{:S(2)}) copy-start(pred[1,4]{1,0:T(4,128)(4,1)S(1)} %get-tuple-element.76) | copy-start | bytes 16
  21.4 57.7 %copy-start.21 = (bf16[1,24,16,128]{3,2,1,0:T(8,128)(2,1)S(1)}, bf16[1,24,16,128]{3,2,1,0:T(8,128)(2,1)}, u32[]{:S(2)}) copy-start(bf16[1,24,16,128]{3,2,1,0:T(8,128)(2,1)} %param.21) | copy-start | bytes 294916
  76.0 20.0 %copy-start.31 = (f32[1,512]{1,0:T(1,128)}, f32[1,512]{1,0:T(1,128)S(1)}, u32[]{:S(2)}) copy-start(f32[1,512]{1,0:T(1,128)S(1)} %fusion.267) | copy-start | bytes 6148
  76.2 19.8 %copy-start.28 = (f32[1,512]{1,0:T(1,128)}, f32[1,512]{1,0:T(1,128)S(1)}, u32[]{:S(2)}) copy-start(f32[1,512]{1,0:T(1,128)S(1)} %fusion.227) | copy-start | bytes 6148
  76.5 10.5 %collective-permute-start.2 = (bf16[1,1,32,512]{3,2,1,0:T(8,128)(2,1)S(1)}, bf16[1,1,32,512]{3,2,1,0:T(8,128)(2,1)S(1)}, u32[]{:S(2)}, u32[]{:S(2)}) collective-permute-start(bf16[1,1,32,512]{3,2,1,0:T(8,128)(2,1)S(1)} %get-tuple-element.86), channel_id=1, source_target_pairs={{0,1},{1,2},{2,3},{4,5},{5,6},{6,7},{8,9},{9,10},{10,11},{12,13},{... | collective-permute-start | bytes 98312 | tf_op jit(solution)/shard_map/ppermute | solution.py:26
  77.8 9.2 collective-permute-start.3
  79.9 71.8 %all-to-all-start.1 = ((bf16[1,24,16,128]{3,2,0,1:T(8,128)(2,1)}), bf16[1,24,16,128]{3,2,0,1:T(8,128)(2,1)}, u32[]{:S(2)}, u32[]{:S(2)}) async-start(bf16[1,24,16,128]{3,2,0,1:T(8,128)(2,1)} %bitcast_multiply_fusion.1), calls=%async_computation.1 | async-start | bytes 196608 | tf_op jit(solution)/shard_map/all_to_all | solution.py:181
  86.4 794.7 %reduce-scatter.5.cloned.1.call-start = ((), (), s32[]{:S(2)}) async-start(), calls=%async_computation.4 | async-start | bytes 31850496 | tf_op jit(solution)/shard_map/reduce_scatter | solution.py:230
  100.3 65.1 %copy-start.3 = (f32[12,32,512]{2,1,0:T(8,128)}, f32[12,32,512]{2,1,0:T(8,128)S(1)}, u32[]{:S(2)}) copy-start(f32[12,32,512]{2,1,0:T(8,128)S(1)} %get-tuple-element.115) | copy-start | bytes 2359300
  143.6 150.1 %copy-start.33 = (f32[1,512]{1,0:T(1,128)}, f32[1,512]{1,0:T(1,128)S(1)}, u32[]{:S(2)}) copy-start(f32[1,512]{1,0:T(1,128)S(1)} %fusion.264) | copy-start | bytes 6148
  144.5 149.2 %copy-start.30 = (f32[1,512]{1,0:T(1,128)}, f32[1,512]{1,0:T(1,128)S(1)}, u32[]{:S(2)}) copy-start(f32[1,512]{1,0:T(1,128)S(1)} %fusion.224) | copy-start | bytes 6148
  148.1 17.3 %collective-permute-start.4 = (bf16[1,1,32,512]{3,2,1,0:T(8,128)(2,1)}, bf16[1,1,32,512]{3,2,1,0:T(8,128)(2,1)}, u32[]{:S(2)}, u32[]{:S(2)}) collective-permute-start(bf16[1,1,32,512]{3,2,1,0:T(8,128)(2,1)} %get-tuple-element.84), channel_id=1, source_target_pairs={{0,1},{1,2},{2,3},{4,5},{5,6},{6,7},{8,9},{9,10},{10,11},{12,13},{... | collective-permute-start | bytes 98312 | tf_op jit(solution)/shard_map/ppermute | solution.py:26
  150.2 15.2 %collective-permute-start.5 = (bf16[1,1,32,512]{3,2,1,0:T(8,128)(2,1)}, bf16[1,1,32,512]{3,2,1,0:T(8,128)(2,1)}, u32[]{:S(2)}, u32[]{:S(2)}) collective-permute-start(bf16[1,1,32,512]{3,2,1,0:T(8,128)(2,1)} %get-tuple-element.85), channel_id=1, source_target_pairs={{1,0},{2,1},{3,2},{5,4},{6,5},{7,6},{9,8},{10,9},{11,10},{13,12},{... | collective-permute-start | bytes 98312 | tf_op jit(solution)/shard_map/ppermute | solution.py:29
  171.2 52.6 %copy-start.57 = (f32[4]{0:T(128)S(1)}, f32[4]{0:T(128)}, u32[]{:S(2)}) copy-start(f32[4]{0:T(128)} %copy-done.56) | copy-start | bytes 52
  171.2 52.6 %copy-start.53 = (pred[1,4]{1,0:T(4,128)(4,1)S(1)}, pred[1,4]{1,0:T(4,128)(4,1)}, u32[]{:S(2)}) copy-start(pred[1,4]{1,0:T(4,128)(4,1)} %copy-done.52) | copy-start | bytes 16
  171.2 53.0 %copy-start.38 = (f32[1,1,512]{2,0,1:T(1,128)S(1)}, f32[1,1,512]{2,0,1:T(1,128)}, u32[]{:S(2)}) copy-start(f32[1,1,512]{2,0,1:T(1,128)} %get-tuple-element.96) | copy-start | bytes 6148
  171.2 53.0 %copy-start.55 = (f32[1,1,512]{2,0,1:T(1,128)S(1)}, f32[1,1,512]{2,0,1:T(1,128)}, u32[]{:S(2)}) copy-start(f32[1,1,512]{2,0,1:T(1,128)} %get-tuple-element.101) | copy-start | bytes 6148
  269.5 8.7 collective-permute-start.6
  270.9 10.9 %collective-permute-start.7 = (bf16[1,1,32,512]{3,2,1,0:T(8,128)(2,1)S(1)}, bf16[1,1,32,512]{3,2,1,0:T(8,128)(2,1)S(1)}, u32[]{:S(2)}, u32[]{:S(2)}) collective-permute-start(bf16[1,1,32,512]{3,2,1,0:T(8,128)(2,1)S(1)} %get-tuple-element.83), channel_id=1, source_target_pairs={{1,0},{2,1},{3,2},{5,4},{6,5},{7,6},{9,8},{10,9},{11,10},{13,12},{... | collective-permute-start | bytes 98312 | tf_op jit(solution)/shard_map/ppermute | solution.py:29
  287.8 54.8 %copy-start.6 = (f32[12,32,512]{2,1,0:T(8,128)S(1)}, f32[12,32,512]{2,1,0:T(8,128)}, u32[]{:S(2)}) copy-start(f32[12,32,512]{2,1,0:T(8,128)} %copy-done.3) | copy-start | bytes 2359300
  344.5 7.9 collective-permute-start.8
  346.0 9.9 %collective-permute-start.9 = (bf16[1,1,32,512]{3,2,1,0:T(8,128)(2,1)S(1)}, bf16[1,1,32,512]{3,2,1,0:T(8,128)(2,1)S(1)}, u32[]{:S(2)}, u32[]{:S(2)}) collective-permute-start(bf16[1,1,32,512]{3,2,1,0:T(8,128)(2,1)S(1)} %get-tuple-element.81), channel_id=1, source_target_pairs={{1,0},{2,1},{3,2},{5,4},{6,5},{7,6},{9,8},{10,9},{11,10},{13,12},{... | collective-permute-start | bytes 98312 | tf_op jit(solution)/shard_map/ppermute | solution.py:29
  362.0 50.8 %copy-start.54 = (pred[1,4]{1,0:T(4,128)(4,1)S(1)}, pred[1,4]{1,0:T(4,128)(4,1)}, u32[]{:S(2)}) copy-start(pred[1,4]{1,0:T(4,128)(4,1)} %copy-done.52) | copy-start | bytes 16
  362.0 50.7 %copy-start.58 = (f32[4]{0:T(128)S(1)}, f32[4]{0:T(128)}, u32[]{:S(2)}) copy-start(f32[4]{0:T(128)} %copy-done.56) | copy-start | bytes 52
  362.0 51.1 %copy-start.44 = (f32[512]{0:T(512)S(1)}, f32[512]{0:T(512)}, u32[]{:S(2)}) copy-start(f32[512]{0:T(512)} %mul.457) | copy-start | bytes 6148
  366.4 47.5 %copy-start.16 = (bf16[1,1,32,512]{3,2,1,0:T(8,128)(2,1)S(1)}, bf16[1,1,32,512]{3,2,1,0:T(8,128)(2,1)}, u32[]{:S(2)}) copy-start(bf16[1,1,32,512]{3,2,1,0:T(8,128)(2,1)} %copy-done.15) | copy-start | bytes 98308
  430.2 499.6 %reduce-scatter.7.cloned.1.call-start = ((), (), s32[]{:S(2)}) async-start(), calls=%async_computation.5 | async-start | bytes 2293760
  884.6 16.8 %copy-start.49 = (f32[4,512]{1,0:T(4,128)S(1)}, f32[4,512]{1,0:T(4,128)}, u32[]{:S(2)}) copy-start(f32[4,512]{1,0:T(4,128)} %copy-done.48) | copy-start | bytes 24580
  884.6 16.9 %copy-start.47 = (f32[4,512]{1,0:T(4,128)S(1)}, f32[4,512]{1,0:T(4,128)}, u32[]{:S(2)}) copy-start(f32[4,512]{1,0:T(4,128)} %copy-done.46) | copy-start | bytes 24580
  884.6 16.9 %copy-start.10 = (bf16[1,12,32,512]{3,2,1,0:T(8,128)(2,1)S(1)}, bf16[1,12,32,512]{3,2,1,0:T(8,128)(2,1)}, u32[]{:S(2)}) copy-start(bf16[1,12,32,512]{3,2,1,0:T(8,128)(2,1)} %get-tuple-element.77) | copy-start | bytes 1179652
  884.6 18.0 %copy-start.11 = (pred[1,6,16,512]{3,2,1,0:T(8,128)(4,1)S(1)}, pred[1,6,16,512]{3,2,1,0:T(8,128)(4,1)}, u32[]{:S(2)}) copy-start(pred[1,6,16,512]{3,2,1,0:T(8,128)(4,1)} %get-tuple-element.68) | copy-start | bytes 147460
  884.6 18.0 %copy-start.12 = (pred[1,6,16,512]{3,2,1,0:T(8,128)(4,1)S(1)}, pred[1,6,16,512]{3,2,1,0:T(8,128)(4,1)}, u32[]{:S(2)}) copy-start(pred[1,6,16,512]{3,2,1,0:T(8,128)(4,1)} %get-tuple-element.91) | copy-start | bytes 147460
  884.6 18.0 %copy-start.13 = (pred[1,6,16,512]{3,2,1,0:T(8,128)(4,1)S(1)}, pred[1,6,16,512]{3,2,1,0:T(8,128)(4,1)}, u32[]{:S(2)}) copy-start(pred[1,6,16,512]{3,2,1,0:T(8,128)(4,1)} %get-tuple-element.93) | copy-start | bytes 147460
  884.6 18.0 %copy-start.14 = (pred[1,6,16,512]{3,2,1,0:T(8,128)(4,1)S(1)}, pred[1,6,16,512]{3,2,1,0:T(8,128)(4,1)}, u32[]{:S(2)}) copy-start(pred[1,6,16,512]{3,2,1,0:T(8,128)(4,1)} %get-tuple-element.95) | copy-start | bytes 147460
  884.6 23.6 %copy-start.51 = (f32[4,512]{1,0:T(4,128)S(1)}, f32[4,512]{1,0:T(4,128)}, u32[]{:S(2)}) copy-start(f32[4,512]{1,0:T(4,128)} %get-tuple-element.50) | copy-start | bytes 24580
  884.7 23.7 %copy-start.50 = (f32[4,512]{1,0:T(4,128)S(1)}, f32[4,512]{1,0:T(4,128)}, u32[]{:S(2)}) copy-start(f32[4,512]{1,0:T(4,128)} %get-tuple-element.51) | copy-start | bytes 24580
  905.0 7.7 all-to-all-start
  908.4 6.4 collective-permute-start.10
  910.8 4.2 collective-permute-start.11
  920.4 57.1 %copy-start.22 = (f32[2,3,512]{2,0,1:T(2,128)S(1)}, f32[2,3,512]{2,0,1:T(2,128)}, u32[]{:S(2)}) copy-start(f32[2,3,512]{2,0,1:T(2,128)} %param.16) | copy-start | bytes 36868
  920.4 57.1 %copy-start.39 = (f32[2,3,512]{2,0,1:T(2,128)S(1)}, f32[2,3,512]{2,0,1:T(2,128)}, u32[]{:S(2)}) copy-start(f32[2,3,512]{2,0,1:T(2,128)} %param.27) | copy-start | bytes 36868
  920.5 57.1 %copy-start.40 = (f32[2,3,512]{2,0,1:T(2,128)S(1)}, f32[2,3,512]{2,0,1:T(2,128)}, u32[]{:S(2)}) copy-start(f32[2,3,512]{2,0,1:T(2,128)} %param.26) | copy-start | bytes 36868
  (33 other events, 192.1 us)
Sparse Core Ops, SparseCore 0:
  430.3 450.7 reduce-scatter.4
  900.8 28.9 reduce-scatter.6
where the time goes:
time: 1000 us; the launch traced here: 992 us
  waiting for transfers between devices  453 us (45%)
  blocking collectives  294 us (29%)
  matrix products  104 us (10%)
  local copies, waits for them, and re-layouts  51.9 us (5%)
  other arithmetic  39.5 us (4%)
  starting transfers between devices  29.6 us (3%)
  between operations  20.1 us (2%)
    reduce_scatter x1, waiting for transfers between devices, local(): lax.psum_scatter(kernel_grad, 'maps', scatter_dimension=2, tiled=True)  451 us
    psum x3, blocking collectives, local(): sums, squares = lax.psum((sums, squares), ('maps', 'rows'))  128 us
    psum x3, blocking collectives, local(): first_sum, second_sum = lax.psum((first_sum, second_sum), ('maps', 'rows'))  127 us
    dot_general x27, matrix products, transpose_taps(): jnp.einsum('mhwd,cd->mhwc', piece, kernel[tap_row * 3 + tap_col], preferr...  42.6 us
    dot_general x27, matrix products, conv_taps(): jnp.einsum('mhwc,cd->mhwd', piece, kernel[tap_row * 3 + tap_col], preferr...  39.9 us
    psum x1, blocking collectives, local(): shard_squares = lax.psum(jnp.sum(shard_grad * shard_grad), ('maps', 'rows'))  39.8 us
    unnamed x139, local copies, waits for them, and re-layouts  34.5 us
  transfers between devices with their start and end apart: 16, of which 3 were waited for; matrix products, arithmetic and copies ran while one was open for 7% of the time, Pallas kernels for 0%

commit v1 on v0

v1 whole, which is shorter than its diff:
```python
import functools
import math

import jax
import jax.numpy as jnp
from jax import lax
from jax.experimental import pallas as pl
from jax.experimental.pallas import tpu as pltpu
from jax.sharding import PartitionSpec as P

DOMAINS = 4
norm_epsilon = 1e-05
clip_limit = 1.0
first_decay = 0.9
second_decay = 0.999
adam_epsilon = 1e-08
norm_rate = 0.5
weight_decay = 0.01

HALO = 6
AXES = ("maps", "rows")
F32 = jnp.float32
BF16 = jnp.bfloat16


class Sizes:
    def __init__(self, maps, bands, rows, width, channels):
        self.maps = maps
        self.bands = bands
        self.devices = maps * bands
        self.rows = rows
        self.width = width
        self.channels = channels
        self.height = rows * bands
        self.short_height = 2 * (self.height * 7 // 16)
        self.short_width = 2 * (width * 13 // 32)
        self.pixels = rows * width
        self.quarter = channels // bands


def spec_vmem():
    return pl.BlockSpec(memory_space=pltpu.VMEM)


def spec_smem():
    return pl.BlockSpec(memory_space=pltpu.SMEM)


def spec_any():
    return pl.BlockSpec(memory_space=pl.ANY)


def params(megabytes):
    return pltpu.CompilerParams(vmem_limit_bytes=megabytes << 20)


def area_of(sz, kind):
    return jnp.where(kind == 1, sz.height * sz.short_width, sz.short_height * sz.width)


def own_count(sz, kind_ref, domain_ref, place_ref):
    own = domain_ref[place_ref[0]]
    total = jnp.int32(0)
    for m in range(sz.maps):
        total = total + jnp.where(domain_ref[m] == own, area_of(sz, kind_ref[m]), 0)
    return total.astype(F32)


def own_sums(sz, gathered_ref, domain_ref, place_ref):
    own = domain_ref[place_ref[0]]
    total = jnp.zeros(gathered_ref.shape[1:], F32)
    for m in range(sz.maps):
        part = gathered_ref[m * sz.bands]
        for b in range(1, sz.bands):
            part = part + gathered_ref[m * sz.bands + b]
        total = total + jnp.where(domain_ref[m] == own, part, 0.0)
    return total


def all_sums(sz, gathered_ref):
    total = gathered_ref[0]
    for k in range(1, sz.devices):
        total = total + gathered_ref[k]
    return total


def split_rows(tile, channels):
    first = jnp.concatenate([tile[k : k + 1, :] for k in range(4)], axis=1)
    second = jnp.concatenate([tile[k : k + 1, :] for k in range(4, 8)], axis=1)
    return first, second


def join_rows(first, second):
    lanes = first.shape[1] // 4
    return jnp.concatenate(
        [row[:, k * lanes : (k + 1) * lanes] for row in (first, second) for k in range(4)], axis=0
    )


def valid_mask(sz, kind_ref, place_ref, first_row, count_rows):
    shape = (count_rows * sz.width, sz.channels)
    pixel = lax.broadcasted_iota(jnp.int32, shape, 0)
    row = pixel // sz.width + (place_ref[1] * sz.rows + first_row)
    col = pixel % sz.width
    tall = kind_ref[place_ref[0]] == 1
    limit = jnp.where(tall, sz.height, sz.short_height)
    wide = jnp.where(tall, sz.short_width, sz.width)
    return (row >= 0) & (row < limit) & (col < wide)


def store_shifted(sz, x3_ref, value, reverse):
    rows = value.shape[0]
    col = lax.broadcasted_iota(jnp.int32, value.shape, 0) % sz.width
    before = jnp.where(col == 0, 0.0, pltpu.roll(value, 1, 0))
    after = jnp.where(col == sz.width - 1, 0.0, pltpu.roll(value, rows - 1, 0))
    if reverse:
        before, after = after, before
    c = sz.channels
    x3_ref[:, 0:c] = before.astype(BF16)
    x3_ref[:, c : 2 * c] = value.astype(BF16)
    x3_ref[:, 2 * c : 3 * c] = after.astype(BF16)


def start_weights(weights_ref, buffer_ref, sems, layer, order):
    copies = {}
    for i in order:
        copies[i] = pltpu.make_async_copy(
            weights_ref.at[layer, pl.ds(3 * i, 3)], buffer_ref.at[pl.ds(3 * i, 3)], sems.at[i]
        )
        copies[i].start()
    return copies


def conv_forward(sz, x3_ref, buffer_ref, copies, out_ref, out_rows):
    c = sz.channels
    n = out_rows * sz.width
    for i in range(3):
        copies[i].wait()
        lhs = x3_ref[i * sz.width : i * sz.width + n, :]
        rhs = buffer_ref[3 * i : 3 * i + 3].reshape(3 * c, c)
        term = jnp.dot(lhs, rhs, preferred_element_type=F32)
        if i == 0:
            out_ref[...] = term
        else:
            out_ref[...] += term


def conv_backward(sz, x3_ref, buffer_ref, copies, acc_ref, out_rows):
    c = sz.channels
    n = out_rows * sz.width
    for i in (0, 1, 2):
        copies[i].wait()
        for j in range(3):
            lhs = x3_ref[(2 - i) * sz.width : (2 - i) * sz.width + n, j * c : (j + 1) * c]
            term = lax.dot_general(
                lhs,
                buffer_ref[3 * i + j],
                (((1,), (1,)), ((), ())),
                preferred_element_type=F32,
            )
            if i == 0 and j == 0:
                acc_ref[...] = term
            else:
                acc_ref[...] += term


def put_stats(sz, first, second, out_ref):
    tile = join_rows(first, second)
    out_ref[...] = jnp.broadcast_to(tile[None], out_ref.shape)


def sigmoid(v):
    return 1.0 / (1.0 + jnp.exp(-v))


def kernel_first(sz, kind_ref, domain_ref, place_ref, up_ref, x_ref, down_ref, weights_ref,
                 conv_ref, stats_ref, x3_ref, buffer_ref, sems):
    copies = start_weights(weights_ref, buffer_ref, sems, 0, (0, 1, 2))
    value = jnp.concatenate([up_ref[...], x_ref[...], down_ref[...]], axis=0).astype(F32)
    store_shifted(sz, x3_ref, value, False)
    rows = sz.rows + 2 * HALO - 2
    conv_forward(sz, x3_ref, buffer_ref, copies, conv_ref, rows)
    start = (HALO - 1) * sz.width
    centre = conv_ref[start : start + sz.pixels, :]
    masked = jnp.where(valid_mask(sz, kind_ref, place_ref, 0, sz.rows), centre, 0.0)
    put_stats(
        sz,
        jnp.sum(masked, axis=0, keepdims=True),
        jnp.sum(masked * centre, axis=0, keepdims=True),
        stats_ref,
    )


def norm_of(sz, gathered_ref, kind_ref, domain_ref, place_ref):
    count = own_count(sz, kind_ref, domain_ref, place_ref)
    tile = own_sums(sz, gathered_ref, domain_ref, place_ref)
    total, squares = split_rows(tile / count, sz.channels)
    return total, lax.rsqrt(squares - total * total + norm_epsilon)


def kernel_forward(sz, layer, kind_ref, domain_ref, place_ref, before_ref, gathered_ref, norm_ref, weights_ref,
                   conv_ref, stats_ref, act_ref, moments_ref, x3_ref, buffer_ref, sems):
    copies = start_weights(weights_ref, buffer_ref, sems, layer, (0, 1, 2))
    mean, inverse = norm_of(sz, gathered_ref, kind_ref, domain_ref, place_ref)
    moments_ref[...] = join_rows(mean, inverse)
    halo = HALO - layer
    rows = sz.rows + 2 * halo
    gain = norm_ref[0, layer - 1 : layer, :]
    shift = norm_ref[1, layer - 1 : layer, :]
    shifted = gain * ((before_ref[...] - mean) * inverse) + shift
    act = jnp.where(
        valid_mask(sz, kind_ref, place_ref, -halo, rows), shifted * sigmoid(shifted), 0.0
    )
    act_ref[...] = act[halo * sz.width : halo * sz.width + sz.pixels, :].astype(BF16)
    store_shifted(sz, x3_ref, act, False)
    conv_forward(sz, x3_ref, buffer_ref, copies, conv_ref, rows - 2)
    start = (halo - 1) * sz.width
    centre = conv_ref[start : start + sz.pixels, :]
    masked = jnp.where(valid_mask(sz, kind_ref, place_ref, 0, sz.rows), centre, 0.0)
    put_stats(
        sz,
        jnp.sum(masked, axis=0, keepdims=True),
        jnp.sum(masked * centre, axis=0, keepdims=True),
        stats_ref,
    )


def kernel_pool(sz, kind_ref, domain_ref, place_ref, before_ref, gathered_ref, norm_ref, index_ref, index_up_ref,
                index_down_ref, cotangent_ref, label_ref, pooled_ref, stats_ref, moments_ref, grad_ref,
                spread_ref, act_ref):
    c, w, q = sz.channels, sz.width, sz.quarter
    half = w // 2
    mean, inverse = norm_of(sz, gathered_ref, kind_ref, domain_ref, place_ref)
    moments_ref[...] = join_rows(mean, inverse)
    gain = norm_ref[0, 2:3, :]
    shift = norm_ref[1, 2:3, :]
    halo = HALO - 3
    rows = sz.rows + 2 * halo
    valid = valid_mask(sz, kind_ref, place_ref, -halo, rows)
    normed = (before_ref[...] - mean) * inverse
    shifted = gain * normed + shift
    sig = sigmoid(shifted)
    act = jnp.where(valid, shifted * sig, 0.0)
    groups = c // 128
    for g in range(groups):
        act_ref[g] = act[:, g * 128 : (g + 1) * 128]
    windows = sz.rows // 2
    for p in range(windows):
        index = index_ref[p * half : (p + 1) * half, :]
        result = jnp.zeros(index.shape, F32)
        for corner in range(4):
            start = (halo + 2 * p + corner // 2) * w + corner % 2
            taken = jnp.concatenate(
                [act_ref[g, pl.ds(start, half, stride=2), :] for g in range(groups)], axis=1
            )
            result = jnp.where(index == corner, taken, result)
        for b in range(sz.bands):
            pooled_ref[b, p * half : (p + 1) * half, :] = result[:, b * q : (b + 1) * q].astype(BF16)
    for p in range(windows + 4):
        if p < 2:
            index = index_up_ref[p * half : (p + 1) * half, :]
        elif p < windows + 2:
            index = index_ref[(p - 2) * half : (p - 1) * half, :]
        else:
            index = index_down_ref[(p - windows - 2) * half : (p - windows - 1) * half, :]
        given = jnp.concatenate(
            [cotangent_ref[b, p * half : (p + 1) * half, :] for b in range(sz.bands)], axis=1
        ).astype(F32)
        given = given * jnp.concatenate([label_ref[p * half : (p + 1) * half, :]] * (c // 128), axis=1)
        for corner in range(4):
            start = (2 * p + corner // 2) * w + corner % 2
            placed = jnp.where(index == corner, given, 0.0)
            for g in range(groups):
                spread_ref[g, pl.ds(start, half, stride=2), :] = placed[:, g * 128 : (g + 1) * 128]
    upstream = jnp.concatenate([spread_ref[g, w : w + rows * w, :] for g in range(groups)], axis=1)
    grad = jnp.where(valid, upstream * (sig * (1.0 + shifted * (1.0 - sig))), 0.0)
    grad_ref[...] = grad
    centre = grad[halo * w : halo * w + sz.pixels, :]
    put_stats(
        sz,
        jnp.sum(centre, axis=0, keepdims=True),
        jnp.sum(centre * normed[halo * w : halo * w + sz.pixels, :], axis=0, keepdims=True),
        stats_ref,
    )


def conv_grad_of(sz, layer, halo, kind_ref, domain_ref, place_ref, grad, conv, moments_ref, gathered_ref, norm_ref):
    mean, inverse = split_rows(moments_ref[...], sz.channels)
    count = own_count(sz, kind_ref, domain_ref, place_ref)
    one, two = split_rows(own_sums(sz, gathered_ref, domain_ref, place_ref) / count, sz.channels)
    normed = (conv - mean) * inverse
    gain = norm_ref[0, layer : layer + 1, :]
    valid = valid_mask(sz, kind_ref, place_ref, -halo, sz.rows + 2 * halo)
    return jnp.where(valid, (gain * inverse) * (grad - one - normed * two), 0.0)


def kernel_backward(sz, layer, kind_ref, domain_ref, place_ref, grad_ref, conv_ref, moments_ref, gathered_ref,
                    norm_ref, weights_ref, conv_below_ref, moments_below_ref,
                    below_ref, stats_ref, conv_grad_ref, totals_ref, x3_ref, acc_ref, buffer_ref, sems):
    w = sz.width
    copies = start_weights(weights_ref, buffer_ref, sems, layer, (0, 1, 2))
    halo = layer + 1
    skip = (HALO - 1 - layer) - halo
    rows = sz.rows + 2 * halo
    totals_ref[...] = all_sums(sz, gathered_ref)
    conv = conv_ref[skip * w : (skip + rows) * w, :]
    conv_grad = conv_grad_of(
        sz, layer, halo, kind_ref, domain_ref, place_ref, grad_ref[...], conv, moments_ref, gathered_ref, norm_ref
    )
    conv_grad_ref[...] = conv_grad[halo * w : halo * w + sz.pixels, :].astype(BF16)
    store_shifted(sz, x3_ref, conv_grad, True)
    conv_backward(sz, x3_ref, buffer_ref, copies, acc_ref, rows - 2)
    below = layer - 1
    mean, inverse = split_rows(moments_below_ref[...], sz.channels)
    gain = norm_ref[0, below : below + 1, :]
    shift = norm_ref[1, below : below + 1, :]
    skip_below = (HALO - 1 - below) - (halo - 1)
    normed = (conv_below_ref[skip_below * w : (skip_below + rows - 2) * w, :] - mean) * inverse
    shifted = gain * normed + shift
    sig = sigmoid(shifted)
    valid = valid_mask(sz, kind_ref, place_ref, -(halo - 1), rows - 2)
    grad = jnp.where(valid, acc_ref[...] * (sig * (1.0 + shifted * (1.0 - sig))), 0.0)
    below_ref[...] = grad
    start = (halo - 1) * w
    centre = grad[start : start + sz.pixels, :]
    put_stats(
        sz,
        jnp.sum(centre, axis=0, keepdims=True),
        jnp.sum(centre * normed[start : start + sz.pixels, :], axis=0, keepdims=True),
        stats_ref,
    )


def kernel_last_grad(sz, kind_ref, domain_ref, place_ref, grad_ref, conv_ref, moments_ref, gathered_ref,
                     norm_ref, conv_grad_ref, chunks_ref, totals_ref):
    w, q = sz.width, sz.quarter
    totals_ref[...] = all_sums(sz, gathered_ref)
    skip = HALO - 2
    rows = sz.rows + 2
    conv_grad = conv_grad_of(
        sz, 0, 1, kind_ref, domain_ref, place_ref, grad_ref[...], conv_ref[skip * w : (skip + rows) * w, :],
        moments_ref, gathered_ref, norm_ref,
    )
    conv_grad_ref[...] = conv_grad
    centre = conv_grad[w : w + sz.pixels, :].astype(BF16)
    for b in range(sz.bands):
        chunks_ref[b] = centre[:, b * q : (b + 1) * q]


def kernel_input_grad(sz, conv_grad_ref, weights_ref, out_ref, x3_ref, acc_ref, buffer_ref, sems):
    copies = start_weights(weights_ref, buffer_ref, sems, 0, (0, 1, 2))
    store_shifted(sz, x3_ref, conv_grad_ref[...], True)
    conv_backward(sz, x3_ref, buffer_ref, copies, acc_ref, sz.rows)
    out_ref[...] = acc_ref[...].astype(BF16)


def kernel_weight_grad(sz, split, place_ref, act_ref, conv_grad_ref, out_ref, x9_ref, part_ref, sem):
    w, q, c = sz.width, sz.quarter, sz.channels
    pixels = sz.height * w
    if split:
        copy = pltpu.make_async_copy(
            conv_grad_ref.at[:, pl.ds(pl.multiple_of(place_ref[1] * q, q), q)], part_ref, sem
        )
        copy.start()
        copy.wait()
        value = part_ref[...].astype(F32)
    else:
        value = conv_grad_ref[...].astype(F32)
    col = lax.broadcasted_iota(jnp.int32, value.shape, 0) % w
    before = jnp.where(col == 0, 0.0, pltpu.roll(value, 1, 0)).astype(BF16)
    after = jnp.where(col == w - 1, 0.0, pltpu.roll(value, pixels - 1, 0)).astype(BF16)
    value = value.astype(BF16)
    blank = jnp.zeros((w, q), BF16)
    for i in range(3):
        for j in range(3):
            piece = (after, value, before)[j]
            lanes = slice((3 * i + j) * q, (3 * i + j + 1) * q)
            if i == 0:
                x9_ref[0 : pixels - w, lanes] = piece[w:, :]
                x9_ref[pixels - w : pixels, lanes] = blank
            elif i == 1:
                x9_ref[:, lanes] = piece
            else:
                x9_ref[w:pixels, lanes] = piece[: pixels - w, :]
                x9_ref[0:w, lanes] = blank
    share = c // sz.maps
    for i in range(3):
        term = lax.dot_general(
            act_ref[...],
            x9_ref[:, 3 * i * q : 3 * (i + 1) * q],
            (((0,), (0,)), ((), ())),
            preferred_element_type=F32,
        )
        for m in range(sz.maps):
            for j in range(3):
                out_ref[m, (3 * i + j) * share : (3 * i + j + 1) * share, :] = term[
                    m * share : (m + 1) * share, j * q : (j + 1) * q
                ].astype(out_ref.dtype)


def kernel_squares(sz, first_ref, second_ref, third_ref, totals2_ref, totals1_ref, totals0_ref,
                   shard_ref, squares_ref, norm_grad_ref):
    taps = third_ref.shape[0]
    received = first_ref[0].astype(F32)
    for m in range(1, sz.maps):
        received = received + first_ref[m].astype(F32)
    shard_ref[...] = received
    total = jnp.sum(received * received, axis=0, keepdims=True)
    for ref in (second_ref, third_ref):
        value = ref[...].astype(F32)
        total = total + jnp.sum(value * value, axis=0, keepdims=True)
    squares_ref[...] = jnp.broadcast_to(total[None], squares_ref.shape)
    for layer, ref in enumerate((totals0_ref, totals1_ref, totals2_ref)):
        shift_row, gain_row = split_rows(ref[...], sz.channels)
        norm_grad_ref[0, layer : layer + 1, :] = gain_row
        norm_grad_ref[1, layer : layer + 1, :] = shift_row


def adam(param, grad, first, second, rate, decay, scale, first_fix, second_fix):
    clipped = scale * grad
    first_new = first_decay * first + (1.0 - first_decay) * clipped
    second_new = second_decay * second + (1.0 - second_decay) * clipped * clipped
    update = first_new / first_fix / (jnp.sqrt(second_new / second_fix) + adam_epsilon)
    return first_new, second_new, param - rate * (update + decay * param)


def local(sz, block_input, conv_weights, norm_params, pool_index, task_mask, map_kind, map_domain, out_grad, step,
          conv_master, conv_moment1, conv_moment2, norm_moment1, norm_moment2):
    w, c, q = sz.width, sz.channels, sz.quarter
    half = w // 2
    n_maps, bands = sz.maps, sz.bands
    place = jnp.stack([lax.axis_index("maps"), lax.axis_index("rows")]).astype(jnp.int32)
    scalars = (map_kind, map_domain, place)
    smem3 = [spec_smem()] * 3
    forward = [(i, i + 1) for i in range(bands - 1)]
    backward = [(i + 1, i) for i in range(bands - 1)]
    x = block_input.reshape(sz.pixels, c)

    up = lax.ppermute(x[sz.pixels - HALO * w :], "rows", forward)
    down = lax.ppermute(x[: HALO * w], "rows", backward)

    def spread(stats):
        return lax.all_to_all(stats, AXES, 0, 0, tiled=True)

    stats_shape = jax.ShapeDtypeStruct((sz.devices, 8, c // 4), F32)
    tile_shape = jax.ShapeDtypeStruct((8, c // 4), F32)

    def pixel_shape(rows, dtype):
        return jax.ShapeDtypeStruct((rows * w, c), dtype)

    def conv_scratch(rows, acc_rows=None):
        shapes = [pltpu.VMEM((rows * w, 3 * c), BF16)]
        if acc_rows is not None:
            shapes.append(pltpu.VMEM((acc_rows * w, c), F32))
        return shapes + [pltpu.VMEM((9, c, c), BF16), pltpu.SemaphoreType.DMA((3,))]

    act_0 = lax.all_gather(x, "rows", axis=0, tiled=True)
    rows = sz.rows + 2 * HALO
    conv0, stats0 = pl.pallas_call(
        functools.partial(kernel_first, sz),
        out_shape=(pixel_shape(rows - 2, F32), stats_shape),
        in_specs=smem3 + [spec_vmem()] * 3 + [spec_any()],
        out_specs=(spec_vmem(), spec_vmem()),
        scratch_shapes=conv_scratch(rows),
        compiler_params=params(40),
        name="first",
    )(*scalars, up, x, down, conv_weights)
    gathered = spread(stats0)

    index = pool_index.reshape(sz.pixels // 4, c)
    index_up = lax.ppermute(index[sz.pixels // 4 - 2 * half :], "rows", forward)
    index_down = lax.ppermute(index[: 2 * half], "rows", backward)
    windows = sz.rows // 2
    padded = jnp.pad(out_grad.reshape(sz.height // 2 * half, q), ((2 * half, 2 * half), (0, 0)))
    pieces = jnp.stack(
        [padded[b * windows * half : (b * windows + windows + 4) * half] for b in range(bands)]
    )
    cotangent = lax.all_to_all(pieces, "rows", 0, 0, tiled=True)
    labels = jnp.pad(task_mask.reshape(sz.height // 2 * half), (2 * half, 2 * half)).astype(F32)
    labels = lax.dynamic_slice_in_dim(labels, place[1] * windows * half, (windows + 4) * half)
    labels = jnp.broadcast_to(labels[:, None], ((windows + 4) * half, 128))

    convs = [conv0]
    moments = []
    acts = [act_0]
    for layer in (1, 2):
        rows = sz.rows + 2 * (HALO - layer)
        conv, stats, act, moment = pl.pallas_call(
            functools.partial(kernel_forward, sz, layer),
            out_shape=(pixel_shape(rows - 2, F32), stats_shape, pixel_shape(sz.rows, BF16), tile_shape),
            in_specs=smem3 + [spec_vmem()] * 3 + [spec_any()],
            out_specs=(spec_vmem(),) * 4,
            scratch_shapes=conv_scratch(rows),
            compiler_params=params(40),
            name="forward",
        )(*scalars, convs[-1], gathered, norm_params, conv_weights)
        convs.append(conv)
        moments.append(moment)
        gathered = spread(stats)
        acts.append(lax.all_gather(act, "rows", axis=0, tiled=True))

    rows = sz.rows + 2 * (HALO - 3)
    pooled_chunks, stats, moment, grad = pl.pallas_call(
        functools.partial(kernel_pool, sz),
        out_shape=(
            jax.ShapeDtypeStruct((bands, sz.pixels // 4, q), BF16),
            stats_shape,
            tile_shape,
            pixel_shape(rows, F32),
        ),
        in_specs=smem3 + [spec_vmem()] * 8,
        out_specs=(spec_vmem(),) * 4,
        scratch_shapes=[pltpu.VMEM((c // 128, (rows + 2) * w, 128), F32), pltpu.VMEM((c // 128, rows * w, 128), F32)],
        compiler_params=params(40),
        name="pool",
    )(*scalars, convs[2], gathered, norm_params, index, index_up, index_down, cotangent, labels)
    moments.append(moment)
    gathered = spread(stats)
    pooled = lax.all_to_all(pooled_chunks, "rows", 0, 0, tiled=True)

    totals = [None, None, None]
    shards = [None, None, None]
    whole = sz.height * w
    share = 9 * (c // n_maps)

    def weight_grad(act, conv_grad, split):
        return pl.pallas_call(
            functools.partial(kernel_weight_grad, sz, split),
            out_shape=jax.ShapeDtypeStruct((n_maps, share, q), BF16),
            in_specs=[spec_smem(), spec_vmem(), spec_any() if split else spec_vmem()],
            out_specs=spec_vmem(),
            scratch_shapes=[
                pltpu.VMEM((whole, 9 * q), BF16),
                pltpu.VMEM((whole, q), BF16),
                pltpu.SemaphoreType.DMA,
            ],
            compiler_params=params(40),
            name="weight_grad",
        )(place, act, conv_grad)

    for layer in (2, 1):
        halo = layer + 1
        rows = sz.rows + 2 * halo
        grad, stats, conv_grad, totals[layer] = pl.pallas_call(
            functools.partial(kernel_backward, sz, layer),
            out_shape=(pixel_shape(rows - 2, F32), stats_shape, pixel_shape(sz.rows, BF16), tile_shape),
            in_specs=smem3 + [spec_vmem()] * 5 + [spec_any()] + [spec_vmem()] * 2,
            out_specs=(spec_vmem(),) * 4,
            scratch_shapes=conv_scratch(rows, rows - 2),
            compiler_params=params(40),
            name="backward",
        )(
            *scalars, grad, convs[layer], moments[layer], gathered, norm_params, conv_weights,
            convs[layer - 1], moments[layer - 1],
        )
        gathered = spread(stats)
        whole_grad = lax.all_gather(conv_grad, "rows", axis=0, tiled=True)
        partial = weight_grad(acts[layer], whole_grad, True)
        shards[layer] = lax.psum_scatter(
            partial.reshape(n_maps * share, q), "maps", scatter_dimension=0, tiled=True
        )

    conv_grad, chunks, totals[0] = pl.pallas_call(
        functools.partial(kernel_last_grad, sz),
        out_shape=(
            pixel_shape(sz.rows + 2, F32),
            jax.ShapeDtypeStruct((bands, sz.pixels, q), BF16),
            tile_shape,
        ),
        in_specs=smem3 + [spec_vmem()] * 5,
        out_specs=(spec_vmem(),) * 3,
        compiler_params=params(40),
        name="last_grad",
    )(*scalars, grad, convs[0], moments[0], gathered, norm_params)
    whole_grad = lax.all_to_all(chunks, "rows", 0, 0, tiled=True).reshape(whole, q)
    input_grad = pl.pallas_call(
        functools.partial(kernel_input_grad, sz),
        out_shape=pixel_shape(sz.rows, BF16),
        in_specs=[spec_vmem(), spec_any()],
        out_specs=spec_vmem(),
        scratch_shapes=conv_scratch(sz.rows + 2, sz.rows),
        compiler_params=params(40),
        name="input_grad",
    )(conv_grad, conv_weights)
    partial = weight_grad(acts[0], whole_grad, False)
    received = lax.all_to_all(partial, "maps", 0, 0, tiled=True)

    shard0, squares, norm_grad = pl.pallas_call(
        functools.partial(kernel_squares, sz),
        out_shape=(
            jax.ShapeDtypeStruct((share, q), F32),
            jax.ShapeDtypeStruct((sz.devices, 1, q), F32),
            jax.ShapeDtypeStruct((2, 3, c), F32),
        ),
        in_specs=[spec_vmem()] * 6,
        out_specs=(spec_vmem(),) * 3,
        compiler_params=params(40),
        name="squares",
    )(received, shards[1], shards[2], totals[2], totals[1], totals[0])
    every = lax.all_to_all(squares, AXES, 0, 0, tiled=True)
    total = jnp.sqrt(jnp.sum(every) + jnp.sum(norm_grad * norm_grad))
    scale = jnp.minimum(1.0, clip_limit / total)
    count = step[0].astype(F32)
    first_fix = 1.0 - jnp.power(first_decay, count)
    second_fix = 1.0 - jnp.power(second_decay, count)
    rate = 2.0 / math.sqrt(9.0 * c)
    kernel_grad = jnp.stack([shard0, shards[1].astype(F32), shards[2].astype(F32)]).reshape(conv_master.shape)
    conv_first, conv_second, conv_new = adam(
        conv_master, kernel_grad, conv_moment1, conv_moment2, rate, weight_decay, scale, first_fix, second_fix
    )
    norm_first, norm_second, norm_new = adam(
        norm_params, norm_grad, norm_moment1, norm_moment2, norm_rate, 0.0, scale, first_fix, second_fix
    )
    return (
        pooled.reshape(1, sz.height // 2, half, q),
        input_grad.reshape(block_input.shape),
        total.reshape(1),
        conv_first,
        conv_second,
        conv_new,
        norm_first,
        norm_second,
        norm_new,
    )


def solution(mesh):
    def run(*args):
        bands = mesh.shape["rows"]
        maps = mesh.shape["maps"]
        shape = args[0].shape
        sz = Sizes(maps, bands, shape[1] // bands, shape[2], shape[3])
        return jax.shard_map(
            functools.partial(local, sz),
            mesh=mesh,
            in_specs=(
                P("maps", "rows", None, None),
                P(),
                P(),
                P("maps", "rows", None, None),
                P("maps", None, None),
                P(),
                P(),
                P("maps", None, None, "rows"),
                P(),
                P(None, None, "maps", "rows"),
                P(None, None, "maps", "rows"),
                P(None, None, "maps", "rows"),
                P(),
                P(),
            ),
            out_specs=(
                P("maps", None, None, "rows"),
                P("maps", "rows", None, None),
                P(),
                P(None, None, "maps", "rows"),
                P(None, None, "maps", "rows"),
                P(None, None, "maps", "rows"),
                P(),
                P(),
                P(),
            ),
            check_vma=False,
        )(*args)

    return run
```

time: 1000 us -> 367 us (0.37)
  waiting for transfers between devices: 453 us -> 183 us
  blocking collectives: 294 us -> 52.8 us
  matrix products: 104 us -> 0 us
  Pallas kernels: 0 us -> 49.2 us
  other arithmetic: 39.5 us -> 5.83 us
  local copies, waits for them, and re-layouts: 51.9 us -> 22 us
    reduce_scatter x1 -> x2, waiting for transfers between devices: 451 us -> 129 us  [local(): lax.psum_scatter(partial.reshape(n_maps * share, q), 'maps', scatter_dime...]
    psum x7 -> x0, blocking collectives: 294 us -> none  [the longest x3 128 us: local(): sums, squares = lax.psum((sums, squares), ('maps', 'rows'))]
    dot_general x94 -> x0, matrix products: 104 us -> none  [the longest x27 42.6 us: transpose_taps(): jnp.einsum('mhwd,cd->mhwc', piece, kernel[tap_row * 3 + tap_col], preferr...]
    all_to_all x0 -> x5, blocking collectives: none -> 52.8 us  [the longest x4 45.3 us: spread(): return lax.all_to_all(stats, AXES, 0, 0, tiled=True)]
    pallas_call x0 -> x12, Pallas kernels: none -> 49.2 us  [the longest x3 13.2 us: weight_grad(): pl.pallas_call(functools.partial(kernel_weight_grad, sz, split), out_shap...]
    all_gather x0 -> x5, waiting for transfers between devices: none -> 31.3 us  [the longest x2 19.7 us: local(): whole_grad = lax.all_gather(conv_grad, 'rows', axis=0, tiled=True)]
    all_to_all x2 -> x6, starting transfers between devices: 9.83 us -> 27.1 us  [the longest x2 11.3 us: spread(): return lax.all_to_all(stats, AXES, 0, 0, tiled=True)]
    all_to_all x2 -> x6, waiting for transfers between devices: 0.01 us -> 15.8 us  [the longest x2 9.38 us: spread(): return lax.all_to_all(stats, AXES, 0, 0, tiled=True)]
  transfers between devices with their start and end apart: 16 -> 17, of which waited for: 3 -> 9; matrix products, arithmetic and copies ran while one was open for 7% -> 1% of each run, Pallas kernels for 0% -> 8%
where the time goes in v1:
time: 367 us; the launch traced here: 366 us
  waiting for transfers between devices  183 us (50%)
  blocking collectives  52.8 us (14%)
  Pallas kernels  49.2 us (13%)
  starting transfers between devices  34.8 us (9%)
  local copies, waits for them, and re-layouts  22 us (6%)
  between operations  17.8 us (5%)
  other arithmetic  5.83 us (2%)
    reduce_scatter x2, waiting for transfers between devices, local(): lax.psum_scatter(partial.reshape(n_maps * share, q), 'maps', scatter_dime...  129 us
    all_to_all x4, blocking collectives, spread(): return lax.all_to_all(stats, AXES, 0, 0, tiled=True)  45.3 us
    unnamed x60, local copies, waits for them, and re-layouts  20 us
    all_gather x2, waiting for transfers between devices, local(): whole_grad = lax.all_gather(conv_grad, 'rows', axis=0, tiled=True)  19.7 us
    pallas_call x3, Pallas kernels, weight_grad(): pl.pallas_call(functools.partial(kernel_weight_grad, sz, split), out_shap...  13.2 us
    all_gather x1, waiting for transfers between devices, local(): act_0 = lax.all_gather(x, 'rows', axis=0, tiled=True)  11.5 us
    all_to_all x2, starting transfers between devices, spread(): return lax.all_to_all(stats, AXES, 0, 0, tiled=True)  11.3 us
    pallas_call x2, Pallas kernels, local(): pl.pallas_call(functools.partial(kernel_forward, sz, layer), out_shape=(p...  11 us
  transfers between devices with their start and end apart: 17, of which 9 were waited for; matrix products, arithmetic and copies ran while one was open for 1% of the time, Pallas kernels for 8%

profile of v1, /device:TPU:0, one launch (start us, length us, event | category | flops | bytes accessed | tf_op | source)
XLA Modules:
  0.0 365.8 jit_solution(16278605577406596007)
XLA Ops:
  7.2 1.1 fusion.8
  8.2 2.4 collective-permute-start
  10.6 1.3 collective-permute-start.1
  12.0 4.0 %collective-permute-done.1.down_ref = bf16[192,512]{1,0:T(8,128)(2,1)S(1)} collective-permute-done((bf16[192,512]{1,0:T(8,128)(2,1)S(1)}, bf16[192,512]{1,0:T(8,128)(2,1)S(1)}, u32[]{:S(2)}, u32[]{:S(2)}) %collective-permute-start.1) | collective-permute-done | bytes 196640 | tf_op jit(solution)/shard_map/ppermute | solution.py:440
  16.0 1.0 copy-done.2
  18.4 6.3 %first.1 = (f32[704,512]{1,0:T(8,128)S(1)}, f32[32,8,128]{2,1,0:T(8,128)}) custom-call(s32[8]{0:T(128)S(1)} %copy-done.17, s32[8]{0:T(128)S(1)} %copy-done.19, s32[2]{0:T(128)S(1)} %pad_add_fusion.place_ref, bf16[192,512]{1,0:T(8,128)(2,1)S(1)} %collective-permute-done.up_ref, bf16[384,512]{1,0:T(8,128)(2,1)S(1)} %bitcast.29, ...), custom_call_target="tpu_custom_call" | custom-call | tf_op jit(solution)/shard_map/first/pallas_call | solution.py:459
  24.6 8.7 %all-to-all-start = ((f32[32,8,128]{2,1,0:T(8,128)}), f32[32,8,128]{2,1,0:T(8,128)S(1)}, u32[]{:S(2)}, u32[]{:S(2)}) async-start(f32[32,8,128]{2,1,0:T(8,128)} %get-tuple-element.38), calls=%async_computation | async-start | bytes 262144 | tf_op jit(solution)/shard_map/all_to_all | solution.py:443
  33.4 8.2 %all-to-all-done.gathered_ref = f32[32,8,128]{2,1,0:T(8,128)S(1)} async-done(((f32[32,8,128]{2,1,0:T(8,128)}), f32[32,8,128]{2,1,0:T(8,128)S(1)}, u32[]{:S(2)}, u32[]{:S(2)}) %all-to-all-start) | async-done | bytes 131104 | tf_op jit(solution)/shard_map/all_to_all | solution.py:443
  41.5 5.3 %forward.2 = (f32[640,512]{1,0:T(8,128)S(1)}, f32[32,8,128]{2,1,0:T(8,128)S(1)}, bf16[384,512]{1,0:T(8,128)(2,1)}, f32[8,128]{1,0:T(8,128)S(1)}) custom-call(s32[8]{0:T(128)S(1)} %copy-done.18, s32[8]{0:T(128)S(1)} %copy-done.20, s32[2]{0:T(128)S(1)} %pad_add_fusion.place_ref, f32[704,512]{1,0:T(8,128)S(1)} %get-tuple-element.37.before_ref.conv_below_ref.conv_ref, ...), custom_call_target="tpu_custom_call" | custom-call | tf_op jit(solution)/shard_map/forward/pallas_call | solution.py:488
  46.8 10.0 %all_to_all.55.gathered_ref = f32[32,8,128]{2,1,0:T(8,128)S(1)} all-to-all(f32[32,8,128]{2,1,0:T(8,128)S(1)} %get-tuple-element.40), channel_id=1, replica_groups=mesh['maps'=8,'rows'=4] {'maps','rows'}, dimensions={0} | all-to-all | bytes 262144 | tf_op jit(solution)/shard_map/all_to_all | solution.py:443
  56.9 5.7 %forward.3 = (f32[576,512]{1,0:T(8,128)S(1)}, f32[32,8,128]{2,1,0:T(8,128)}, bf16[384,512]{1,0:T(8,128)(2,1)}, f32[8,128]{1,0:T(8,128)S(1)}) custom-call(s32[8]{0:T(128)S(1)} %copy-done.18, s32[8]{0:T(128)S(1)} %copy-done.20, s32[2]{0:T(128)S(1)} %pad_add_fusion.place_ref, f32[640,512]{1,0:T(8,128)S(1)} %get-tuple-element.39.before_ref.conv_below_ref.conv_ref, ...), custom_call_target="tpu_custom_call" | custom-call | tf_op jit(solution)/shard_map/forward/pallas_call | solution.py:488
  62.5 1.0 copy-done
  63.7 7.5 %all_to_all.56.cotangent_ref = bf16[4,160,128]{2,1,0:T(8,128)(2,1)S(1)} all-to-all(bf16[4,160,128]{2,1,0:T(8,128)(2,1)S(1)} %pad_maximum_fusion), channel_id=1, replica_groups=mesh['maps'=8,'rows'=4] {'rows'}, dimensions={0} | all-to-all | bytes 327680 | tf_op jit(solution)/shard_map/all_to_all | solution.py:478
  71.2 2.6 all-to-all-start.2
  74.5 2.0 collective-permute-start.2
  76.5 1.5 collective-permute-start.3
  78.3 2.5 collective-permute-done.3.index_down_ref
  80.8 1.2 all-to-all-done.2.gathered_ref
  82.1 1.3 copy-done.1
  83.4 2.2 pool.1
  85.6 14.1 %all_to_all.57.gathered_ref = f32[32,8,128]{2,1,0:T(8,128)S(1)} all-to-all(f32[32,8,128]{2,1,0:T(8,128)S(1)} %get-tuple-element.46), channel_id=1, replica_groups=mesh['maps'=8,'rows'=4] {'maps','rows'}, dimensions={0} | all-to-all | bytes 262144 | tf_op jit(solution)/shard_map/all_to_all | solution.py:443
  99.7 5.2 %backward.2 = (f32[512,512]{1,0:T(8,128)S(1)}, f32[32,8,128]{2,1,0:T(8,128)S(1)}, bf16[384,512]{1,0:T(8,128)(2,1)}, f32[8,128]{1,0:T(8,128)S(1)}) custom-call(s32[8]{0:T(128)S(1)} %copy-done.18, s32[8]{0:T(128)S(1)} %copy-done.20, s32[2]{0:T(128)S(1)} %pad_add_fusion.place_ref, f32[576,512]{1,0:T(8,128)S(1)} %get-tuple-element.44.grad_ref, ...), custom_call_target="tpu_custom_call" | custom-call | tf_op jit(solution)/shard_map/backward/pallas_call | solution.py:544
  104.9 1.0 copy-done.8
  106.7 10.0 %all_to_all.58.gathered_ref = f32[32,8,128]{2,1,0:T(8,128)S(1)} all-to-all(f32[32,8,128]{2,1,0:T(8,128)S(1)} %get-tuple-element.49), channel_id=1, replica_groups=mesh['maps'=8,'rows'=4] {'maps','rows'}, dimensions={0} | all-to-all | bytes 262144 | tf_op jit(solution)/shard_map/all_to_all | solution.py:443
  116.7 1.2 copy-done.9
  117.9 5.1 %backward.3 = (f32[448,512]{1,0:T(8,128)S(1)}, f32[32,8,128]{2,1,0:T(8,128)S(1)}, bf16[384,512]{1,0:T(8,128)(2,1)}, f32[8,128]{1,0:T(8,128)S(1)}) custom-call(s32[8]{0:T(128)S(1)} %copy-done.18, s32[8]{0:T(128)S(1)} %copy-done.20, s32[2]{0:T(128)S(1)} %pad_add_fusion.place_ref, f32[512,512]{1,0:T(8,128)S(1)} %copy-done.9, ...), custom_call_target="tpu_custom_call" | custom-call | tf_op jit(solution)/shard_map/backward/pallas_call | solution.py:544
  123.1 1.0 copy-done.10
  124.8 1.4 copy-done.3
  126.2 1.4 copy-done.6
  127.6 4.4 %weight_grad.5 = bf16[8,576,128]{2,1,0:T(8,128)(2,1)} custom-call(s32[2]{0:T(128)S(1)} %pad_add_fusion.place_ref, bf16[1536,512]{1,0:T(8,128)(2,1)S(1)} %copy-done.3, bf16[1536,512]{1,0:T(8,128)(2,1)S(1)} %copy-done.6), custom_call_target="tpu_custom_call" | custom-call | tf_op jit(solution)/shard_map/weight_grad/pallas_call | solution.py:527
  132.0 11.2 %all_to_all.59.gathered_ref = f32[32,8,128]{2,1,0:T(8,128)S(1)} all-to-all(f32[32,8,128]{2,1,0:T(8,128)S(1)} %get-tuple-element.52), channel_id=1, replica_groups=mesh['maps'=8,'rows'=4] {'maps','rows'}, dimensions={0} | all-to-all | bytes 262144 | tf_op jit(solution)/shard_map/all_to_all | solution.py:443
  144.8 3.5 all-to-all-start.8
  148.6 19.7 %all-gather.10.cloned.1.call-done.conv_grad_ref = bf16[1536,512]{1,0:T(8,128)(2,1)} async-done(((bf16[384,512]{1,0:T(8,128)(2,1)}), bf16[1536,512]{1,0:T(8,128)(2,1)}) %all-gather.10.cloned.1.call-update) | async-done | bytes 1572880 | tf_op jit(solution)/shard_map/all_gather | solution.py:557
  168.3 1.4 copy-done.4
  169.7 1.4 copy-done.5
  171.1 4.4 %weight_grad.4 = bf16[8,576,128]{2,1,0:T(8,128)(2,1)} custom-call(s32[2]{0:T(128)S(1)} %pad_add_fusion.place_ref, bf16[1536,512]{1,0:T(8,128)(2,1)S(1)} %copy-done.4, bf16[1536,512]{1,0:T(8,128)(2,1)S(1)} %copy-done.5), custom_call_target="tpu_custom_call" | custom-call | tf_op jit(solution)/shard_map/weight_grad/pallas_call | solution.py:527
  175.6 3.3 all-to-all-start.4
  178.9 11.5 %all-gather.6.cloned.1.call-done.act_ref = bf16[1536,512]{1,0:T(8,128)(2,1)} async-done(((bf16[384,512]{1,0:T(8,128)(2,1)}), bf16[1536,512]{1,0:T(8,128)(2,1)}) %all-gather.6.cloned.1.call-update) | async-done | bytes 1572880 | tf_op jit(solution)/shard_map/all_gather | solution.py:457
  190.4 1.4 copy-done.7
  191.8 4.4 %weight_grad.3 = bf16[8,576,128]{2,1,0:T(8,128)(2,1)} custom-call(s32[2]{0:T(128)S(1)} %pad_add_fusion.place_ref, bf16[1536,512]{1,0:T(8,128)(2,1)S(1)} %copy-done.7, bf16[1536,128]{1,0:T(8,128)(2,1)S(1)} %bitcast.30), custom_call_target="tpu_custom_call" | custom-call | tf_op jit(solution)/shard_map/weight_grad/pallas_call | solution.py:527
  196.2 5.5 %all-to-all-start.9 = ((bf16[8,576,128]{2,1,0:T(8,128)(2,1)}), bf16[8,576,128]{2,1,0:T(8,128)(2,1)S(1)}, u32[]{:S(2)}, u32[]{:S(2)}) async-start(bf16[8,576,128]{2,1,0:T(8,128)(2,1)} %weight_grad.3), calls=%async_computation.9 | async-start | bytes 2359296 | tf_op jit(solution)/shard_map/all_to_all | solution.py:586
  202.5 4.5 %input_grad.1 = bf16[384,512]{1,0:T(8,128)(2,1)} custom-call(f32[448,512]{1,0:T(8,128)S(1)} %get-tuple-element.53.conv_grad_ref, bf16[3,9,512,512]{3,2,1,0:T(8,128)(2,1)} %weights_ref.11), custom_call_target="tpu_custom_call" | custom-call | tf_op jit(solution)/shard_map/input_grad/pallas_call | solution.py:576
  207.0 63.0 %reduce-scatter.5.cloned.1.call-done.third_ref = bf16[576,128]{1,0:T(8,128)(2,1)} async-done(((bf16[4608,128]{1,0:T(8,128)(2,1)}), bf16[576,128]{1,0:T(8,128)(2,1)}) %reduce-scatter.5.cloned.1.call-update) | async-done | bytes 147472 | tf_op jit(solution)/shard_map/reduce_scatter | solution.py:559
  271.0 65.5 %reduce-scatter.3.cloned.1.call-done.second_ref = bf16[576,128]{1,0:T(8,128)(2,1)} async-done(((bf16[4608,128]{1,0:T(8,128)(2,1)}), bf16[576,128]{1,0:T(8,128)(2,1)}) %reduce-scatter.3.cloned.1.call-update) | async-done | bytes 147472 | tf_op jit(solution)/shard_map/reduce_scatter | solution.py:559
  338.3 0.9 squares.1
  339.2 3.6 all-to-all-start.10
  343.4 6.4 %all-to-all-done.10 = f32[32,1,128]{2,1,0:T(1,128)S(1)} async-done(((f32[32,1,128]{2,1,0:T(1,128)}), f32[32,1,128]{2,1,0:T(1,128)S(1)}, u32[]{:S(2)}, u32[]{:S(2)}) %all-to-all-start.10) | async-done | bytes 16416 | tf_op jit(solution)/shard_map/all_to_all | solution.py:600
  353.8 3.4 multiply_subtract_fusion
  (86 shorter events, 12.5 us)
Async XLA Ops:
  8.2 3.8 %collective-permute-start = (bf16[192,512]{1,0:T(8,128)(2,1)S(1)}, bf16[192,512]{1,0:T(8,128)(2,1)S(1)}, u32[]{:S(2)}, u32[]{:S(2)}) collective-permute-start(bf16[192,512]{1,0:T(8,128)(2,1)S(1)} %bitcast.39), channel_id=1, source_target_pairs={{0,1},{1,2},{2,3},{4,5},{5,6},{6,7},{8,9},{9,10},{10,11},{12,13},{... | collective-permute-start | bytes 589832 | tf_op jit(solution)/shard_map/ppermute | solution.py:439
  10.6 5.4 %collective-permute-start.1 = (bf16[192,512]{1,0:T(8,128)(2,1)S(1)}, bf16[192,512]{1,0:T(8,128)(2,1)S(1)}, u32[]{:S(2)}, u32[]{:S(2)}) collective-permute-start(bf16[192,512]{1,0:T(8,128)(2,1)S(1)} %bitcast.38), channel_id=1, source_target_pairs={{1,0},{2,1},{3,2},{5,4},{6,5},{7,6},{9,8},{10,9},{11,10},{13,12},{... | collective-permute-start | bytes 589832 | tf_op jit(solution)/shard_map/ppermute | solution.py:440
  16.0 1.0 copy-start.2
  17.0 0.7 copy-start.17
  17.7 0.7 copy-start.19
  18.3 15.0 %copy-start.23 = (f32[2,3,512]{2,0,1:T(2,128)S(1)}, f32[2,3,512]{2,0,1:T(2,128)}, u32[]{:S(2)}) copy-start(f32[2,3,512]{2,0,1:T(2,128)} %param.16) | copy-start | bytes 36868
  18.3 23.2 %copy-start.18 = (s32[8]{0:T(128)S(1)}, s32[8]{0:T(128)}, u32[]{:S(2)}) copy-start(s32[8]{0:T(128)} %kind_ref.13) | copy-start | bytes 100
  18.3 23.2 %copy-start.20 = (s32[8]{0:T(128)S(1)}, s32[8]{0:T(128)}, u32[]{:S(2)}) copy-start(s32[8]{0:T(128)} %domain_ref.13) | copy-start | bytes 100
  24.6 16.9 %all-to-all-start = ((f32[32,8,128]{2,1,0:T(8,128)}), f32[32,8,128]{2,1,0:T(8,128)S(1)}, u32[]{:S(2)}, u32[]{:S(2)}) async-start(f32[32,8,128]{2,1,0:T(8,128)} %get-tuple-element.38), calls=%async_computation | async-start | bytes 262144 | tf_op jit(solution)/shard_map/all_to_all | solution.py:443
  33.3 91.4 %all-gather.12.cloned.1.call-start = ((), (), s32[]{:S(2)}) async-start(), calls=%async_computation.17 | async-start | bytes 1966080 | tf_op jit(solution)/shard_map/all_gather | solution.py:500
  56.9 6.8 %copy-start.22 = (bf16[1,24,16,128]{3,2,1,0:T(8,128)(2,1)S(1)}, bf16[1,24,16,128]{3,2,1,0:T(8,128)(2,1)}, u32[]{:S(2)}) copy-start(bf16[1,24,16,128]{3,2,1,0:T(8,128)(2,1)} %param.21) | copy-start | bytes 294916
  62.5 1.1 copy-start
  63.6 10.2 %copy-start.15 = (s32[1,6,16,512]{3,2,1,0:T(8,128)S(1)}, s32[1,6,16,512]{3,2,1,0:T(8,128)}, u32[]{:S(2)}) copy-start(s32[1,6,16,512]{3,2,1,0:T(8,128)} %param.17) | copy-start | bytes 589828
  63.6 14.4 %copy-start.26 = (s32[1,24,16]{1,2,0:T(8,128)S(1)}, s32[1,24,16]{1,2,0:T(8,128)}, u32[]{:S(2)}) copy-start(s32[1,24,16]{1,2,0:T(8,128)} %param.18) | copy-start | bytes 4612
  71.2 10.8 %all-to-all-start.2 = ((f32[32,8,128]{2,1,0:T(8,128)}), f32[32,8,128]{2,1,0:T(8,128)S(1)}, u32[]{:S(2)}, u32[]{:S(2)}) async-start(f32[32,8,128]{2,1,0:T(8,128)} %get-tuple-element.42), calls=%async_computation.2 | async-start | bytes 262144 | tf_op jit(solution)/shard_map/all_to_all | solution.py:443
  73.8 51.0 %all-gather.14.cloned.1.call-start = ((), (), s32[]{:S(2)}) async-start(), calls=%async_computation.18 | async-start | bytes 1966080 | tf_op jit(solution)/shard_map/all_gather | solution.py:557
  74.5 3.8 %collective-permute-start.2 = (s32[32,512]{1,0:T(8,128)}, s32[32,512]{1,0:T(8,128)S(1)}, u32[]{:S(2)}, u32[]{:S(2)}) collective-permute-start(s32[32,512]{1,0:T(8,128)} %bitcast.6), channel_id=1, source_target_pairs={{0,1},{1,2},{2,3},{4,5},{5,6},{6,7},{8,9},{9,10},{10,11},{12,13},{... | collective-permute-start | bytes 196616 | tf_op jit(solution)/shard_map/ppermute | solution.py:471
  76.5 4.3 %collective-permute-start.3 = (s32[32,512]{1,0:T(8,128)S(1)}, s32[32,512]{1,0:T(8,128)S(1)}, u32[]{:S(2)}, u32[]{:S(2)}) collective-permute-start(s32[32,512]{1,0:T(8,128)S(1)} %bitcast.42), channel_id=1, source_target_pairs={{1,0},{2,1},{3,2},{5,4},{6,5},{7,6},{9,8},{10,9},{11,10},{13,12},{... | collective-permute-start | bytes 196616 | tf_op jit(solution)/shard_map/ppermute | solution.py:472
  82.1 1.3 copy-start.1
  104.9 1.0 copy-start.8
  105.9 42.7 %all-gather.8.cloned.1.call-start = ((), (), s32[]{:S(2)}) async-start(), calls=%async_computation.14 | async-start | bytes 1966080 | tf_op jit(solution)/shard_map/all_gather | solution.py:500
  106.7 61.6 %all-gather.10.cloned.1.call-start = ((), (), s32[]{:S(2)}) async-start(), calls=%async_computation.15 | async-start | bytes 1966080 | tf_op jit(solution)/shard_map/all_gather | solution.py:557
  116.7 1.2 copy-start.9
  123.1 1.0 copy-start.10
  124.1 66.4 %all-gather.6.cloned.1.call-start = ((), (), s32[]{:S(2)}) async-start(), calls=%async_computation.13 | async-start | bytes 1966080 | tf_op jit(solution)/shard_map/all_gather | solution.py:457
  124.7 145.4 %reduce-scatter.5.cloned.1.call-start = ((), (), s32[]{:S(2)}) async-start(), calls=%async_computation.19 | async-start | bytes 1327104 | tf_op jit(solution)/shard_map/reduce_scatter | solution.py:559
  124.8 1.4 copy-start.3
  126.2 1.4 copy-start.6
  132.0 11.2 %copy-start.11 = (f32[448,512]{1,0:T(8,128)S(1)}, f32[448,512]{1,0:T(8,128)}, u32[]{:S(2)}) copy-start(f32[448,512]{1,0:T(8,128)} %copy-done.10) | copy-start | bytes 2752516
  144.1 0.7 copy-start.16
  144.8 30.7 %all-to-all-start.8 = ((bf16[4,384,128]{2,1,0:T(8,128)(2,1)}), bf16[4,384,128]{2,1,0:T(8,128)(2,1)S(1)}, u32[]{:S(2)}, u32[]{:S(2)}) async-start(bf16[4,384,128]{2,1,0:T(8,128)(2,1)} %copy-done.16), calls=%async_computation.8 | async-start | bytes 786432 | tf_op jit(solution)/shard_map/all_to_all | solution.py:575
  148.3 188.1 %reduce-scatter.3.cloned.1.call-start = ((), (), s32[]{:S(2)}) async-start(), calls=%async_computation.16 | async-start | bytes 1327104 | tf_op jit(solution)/shard_map/reduce_scatter | solution.py:559
  168.3 1.4 copy-start.4
  169.7 1.4 copy-start.5
  175.6 20.6 %all-to-all-start.4 = ((bf16[4,96,128]{2,1,0:T(8,128)(2,1)}), bf16[4,96,128]{2,1,0:T(8,128)(2,1)S(1)}, u32[]{:S(2)}, u32[]{:S(2)}) async-start(bf16[4,96,128]{2,1,0:T(8,128)(2,1)} %get-tuple-element.43), calls=%async_computation.4 | async-start | bytes 196608 | tf_op jit(solution)/shard_map/all_to_all | solution.py:519
  190.4 1.4 copy-start.7
  196.2 74.7 %all-to-all-start.9 = ((bf16[8,576,128]{2,1,0:T(8,128)(2,1)}), bf16[8,576,128]{2,1,0:T(8,128)(2,1)S(1)}, u32[]{:S(2)}, u32[]{:S(2)}) async-start(bf16[8,576,128]{2,1,0:T(8,128)(2,1)} %weight_grad.3), calls=%async_computation.9 | async-start | bytes 2359296 | tf_op jit(solution)/shard_map/all_to_all | solution.py:586
  202.5 151.3 %copy-start.21 = (f32[3,9,64,128]{3,2,1,0:T(8,128)S(1)}, f32[3,9,64,128]{3,2,1,0:T(8,128)}, u32[]{:S(2)}) copy-start(f32[3,9,64,128]{3,2,1,0:T(8,128)} %param.23) | copy-start | bytes 2654212
  207.0 144.9 %copy-start.24 = (f32[2,3,512]{2,0,1:T(2,128)S(1)}, f32[2,3,512]{2,0,1:T(2,128)}, u32[]{:S(2)}) copy-start(f32[2,3,512]{2,0,1:T(2,128)} %param.27) | copy-start | bytes 36868
  207.0 144.9 %copy-start.25 = (f32[2,3,512]{2,0,1:T(2,128)S(1)}, f32[2,3,512]{2,0,1:T(2,128)}, u32[]{:S(2)}) copy-start(f32[2,3,512]{2,0,1:T(2,128)} %param.26) | copy-start | bytes 36868
  336.5 0.9 copy-start.12
  337.4 0.9 copy-start.13
  338.3 5.1 %copy-start.14 = (bf16[576,128]{1,0:T(8,128)(2,1)S(1)}, bf16[576,128]{1,0:T(8,128)(2,1)}, u32[]{:S(2)}) copy-start(bf16[576,128]{1,0:T(8,128)(2,1)} %reduce-scatter.3.cloned.1.call-done.second_ref) | copy-start | bytes 442372
  339.2 10.6 %all-to-all-start.10 = ((f32[32,1,128]{2,1,0:T(1,128)}), f32[32,1,128]{2,1,0:T(1,128)S(1)}, u32[]{:S(2)}, u32[]{:S(2)}) async-start(f32[32,1,128]{2,1,0:T(1,128)} %get-tuple-element.62), calls=%async_computation.12 | async-start | bytes 32768 | tf_op jit(solution)/shard_map/all_to_all | solution.py:600
Sparse Core Ops, SparseCore 0:
  63.7 18.4 all-gather.11
  106.0 17.7 all-gather.13
  125.9 20.5 all-gather.7
  148.5 19.6 all-gather.9
  169.7 20.7 all-gather.5
  193.7 76.2 reduce-scatter.4
  273.4 62.9 reduce-scatter.2

commit v2 on v0

v2 whole, which is shorter than its diff:
```python
import functools
import math

import jax
import jax.numpy as jnp
from jax import lax
from jax.experimental import pallas as pl
from jax.experimental.pallas import tpu as pltpu
from jax.sharding import PartitionSpec as P

DOMAINS = 4
norm_epsilon = 1e-05
clip_limit = 1.0
first_decay = 0.9
second_decay = 0.999
adam_epsilon = 1e-08
norm_rate = 0.5
weight_decay = 0.01

HALO = 6
SPACE = 28
AXES = ("maps", "rows")
F32 = jnp.float32
BF16 = jnp.bfloat16


class Sizes:
    def __init__(self, maps, bands, rows, width, channels):
        self.maps = maps
        self.bands = bands
        self.devices = maps * bands
        self.rows = rows
        self.width = width
        self.channels = channels
        self.height = rows * bands
        self.short_height = 2 * (self.height * 7 // 16)
        self.short_width = 2 * (width * 13 // 32)
        self.pixels = rows * width
        self.quarter = channels // bands


def spec(space):
    return pl.BlockSpec(memory_space=space)


def params(megabytes):
    return pltpu.CompilerParams(vmem_limit_bytes=megabytes << 20)


class Copies:
    def __init__(self, sems):
        self.sems = sems
        self.used = 0

    def start(self, source, target):
        copy = pltpu.make_async_copy(source, target, self.sems.at[self.used])
        self.used += 1
        copy.start()
        return copy


def wait(*copies):
    for copy in copies:
        copy.wait()


def line_share(ref, start, step, size):
    return ref.at[pl.ds(pl.multiple_of(start, step), size)]


def own_sums(gathered_ref, weights_ref):
    return jnp.sum(gathered_ref[...] * weights_ref[...], axis=0)


def all_sums(gathered_ref):
    return jnp.sum(gathered_ref[...], axis=0)


def split_rows(tile, channels):
    first = jnp.concatenate([tile[k : k + 1, :] for k in range(4)], axis=1)
    second = jnp.concatenate([tile[k : k + 1, :] for k in range(4, 8)], axis=1)
    return first, second


def join_rows(first, second):
    lanes = first.shape[1] // 4
    return jnp.concatenate(
        [row[:, k * lanes : (k + 1) * lanes] for row in (first, second) for k in range(4)], axis=0
    )


def tiled(sz, value):
    return jnp.concatenate([value] * (sz.channels // value.shape[1]), axis=1)


class Masks:
    def __init__(self, sz, limits_ref):
        self.col = lax.broadcasted_iota(jnp.int32, (sz.width, 128), 0)
        self.wide = jnp.where(self.col < limits_ref[2:3, :], 1.0, 0.0)
        self.inner_left = jnp.where(self.col > 0, 1.0, 0.0)
        self.inner_right = jnp.where(self.col < sz.width - 1, 1.0, 0.0)
        self.limits_ref = limits_ref

    def valid(self, row):
        inside = (self.limits_ref[0:1, :] <= row) & (self.limits_ref[1:2, :] > row)
        return self.wide * jnp.where(inside, 1.0, 0.0)

    def valid_of_map(self, row):
        return self.wide * jnp.where(self.limits_ref[3:4, :] > row, 1.0, 0.0)


def line(sz, row):
    return slice(row * sz.width, (row + 1) * sz.width)


def shifted_right(sz, masks, value):
    mask = masks.inner_left
    return pltpu.roll(value, 1, 0) * (mask if value.shape[1] == 128 else tiled(sz, mask))


def shifted_left(sz, masks, value):
    mask = masks.inner_right
    return pltpu.roll(value, sz.width - 1, 0) * (mask if value.shape[1] == 128 else tiled(sz, mask))


def put_shifted(sz, masks, x3_ref, row, value, reverse=False):
    before = shifted_right(sz, masks, value)
    after = shifted_left(sz, masks, value)
    if reverse:
        before, after = after, before
    c = sz.channels
    x3_ref[line(sz, row), 0:c] = before.astype(BF16)
    x3_ref[line(sz, row), c : 2 * c] = value.astype(BF16)
    x3_ref[line(sz, row), 2 * c : 3 * c] = after.astype(BF16)


def fold(value):
    total = value[0:8, :]
    for k in range(1, value.shape[0] // 8):
        total = total + value[8 * k : 8 * (k + 1), :]
    return total


HEAD = 2


class Weights:
    def __init__(self, copies, head_ref, weights_hbm, buffer_ref, layer):
        self.head_ref, self.buffer_ref = head_ref, buffer_ref
        self.loads = {
            first: copies.start(
                weights_hbm.at[layer, pl.ds(first, 3 - first % 3)],
                buffer_ref.at[pl.ds(first - HEAD, 3 - first % 3)],
            )
            for first in (HEAD, 3, 6)
        }

    def wait(self, tap):
        if tap in self.loads:
            wait(self.loads[tap])

    def taps(self, first, last):
        if first < HEAD:
            part = self.head_ref[first:last]
        else:
            part = self.buffer_ref[first - HEAD : last - HEAD]
        return part.reshape(-1, part.shape[-1])


def conv_rows(sz, x3_ref, weights, out_ref, rows, reverse=False):
    c, w = sz.channels, sz.width
    n = rows * w
    spans = [(0, HEAD), (HEAD, 3), (3, 6), (6, 9)]
    if reverse:
        spans = [(tap, tap + 1) for tap in range(9)]
    for first, last in spans:
        weights.wait(first)
        i = first // 3
        start = (2 - i if reverse else i) * w
        lhs = x3_ref[start : start + n, (first - 3 * i) * c : (last - 3 * i) * c]
        across = 1 if reverse else 0
        term = lax.dot_general(
            lhs, weights.taps(first, last), (((1,), (across,)), ((), ())), preferred_element_type=F32
        )
        if first == 0:
            out_ref[...] = term
        else:
            out_ref[...] += term


def put_stats(sz, first, second, out_ref):
    tile = join_rows(jnp.sum(first, axis=0, keepdims=True), jnp.sum(second, axis=0, keepdims=True))
    out_ref[...] = jnp.broadcast_to(tile[None], out_ref.shape)


def silu_parts(half):
    t = jnp.tanh(half)
    product = half * t
    return half + product, (0.5 + 0.5 * t) * (1.0 + (half - product))


class Stats:
    def __init__(self, sz):
        self.first = jnp.zeros((8, sz.channels), F32)
        self.second = jnp.zeros((8, sz.channels), F32)

    def add(self, first, second):
        self.first = self.first + fold(first)
        self.second = self.second + fold(second)


def add_conv_rows(sz, masks, stats, conv_ref, skip, first, last):
    for row in range(max(first, skip), min(last, skip + sz.rows)):
        value = conv_ref[line(sz, row), :]
        masked = value * tiled(sz, masks.valid(row - skip))
        stats.add(masked, masked * value)


def band_lanes(sz, n):
    return pl.ds(pl.multiple_of((lax.axis_index("rows") ^ n) * sz.quarter, sz.quarter), sz.quarter)


def send_shares(sz, copies, source_ref, targets, first):
    lines = source_ref.shape[0]
    return [
        copies.start(source_ref.at[:, band_lanes(sz, n)], target.at[pl.ds(first, lines)])
        for n, target in enumerate(targets)
    ]


def kernel_spans(sz, given_ref, *rest):
    shares = rest[: sz.bands]
    span = sz.rows // 2 * (sz.width // 2)
    for n, share in enumerate(shares):
        start = pl.multiple_of((lax.axis_index("rows") ^ n) * span, span)
        share[...] = given_ref[pl.ds(start, share.shape[0]), :]


def kernel_edges(sz, x_hbm, index_hbm, low_ref, high_ref, index_ref, sems):
    copies = Copies(sems)
    edge = HALO * sz.width
    few = sz.width
    lines = index_hbm.shape[0]
    first = copies.start(index_hbm.at[pl.ds(lines - few, few)], index_ref.at[0])
    second = copies.start(index_hbm.at[pl.ds(0, few)], index_ref.at[1])
    rest = [
        copies.start(x_hbm.at[pl.ds(sz.pixels - edge, edge)], low_ref.at[pl.ds(0, edge)]),
        copies.start(x_hbm.at[pl.ds(0, edge)], high_ref.at[pl.ds(0, edge)]),
    ]
    wait(first, second)
    low_ref[edge : edge + few, :] = index_ref[0].astype(BF16)
    high_ref[edge : edge + few, :] = index_ref[1].astype(BF16)
    wait(*rest)


def kernel_places(sz, kind_ref, domain_ref, limits_ref, member_ref, _):
    m, r = lax.axis_index("maps"), lax.axis_index("rows")
    start = r * sz.rows

    def rows_of(k):
        return jnp.where(kind_ref[k] == 1, sz.height, sz.short_height)

    def cols_of(k):
        return jnp.where(kind_ref[k] == 1, sz.short_width, sz.width)

    own = domain_ref[m]
    area = jnp.int32(0)
    for k in range(sz.maps):
        area = area + jnp.where(domain_ref[k] == own, rows_of(k) * cols_of(k), 0)
    tile = member_ref.shape[1:]
    weight = 1.0 / jnp.full(tile, area.astype(F32))
    for k in range(sz.maps):
        value = jnp.where(domain_ref[k] == own, weight, 0.0)
        for b in range(sz.bands):
            member_ref[k * sz.bands + b] = value
    line = lax.broadcasted_iota(jnp.int32, limits_ref.shape, 0)
    limits_ref[...] = jnp.where(
        line == 0, -start, jnp.where(line == 1, rows_of(m) - start, jnp.where(line == 2, cols_of(m), rows_of(m)))
    )


def kernel_first(sz, limits_ref, up_ref, x_ref, down_ref, head_ref, weights_hbm, stats_ref, conv_ref, x3_ref, buffer_ref, sems):
    weights = Weights(Copies(sems), head_ref, weights_hbm, buffer_ref, 0)
    masks = Masks(sz, limits_ref)
    stats = Stats(sz)

    def prepare(row):
        if row < HALO:
            value = up_ref[line(sz, row), :]
        elif row < HALO + sz.rows:
            value = x_ref[line(sz, row - HALO), :]
        else:
            value = down_ref[line(sz, row - HALO - sz.rows), :]
        put_shifted(sz, masks, x3_ref, row, value.astype(F32))

    def work(first, last):
        conv_rows(sz, x3_ref, weights, conv_ref, last)
        add_conv_rows(sz, masks, stats, conv_ref, HALO - 1, first, last)

    for row in range(sz.rows + 2 * HALO):
        prepare(row)
    work(0, sz.rows + 2 * HALO - 2)
    put_stats(sz, stats.first, stats.second, stats_ref)


def norm_of(sz, gathered_ref, member_ref):
    mean, squares = split_rows(own_sums(gathered_ref, member_ref), sz.channels)
    return mean, lax.rsqrt(squares - mean * mean + norm_epsilon)


def kernel_forward(sz, layer, limits_ref, member_ref, gathered_ref, before_ref, norm_ref, head_ref, weights_hbm, *rest):
    if layer == 1:
        stats_ref, conv_ref, moments_ref, act_hbm, saved_hbm, *shares, normed_ref, x3_ref, buffer_ref, sems = rest
    else:
        stats_ref, conv_ref, moments_ref, act_hbm, saved_hbm, x3_ref, buffer_ref, sems = rest
    copies = Copies(sems)
    weights = Weights(copies, head_ref, weights_hbm, buffer_ref, layer)
    halo = HALO - layer
    rows = sz.rows + 2 * halo
    skip = (halo - layer) * sz.width
    outs = []
    mean, inverse = norm_of(sz, gathered_ref, member_ref)
    moments_ref[...] = join_rows(mean, inverse)
    scale = 0.5 * norm_ref[layer - 1, 0:1, :] * inverse
    offset = 0.5 * norm_ref[layer - 1, 1:2, :] - mean * scale
    masks = Masks(sz, limits_ref)
    stats = Stats(sz)
    c = sz.channels

    def prepare(row):
        value = before_ref[line(sz, row), :]
        act, _ = silu_parts(value * scale + offset)
        put_shifted(sz, masks, x3_ref, row, act * tiled(sz, masks.valid(row - halo)))
        if layer == 1 and halo <= row < halo + sz.rows:
            normed_ref[line(sz, row - halo), :] = ((value - mean) * inverse).astype(BF16)
        if row == halo + sz.rows - 1:
            outs.append(copies.start(x3_ref.at[pl.ds(halo * sz.width, sz.pixels), pl.ds(c, c)], act_hbm))
            if layer == 1:
                outs.extend(send_shares(sz, copies, normed_ref, shares, 0))

    def work(first, last):
        conv_rows(sz, x3_ref, weights, conv_ref, last)
        outs.append(copies.start(before_ref.at[pl.ds(skip, saved_hbm.shape[0])], saved_hbm))
        add_conv_rows(sz, masks, stats, conv_ref, halo - 1, first, last)

    for row in range(rows):
        prepare(row)
    work(0, rows - 2)
    put_stats(sz, stats.first, stats.second, stats_ref)
    wait(*outs)


def kernel_pool(sz, limits_ref, member_ref, gathered_ref, before_ref, norm_ref, index_hbm, up_hbm, down_hbm, *rest):
    cotangents, rest = rest[: sz.bands], rest[sz.bands :]
    (stats_ref, grad_ref, normed_ref, moments_ref), rest = rest[:4], rest[4:]
    shares, rest = rest[: sz.bands], rest[sz.bands :]
    (index_ref, up_ref, down_ref, cotangent_ref, spread_ref, act_ref, pooled_ref, grad16_ref, normed16_ref, sems) = rest
    c, w = sz.channels, sz.width
    half = w // 2
    windows = sz.rows // 2
    edge = HALO * w
    copies = Copies(sems)
    inputs = [
        copies.start(index_hbm, index_ref),
        copies.start(up_hbm.at[pl.ds(edge, w)], up_ref),
        copies.start(down_hbm.at[pl.ds(edge, w)], down_ref),
    ]
    inputs += [
        copies.start(
            ref, cotangent_ref.at[:, band_lanes(sz, n)]
        )
        for n, ref in enumerate(cotangents)
    ]
    mean, inverse = norm_of(sz, gathered_ref, member_ref)
    moments_ref[...] = join_rows(mean, inverse)
    gain = 0.5 * norm_ref[2, 0:1, :]
    shift = 0.5 * norm_ref[2, 1:2, :]
    halo = HALO - 3
    rows = sz.rows + 2 * halo
    lines = sz.pixels // 4
    groups = c // 128
    masks = Masks(sz, limits_ref)
    for row in range(rows):
        normed = (before_ref[line(sz, row), :] - mean) * inverse
        normed_ref[line(sz, row), :] = normed.astype(BF16)
        act, slope = silu_parts(normed * gain + shift)
        valid = tiled(sz, masks.valid(row - halo))
        grad_ref[line(sz, row), :] = slope * valid
        if halo <= row < halo + sz.rows:
            normed16_ref[line(sz, row - halo), :] = normed.astype(BF16)
            act = act * valid
            for g in range(groups):
                act_ref[g, line(sz, row - halo), :] = act[:, g * 128 : (g + 1) * 128]
    outs = send_shares(sz, copies, normed16_ref, shares, lines + sz.pixels)
    wait(*inputs)
    for p in range(windows):
        index = index_ref[p * half : (p + 1) * half, :]
        result = jnp.zeros(index.shape, F32)
        for corner in range(4):
            start = (2 * p + corner // 2) * w + corner % 2
            taken = jnp.concatenate(
                [act_ref[g, pl.ds(start, half, stride=2), :] for g in range(groups)], axis=1
            )
            result = jnp.where(index == corner, taken, result)
        pooled_ref[p * half : (p + 1) * half, :] = result.astype(BF16)
    outs += send_shares(sz, copies, pooled_ref, shares, 0)
    for p in range(windows + 4):
        if p < 2:
            index = up_ref[p * half : (p + 1) * half, :].astype(jnp.int32)
        elif p < windows + 2:
            index = index_ref[(p - 2) * half : (p - 1) * half, :]
        else:
            first = (p - windows - 2) * half
            index = down_ref[first : first + half, :].astype(jnp.int32)
        given = cotangent_ref[p * half : (p + 1) * half, :].astype(F32)
        for corner in range(4):
            start = (2 * p + corner // 2) * w + corner % 2
            placed = jnp.where(index == corner, given, 0.0)
            for g in range(groups):
                spread_ref[g, pl.ds(start, half, stride=2), :] = placed[:, g * 128 : (g + 1) * 128]
    stats = Stats(sz)
    for row in range(rows):
        upstream = jnp.concatenate([spread_ref[g, line(sz, row + 1), :] for g in range(groups)], axis=1)
        grad = upstream * grad_ref[line(sz, row), :]
        grad_ref[line(sz, row), :] = grad
        if halo <= row < halo + sz.rows:
            grad16_ref[line(sz, row - halo), :] = grad.astype(BF16)
            stats.add(grad, grad * normed_ref[line(sz, row), :].astype(F32))
    outs += send_shares(sz, copies, grad16_ref, shares, lines)
    put_stats(sz, stats.first, stats.second, stats_ref)
    wait(*outs)


class ConvGrad:
    def __init__(self, sz, layer, masks, member_ref, moments_ref, gathered_ref, norm_ref):
        self.sz, self.masks = sz, masks
        _, inverse = split_rows(moments_ref[...], sz.channels)
        one, two = split_rows(own_sums(gathered_ref, member_ref), sz.channels)
        self.scale = norm_ref[layer, 0:1, :] * inverse
        self.one, self.two = one, two

    def row(self, row, grad, normed):
        value = self.scale * (grad - self.one - normed * self.two)
        return value * tiled(self.sz, self.masks.valid(row))


def kernel_backward(sz, layer, limits_ref, member_ref, gathered_ref, grad_ref, normed_ref, moments_ref, norm_ref,
                    head_ref, weights_hbm, saved_hbm, moments_below_ref, stats_ref, below_ref, normed_below_ref, totals_ref,
                    *rest):
    shares, (saved_ref, x3_ref, buffer_ref, grad16_ref, normed16_ref, sems) = rest[: sz.bands], rest[sz.bands :]
    copies = Copies(sems)
    weights = Weights(copies, head_ref, weights_hbm, buffer_ref, layer)
    saved = copies.start(saved_hbm, saved_ref)
    halo = layer + 1
    rows = sz.rows + 2 * halo
    masks = Masks(sz, limits_ref)
    conv_grad = ConvGrad(sz, layer, masks, member_ref, moments_ref, gathered_ref, norm_ref)
    below = layer - 1
    mean, inverse = split_rows(moments_below_ref[...], sz.channels)
    gain = 0.5 * norm_ref[below, 0:1, :]
    shift = 0.5 * norm_ref[below, 1:2, :]
    stats = Stats(sz)
    outs = []

    def prepare(row):
        value = conv_grad.row(row - halo, grad_ref[line(sz, row), :], normed_ref[line(sz, row), :].astype(F32))
        put_shifted(sz, masks, x3_ref, row, value, True)

    def work(first, last):
        conv_rows(sz, x3_ref, weights, below_ref, last, True)
        if first == 0:
            wait(saved)
        for row in range(first, last):
            normed = (saved_ref[line(sz, row), :] - mean) * inverse
            normed_below_ref[line(sz, row), :] = normed.astype(BF16)
            _, slope = silu_parts(normed * gain + shift)
            own = row - (halo - 1)
            grad = below_ref[line(sz, row), :] * slope * tiled(sz, masks.valid(own))
            below_ref[line(sz, row), :] = grad
            if 0 <= own < sz.rows:
                grad16_ref[line(sz, own), :] = grad.astype(BF16)
                if below > 0:
                    normed16_ref[line(sz, own), :] = normed.astype(BF16)
                stats.add(grad, grad * normed)

    for row in range(rows):
        prepare(row)
    work(0, rows - 2)
    outs += send_shares(sz, copies, grad16_ref, shares, 0)
    if below > 0:
        outs += send_shares(sz, copies, normed16_ref, shares, sz.pixels)
    put_stats(sz, stats.first, stats.second, stats_ref)
    totals_ref[...] = all_sums(gathered_ref)
    wait(*outs)


def kernel_last(sz, limits_ref, member_ref, gathered_ref, grad_ref, normed_ref, moments_ref, norm_ref, head_ref,
                weights_hbm, *rest):
    parts, (out_hbm, totals_ref, pooled_hbm, x3_ref, buffer_ref, acc_ref, out_ref, sems) = (
        rest[: sz.bands], rest[sz.bands :]
    )
    copies = Copies(sems)
    weights = Weights(copies, head_ref, weights_hbm, buffer_ref, 0)
    lines = sz.pixels // 4
    outs = []
    for n, ref in enumerate(parts):
        target = line_share(pooled_hbm, (lax.axis_index("rows") ^ n) * lines, lines, lines)
        outs.append(copies.start(ref.at[pl.ds(0, lines)], target))
    totals_ref[...] = all_sums(gathered_ref)
    masks = Masks(sz, limits_ref)
    conv_grad = ConvGrad(sz, 0, masks, member_ref, moments_ref, gathered_ref, norm_ref)

    def prepare(row):
        value = conv_grad.row(row - 1, grad_ref[line(sz, row), :], normed_ref[line(sz, row), :].astype(F32))
        put_shifted(sz, masks, x3_ref, row, value, True)

    def work(first, last):
        conv_rows(sz, x3_ref, weights, acc_ref, last, True)
        pixels = slice(first * sz.width, last * sz.width)
        out_ref[pixels, :] = acc_ref[pixels, :].astype(BF16)

    for row in range(sz.rows + 2):
        prepare(row)
    work(0, sz.rows)
    outs.append(copies.start(out_ref, out_hbm))
    wait(*outs)


def kernel_weight_grad(sz, layer, first, limits_ref, member_ref, gathered_ref, moments_ref, norm_ref, *rest):
    w, q, c, bands = sz.width, sz.quarter, sz.channels, sz.bands
    pixels = sz.height * w
    given, rest = rest[:bands], rest[bands:]
    values, rest = rest[:bands], rest[bands:]
    acts, rest = rest[:bands], rest[bands:]
    if layer == 0:
        out_ref, grad_ref, normed_ref, act_ref, x9_ref, sems = rest
    else:
        (keep_hbm, send_hbm, grad_ref, normed_ref, act_ref, x9_ref, keep_ref, send_ref, term_ref,
         sems) = rest
    copies = Copies(sems)
    inputs = []
    for n in range(bands):
        start = (lax.axis_index("rows") ^ n) * sz.pixels
        for source, target, top in ((given[n], grad_ref, first[0]), (values[n], normed_ref, first[1])):
            inputs.append(
                copies.start(source.at[pl.ds(top, sz.pixels)], line_share(target, start, sz.pixels, sz.pixels))
            )
    act_loads = [
        copies.start(
            acts[n], line_share(act_ref, (lax.axis_index("rows") ^ n) * sz.pixels, sz.pixels, sz.pixels)
        )
        for n in range(bands)
    ]
    band = lax.axis_index("rows")
    own = lax.axis_index("maps")
    tile = own_sums(gathered_ref, member_ref)
    one, two, inverse, gain = (jnp.zeros((1, q), F32) for _ in range(4))
    for b in range(bands):
        here = band == b
        one = jnp.where(here, tile[b : b + 1, :], one)
        two = jnp.where(here, tile[b + 4 : b + 5, :], two)
        inverse = jnp.where(here, moments_ref[b + 4 : b + 5, :], inverse)
        gain = jnp.where(here, norm_ref[layer, 0:1, b * q : (b + 1) * q], gain)
    wait(*inputs)
    masks = Masks(sz, limits_ref)
    blank = jnp.zeros((w, q), BF16)
    for row in range(sz.height):
        value = grad_ref[line(sz, row), :].astype(F32) - one - normed_ref[line(sz, row), :].astype(F32) * two
        value = (gain * inverse) * value * masks.valid_of_map(row)
        for j, piece in enumerate((shifted_left(sz, masks, value), value, shifted_right(sz, masks, value))):
            piece = piece.astype(BF16)
            for i in range(3):
                if 0 <= row + i - 1 < sz.height:
                    x9_ref[line(sz, row + i - 1), (3 * i + j) * q : (3 * i + j + 1) * q] = piece
    for j in range(3):
        x9_ref[line(sz, sz.height - 1), j * q : (j + 1) * q] = blank
        x9_ref[line(sz, 0), (6 + j) * q : (7 + j) * q] = blank
    share = c // sz.maps
    wait(*act_loads)
    term = lax.dot_general(
        act_ref[...], x9_ref[...], (((0,), (0,)), ((), ())), preferred_element_type=F32
    )
    if layer == 0:
        for tap in range(9):
            part = term[:, tap * q : (tap + 1) * q].astype(BF16)
            for m in range(sz.maps):
                out_ref[m, tap * share : (tap + 1) * share, :] = part[m * share : (m + 1) * share, :]
        return
    term_ref[...] = term
    for position, relative in enumerate(halving_order(sz.maps)):
        lines = pl.ds(pl.multiple_of((own ^ relative) * share, share), share)
        for tap in range(9):
            place = slice(tap * share, (tap + 1) * share)
            part = term_ref[lines, tap * q : (tap + 1) * q]
            if position < sz.maps // 2:
                keep_ref[position, place, :] = part
            else:
                send_ref[position - sz.maps // 2, place, :] = part.astype(BF16)
    wait(copies.start(keep_ref, keep_hbm), copies.start(send_ref, send_hbm))


def halving_order(maps):
    bits = maps.bit_length() - 1
    return [sum(((place >> (bits - 1 - k)) & 1) << k for k in range(bits)) for place in range(maps)]


def kernel_halve(keep_hbm, received_hbm, next_keep_hbm, next_send_hbm, keep_ref, received_ref, send_ref, sems):
    half = next_keep_hbm.shape[0]
    copies = Copies(sems)
    loads = [
        [
            copies.start(source.at[part], target.at[part])
            for source, target in ((keep_hbm, keep_ref), (received_hbm, received_ref))
        ]
        for part in (pl.ds(half, half), pl.ds(0, half))
    ]
    wait(*loads[0])
    send_ref[...] = (keep_ref[half:] + received_ref[half:].astype(F32)).astype(BF16)
    first = copies.start(send_ref, next_send_hbm)
    wait(*loads[1])
    keep_ref[:half] += received_ref[:half].astype(F32)
    wait(first, copies.start(keep_ref.at[pl.ds(0, half)], next_keep_hbm))


def kernel_squares(sz, received_ref, keep1_ref, last1_ref, keep2_ref, last2_ref, totals2_ref, totals1_ref,
                   totals0_ref, squares_ref, shard_ref, norm_grad_ref, _):
    value = received_ref[0].astype(F32)
    for m in range(1, sz.maps):
        value = value + received_ref[m].astype(F32)
    values = [value, keep1_ref[0] + last1_ref[0].astype(F32), keep2_ref[0] + last2_ref[0].astype(F32)]
    total = jnp.zeros((1, sz.quarter), F32)
    for layer, value in enumerate(values):
        shard_ref[layer] = value
        total = total + jnp.sum(value * value, axis=0, keepdims=True)
    squares_ref[...] = jnp.broadcast_to(total[None], squares_ref.shape)
    for layer, ref in enumerate((totals0_ref, totals1_ref, totals2_ref)):
        shift_row, gain_row = split_rows(ref[...], sz.channels)
        norm_grad_ref[layer, 0:1, :] = gain_row
        norm_grad_ref[layer, 1:2, :] = shift_row


def kernel_adam(sz, rate, every_ref, step_ref, shard_ref, master_hbm, first_hbm, second_hbm, norm_grad_ref, norm_ref,
                norm_first_ref, norm_second_ref, total_hbm, first_out_hbm, second_out_hbm, master_out_hbm,
                norm_first_hbm, norm_second_hbm, norm_hbm,
                total_ref, master_ref, first_ref, second_ref, small_ref, sems):
    copies = Copies(sems)
    loads = [
        [
            copies.start(source.at[layer], target.at[layer])
            for source, target in ((master_hbm, master_ref), (first_hbm, first_ref), (second_hbm, second_ref))
        ]
        for layer in range(3)
    ]
    norm_grad = norm_grad_ref[...]
    square = jnp.sum(jnp.sum(every_ref[...], axis=0)) + jnp.sum(norm_grad * norm_grad)
    total = jnp.sqrt(jnp.full((1, 128), square, F32))
    total_ref[...] = total
    outs = [copies.start(total_ref, total_hbm)]
    scale = jnp.minimum(1.0, clip_limit / total)
    count = jnp.full((1, 128), step_ref[0].astype(F32), F32)
    first_fix = 1.0 - jnp.exp(count * math.log(first_decay))
    second_fix = 1.0 - jnp.exp(count * math.log(second_decay))
    for layer in range(3):
        wait(*loads[layer])
        first_ref[layer], second_ref[layer], master_ref[layer] = adam(
            master_ref[layer], shard_ref[layer], first_ref[layer], second_ref[layer], rate, weight_decay,
            scale, first_fix, second_fix,
        )
        for source, target in (
            (first_ref, first_out_hbm), (second_ref, second_out_hbm), (master_ref, master_out_hbm)
        ):
            outs.append(copies.start(source.at[layer], target.at[layer]))
    wide = [jnp.concatenate([v] * (sz.channels // 128), axis=1) for v in (scale, first_fix, second_fix)]
    for layer in range(3):
        small_ref[0, layer], small_ref[1, layer], small_ref[2, layer] = adam(
            norm_ref[layer], norm_grad[layer], norm_first_ref[layer], norm_second_ref[layer], norm_rate, 0.0, *wide
        )
    for k, target in enumerate((norm_first_hbm, norm_second_hbm, norm_hbm)):
        outs.append(copies.start(small_ref.at[k], target))
    wait(*outs)


def adam(param, grad, first, second, rate, decay, scale, first_fix, second_fix):
    clipped = scale * grad
    first_new = first_decay * first + (1.0 - first_decay) * clipped
    second_new = second_decay * second + (1.0 - second_decay) * clipped * clipped
    update = first_new / first_fix / (jnp.sqrt(second_new / second_fix) + adam_epsilon)
    return first_new, second_new, param - rate * (update + decay * param)


def call(kernel, name, outs, ins, scratch=(), flops=0, moved=0, hbm_ins=(), hbm_outs=(), smem_ins=()):
    spaces_in = [
        pltpu.SMEM if k in smem_ins else pltpu.HBM if k in hbm_ins else pltpu.VMEM for k in range(len(ins))
    ]
    spaces_out = [pltpu.HBM if k in hbm_outs else pltpu.VMEM for k in range(len(outs))]
    return pl.pallas_call(
        kernel,
        out_shape=tuple(space(out.shape, out.dtype) for space, out in zip(spaces_out, outs)),
        in_specs=[spec(space) for space in spaces_in],
        out_specs=tuple(spec(space) for space in spaces_out),
        scratch_shapes=list(scratch) + [pltpu.SemaphoreType.DMA((32,))],
        compiler_params=params(SPACE),
        cost_estimate=pl.CostEstimate(flops=flops // 8, bytes_accessed=moved, transcendentals=0),
        name=name,
    )(*[v if k in smem_ins else pltpu.with_memory_space_constraint(v, spaces_in[k]) for k, v in enumerate(ins)])


def local(sz, block_input, conv_weights, norm_params, pool_index, task_mask, map_kind, map_domain, out_grad, step,
          conv_master, conv_moment1, conv_moment2, norm_moment1, norm_moment2):
    w, c, q = sz.width, sz.channels, sz.quarter
    half = w // 2
    n_maps, bands = sz.maps, sz.bands
    forward = [(i, i + 1) for i in range(bands - 1)]
    backward = [(i + 1, i) for i in range(bands - 1)]
    x = block_input.reshape(sz.pixels, c)
    index = pool_index.reshape(sz.pixels // 4, c)
    norms, norm_first, norm_second = (v.transpose(1, 0, 2) for v in (norm_params, norm_moment1, norm_moment2))
    edge = HALO * w
    lines = sz.pixels // 4

    def shape(dims, dtype):
        return jax.ShapeDtypeStruct(dims, dtype)

    def pixel_shape(rows, dtype):
        return shape((rows * w, c), dtype)

    def pixel_space(rows, dtype, times=1):
        return pltpu.VMEM((rows * w, times * c), dtype)

    def share_shapes(count):
        return [shape((count, q), BF16)] * bands

    stats_shape = shape((sz.devices, 8, c // 4), F32)
    tile_shape = shape((8, c // 4), F32)
    weight_space = pltpu.VMEM((9 - HEAD, c, c), BF16)


    def conv_flops(rows):
        return rows * w * 9 * c * c * 2

    def spread(stats):
        return lax.all_to_all(stats, AXES, 0, 0, tiled=True)

    def trade(shares):
        return [shares[0]] + [
            lax.ppermute(shares[n], "rows", [(i, i ^ n) for i in range(bands)]) for n in range(1, bands)
        ]

    def swap(act, n):
        return lax.ppermute(act, "rows", [(i, i ^ n) for i in range(bands)])

    tie = lax.optimization_barrier

    low, high = call(
        functools.partial(kernel_edges, sz), "edges",
        [shape((edge + 2 * half, c), BF16)] * 2, [x, index],
        [pltpu.VMEM((2, 2 * half, c), jnp.int32)], hbm_ins=(0, 1),
    )
    up = lax.ppermute(low, "rows", forward)
    down = lax.ppermute(high, "rows", backward)

    limits, member = call(
        functools.partial(kernel_places, sz), "places", [shape((8, 128), jnp.int32), stats_shape],
        [map_kind, map_domain], smem_ins=(0, 1),
    )
    labelled = (out_grad * task_mask[..., None].astype(BF16)).reshape(sz.height // 2 * half, q)
    labelled = jnp.pad(labelled, ((2 * half, 2 * half), (0, 0)))
    consts = [limits, member]

    rows = sz.rows + 2 * HALO
    stats, conv = call(
        functools.partial(kernel_first, sz), "first",
        [stats_shape, pixel_shape(rows - 2, F32)], [limits, up, x, down, conv_weights[0, :HEAD], conv_weights],
        [pixel_space(rows, BF16, 3), weight_space], conv_flops(rows - 2), hbm_ins=(5,),
    )
    def head(layer, weights):
        return weights[layer, :HEAD]

    cot_lines = (sz.rows // 2 + 4) * half
    cots = call(functools.partial(kernel_spans, sz), "spans", share_shapes(cot_lines), [labelled])
    stats, kept, weights, *cots = tie((stats, x, conv_weights, *cots))
    gathered = spread(stats)
    cots = trade(cots)
    acts = [[kept, swap(kept, 1), swap(kept, 2)]]
    moments = []
    saves = []
    for layer in (1, 2):
        rows = sz.rows + 2 * (HALO - layer)
        outs = [
            stats_shape, pixel_shape(rows - 2, F32), tile_shape, pixel_shape(sz.rows, BF16),
            pixel_shape(sz.rows + 2 * layer, F32),
        ]
        scratch = [pixel_space(rows, BF16, 3), weight_space]
        if layer == 1:
            outs += share_shapes(sz.pixels)
            scratch = [pixel_space(sz.rows, BF16)] + scratch
        stats, conv, moment, act, saved, *shares = call(
            functools.partial(kernel_forward, sz, layer), "forward", outs,
            consts + [gathered, conv, norms, head(layer, weights), conv_weights], scratch,
            conv_flops(rows - 2), hbm_ins=(6,), hbm_outs=range(3, 9),
        )
        moments.append(moment)
        saves.append(saved)
        if layer == 1:
            stats, weights = tie((stats, conv_weights))
            gathered = spread(stats)
            given0 = trade(shares)
        else:
            stats, *rest = tie((stats, *cots, *acts[0]))
            cots, acts[0] = rest[:bands], rest[bands:]
            gathered = spread(stats)
            acts[0].append(swap(acts[0][2], 1))
        acts.append([act, swap(act, 1), swap(act, 2)])

    rows = sz.rows + 2 * (HALO - 3)
    stats, grad, normed, moment, *shares = call(
        functools.partial(kernel_pool, sz), "pool",
        [stats_shape, pixel_shape(rows, F32), pixel_shape(rows, BF16), tile_shape]
        + share_shapes(lines + 2 * sz.pixels),
        consts + [gathered, conv, norms, index, up, down] + cots,
        [
            pltpu.VMEM((lines, c), jnp.int32), pltpu.VMEM((2 * half, c), BF16), pltpu.VMEM((2 * half, c), BF16),
            pltpu.VMEM((cot_lines, c), BF16),
            pltpu.VMEM((c // 128, (rows + 2) * w, 128), F32), pltpu.VMEM((c // 128, sz.pixels, 128), F32),
            pltpu.VMEM((lines, c), BF16), pixel_space(sz.rows, BF16), pixel_space(sz.rows, BF16),
        ],
        conv_flops(4), hbm_ins=range(5, 12), hbm_outs=range(4, 8),
    )
    moments.append(moment)
    stats, weights, *rest = tie((stats, conv_weights, *given0, *acts[1]))
    given0, acts[1] = rest[:bands], rest[bands:]
    gathered = spread(stats)
    exchanged = trade(shares)
    acts[1].append(swap(acts[1][2], 1))
    pooled_parts = exchanged

    totals = [None, None, None]
    share = 9 * (c // n_maps)
    steps = n_maps.bit_length() - 1

    def part_shape(parts, dtype):
        return shape((parts, share, q), dtype)

    def part_space(parts, dtype):
        return pltpu.VMEM((parts, share, q), dtype)

    def weight_grad(layer, gathered, given, first, normed=None):
        scratch = [
            pltpu.VMEM((sz.height * w, q), BF16),
            pltpu.VMEM((sz.height * w, q), BF16),
            pltpu.VMEM((sz.height * w, c), BF16),
            pltpu.VMEM((sz.height * w, 9 * q), BF16),
        ]
        if layer == 0:
            outs = [part_shape(n_maps, BF16)]
        else:
            outs = [part_shape(n_maps // 2, dtype) for dtype in (F32, BF16)]
            scratch += [part_space(n_maps // 2, dtype) for dtype in (F32, BF16)]
            scratch.append(pltpu.VMEM((c, 9 * q), F32))
        return call(
            functools.partial(kernel_weight_grad, sz, layer, first), "weight_grad", outs,
            consts + [gathered, moments[layer], norms] + given + (normed or given) + acts[layer], scratch, conv_flops(sz.rows),
            hbm_ins=range(5, 17), hbm_outs=() if layer == 0 else (0, 1),
        )

    def halve(keep, send):
        for k in range(steps):
            received = lax.ppermute(send, "maps", [(m, m ^ (1 << k)) for m in range(n_maps)])
            if k == steps - 1:
                return keep, received
            size = keep.shape[0] // 2
            keep, send = call(
                kernel_halve, "halve", [part_shape(size, dtype) for dtype in (F32, BF16)], [keep, received],
                [part_space(2 * size, F32), part_space(2 * size, BF16), part_space(size, BF16)],
                hbm_ins=(0, 1), hbm_outs=(0, 1),
            )

    shards = [None, None, None]
    for layer in (2, 1):
        halo = layer + 1
        rows = sz.rows + 2 * halo
        received, gathered_here = exchanged, gathered
        stats, grad, normed, totals[layer], *shares = call(
            functools.partial(kernel_backward, sz, layer), "backward",
            [stats_shape, pixel_shape(rows - 2, F32), pixel_shape(rows - 2, BF16), tile_shape]
            + share_shapes(sz.pixels * (2 if layer == 2 else 1)),
            consts + [
                gathered, grad, normed, moments[layer], norms, head(layer, weights), conv_weights, saves[layer - 1],
                moments[layer - 1],
            ],
            [
                pixel_space(rows - 2, F32), pixel_space(rows, BF16, 3), weight_space, pixel_space(sz.rows, BF16),
                pixel_space(sz.rows, BF16),
            ],
            conv_flops(rows - 2), hbm_ins=(8, 9), hbm_outs=range(4, 8),
        )
        if layer == 2:
            stats, weights, acts[0][3], acts[1][3], *acts[2] = tie(
                (stats, conv_weights, acts[0][3], acts[1][3], *acts[2])
            )
            gathered = spread(stats)
            exchanged = trade(shares)
            acts[2].append(swap(acts[2][2], 1))
            keep2, send2 = weight_grad(2, gathered_here, received, (lines, lines + sz.pixels))
        else:
            stats, weights, send2 = tie((stats, conv_weights, send2))
            gathered = spread(stats)
            exchanged = trade(shares)
            keep1, send1 = weight_grad(1, gathered_here, received, (0, sz.pixels))

    send1, late = tie((send1, exchanged))
    (partial,) = weight_grad(0, gathered, late, (0, 0), given0)
    received = lax.all_to_all(partial, "maps", 0, 0, tiled=True)
    shards[2] = halve(keep2, send2)
    shards[1] = halve(keep1, send1)
    input_grad, totals[0], pooled = call(
        functools.partial(kernel_last, sz), "last",
        [pixel_shape(sz.rows, BF16), tile_shape, shape((sz.height // 2 * half, q), BF16)],
        consts + [gathered, grad, normed, moments[0], norms, head(0, weights), conv_weights] + pooled_parts,
        [pixel_space(sz.rows + 2, BF16, 3), weight_space, pixel_space(sz.rows, F32), pixel_space(sz.rows, BF16)],
        conv_flops(sz.rows), hbm_ins=range(8, 13), hbm_outs=(0, 2),
    )

    norm_shape = shape((3, 2, c), F32)
    squares, shard, norm_grad = call(
        functools.partial(kernel_squares, sz), "squares",
        [shape((sz.devices, 1, q), F32), part_shape(3, F32), norm_shape],
        [received, *shards[1], *shards[2], totals[2], totals[1], totals[0]],
    )
    every = lax.all_to_all(squares, AXES, 0, 0, tiled=True)
    rate = 2.0 / math.sqrt(9.0 * c)
    total, conv_first, conv_second, conv_new, norm_first, norm_second, norm_new = call(
        functools.partial(kernel_adam, sz, rate), "adam",
        [shape((1, 128), F32)] + [part_shape(3, F32)] * 3 + [norm_shape] * 3,
        [every, step, shard]
        + [v.reshape(3, share, q) for v in (conv_master, conv_moment1, conv_moment2)]
        + [norm_grad, norms, norm_first, norm_second],
        [pltpu.VMEM((1, 128), F32)] + [part_space(3, F32)] * 3 + [pltpu.VMEM((3, 3, 2, c), F32)],
        hbm_ins=(3, 4, 5), hbm_outs=range(7), smem_ins=(1,),
    )
    return (
        pooled.reshape(1, sz.height // 2, half, q),
        input_grad.reshape(block_input.shape),
        total[0, :1],
        conv_first.reshape(conv_master.shape),
        conv_second.reshape(conv_master.shape),
        conv_new.reshape(conv_master.shape),
        norm_first.transpose(1, 0, 2),
        norm_second.transpose(1, 0, 2),
        norm_new.transpose(1, 0, 2),
    )


def solution(mesh):
    def run(*args):
        bands = mesh.shape["rows"]
        maps = mesh.shape["maps"]
        shape = args[0].shape
        sz = Sizes(maps, bands, shape[1] // bands, shape[2], shape[3])
        return jax.shard_map(
            functools.partial(local, sz),
            mesh=mesh,
            in_specs=(
                P("maps", "rows", None, None),
                P(),
                P(),
                P("maps", "rows", None, None),
                P("maps", None, None),
                P(),
                P(),
                P("maps", None, None, "rows"),
                P(),
                P(None, None, "maps", "rows"),
                P(None, None, "maps", "rows"),
                P(None, None, "maps", "rows"),
                P(),
                P(),
            ),
            out_specs=(
                P("maps", None, None, "rows"),
                P("maps", "rows", None, None),
                P(),
                P(None, None, "maps", "rows"),
                P(None, None, "maps", "rows"),
                P(None, None, "maps", "rows"),
                P(),
                P(),
                P(),
            ),
            check_vma=False,
        )(*args)

    return run
```

time: 1000 us -> 242 us (0.24)
  waiting for transfers between devices: 453 us -> 85.1 us
  blocking collectives: 294 us -> 0 us
  matrix products: 104 us -> 0 us
  Pallas kernels: 0 us -> 67.8 us
  other arithmetic: 39.5 us -> 1.71 us
  starting transfers between devices: 29.6 us -> 62.2 us
  local copies, waits for them, and re-layouts: 51.9 us -> 21.4 us
  between operations: 20.1 us -> 2.27 us
    reduce_scatter x1 -> x0, waiting for transfers between devices: 451 us -> none  [local(): lax.psum_scatter(kernel_grad, 'maps', scatter_dimension=2, tiled=True)]
    psum x7 -> x0, blocking collectives: 294 us -> none  [the longest x3 128 us: local(): sums, squares = lax.psum((sums, squares), ('maps', 'rows'))]
    dot_general x94 -> x0, matrix products: 104 us -> none  [the longest x27 42.6 us: transpose_taps(): jnp.einsum('mhwd,cd->mhwc', piece, kernel[tap_row * 3 + tap_col], preferr...]
    pallas_call x0 -> x19, Pallas kernels: none -> 67.8 us  [call(): pl.pallas_call(kernel, out_shape=tuple((space(out.shape, out.dtype) for s...]
    ppermute x12 -> x32, waiting for transfers between devices: 0.22 us -> 46.1 us  [the longest x6 38.1 us: halve(): lax.ppermute(send, 'maps', [(m, m ^ 1 << k) for m in range(n_maps)])]
    all_to_all x2 -> x8, waiting for transfers between devices: 0.01 us -> 38.9 us  [the longest x6 32.5 us: spread(): return lax.all_to_all(stats, AXES, 0, 0, tiled=True)]
    all_to_all x2 -> x8, starting transfers between devices: 9.83 us -> 31.1 us  [the longest x6 20.1 us: spread(): return lax.all_to_all(stats, AXES, 0, 0, tiled=True)]
    unnamed x139 -> x102, local copies, waits for them, and re-layouts: 34.5 us -> 13.6 us
  transfers between devices with their start and end apart: 16 -> 40, of which waited for: 3 -> 11; matrix products, arithmetic and copies ran while one was open for 7% -> 4% of each run, Pallas kernels for 0% -> 22%
where the time goes in v2:
time: 242 us; the launch traced here: 241 us
  waiting for transfers between devices  85.1 us (35%)
  Pallas kernels  67.8 us (28%)
  starting transfers between devices  62.2 us (26%)
  local copies, waits for them, and re-layouts  21.4 us (9%)
    pallas_call x19, Pallas kernels, call(): pl.pallas_call(kernel, out_shape=tuple((space(out.shape, out.dtype) for s...  67.8 us
    ppermute x6, waiting for transfers between devices, halve(): lax.ppermute(send, 'maps', [(m, m ^ 1 << k) for m in range(n_maps)])  38.1 us
    all_to_all x6, waiting for transfers between devices, spread(): return lax.all_to_all(stats, AXES, 0, 0, tiled=True)  32.5 us
    all_to_all x6, starting transfers between devices, spread(): return lax.all_to_all(stats, AXES, 0, 0, tiled=True)  20.1 us
    unnamed x102, local copies, waits for them, and re-layouts  13.6 us
    ppermute x15, starting transfers between devices, trade(): lax.ppermute(shares[n], 'rows', [(i, i ^ n) for i in range(bands)])  10.3 us
    ppermute x6, starting transfers between devices, halve(): lax.ppermute(send, 'maps', [(m, m ^ 1 << k) for m in range(n_maps)])  8.83 us
    ppermute x9, starting transfers between devices, swap(): return lax.ppermute(act, 'rows', [(i, i ^ n) for i in range(bands)])  8.15 us
  transfers between devices with their start and end apart: 40, of which 11 were waited for; matrix products, arithmetic and copies ran while one was open for 4% of the time, Pallas kernels for 22%

profile of v2, /device:TPU:0, one launch (start us, length us, event | category | flops | bytes accessed | tf_op | source)
XLA Modules:
  0.0 240.5 jit_solution(5948435485199818611)
XLA Ops:
  0.6 1.4 edges.1
  2.0 2.5 %collective-permute-start = (bf16[224,512]{1,0:T(8,128)(2,1)S(1)}, bf16[224,512]{1,0:T(8,128)(2,1)S(1)}, u32[]{:S(2)}, u32[]{:S(2)}) collective-permute-start(bf16[224,512]{1,0:T(8,128)(2,1)S(1)} %get-tuple-element.125), channel_id=1, source_target_pairs={{0,1},{1,2},{2,3},{4,5},{5,6},{6,7},{8,9},{9,10},{10,11},{12,13},{... | collective-permute-start | bytes 688136 | tf_op jit(solution)/shard_map/ppermute | solution.py:759
  12.2 5.1 %first.1 = (f32[32,8,128]{2,1,0:T(8,128)}, f32[704,512]{1,0:T(8,128)S(1)}) custom-call(s32[8,128]{1,0:T(8,128)S(1)} %get-tuple-element.123.limits_ref, bf16[224,512]{1,0:T(8,128)(2,1)S(1)} %collective-permute-done.up_ref.up_hbm, bf16[384,512]{1,0:T(8,128)(2,1)S(1)} %bitcast.35, bf16[224,512]{1,0:T(8,128)(2,1)S(1)} %collective-permute-done.1.down_ref.down_hbm, ...), custom_call_target="tpu_custom_call" | custom-call | flops 415236096 | tf_op jit(solution)/shard_map/first/pallas_call | solution.py:696
  17.3 3.3 %collective-permute-start.5 = (bf16[384,512]{1,0:T(8,128)(2,1)S(1)}, bf16[384,512]{1,0:T(8,128)(2,1)}, u32[]{:S(2)}, u32[]{:S(2)}) collective-permute-start(bf16[384,512]{1,0:T(8,128)(2,1)S(1)} %bitcast.36), channel_id=1, source_target_pairs={{0,1},{1,0},{2,3},{3,2},{4,5},{5,4},{6,7},{7,6},{8,9},{9,8},{10,11... | collective-permute-start | bytes 1179656 | tf_op jit(solution)/shard_map/ppermute | solution.py:750
  20.6 1.7 collective-permute-start.6
  22.3 4.9 %all-to-all-start = ((f32[32,8,128]{2,1,0:T(8,128)}), f32[32,8,128]{2,1,0:T(8,128)S(1)}, u32[]{:S(2)}, u32[]{:S(2)}) async-start(f32[32,8,128]{2,1,0:T(8,128)} %get-tuple-element.132), calls=%async_computation | async-start | bytes 262144 | tf_op jit(solution)/shard_map/all_to_all | solution.py:742
  27.6 1.7 collective-permute-start.3
  30.6 4.9 %all-to-all-done.gathered_ref = f32[32,8,128]{2,1,0:T(8,128)S(1)} async-done(((f32[32,8,128]{2,1,0:T(8,128)}), f32[32,8,128]{2,1,0:T(8,128)S(1)}, u32[]{:S(2)}, u32[]{:S(2)}) %all-to-all-start) | async-done | bytes 131104 | tf_op jit(solution)/shard_map/all_to_all | solution.py:742
  35.5 4.9 %forward.2 = (f32[32,8,128]{2,1,0:T(8,128)}, f32[640,512]{1,0:T(8,128)S(1)}, f32[8,128]{1,0:T(8,128)S(1)}, bf16[384,512]{1,0:T(8,128)(2,1)}, f32[448,512]{1,0:T(...) custom-call(s32[8,128]{1,0:T(8,128)S(1)} %get-tuple-element.123.limi, ...), custom_call_target="tpu_custom_call" | custom-call | flops 377487360 | tf_op jit(solution)/shard_map/forward/pallas_call | solution.py:696
  41.6 4.3 %all-to-all-start.1 = ((f32[32,8,128]{2,1,0:T(8,128)}), f32[32,8,128]{2,1,0:T(8,128)S(1)}, u32[]{:S(2)}, u32[]{:S(2)}) async-start(f32[32,8,128]{2,1,0:T(8,128)} %get-tuple-element.136), calls=%async_computation.1 | async-start | bytes 262144 | tf_op jit(solution)/shard_map/all_to_all | solution.py:742
  46.2 1.7 collective-permute-start.11
  49.2 4.9 %all-to-all-done.1.gathered_ref = f32[32,8,128]{2,1,0:T(8,128)S(1)} async-done(((f32[32,8,128]{2,1,0:T(8,128)}), f32[32,8,128]{2,1,0:T(8,128)S(1)}, u32[]{:S(2)}, u32[]{:S(2)}) %all-to-all-start.1) | async-done | bytes 131104 | tf_op jit(solution)/shard_map/all_to_all | solution.py:742
  54.1 4.6 %forward.3 = (f32[32,8,128]{2,1,0:T(8,128)}, f32[576,512]{1,0:T(8,128)S(1)}, f32[8,128]{1,0:T(8,128)S(1)}, bf16[384,512]{1,0:T(8,128)(2,1)}, f32[512,512]{1,0:T(8,128)}) custom-call(s32[8,128]{1,0:T(8,128)S(1)} %get-tuple-element.123.limits_ref, f32[32,8,128]{2,1,0:T(8,128)S(1)} %get-tuple-element.124.member_ref, ...), custom_call_target="tpu_custom_call" | custom-call | flops 339738624 | tf_op jit(solution)/shard_map/forward/pallas_call | solution.py:696
  59.9 2.6 %all-to-all-start.2 = ((f32[32,8,128]{2,1,0:T(8,128)}), f32[32,8,128]{2,1,0:T(8,128)S(1)}, u32[]{:S(2)}, u32[]{:S(2)}) async-start(f32[32,8,128]{2,1,0:T(8,128)} %get-tuple-element.145), calls=%async_computation.2 | async-start | bytes 262144 | tf_op jit(solution)/shard_map/all_to_all | solution.py:742
  62.6 1.7 collective-permute-start.8
  64.4 6.3 %all-to-all-done.2.gathered_ref = f32[32,8,128]{2,1,0:T(8,128)S(1)} async-done(((f32[32,8,128]{2,1,0:T(8,128)}), f32[32,8,128]{2,1,0:T(8,128)S(1)}, u32[]{:S(2)}, u32[]{:S(2)}) %all-to-all-start.2) | async-done | bytes 131104 | tf_op jit(solution)/shard_map/all_to_all | solution.py:742
  72.0 3.1 %pool.1 = (f32[32,8,128]{2,1,0:T(8,128)}, f32[576,512]{1,0:T(8,128)S(1)}, bf16[576,512]{1,0:T(8,128)(2,1)S(1)}, f32[8,128]{1,0:T(8,128)S(1)}, bf16[864,128]{1,0:...) custom-call(s32[8,128]{1,0:T(8,128)S(1)} %get-tuple-element.123.limits_ref, ...), custom_call_target="tpu_custom_call" | custom-call | flops 75497472 | tf_op jit(solution)/shard_map/pool/pallas_call | solution.py:696
  77.0 2.8 %all-to-all-start.3 = ((f32[32,8,128]{2,1,0:T(8,128)}), f32[32,8,128]{2,1,0:T(8,128)S(1)}, u32[]{:S(2)}, u32[]{:S(2)}) async-start(f32[32,8,128]{2,1,0:T(8,128)} %get-tuple-element.157), calls=%async_computation.3 | async-start | bytes 262144 | tf_op jit(solution)/shard_map/all_to_all | solution.py:742
  81.1 8.0 %all-to-all-done.3.gathered_ref = f32[32,8,128]{2,1,0:T(8,128)S(1)} async-done(((f32[32,8,128]{2,1,0:T(8,128)}), f32[32,8,128]{2,1,0:T(8,128)S(1)}, u32[]{:S(2)}, u32[]{:S(2)}) %all-to-all-start.3) | async-done | bytes 131104 | tf_op jit(solution)/shard_map/all_to_all | solution.py:742
  90.9 6.3 %backward.2 = (f32[32,8,128]{2,1,0:T(8,128)}, f32[512,512]{1,0:T(8,128)S(1)}, bf16[512,512]{1,0:T(8,128)(2,1)S(1)}, f32[8,128]{1,0:T(8,128)S(1)}, bf16[768,128]{...) custom-call(s32[8,128]{1,0:T(8,128)S(1)} %get-tuple-element.123.limits_ref, ...), custom_call_target="tpu_custom_call" | custom-call | flops 301989888 | tf_op jit(solution)/shard_map/backward/pallas_call | solution.py:696
  101.0 2.6 %all-to-all-start.4 = ((f32[32,8,128]{2,1,0:T(8,128)}), f32[32,8,128]{2,1,0:T(8,128)S(1)}, u32[]{:S(2)}, u32[]{:S(2)}) async-start(f32[32,8,128]{2,1,0:T(8,128)} %get-tuple-element.168), calls=%async_computation.4 | async-start | bytes 262144 | tf_op jit(solution)/shard_map/all_to_all | solution.py:742
  104.9 8.5 %all-to-all-done.4.gathered_ref = f32[32,8,128]{2,1,0:T(8,128)S(1)} async-done(((f32[32,8,128]{2,1,0:T(8,128)}), f32[32,8,128]{2,1,0:T(8,128)S(1)}, u32[]{:S(2)}, u32[]{:S(2)}) %all-to-all-start.4) | async-done | bytes 131104 | tf_op jit(solution)/shard_map/all_to_all | solution.py:742
  113.4 6.0 %backward.3 = (f32[32,8,128]{2,1,0:T(8,128)}, f32[448,512]{1,0:T(8,128)S(1)}, bf16[448,512]{1,0:T(8,128)(2,1)S(1)}, f32[8,128]{1,0:T(8,128)S(1)}, bf16[384,128]{...) custom-call(s32[8,128]{1,0:T(8,128)S(1)} %get-tuple-element.123.limits_ref, ...), custom_call_target="tpu_custom_call" | custom-call | flops 264241152 | tf_op jit(solution)/shard_map/backward/pallas_call | solution.py:696
  120.2 5.6 %weight_grad.3 = (f32[4,576,128]{2,1,0:T(8,128)}, bf16[4,576,128]{2,1,0:T(8,128)(2,1)}) custom-call(s32[8,128]{1,0:T(8,128)S(1)} %get-tuple-element.123.limits_ref, f32[32,8,128]{2,1,0:T(8,128)S(1)} %get-tuple-element.124.member_ref, f32[32,8,128]{2,1,0:T(8,128)S(1)} %all-to-all-done.3.gathered_ref, f32[8,128]{1,0:T(8,128)S(1)} %get-tuple-element.160.moments_ref, ...), custom_call_target="tpu_custom_call" | custom-call | flops 226492416 | tf_op jit(solution)/shard_map/weight_grad/pallas_call | solution.py:696
  125.8 2.8 %all-to-all-start.5 = ((f32[32,8,128]{2,1,0:T(8,128)}), f32[32,8,128]{2,1,0:T(8,128)S(1)}, u32[]{:S(2)}, u32[]{:S(2)}) async-start(f32[32,8,128]{2,1,0:T(8,128)} %get-tuple-element.183), calls=%async_computation.5 | async-start | bytes 262144 | tf_op jit(solution)/shard_map/all_to_all | solution.py:742
  128.6 1.5 collective-permute-start.21
  130.8 1.4 collective-permute-start.24
  132.3 5.2 %collective-permute-done.21.rest_2_.rest_6_ = bf16[768,128]{1,0:T(8,128)(2,1)S(1)} collective-permute-done((bf16[768,128]{1,0:T(8,128)(2,1)S(1)}, bf16[768,128]{1,0:T(8,128)(2,1)S(1)}, u32[]{:S(2)}, u32[]{:S(2)}) %collective-permute-start.21) | collective-permute-done | bytes 196640 | tf_op jit(solution)/shard_map/ppermute | solution.py:746
  137.5 2.8 %collective-permute-done.22.rest_3_.rest_7_ = bf16[768,128]{1,0:T(8,128)(2,1)S(1)} collective-permute-done((bf16[768,128]{1,0:T(8,128)(2,1)S(1)}, bf16[768,128]{1,0:T(8,128)(2,1)S(1)}, u32[]{:S(2)}, u32[]{:S(2)}) %collective-permute-start.22) | collective-permute-done | bytes 196640 | tf_op jit(solution)/shard_map/ppermute | solution.py:746
  141.0 5.5 %weight_grad.4 = (f32[4,576,128]{2,1,0:T(8,128)}, bf16[4,576,128]{2,1,0:T(8,128)(2,1)}) custom-call(s32[8,128]{1,0:T(8,128)S(1)} %get-tuple-element.123.limits_ref, f32[32,8,128]{2,1,0:T(8,128)S(1)} %get-tuple-element.124.member_ref, f32[32,8,128]{2,1,0:T(8,128)S(1)} %all-to-all-done.4.gathered_ref, f32[8,128]{1,0:T(8,128)S(1)} %copy-done.21, ...), custom_call_target="tpu_custom_call" | custom-call | flops 226492416 | tf_op jit(solution)/shard_map/weight_grad/pallas_call | solution.py:696
  147.2 5.2 %weight_grad.5 = bf16[8,576,128]{2,1,0:T(8,128)(2,1)} custom-call(s32[8,128]{1,0:T(8,128)S(1)} %get-tuple-element.123.limits_ref, f32[32,8,128]{2,1,0:T(8,128)S(1)} %get-tuple-element.124.member_ref, f32[32,8,128]{2,1,0:T(8,128)S(1)} %all-to-all-done.5.gathered_ref, f32[8,128]{1,0:T(8,128)S(1)} %copy-done.23, f32[3,2,512]{2,1,0:T(2,128)S(1)} %bitcast.45, ...), custom_call_target="tpu_custom_call" | custom-call | flops 226492416 | tf_op jit(solution)/shard_map/weight_grad/pallas_call | solution.py:696
  152.4 6.3 %all-to-all-start.6 = ((bf16[8,576,128]{2,1,0:T(8,128)(2,1)}), bf16[8,576,128]{2,1,0:T(8,128)(2,1)S(1)}, u32[]{:S(2)}, u32[]{:S(2)}) async-start(bf16[8,576,128]{2,1,0:T(8,128)(2,1)} %weight_grad.5), calls=%async_computation.6 | async-start | bytes 2359296 | tf_op jit(solution)/shard_map/all_to_all | solution.py:913
  158.7 2.0 collective-permute-start.26
  160.8 26.9 %collective-permute-done.26.received_hbm = bf16[4,576,128]{2,1,0:T(8,128)(2,1)S(1)} collective-permute-done((bf16[4,576,128]{2,1,0:T(8,128)(2,1)S(1)}, bf16[4,576,128]{2,1,0:T(8,128)(2,1)S(1)}, u32[]{:S(2)}, u32[]{:S(2)}) %collective-permute-start.26) | collective-permute-done | bytes 589856 | tf_op jit(solution)/shard_map/ppermute | solution.py:868
  188.6 2.6 %halve.4 = (f32[2,576,128]{2,1,0:T(8,128)}, bf16[2,576,128]{2,1,0:T(8,128)(2,1)}) custom-call(f32[4,576,128]{2,1,0:T(8,128)} %get-tuple-element.212.keep_hbm, bf16[4,576,128]{2,1,0:T(8,128)(2,1)} %copy-done.32), custom_call_target="tpu_custom_call" | custom-call | tf_op jit(solution)/shard_map/halve/pallas_call | solution.py:696
  191.1 1.5 collective-permute-start.27
  192.7 6.7 %collective-permute-done.29.received_hbm = bf16[4,576,128]{2,1,0:T(8,128)(2,1)S(1)} collective-permute-done((bf16[4,576,128]{2,1,0:T(8,128)(2,1)S(1)}, bf16[4,576,128]{2,1,0:T(8,128)(2,1)S(1)}, u32[]{:S(2)}, u32[]{:S(2)}) %collective-permute-start.29) | collective-permute-done | bytes 589856 | tf_op jit(solution)/shard_map/ppermute | solution.py:868
  200.1 2.6 %halve.6 = (f32[2,576,128]{2,1,0:T(8,128)}, bf16[2,576,128]{2,1,0:T(8,128)(2,1)}) custom-call(f32[4,576,128]{2,1,0:T(8,128)} %get-tuple-element.218.keep_hbm, bf16[4,576,128]{2,1,0:T(8,128)(2,1)} %copy-done.31), custom_call_target="tpu_custom_call" | custom-call | tf_op jit(solution)/shard_map/halve/pallas_call | solution.py:696
  202.7 1.5 collective-permute-start.30
  204.9 2.2 halve.5
  207.1 2.4 %collective-permute-start.28 = (bf16[1,576,128]{2,1,0:T(8,128)(2,1)}, bf16[1,576,128]{2,1,0:T(8,128)(2,1)S(1)}, u32[]{:S(2)}, u32[]{:S(2)}) collective-permute-start(bf16[1,576,128]{2,1,0:T(8,128)(2,1)} %get-tuple-element.217), channel_id=1, source_target_pairs={{0,16},{4,20},{8,24},{12,28},{16,0},{20,4},{24,8},{28,12},{1,17},{... | collective-permute-start | bytes 442376 | tf_op jit(solution)/shard_map/ppermute | solution.py:868
  209.6 4.5 %collective-permute-done.30.received_hbm = bf16[2,576,128]{2,1,0:T(8,128)(2,1)S(1)} collective-permute-done((bf16[2,576,128]{2,1,0:T(8,128)(2,1)}, bf16[2,576,128]{2,1,0:T(8,128)(2,1)S(1)}, u32[]{:S(2)}, u32[]{:S(2)}) %collective-permute-start.30) | collective-permute-done | bytes 294944 | tf_op jit(solution)/shard_map/ppermute | solution.py:868
  214.7 2.3 halve.7
  219.6 4.4 %last.1 = (bf16[384,512]{1,0:T(8,128)(2,1)}, f32[8,128]{1,0:T(8,128)S(1)}, bf16[384,128]{1,0:T(8,128)(2,1)}) custom-call(s32[8,128]{1,0:T(8,128)S(1)} %get-tuple-element.123.limits_ref, f32[32,8,128]{2,1,0:T(8,128)S(1)} %get-tuple-element.124.member_ref, f32[32,8,128]{2,1,0:T(8,128)S(1)} %all-to-all-done.5.gathered_ref, f32[448,512]{1,0:T(8,128)S(1)} %copy-done.11, ...), custom_call_target="tpu_custom_call" | custom-call | flops 226492416 | tf_op jit(solution)/shard_map/last/pallas_call | solution.py:696
  224.1 1.3 squares.1
  225.4 4.8 %all-to-all-start.7 = ((f32[32,1,128]{2,1,0:T(1,128)}), f32[32,1,128]{2,1,0:T(1,128)S(1)}, u32[]{:S(2)}, u32[]{:S(2)}) async-start(f32[32,1,128]{2,1,0:T(1,128)} %get-tuple-element.227), calls=%async_computation.7 | async-start | bytes 32768 | tf_op jit(solution)/shard_map/all_to_all | solution.py:930
  230.9 6.4 %all-to-all-done.7.every_ref = f32[32,1,128]{2,1,0:T(1,128)S(1)} async-done(((f32[32,1,128]{2,1,0:T(1,128)}), f32[32,1,128]{2,1,0:T(1,128)S(1)}, u32[]{:S(2)}, u32[]{:S(2)}) %all-to-all-start.7) | async-done | bytes 16416 | tf_op jit(solution)/shard_map/all_to_all | solution.py:930
  237.3 3.0 %adam.1 = (f32[1,128]{1,0:T(1,128)}, f32[3,576,128]{2,1,0:T(8,128)}, f32[3,576,128]{2,1,0:T(8,128)}, f32[3,576,128]{2,1,0:T(8,128)}, f32[3,2,512]{2,1,0:T(2,128)...) custom-call(f32[32,1,128]{2,1,0:T(1,128)S(1)} %all-to-all-done.7.every_ref, s32[1]{0:T(128)S(6)} %copy.24.step_ref, ...), custom_call_target="tpu_custom_call" | custom-call | tf_op jit(solution)/shard_map/adam/pallas_call | solution.py:696
  (163 shorter events, 33.2 us)
Async XLA Ops:
  2.0 10.1 %collective-permute-start = (bf16[224,512]{1,0:T(8,128)(2,1)S(1)}, bf16[224,512]{1,0:T(8,128)(2,1)S(1)}, u32[]{:S(2)}, u32[]{:S(2)}) collective-permute-start(bf16[224,512]{1,0:T(8,128)(2,1)S(1)} %get-tuple-element.125), channel_id=1, source_target_pairs={{0,1},{1,2},{2,3},{4,5},{5,6},{6,7},{8,9},{9,10},{10,11},{12,13},{... | collective-permute-start | bytes 688136 | tf_op jit(solution)/shard_map/ppermute | solution.py:759
  4.5 7.6 %collective-permute-start.1 = (bf16[224,512]{1,0:T(8,128)(2,1)S(1)}, bf16[224,512]{1,0:T(8,128)(2,1)S(1)}, u32[]{:S(2)}, u32[]{:S(2)}) collective-permute-start(bf16[224,512]{1,0:T(8,128)(2,1)S(1)} %get-tuple-element.126), channel_id=1, source_target_pairs={{1,0},{2,1},{3,2},{5,4},{6,5},{7,6},{9,8},{10,9},{11,10},{13,12},{... | collective-permute-start | bytes 688136 | tf_op jit(solution)/shard_map/ppermute | solution.py:760
  17.3 18.2 %copy-start.3 = (f32[2,3,512]{2,0,1:T(2,128)S(1)}, f32[2,3,512]{2,0,1:T(2,128)}, u32[]{:S(2)}) copy-start(f32[2,3,512]{2,0,1:T(2,128)} %param.16) | copy-start | bytes 36868
  17.3 42.5 %collective-permute-start.5 = (bf16[384,512]{1,0:T(8,128)(2,1)S(1)}, bf16[384,512]{1,0:T(8,128)(2,1)}, u32[]{:S(2)}, u32[]{:S(2)}) collective-permute-start(bf16[384,512]{1,0:T(8,128)(2,1)S(1)} %bitcast.36), channel_id=1, source_target_pairs={{0,1},{1,0},{2,3},{3,2},{4,5},{5,4},{6,7},{7,6},{8,9},{9,8},{10,11... | collective-permute-start | bytes 1179656 | tf_op jit(solution)/shard_map/ppermute | solution.py:750
  20.6 39.2 %collective-permute-start.6 = (bf16[384,512]{1,0:T(8,128)(2,1)S(1)}, bf16[384,512]{1,0:T(8,128)(2,1)}, u32[]{:S(2)}, u32[]{:S(2)}) collective-permute-start(bf16[384,512]{1,0:T(8,128)(2,1)S(1)} %bitcast.37), channel_id=1, source_target_pairs={{0,2},{1,3},{2,0},{3,1},{4,6},{5,7},{6,4},{7,5},{8,10},{9,11},{10,... | collective-permute-start | bytes 1179656 | tf_op jit(solution)/shard_map/ppermute | solution.py:750
  22.3 13.2 %all-to-all-start = ((f32[32,8,128]{2,1,0:T(8,128)}), f32[32,8,128]{2,1,0:T(8,128)S(1)}, u32[]{:S(2)}, u32[]{:S(2)}) async-start(f32[32,8,128]{2,1,0:T(8,128)} %get-tuple-element.132), calls=%async_computation | async-start | bytes 262144 | tf_op jit(solution)/shard_map/all_to_all | solution.py:742
  27.2 18.7 %collective-permute-start.2 = (bf16[160,128]{1,0:T(8,128)(2,1)}, bf16[160,128]{1,0:T(8,128)(2,1)S(1)}, u32[]{:S(2)}, u32[]{:S(2)}) collective-permute-start(bf16[160,128]{1,0:T(8,128)(2,1)} %get-tuple-element.141), channel_id=1, source_target_pairs={{0,1},{1,0},{2,3},{3,2},{4,5},{5,4},{6,7},{7,6},{8,9},{9,8},{10,11... | collective-permute-start | bytes 122888 | tf_op jit(solution)/shard_map/ppermute | solution.py:746
  27.6 18.7 %collective-permute-start.3 = (bf16[160,128]{1,0:T(8,128)(2,1)}, bf16[160,128]{1,0:T(8,128)(2,1)S(1)}, u32[]{:S(2)}, u32[]{:S(2)}) collective-permute-start(bf16[160,128]{1,0:T(8,128)(2,1)} %get-tuple-element.142), channel_id=1, source_target_pairs={{0,2},{1,3},{2,0},{3,1},{4,6},{5,7},{6,4},{7,5},{8,10},{9,11},{10,... | collective-permute-start | bytes 122888 | tf_op jit(solution)/shard_map/ppermute | solution.py:746
  30.5 29.3 %collective-permute-start.4 = (bf16[160,128]{1,0:T(8,128)(2,1)S(1)}, bf16[160,128]{1,0:T(8,128)(2,1)S(1)}, u32[]{:S(2)}, u32[]{:S(2)}) collective-permute-start(bf16[160,128]{1,0:T(8,128)(2,1)S(1)} %get-tuple-element.143), channel_id=1, source_target_pairs={{0,3},{1,2},{2,1},{3,0},{4,7},{5,6},{6,5},{7,4},{8,11},{9,10},{10,... | collective-permute-start | bytes 122888 | tf_op jit(solution)/shard_map/ppermute | solution.py:746
  41.5 17.2 %copy-start.22 = (f32[8,128]{1,0:T(8,128)}, f32[8,128]{1,0:T(8,128)S(1)}, u32[]{:S(2)}) copy-start(f32[8,128]{1,0:T(8,128)S(1)} %get-tuple-element.173.moments_below_ref.moments_ref) | copy-start | bytes 12292
  41.6 12.6 %all-to-all-start.1 = ((f32[32,8,128]{2,1,0:T(8,128)}), f32[32,8,128]{2,1,0:T(8,128)S(1)}, u32[]{:S(2)}, u32[]{:S(2)}) async-start(f32[32,8,128]{2,1,0:T(8,128)} %get-tuple-element.136), calls=%async_computation.1 | async-start | bytes 262144 | tf_op jit(solution)/shard_map/all_to_all | solution.py:742
  45.9 30.6 %collective-permute-start.10 = (bf16[384,512]{1,0:T(8,128)(2,1)}, bf16[384,512]{1,0:T(8,128)(2,1)}, u32[]{:S(2)}, u32[]{:S(2)}) collective-permute-start(bf16[384,512]{1,0:T(8,128)(2,1)} %get-tuple-element.193.rest_8_), channel_id=1, source_target_pairs={{0,1},{1,0},{2,3},{3,2},{4,5},{5,4},{6,7},{7,6},{8,9},{9,8},{10,11... | collective-permute-start | bytes 1179656 | tf_op jit(solution)/shard_map/ppermute | solution.py:750
  46.2 30.3 %collective-permute-start.11 = (bf16[384,512]{1,0:T(8,128)(2,1)}, bf16[384,512]{1,0:T(8,128)(2,1)}, u32[]{:S(2)}, u32[]{:S(2)}) collective-permute-start(bf16[384,512]{1,0:T(8,128)(2,1)} %get-tuple-element.193.rest_8_), channel_id=1, source_target_pairs={{0,2},{1,3},{2,0},{3,1},{4,6},{5,7},{6,4},{7,5},{8,10},{9,11},{10,... | collective-permute-start | bytes 1179656 | tf_op jit(solution)/shard_map/ppermute | solution.py:750
  59.8 21.3 %copy-start.19 = (f32[8,128]{1,0:T(8,128)}, f32[8,128]{1,0:T(8,128)S(1)}, u32[]{:S(2)}) copy-start(f32[8,128]{1,0:T(8,128)S(1)} %get-tuple-element.163.moments_below_ref.moments_ref) | copy-start | bytes 12292
  59.9 10.8 %all-to-all-start.2 = ((f32[32,8,128]{2,1,0:T(8,128)}), f32[32,8,128]{2,1,0:T(8,128)S(1)}, u32[]{:S(2)}, u32[]{:S(2)}) async-start(f32[32,8,128]{2,1,0:T(8,128)} %get-tuple-element.145), calls=%async_computation.2 | async-start | bytes 262144 | tf_op jit(solution)/shard_map/all_to_all | solution.py:742
  62.5 13.4 %collective-permute-start.7 = (bf16[384,128]{1,0:T(8,128)(2,1)}, bf16[384,128]{1,0:T(8,128)(2,1)S(1)}, u32[]{:S(2)}, u32[]{:S(2)}) collective-permute-start(bf16[384,128]{1,0:T(8,128)(2,1)} %get-tuple-element.153), channel_id=1, source_target_pairs={{0,1},{1,0},{2,3},{3,2},{4,5},{5,4},{6,7},{7,6},{8,9},{9,8},{10,11... | collective-permute-start | bytes 294920 | tf_op jit(solution)/shard_map/ppermute | solution.py:746
  62.6 13.4 %collective-permute-start.8 = (bf16[384,128]{1,0:T(8,128)(2,1)}, bf16[384,128]{1,0:T(8,128)(2,1)S(1)}, u32[]{:S(2)}, u32[]{:S(2)}) collective-permute-start(bf16[384,128]{1,0:T(8,128)(2,1)} %get-tuple-element.154), channel_id=1, source_target_pairs={{0,2},{1,3},{2,0},{3,1},{4,6},{5,7},{6,4},{7,5},{8,10},{9,11},{10,... | collective-permute-start | bytes 294920 | tf_op jit(solution)/shard_map/ppermute | solution.py:746
  64.3 12.1 %collective-permute-start.9 = (bf16[384,128]{1,0:T(8,128)(2,1)}, bf16[384,128]{1,0:T(8,128)(2,1)S(1)}, u32[]{:S(2)}, u32[]{:S(2)}) collective-permute-start(bf16[384,128]{1,0:T(8,128)(2,1)} %get-tuple-element.155), channel_id=1, source_target_pairs={{0,3},{1,2},{2,1},{3,0},{4,7},{5,6},{6,5},{7,4},{8,11},{9,10},{10,... | collective-permute-start | bytes 294920 | tf_op jit(solution)/shard_map/ppermute | solution.py:746
  75.9 21.4 %copy-start.35 = (bf16[384,128]{1,0:T(8,128)(2,1)}, bf16[384,128]{1,0:T(8,128)(2,1)S(1)}, u32[]{:S(2)}) copy-start(bf16[384,128]{1,0:T(8,128)(2,1)S(1)} %collective-permute-done.7.rest_5_) | copy-start | bytes 294916
  75.9 22.4 %collective-permute-start.14 = (bf16[384,512]{1,0:T(8,128)(2,1)}, bf16[384,512]{1,0:T(8,128)(2,1)}, u32[]{:S(2)}, u32[]{:S(2)}) collective-permute-start(bf16[384,512]{1,0:T(8,128)(2,1)} %get-tuple-element.179.rest_8_), channel_id=1, source_target_pairs={{0,1},{1,0},{2,3},{3,2},{4,5},{5,4},{6,7},{7,6},{8,9},{9,8},{10,11... | collective-permute-start | bytes 1179656 | tf_op jit(solution)/shard_map/ppermute | solution.py:750
  76.1 21.1 %copy-start.36 = (bf16[384,128]{1,0:T(8,128)(2,1)}, bf16[384,128]{1,0:T(8,128)(2,1)S(1)}, u32[]{:S(2)}) copy-start(bf16[384,128]{1,0:T(8,128)(2,1)S(1)} %collective-permute-done.8.rest_6_) | copy-start | bytes 294916
  76.1 22.2 %collective-permute-start.15 = (bf16[384,512]{1,0:T(8,128)(2,1)}, bf16[384,512]{1,0:T(8,128)(2,1)}, u32[]{:S(2)}, u32[]{:S(2)}) collective-permute-start(bf16[384,512]{1,0:T(8,128)(2,1)} %get-tuple-element.179.rest_8_), channel_id=1, source_target_pairs={{0,2},{1,3},{2,0},{3,1},{4,6},{5,7},{6,4},{7,5},{8,10},{9,11},{10,... | collective-permute-start | bytes 1179656 | tf_op jit(solution)/shard_map/ppermute | solution.py:750
  76.5 21.8 %collective-permute-start.12 = (bf16[384,512]{1,0:T(8,128)(2,1)}, bf16[384,512]{1,0:T(8,128)(2,1)}, u32[]{:S(2)}, u32[]{:S(2)}) collective-permute-start(bf16[384,512]{1,0:T(8,128)(2,1)} %collective-permute-done.6.rest_10_), channel_id=1, source_target_pairs={{0,1},{1,0},{2,3},{3,2},{4,5},{5,4},{6,7},{7,6},{8,9},{9,8},{10,11... | collective-permute-start | bytes 1179656 | tf_op jit(solution)/shard_map/ppermute | solution.py:750
  76.5 21.8 %collective-permute-start.13 = (bf16[384,512]{1,0:T(8,128)(2,1)}, bf16[384,512]{1,0:T(8,128)(2,1)}, u32[]{:S(2)}, u32[]{:S(2)}) collective-permute-start(bf16[384,512]{1,0:T(8,128)(2,1)} %collective-permute-done.11.rest_10_), channel_id=1, source_target_pairs={{0,1},{1,0},{2,3},{3,2},{4,5},{5,4},{6,7},{7,6},{8,9},{9,8},{10,11... | collective-permute-start | bytes 1179656 | tf_op jit(solution)/shard_map/ppermute | solution.py:750
  77.0 12.1 %all-to-all-start.3 = ((f32[32,8,128]{2,1,0:T(8,128)}), f32[32,8,128]{2,1,0:T(8,128)S(1)}, u32[]{:S(2)}, u32[]{:S(2)}) async-start(f32[32,8,128]{2,1,0:T(8,128)} %get-tuple-element.157), calls=%async_computation.3 | async-start | bytes 262144 | tf_op jit(solution)/shard_map/all_to_all | solution.py:742
  98.3 15.1 %copy-start.21 = (f32[8,128]{1,0:T(8,128)S(1)}, f32[8,128]{1,0:T(8,128)}, u32[]{:S(2)}) copy-start(f32[8,128]{1,0:T(8,128)} %copy-done.19) | copy-start | bytes 12292
  98.3 15.1 %copy-start.23 = (f32[8,128]{1,0:T(8,128)S(1)}, f32[8,128]{1,0:T(8,128)}, u32[]{:S(2)}) copy-start(f32[8,128]{1,0:T(8,128)} %copy-done.22) | copy-start | bytes 12292
  98.3 15.1 %copy-start.7 = (f32[512,512]{1,0:T(8,128)S(1)}, f32[512,512]{1,0:T(8,128)}, u32[]{:S(2)}) copy-start(f32[512,512]{1,0:T(8,128)} %copy-done.6) | copy-start | bytes 3145732
  98.3 21.1 %collective-permute-start.19 = (bf16[384,512]{1,0:T(8,128)(2,1)}, bf16[384,512]{1,0:T(8,128)(2,1)}, u32[]{:S(2)}, u32[]{:S(2)}) collective-permute-start(bf16[384,512]{1,0:T(8,128)(2,1)} %collective-permute-done.15.rest_10_), channel_id=1, source_target_pairs={{0,1},{1,0},{2,3},{3,2},{4,5},{5,4},{6,7},{7,6},{8,9},{9,8},{10,11... | collective-permute-start | bytes 1179656 | tf_op jit(solution)/shard_map/ppermute | solution.py:750
  98.4 21.0 %collective-permute-start.16 = (bf16[864,128]{1,0:T(8,128)(2,1)}, bf16[864,128]{1,0:T(8,128)(2,1)S(1)}, u32[]{:S(2)}, u32[]{:S(2)}) collective-permute-start(bf16[864,128]{1,0:T(8,128)(2,1)} %get-tuple-element.176), channel_id=1, source_target_pairs={{0,1},{1,0},{2,3},{3,2},{4,5},{5,4},{6,7},{7,6},{8,9},{9,8},{10,11... | collective-permute-start | bytes 663560 | tf_op jit(solution)/shard_map/ppermute | solution.py:746
  98.9 20.5 %collective-permute-start.17 = (bf16[864,128]{1,0:T(8,128)(2,1)}, bf16[864,128]{1,0:T(8,128)(2,1)}, u32[]{:S(2)}, u32[]{:S(2)}) collective-permute-start(bf16[864,128]{1,0:T(8,128)(2,1)} %get-tuple-element.177), channel_id=1, source_target_pairs={{0,2},{1,3},{2,0},{3,1},{4,6},{5,7},{6,4},{7,5},{8,10},{9,11},{10,... | collective-permute-start | bytes 663560 | tf_op jit(solution)/shard_map/ppermute | solution.py:746
  99.5 19.9 %collective-permute-start.18 = (bf16[864,128]{1,0:T(8,128)(2,1)}, bf16[864,128]{1,0:T(8,128)(2,1)}, u32[]{:S(2)}, u32[]{:S(2)}) collective-permute-start(bf16[864,128]{1,0:T(8,128)(2,1)} %get-tuple-element.178), channel_id=1, source_target_pairs={{0,3},{1,2},{2,1},{3,0},{4,7},{5,6},{6,5},{7,4},{8,11},{9,10},{10,... | collective-permute-start | bytes 663560 | tf_op jit(solution)/shard_map/ppermute | solution.py:746
  100.3 31.9 %collective-permute-start.20 = (bf16[768,128]{1,0:T(8,128)(2,1)}, bf16[768,128]{1,0:T(8,128)(2,1)}, u32[]{:S(2)}, u32[]{:S(2)}) collective-permute-start(bf16[768,128]{1,0:T(8,128)(2,1)} %get-tuple-element.190), channel_id=1, source_target_pairs={{0,1},{1,0},{2,3},{3,2},{4,5},{5,4},{6,7},{7,6},{8,9},{9,8},{10,11... | collective-permute-start | bytes 589832 | tf_op jit(solution)/shard_map/ppermute | solution.py:746
  101.0 12.4 %all-to-all-start.4 = ((f32[32,8,128]{2,1,0:T(8,128)}), f32[32,8,128]{2,1,0:T(8,128)S(1)}, u32[]{:S(2)}, u32[]{:S(2)}) async-start(f32[32,8,128]{2,1,0:T(8,128)} %get-tuple-element.168), calls=%async_computation.4 | async-start | bytes 262144 | tf_op jit(solution)/shard_map/all_to_all | solution.py:742
  125.8 20.8 %all-to-all-start.5 = ((f32[32,8,128]{2,1,0:T(8,128)}), f32[32,8,128]{2,1,0:T(8,128)S(1)}, u32[]{:S(2)}, u32[]{:S(2)}) async-start(f32[32,8,128]{2,1,0:T(8,128)} %get-tuple-element.183), calls=%async_computation.5 | async-start | bytes 262144 | tf_op jit(solution)/shard_map/all_to_all | solution.py:742
  128.6 8.9 %collective-permute-start.21 = (bf16[768,128]{1,0:T(8,128)(2,1)S(1)}, bf16[768,128]{1,0:T(8,128)(2,1)S(1)}, u32[]{:S(2)}, u32[]{:S(2)}) collective-permute-start(bf16[768,128]{1,0:T(8,128)(2,1)S(1)} %copy-done.47), channel_id=1, source_target_pairs={{0,2},{1,3},{2,0},{3,1},{4,6},{5,7},{6,4},{7,5},{8,10},{9,11},{10,... | collective-permute-start | bytes 589832 | tf_op jit(solution)/shard_map/ppermute | solution.py:746
  130.1 10.2 %collective-permute-start.22 = (bf16[768,128]{1,0:T(8,128)(2,1)S(1)}, bf16[768,128]{1,0:T(8,128)(2,1)S(1)}, u32[]{:S(2)}, u32[]{:S(2)}) collective-permute-start(bf16[768,128]{1,0:T(8,128)(2,1)S(1)} %copy-done.46), channel_id=1, source_target_pairs={{0,3},{1,2},{2,1},{3,0},{4,7},{5,6},{6,5},{7,4},{8,11},{9,10},{10,... | collective-permute-start | bytes 589832 | tf_op jit(solution)/shard_map/ppermute | solution.py:746
  130.1 16.4 %collective-permute-start.23 = (bf16[384,128]{1,0:T(8,128)(2,1)S(1)}, bf16[384,128]{1,0:T(8,128)(2,1)S(1)}, u32[]{:S(2)}, u32[]{:S(2)}) collective-permute-start(bf16[384,128]{1,0:T(8,128)(2,1)S(1)} %copy-done.50), channel_id=1, source_target_pairs={{0,1},{1,0},{2,3},{3,2},{4,5},{5,4},{6,7},{7,6},{8,9},{9,8},{10,11... | collective-permute-start | bytes 294920 | tf_op jit(solution)/shard_map/ppermute | solution.py:746
  130.8 15.7 %collective-permute-start.24 = (bf16[384,128]{1,0:T(8,128)(2,1)S(1)}, bf16[384,128]{1,0:T(8,128)(2,1)S(1)}, u32[]{:S(2)}, u32[]{:S(2)}) collective-permute-start(bf16[384,128]{1,0:T(8,128)(2,1)S(1)} %copy-done.49), channel_id=1, source_target_pairs={{0,2},{1,3},{2,0},{3,1},{4,6},{5,7},{6,4},{7,5},{8,10},{9,11},{10,... | collective-permute-start | bytes 294920 | tf_op jit(solution)/shard_map/ppermute | solution.py:746
  132.2 14.3 %collective-permute-start.25 = (bf16[384,128]{1,0:T(8,128)(2,1)S(1)}, bf16[384,128]{1,0:T(8,128)(2,1)S(1)}, u32[]{:S(2)}, u32[]{:S(2)}) collective-permute-start(bf16[384,128]{1,0:T(8,128)(2,1)S(1)} %copy-done.48), channel_id=1, source_target_pairs={{0,3},{1,2},{2,1},{3,0},{4,7},{5,6},{6,5},{7,4},{8,11},{9,10},{10,... | collective-permute-start | bytes 294920 | tf_op jit(solution)/shard_map/ppermute | solution.py:746
  152.4 71.6 %all-to-all-start.6 = ((bf16[8,576,128]{2,1,0:T(8,128)(2,1)}), bf16[8,576,128]{2,1,0:T(8,128)(2,1)S(1)}, u32[]{:S(2)}, u32[]{:S(2)}) async-start(bf16[8,576,128]{2,1,0:T(8,128)(2,1)} %weight_grad.5), calls=%async_computation.6 | async-start | bytes 2359296 | tf_op jit(solution)/shard_map/all_to_all | solution.py:913
  158.7 29.0 %collective-permute-start.26 = (bf16[4,576,128]{2,1,0:T(8,128)(2,1)S(1)}, bf16[4,576,128]{2,1,0:T(8,128)(2,1)S(1)}, u32[]{:S(2)}, u32[]{:S(2)}) collective-permute-start(bf16[4,576,128]{2,1,0:T(8,128)(2,1)S(1)} %copy-done.45), channel_id=1, source_target_pairs={{0,4},{4,0},{8,12},{12,8},{16,20},{20,16},{24,28},{28,24},{1,5},{5... | collective-permute-start | bytes 1769480 | tf_op jit(solution)/shard_map/ppermute | solution.py:868
  160.7 38.6 %collective-permute-start.29 = (bf16[4,576,128]{2,1,0:T(8,128)(2,1)S(1)}, bf16[4,576,128]{2,1,0:T(8,128)(2,1)S(1)}, u32[]{:S(2)}, u32[]{:S(2)}) collective-permute-start(bf16[4,576,128]{2,1,0:T(8,128)(2,1)S(1)} %copy-done.44), channel_id=1, source_target_pairs={{0,4},{4,0},{8,12},{12,8},{16,20},{20,16},{24,28},{28,24},{1,5},{5... | collective-permute-start | bytes 1769480 | tf_op jit(solution)/shard_map/ppermute | solution.py:868
  191.1 13.1 %collective-permute-start.27 = (bf16[2,576,128]{2,1,0:T(8,128)(2,1)}, bf16[2,576,128]{2,1,0:T(8,128)(2,1)S(1)}, u32[]{:S(2)}, u32[]{:S(2)}) collective-permute-start(bf16[2,576,128]{2,1,0:T(8,128)(2,1)} %get-tuple-element.215), channel_id=1, source_target_pairs={{0,8},{4,12},{8,0},{12,4},{16,24},{20,28},{24,16},{28,20},{1,9},{5... | collective-permute-start | bytes 884744 | tf_op jit(solution)/shard_map/ppermute | solution.py:868
  202.7 11.3 %collective-permute-start.30 = (bf16[2,576,128]{2,1,0:T(8,128)(2,1)}, bf16[2,576,128]{2,1,0:T(8,128)(2,1)S(1)}, u32[]{:S(2)}, u32[]{:S(2)}) collective-permute-start(bf16[2,576,128]{2,1,0:T(8,128)(2,1)} %get-tuple-element.221), channel_id=1, source_target_pairs={{0,8},{4,12},{8,0},{12,4},{16,24},{20,28},{24,16},{28,20},{1,9},{5... | collective-permute-start | bytes 884744 | tf_op jit(solution)/shard_map/ppermute | solution.py:868
  207.1 16.9 %collective-permute-start.28 = (bf16[1,576,128]{2,1,0:T(8,128)(2,1)}, bf16[1,576,128]{2,1,0:T(8,128)(2,1)S(1)}, u32[]{:S(2)}, u32[]{:S(2)}) collective-permute-start(bf16[1,576,128]{2,1,0:T(8,128)(2,1)} %get-tuple-element.217), channel_id=1, source_target_pairs={{0,16},{4,20},{8,24},{12,28},{16,0},{20,4},{24,8},{28,12},{1,17},{... | collective-permute-start | bytes 442376 | tf_op jit(solution)/shard_map/ppermute | solution.py:868
  217.0 7.0 %collective-permute-start.31 = (bf16[1,576,128]{2,1,0:T(8,128)(2,1)}, bf16[1,576,128]{2,1,0:T(8,128)(2,1)S(1)}, u32[]{:S(2)}, u32[]{:S(2)}) collective-permute-start(bf16[1,576,128]{2,1,0:T(8,128)(2,1)} %get-tuple-element.223), channel_id=1, source_target_pairs={{0,16},{4,20},{8,24},{12,28},{16,0},{20,4},{24,8},{28,12},{1,17},{... | collective-permute-start | bytes 442376 | tf_op jit(solution)/shard_map/ppermute | solution.py:868
  225.4 11.9 %all-to-all-start.7 = ((f32[32,1,128]{2,1,0:T(1,128)}), f32[32,1,128]{2,1,0:T(1,128)S(1)}, u32[]{:S(2)}, u32[]{:S(2)}) async-start(f32[32,1,128]{2,1,0:T(1,128)} %get-tuple-element.227), calls=%async_computation.7 | async-start | bytes 32768 | tf_op jit(solution)/shard_map/all_to_all | solution.py:930
  (43 other events, 230.3 us)

commit v3 on v2

--- a/solution.py
+++ b/solution.py
@@ -141,7 +141,7 @@
     return total
 
 
-HEAD = 2
+HEAD = 1
 
 
 class Weights:
@@ -229,14 +229,16 @@
 
 
 def kernel_spans(sz, given_ref, *rest):
-    shares = rest[: sz.bands]
+    shares, sems = rest[: sz.bands], rest[sz.bands]
+    copies = Copies(sems)
     span = sz.rows // 2 * (sz.width // 2)
-    for n, share in enumerate(shares):
-        start = pl.multiple_of((lax.axis_index("rows") ^ n) * span, span)
-        share[...] = given_ref[pl.ds(start, share.shape[0]), :]
-
-
-def kernel_edges(sz, x_hbm, index_hbm, low_ref, high_ref, index_ref, sems):
+    wait(*[
+        copies.start(line_share(given_ref, (lax.axis_index("rows") ^ n) * span, span, share.shape[0]), share)
+        for n, share in enumerate(shares)
+    ])
+
+
+def kernel_edges(sz, x_hbm, index_hbm, low_ref, high_ref, x_ref, index_ref, sems):
     copies = Copies(sems)
     edge = HALO * sz.width
     few = sz.width
@@ -246,6 +248,7 @@
     rest = [
         copies.start(x_hbm.at[pl.ds(sz.pixels - edge, edge)], low_ref.at[pl.ds(0, edge)]),
         copies.start(x_hbm.at[pl.ds(0, edge)], high_ref.at[pl.ds(0, edge)]),
+        copies.start(x_hbm, x_ref),
     ]
     wait(first, second)
     low_ref[edge : edge + few, :] = index_ref[0].astype(BF16)
@@ -279,8 +282,10 @@
     )
 
 
-def kernel_first(sz, limits_ref, up_ref, x_ref, down_ref, head_ref, weights_hbm, stats_ref, conv_ref, x3_ref, buffer_ref, sems):
-    weights = Weights(Copies(sems), head_ref, weights_hbm, buffer_ref, 0)
+def kernel_first(sz, limits_ref, up_ref, x_ref, down_ref, head_ref, weights_hbm, stats_ref, conv_ref, act_hbm, x3_ref,
+                 buffer_ref, sems):
+    copies = Copies(sems)
+    weights = Weights(copies, head_ref, weights_hbm, buffer_ref, 0)
     masks = Masks(sz, limits_ref)
     stats = Stats(sz)
 
@@ -300,7 +305,9 @@
     for row in range(sz.rows + 2 * HALO):
         prepare(row)
     work(0, sz.rows + 2 * HALO - 2)
+    out = copies.start(x_ref, act_hbm)
     put_stats(sz, stats.first, stats.second, stats_ref)
+    wait(out)
 
 
 def norm_of(sz, gathered_ref, member_ref):
@@ -309,10 +316,7 @@
 
 
 def kernel_forward(sz, layer, limits_ref, member_ref, gathered_ref, before_ref, norm_ref, head_ref, weights_hbm, *rest):
-    if layer == 1:
-        stats_ref, conv_ref, moments_ref, act_hbm, saved_hbm, *shares, normed_ref, x3_ref, buffer_ref, sems = rest
-    else:
-        stats_ref, conv_ref, moments_ref, act_hbm, saved_hbm, x3_ref, buffer_ref, sems = rest
+    stats_ref, conv_ref, moments_ref, act_hbm, saved_hbm, x3_ref, buffer_ref, sems = rest
     copies = Copies(sems)
     weights = Weights(copies, head_ref, weights_hbm, buffer_ref, layer)
     halo = HALO - layer
@@ -331,12 +335,8 @@
         value = before_ref[line(sz, row), :]
         act, _ = silu_parts(value * scale + offset)
         put_shifted(sz, masks, x3_ref, row, act * tiled(sz, masks.valid(row - halo)))
-        if layer == 1 and halo <= row < halo + sz.rows:
-            normed_ref[line(sz, row - halo), :] = ((value - mean) * inverse).astype(BF16)
         if row == halo + sz.rows - 1:
             outs.append(copies.start(x3_ref.at[pl.ds(halo * sz.width, sz.pixels), pl.ds(c, c)], act_hbm))
-            if layer == 1:
-                outs.extend(send_shares(sz, copies, normed_ref, shares, 0))
 
     def work(first, last):
         conv_rows(sz, x3_ref, weights, conv_ref, last)
@@ -479,16 +479,14 @@
             below_ref[line(sz, row), :] = grad
             if 0 <= own < sz.rows:
                 grad16_ref[line(sz, own), :] = grad.astype(BF16)
-                if below > 0:
-                    normed16_ref[line(sz, own), :] = normed.astype(BF16)
+                normed16_ref[line(sz, own), :] = normed.astype(BF16)
                 stats.add(grad, grad * normed)
 
     for row in range(rows):
         prepare(row)
     work(0, rows - 2)
     outs += send_shares(sz, copies, grad16_ref, shares, 0)
-    if below > 0:
-        outs += send_shares(sz, copies, normed16_ref, shares, sz.pixels)
+    outs += send_shares(sz, copies, normed16_ref, shares, sz.pixels)
     put_stats(sz, stats.first, stats.second, stats_ref)
     totals_ref[...] = all_sums(gathered_ref)
     wait(*outs)
@@ -530,7 +528,6 @@
     w, q, c, bands = sz.width, sz.quarter, sz.channels, sz.bands
     pixels = sz.height * w
     given, rest = rest[:bands], rest[bands:]
-    values, rest = rest[:bands], rest[bands:]
     acts, rest = rest[:bands], rest[bands:]
     if layer == 0:
         out_ref, grad_ref, normed_ref, act_ref, x9_ref, sems = rest
@@ -541,7 +538,7 @@
     inputs = []
     for n in range(bands):
         start = (lax.axis_index("rows") ^ n) * sz.pixels
-        for source, target, top in ((given[n], grad_ref, first[0]), (values[n], normed_ref, first[1])):
+        for source, target, top in ((given[n], grad_ref, first[0]), (given[n], normed_ref, first[1])):
             inputs.append(
                 copies.start(source.at[pl.ds(top, sz.pixels)], line_share(target, start, sz.pixels, sz.pixels))
             )
@@ -622,21 +619,29 @@
     wait(first, copies.start(keep_ref.at[pl.ds(0, half)], next_keep_hbm))
 
 
-def kernel_squares(sz, received_ref, keep1_ref, last1_ref, keep2_ref, last2_ref, totals2_ref, totals1_ref,
-                   totals0_ref, squares_ref, shard_ref, norm_grad_ref, _):
-    value = received_ref[0].astype(F32)
-    for m in range(1, sz.maps):
-        value = value + received_ref[m].astype(F32)
-    values = [value, keep1_ref[0] + last1_ref[0].astype(F32), keep2_ref[0] + last2_ref[0].astype(F32)]
-    total = jnp.zeros((1, sz.quarter), F32)
-    for layer, value in enumerate(values):
-        shard_ref[layer] = value
-        total = total + jnp.sum(value * value, axis=0, keepdims=True)
-    squares_ref[...] = jnp.broadcast_to(total[None], squares_ref.shape)
+def kernel_squares(sz, received_ref, keep1_hbm, last1_hbm, keep2_hbm, last2_hbm, totals2_ref, totals1_ref,
+                   totals0_ref, squares_ref, shard_ref, norm_grad_ref, keep_ref, last_ref, sems):
+    copies = Copies(sems)
+    loads = [
+        copies.start(source.at[0], target.at[k])
+        for k, pair in enumerate(((keep1_hbm, last1_hbm), (keep2_hbm, last2_hbm)))
+        for source, target in zip(pair, (keep_ref, last_ref))
+    ]
     for layer, ref in enumerate((totals0_ref, totals1_ref, totals2_ref)):
         shift_row, gain_row = split_rows(ref[...], sz.channels)
         norm_grad_ref[layer, 0:1, :] = gain_row
         norm_grad_ref[layer, 1:2, :] = shift_row
+    value = received_ref[0].astype(F32)
+    for m in range(1, sz.maps):
+        value = value + received_ref[m].astype(F32)
+    shard_ref[0] = value
+    total = jnp.sum(value * value, axis=0, keepdims=True)
+    wait(*loads)
+    for layer in (1, 2):
+        value = keep_ref[layer - 1] + last_ref[layer - 1].astype(F32)
+        shard_ref[layer] = value
+        total = total + jnp.sum(value * value, axis=0, keepdims=True)
+    squares_ref[...] = jnp.broadcast_to(total[None], squares_ref.shape)
 
 
 def kernel_adam(sz, rate, every_ref, step_ref, shard_ref, master_hbm, first_hbm, second_hbm, norm_grad_ref, norm_ref,
@@ -688,7 +693,7 @@
     return first_new, second_new, param - rate * (update + decay * param)
 
 
-def call(kernel, name, outs, ins, scratch=(), flops=0, moved=0, hbm_ins=(), hbm_outs=(), smem_ins=()):
+def call(kernel, name, outs, ins, scratch=(), flops=0, moved=0, hbm_ins=(), hbm_outs=(), smem_ins=(), sems=1):
     spaces_in = [
         pltpu.SMEM if k in smem_ins else pltpu.HBM if k in hbm_ins else pltpu.VMEM for k in range(len(ins))
     ]
@@ -698,9 +703,9 @@
         out_shape=tuple(space(out.shape, out.dtype) for space, out in zip(spaces_out, outs)),
         in_specs=[spec(space) for space in spaces_in],
         out_specs=tuple(spec(space) for space in spaces_out),
-        scratch_shapes=list(scratch) + [pltpu.SemaphoreType.DMA((32,))],
+        scratch_shapes=list(scratch) + [pltpu.SemaphoreType.DMA((sems,))],
         compiler_params=params(SPACE),
-        cost_estimate=pl.CostEstimate(flops=flops // 8, bytes_accessed=moved, transcendentals=0),
+        cost_estimate=pl.CostEstimate(flops=flops, bytes_accessed=moved, transcendentals=0),
         name=name,
     )(*[v if k in smem_ins else pltpu.with_memory_space_constraint(v, spaces_in[k]) for k, v in enumerate(ins)])
 
@@ -751,10 +756,10 @@
 
     tie = lax.optimization_barrier
 
-    low, high = call(
+    low, high, near = call(
         functools.partial(kernel_edges, sz), "edges",
-        [shape((edge + 2 * half, c), BF16)] * 2, [x, index],
-        [pltpu.VMEM((2, 2 * half, c), jnp.int32)], hbm_ins=(0, 1),
+        [shape((edge + 2 * half, c), BF16)] * 2 + [pixel_shape(sz.rows, BF16)], [x, index],
+        [pltpu.VMEM((2, 2 * half, c), jnp.int32)], hbm_ins=(0, 1), sems=5,
     )
     up = lax.ppermute(low, "rows", forward)
     down = lax.ppermute(high, "rows", backward)
@@ -768,17 +773,17 @@
     consts = [limits, member]
 
     rows = sz.rows + 2 * HALO
-    stats, conv = call(
+    stats, conv, kept = call(
         functools.partial(kernel_first, sz), "first",
-        [stats_shape, pixel_shape(rows - 2, F32)], [limits, up, x, down, conv_weights[0, :HEAD], conv_weights],
-        [pixel_space(rows, BF16, 3), weight_space], conv_flops(rows - 2), hbm_ins=(5,),
+        [stats_shape, pixel_shape(rows - 2, F32), pixel_shape(sz.rows, BF16)], [limits, up, near, down, conv_weights[0, :HEAD], conv_weights],
+        [pixel_space(rows, BF16, 3), weight_space], conv_flops(rows - 2), hbm_ins=(5,), hbm_outs=(2,), sems=4,
     )
     def head(layer, weights):
         return weights[layer, :HEAD]
 
     cot_lines = (sz.rows // 2 + 4) * half
-    cots = call(functools.partial(kernel_spans, sz), "spans", share_shapes(cot_lines), [labelled])
-    stats, kept, weights, *cots = tie((stats, x, conv_weights, *cots))
+    cots = call(functools.partial(kernel_spans, sz), "spans", share_shapes(cot_lines), [labelled], hbm_outs=range(bands), sems=bands)
+    stats, weights, *cots = tie((stats, conv_weights, *cots))
     gathered = spread(stats)
     cots = trade(cots)
     acts = [[kept, swap(kept, 1), swap(kept, 2)]]
@@ -791,25 +796,21 @@
             pixel_shape(sz.rows + 2 * layer, F32),
         ]
         scratch = [pixel_space(rows, BF16, 3), weight_space]
-        if layer == 1:
-            outs += share_shapes(sz.pixels)
-            scratch = [pixel_space(sz.rows, BF16)] + scratch
-        stats, conv, moment, act, saved, *shares = call(
+        stats, conv, moment, act, saved = call(
             functools.partial(kernel_forward, sz, layer), "forward", outs,
             consts + [gathered, conv, norms, head(layer, weights), conv_weights], scratch,
-            conv_flops(rows - 2), hbm_ins=(6,), hbm_outs=range(3, 9),
+            conv_flops(rows - 2), hbm_ins=(6,), hbm_outs=(3, 4), sems=5,
         )
         moments.append(moment)
         saves.append(saved)
         if layer == 1:
-            stats, weights = tie((stats, conv_weights))
-            gathered = spread(stats)
-            given0 = trade(shares)
-        else:
-            stats, *rest = tie((stats, *cots, *acts[0]))
+            stats, weights, *rest = tie((stats, conv_weights, *cots, *acts[0]))
             cots, acts[0] = rest[:bands], rest[bands:]
             gathered = spread(stats)
-            acts[0].append(swap(acts[0][2], 1))
+        else:
+            stats, *acts[1] = tie((stats, *acts[1]))
+            gathered = spread(stats)
+        acts[layer - 1].append(swap(acts[layer - 1][2], 1))
         acts.append([act, swap(act, 1), swap(act, 2)])
 
     rows = sz.rows + 2 * (HALO - 3)
@@ -824,14 +825,13 @@
             pltpu.VMEM((c // 128, (rows + 2) * w, 128), F32), pltpu.VMEM((c // 128, sz.pixels, 128), F32),
             pltpu.VMEM((lines, c), BF16), pixel_space(sz.rows, BF16), pixel_space(sz.rows, BF16),
         ],
-        conv_flops(4), hbm_ins=range(5, 12), hbm_outs=range(4, 8),
+        conv_flops(4), hbm_ins=range(5, 8 + bands), hbm_outs=range(4, 4 + bands), sems=3 + 4 * bands,
     )
     moments.append(moment)
-    stats, weights, *rest = tie((stats, conv_weights, *given0, *acts[1]))
-    given0, acts[1] = rest[:bands], rest[bands:]
+    stats, weights, acts[0][3], *acts[2] = tie((stats, conv_weights, acts[0][3], *acts[2]))
     gathered = spread(stats)
     exchanged = trade(shares)
-    acts[1].append(swap(acts[1][2], 1))
+    acts[2].append(swap(acts[2][2], 1))
     pooled_parts = exchanged
 
     totals = [None, None, None]
@@ -844,7 +844,7 @@
     def part_space(parts, dtype):
         return pltpu.VMEM((parts, share, q), dtype)
 
-    def weight_grad(layer, gathered, given, first, normed=None):
+    def weight_grad(layer, gathered, given, first):
         scratch = [
             pltpu.VMEM((sz.height * w, q), BF16),
             pltpu.VMEM((sz.height * w, q), BF16),
@@ -859,21 +859,27 @@
             scratch.append(pltpu.VMEM((c, 9 * q), F32))
         return call(
             functools.partial(kernel_weight_grad, sz, layer, first), "weight_grad", outs,
-            consts + [gathered, moments[layer], norms] + given + (normed or given) + acts[layer], scratch, conv_flops(sz.rows),
-            hbm_ins=range(5, 17), hbm_outs=() if layer == 0 else (0, 1),
+            consts + [gathered, moments[layer], norms] + given + acts[layer], scratch, conv_flops(sz.rows),
+            hbm_ins=range(5, 5 + 2 * bands), hbm_outs=() if layer == 0 else (0, 1), sems=3 * bands + 2,
         )
 
-    def halve(keep, send):
-        for k in range(steps):
-            received = lax.ppermute(send, "maps", [(m, m ^ (1 << k)) for m in range(n_maps)])
-            if k == steps - 1:
-                return keep, received
-            size = keep.shape[0] // 2
-            keep, send = call(
-                kernel_halve, "halve", [part_shape(size, dtype) for dtype in (F32, BF16)], [keep, received],
-                [part_space(2 * size, F32), part_space(2 * size, BF16), part_space(size, BF16)],
-                hbm_ins=(0, 1), hbm_outs=(0, 1),
-            )
+    def step_of(send, k):
+        return lax.ppermute(send, "maps", [(m, m ^ (1 << k)) for m in range(n_maps)])
+
+    def halved(keep, received):
+        size = keep.shape[0] // 2
+        return call(
+            kernel_halve, "halve", [part_shape(size, dtype) for dtype in (F32, BF16)], [keep, received],
+            [part_space(2 * size, F32), part_space(2 * size, BF16), part_space(size, BF16)],
+            hbm_ins=(0, 1), hbm_outs=(0, 1), sems=6,
+        )
+
+    def halve(keep, received, k):
+        while k < steps - 1:
+            k += 1
+            keep, send = halved(keep, received)
+            received = step_of(send, k)
+        return keep, received
 
     shards = [None, None, None]
     for layer in (2, 1):
@@ -883,7 +889,7 @@
         stats, grad, normed, totals[layer], *shares = call(
             functools.partial(kernel_backward, sz, layer), "backward",
             [stats_shape, pixel_shape(rows - 2, F32), pixel_shape(rows - 2, BF16), tile_shape]
-            + share_shapes(sz.pixels * (2 if layer == 2 else 1)),
+            + share_shapes(2 * sz.pixels),
             consts + [
                 gathered, grad, normed, moments[layer], norms, head(layer, weights), conv_weights, saves[layer - 1],
                 moments[layer - 1],
@@ -892,33 +898,38 @@
                 pixel_space(rows - 2, F32), pixel_space(rows, BF16, 3), weight_space, pixel_space(sz.rows, BF16),
                 pixel_space(sz.rows, BF16),
             ],
-            conv_flops(rows - 2), hbm_ins=(8, 9), hbm_outs=range(4, 8),
+            conv_flops(rows - 2), hbm_ins=(8, 9), hbm_outs=range(4, 4 + bands), sems=4 + 2 * bands,
         )
         if layer == 2:
-            stats, weights, acts[0][3], acts[1][3], *acts[2] = tie(
-                (stats, conv_weights, acts[0][3], acts[1][3], *acts[2])
+            stats, weights, acts[1][3], acts[2][3], *received = tie(
+                (stats, conv_weights, acts[1][3], acts[2][3], *received)
             )
             gathered = spread(stats)
             exchanged = trade(shares)
-            acts[2].append(swap(acts[2][2], 1))
             keep2, send2 = weight_grad(2, gathered_here, received, (lines, lines + sz.pixels))
+            gathered, send2 = tie((gathered, send2))
+            arrived2 = step_of(send2, 0)
         else:
-            stats, weights, send2 = tie((stats, conv_weights, send2))
+            stats, weights, *received = tie((stats, conv_weights, *received))
             gathered = spread(stats)
             exchanged = trade(shares)
             keep1, send1 = weight_grad(1, gathered_here, received, (0, sz.pixels))
-
-    send1, late = tie((send1, exchanged))
-    (partial,) = weight_grad(0, gathered, late, (0, 0), given0)
+            gathered, send1, arrived2 = tie((gathered, send1, arrived2))
+            arrived1 = step_of(send1, 0)
+            keep2, send2 = halved(keep2, arrived2)
+
+    arrived2 = step_of(send2, 1)
+    (partial,) = weight_grad(0, gathered, exchanged, (0, sz.pixels))
+    partial, arrived1, arrived2 = tie((partial, arrived1, arrived2))
     received = lax.all_to_all(partial, "maps", 0, 0, tiled=True)
-    shards[2] = halve(keep2, send2)
-    shards[1] = halve(keep1, send1)
+    shards[2] = halve(keep2, arrived2, 1)
+    shards[1] = halve(keep1, arrived1, 0)
     input_grad, totals[0], pooled = call(
         functools.partial(kernel_last, sz), "last",
         [pixel_shape(sz.rows, BF16), tile_shape, shape((sz.height // 2 * half, q), BF16)],
         consts + [gathered, grad, normed, moments[0], norms, head(0, weights), conv_weights] + pooled_parts,
         [pixel_space(sz.rows + 2, BF16, 3), weight_space, pixel_space(sz.rows, F32), pixel_space(sz.rows, BF16)],
-        conv_flops(sz.rows), hbm_ins=range(8, 13), hbm_outs=(0, 2),
+        conv_flops(sz.rows), hbm_ins=range(8, 9 + bands), hbm_outs=(0, 2), sems=4 + bands,
     )
 
     norm_shape = shape((3, 2, c), F32)
@@ -926,6 +937,7 @@
         functools.partial(kernel_squares, sz), "squares",
         [shape((sz.devices, 1, q), F32), part_shape(3, F32), norm_shape],
         [received, *shards[1], *shards[2], totals[2], totals[1], totals[0]],
+        [part_space(2, F32), part_space(2, BF16)], hbm_ins=range(1, 5), sems=4,
     )
     every = lax.all_to_all(squares, AXES, 0, 0, tiled=True)
     rate = 2.0 / math.sqrt(9.0 * c)
@@ -936,7 +948,7 @@
         + [v.reshape(3, share, q) for v in (conv_master, conv_moment1, conv_moment2)]
         + [norm_grad, norms, norm_first, norm_second],
         [pltpu.VMEM((1, 128), F32)] + [part_space(3, F32)] * 3 + [pltpu.VMEM((3, 3, 2, c), F32)],
-        hbm_ins=(3, 4, 5), hbm_outs=range(7), smem_ins=(1,),
+        hbm_ins=(3, 4, 5), hbm_outs=range(7), smem_ins=(1,), sems=22,
     )
     return (
         pooled.reshape(1, sz.height // 2, half, q),

time: 242 us -> 206 us (0.85)
  waiting for transfers between devices: 85.1 us -> 51.6 us
  blocking collectives: 0 us -> 13 us
  local copies, waits for them, and re-layouts: 21.4 us -> 14 us
  starting transfers between devices: 62.2 us -> 57.8 us
  Pallas kernels: 67.8 us -> 64.3 us
    all_to_all x6 -> x5, waiting for transfers between devices: 32.5 us -> 15.9 us  [spread(): return lax.all_to_all(stats, AXES, 0, 0, tiled=True)]
    ppermute x6, waiting for transfers between devices: 38.1 us -> 21.9 us  [step_of(): return lax.ppermute(send, 'maps', [(m, m ^ 1 << k) for m in range(n_maps)])]
    all_to_all x0 -> x1, blocking collectives: none -> 13 us  [spread(): return lax.all_to_all(stats, AXES, 0, 0, tiled=True)]
    unnamed x102 -> x66, local copies, waits for them, and re-layouts: 13.6 us -> 7.47 us
    all_to_all x6 -> x5, starting transfers between devices: 20.1 us -> 24.2 us  [spread(): return lax.all_to_all(stats, AXES, 0, 0, tiled=True)]
    pallas_call x19, Pallas kernels: 67.8 us -> 64.3 us  [call(): pl.pallas_call(kernel, out_shape=tuple((space(out.shape, out.dtype) for s...]
    all_to_all x1, starting transfers between devices: 6.26 us -> 3.58 us  [local(): received = lax.all_to_all(partial, 'maps', 0, 0, tiled=True)]
    ppermute x9, starting transfers between devices: 8.15 us -> 5.5 us  [swap(): return lax.ppermute(act, 'rows', [(i, i ^ n) for i in range(bands)])]
  transfers between devices with their start and end apart: 40 -> 36, of which waited for: 11 -> 14; matrix products, arithmetic and copies ran while one was open for 4% -> 4% of each run, Pallas kernels for 22% -> 26%
where the time goes in v3:
time: 206 us; the launch traced here: 205 us
  Pallas kernels  64.3 us (31%)
  starting transfers between devices  57.8 us (28%)
  waiting for transfers between devices  51.6 us (25%)
  local copies, waits for them, and re-layouts  14 us (7%)
  blocking collectives  13 us (6%)
  between operations  2.08 us (1%)
    pallas_call x19, Pallas kernels, call(): pl.pallas_call(kernel, out_shape=tuple((space(out.shape, out.dtype) for s...  64.3 us
    all_to_all x5, starting transfers between devices, spread(): return lax.all_to_all(stats, AXES, 0, 0, tiled=True)  24.2 us
    ppermute x6, waiting for transfers between devices, step_of(): return lax.ppermute(send, 'maps', [(m, m ^ 1 << k) for m in range(n_maps)])  21.9 us
    all_to_all x5, waiting for transfers between devices, spread(): return lax.all_to_all(stats, AXES, 0, 0, tiled=True)  15.9 us
    all_to_all x1, blocking collectives, spread(): return lax.all_to_all(stats, AXES, 0, 0, tiled=True)  13 us
    ppermute x6, starting transfers between devices, step_of(): return lax.ppermute(send, 'maps', [(m, m ^ 1 << k) for m in range(n_maps)])  10.2 us
    ppermute x12, starting transfers between devices, trade(): lax.ppermute(shares[n], 'rows', [(i, i ^ n) for i in range(bands)])  7.71 us
    unnamed x66, local copies, waits for them, and re-layouts  7.47 us
  transfers between devices with their start and end apart: 36, of which 14 were waited for; matrix products, arithmetic and copies ran while one was open for 4% of the time, Pallas kernels for 26%

profile of v3, /device:TPU:0, one launch (start us, length us, event | category | flops | bytes accessed | tf_op | source)
XLA Modules:
  0.0 204.5 jit_solution(14450925842325282720)
XLA Ops:
  0.6 1.3 edges.1
  2.0 2.4 %collective-permute-start = (bf16[224,512]{1,0:T(8,128)(2,1)S(1)}, bf16[224,512]{1,0:T(8,128)(2,1)S(1)}, u32[]{:S(2)}, u32[]{:S(2)}) collective-permute-start(bf16[224,512]{1,0:T(8,128)(2,1)S(1)} %get-tuple-element.129), channel_id=1, source_target_pairs={{0,1},{1,2},{2,3},{4,5},{5,6},{6,7},{8,9},{9,10},{10,11},{12,13},{... | collective-permute-start | bytes 688136 | tf_op jit(solution)/shard_map/ppermute | solution.py:764
  4.3 1.3 collective-permute-start.1
  10.1 1.1 slice_bitcast_fusion.5.head_ref
  11.2 5.5 %first.1 = (f32[32,8,128]{2,1,0:T(8,128)}, f32[704,512]{1,0:T(8,128)S(1)}, bf16[384,512]{1,0:T(8,128)(2,1)}) custom-call(s32[8,128]{1,0:T(8,128)S(1)} %get-tuple-element.127.limits_ref, bf16[224,512]{1,0:T(8,128)(2,1)S(1)} %collective-permute-done.up_ref.up_hbm, bf16[384,512]{1,0:T(8,128)(2,1)S(1)} %get-tuple-element.130.x_ref, ...), custom_call_target="tpu_custom_call" | custom-call | flops 3321888768 | tf_op jit(solution)/shard_map/first/pallas_call | solution.py:701
  16.8 9.2 %all-to-all-start = ((f32[32,8,128]{2,1,0:T(8,128)}), f32[32,8,128]{2,1,0:T(8,128)S(1)}, u32[]{:S(2)}, u32[]{:S(2)}) async-start(f32[32,8,128]{2,1,0:T(8,128)} %get-tuple-element.137), calls=%async_computation | async-start | bytes 262144 | tf_op jit(solution)/shard_map/all_to_all | solution.py:747
  26.3 1.7 collective-permute-start.6
  28.0 1.1 slice_bitcast_fusion.4.head_ref
  29.6 1.4 collective-permute-start.4
  31.0 3.2 %all-to-all-done.gathered_ref = f32[32,8,128]{2,1,0:T(8,128)S(1)} async-done(((f32[32,8,128]{2,1,0:T(8,128)}), f32[32,8,128]{2,1,0:T(8,128)S(1)}, u32[]{:S(2)}, u32[]{:S(2)}) %all-to-all-start) | async-done | bytes 131104 | tf_op jit(solution)/shard_map/all_to_all | solution.py:747
  34.2 4.3 %forward.2 = (f32[32,8,128]{2,1,0:T(8,128)S(1)}, f32[640,512]{1,0:T(8,128)S(1)}, f32[8,128]{1,0:T(8,128)S(1)}, bf16[384,512]{1,0:T(8,128)(2,1)}, f32[448,512]{1,0:T(8,128)}) custom-call(s32[8,128]{1,0:T(8,128)S(1)} %get-tuple-element.127.limits_ref, f32[32,8,128]{2,1,0:T(8,128)S(1)} %get-tuple-element.128.member_ref, ...), custom_call_target="tpu_custom_call" | custom-call | flops 3019898880 | tf_op jit(solution)/shard_map/forward/pallas_call | solution.py:701
  40.6 4.7 %all-to-all-start.1 = ((f32[32,8,128]{2,1,0:T(8,128)}), f32[32,8,128]{2,1,0:T(8,128)S(1)}, u32[]{:S(2)}, u32[]{:S(2)}) async-start(f32[32,8,128]{2,1,0:T(8,128)} %copy-done.9), calls=%async_computation.1 | async-start | bytes 262144 | tf_op jit(solution)/shard_map/all_to_all | solution.py:747
  45.6 1.7 collective-permute-start.8
  47.3 1.1 slice_bitcast_fusion.3.head_ref
  48.5 5.0 %all-to-all-done.1.gathered_ref = f32[32,8,128]{2,1,0:T(8,128)S(1)} async-done(((f32[32,8,128]{2,1,0:T(8,128)}), f32[32,8,128]{2,1,0:T(8,128)S(1)}, u32[]{:S(2)}, u32[]{:S(2)}) %all-to-all-start.1) | async-done | bytes 131104 | tf_op jit(solution)/shard_map/all_to_all | solution.py:747
  53.6 4.0 %forward.3 = (f32[32,8,128]{2,1,0:T(8,128)S(1)}, f32[576,512]{1,0:T(8,128)S(1)}, f32[8,128]{1,0:T(8,128)S(1)}, bf16[384,512]{1,0:T(8,128)(2,1)}, f32[512,512]{1,0:T(8,128)}) custom-call(s32[8,128]{1,0:T(8,128)S(1)} %get-tuple-element.127.limits_ref, f32[32,8,128]{2,1,0:T(8,128)S(1)} %get-tuple-element.128.member_ref, ...), custom_call_target="tpu_custom_call" | custom-call | flops 2717908992 | tf_op jit(solution)/shard_map/forward/pallas_call | solution.py:701
  58.5 13.0 %all_to_all.40.gathered_ref = f32[32,8,128]{2,1,0:T(8,128)S(1)} all-to-all(f32[32,8,128]{2,1,0:T(8,128)S(1)} %get-tuple-element.151), channel_id=1, replica_groups=mesh['maps'=8,'rows'=4] {'maps','rows'}, dimensions={0} | all-to-all | bytes 262144 | tf_op jit(solution)/shard_map/all_to_all | solution.py:747
  71.5 2.9 %pool.1 = (f32[32,8,128]{2,1,0:T(8,128)}, f32[576,512]{1,0:T(8,128)S(1)}, bf16[576,512]{1,0:T(8,128)(2,1)S(1)}, f32[8,128]{1,0:T(8,128)S(1)}, bf16[864,128]{1,0:...) custom-call(s32[8,128]{1,0:T(8,128)S(1)} %get-tuple-element.127.limits_ref, ...), custom_call_target="tpu_custom_call" | custom-call | flops 603979776 | tf_op jit(solution)/shard_map/pool/pallas_call | solution.py:701
  74.4 2.7 %all-to-all-start.3 = ((f32[32,8,128]{2,1,0:T(8,128)}), f32[32,8,128]{2,1,0:T(8,128)S(1)}, u32[]{:S(2)}, u32[]{:S(2)}) async-start(f32[32,8,128]{2,1,0:T(8,128)} %get-tuple-element.160), calls=%async_computation.3 | async-start | bytes 262144 | tf_op jit(solution)/shard_map/all_to_all | solution.py:747
  77.8 1.5 collective-permute-start.15
  79.9 1.1 slice_bitcast_fusion.2.head_ref
  81.0 4.3 %all-to-all-done.3.gathered_ref = f32[32,8,128]{2,1,0:T(8,128)S(1)} async-done(((f32[32,8,128]{2,1,0:T(8,128)}), f32[32,8,128]{2,1,0:T(8,128)S(1)}, u32[]{:S(2)}, u32[]{:S(2)}) %all-to-all-start.3) | async-done | bytes 131104 | tf_op jit(solution)/shard_map/all_to_all | solution.py:747
  86.3 5.9 %backward.2 = (f32[32,8,128]{2,1,0:T(8,128)}, f32[512,512]{1,0:T(8,128)S(1)}, bf16[512,512]{1,0:T(8,128)(2,1)S(1)}, f32[8,128]{1,0:T(8,128)S(1)}, bf16[768,128]{...) custom-call(s32[8,128]{1,0:T(8,128)S(1)} %get-tuple-element.127.limits_ref, ...), custom_call_target="tpu_custom_call" | custom-call | flops 2415919104 | tf_op jit(solution)/shard_map/backward/pallas_call | solution.py:701
  93.1 2.6 %all-to-all-start.4 = ((f32[32,8,128]{2,1,0:T(8,128)}), f32[32,8,128]{2,1,0:T(8,128)S(1)}, u32[]{:S(2)}, u32[]{:S(2)}) async-start(f32[32,8,128]{2,1,0:T(8,128)} %get-tuple-element.174), calls=%async_computation.4 | async-start | bytes 262144 | tf_op jit(solution)/shard_map/all_to_all | solution.py:747
  95.9 1.7 collective-permute-start.18
  97.6 5.4 %weight_grad.3 = (f32[4,576,128]{2,1,0:T(8,128)}, bf16[4,576,128]{2,1,0:T(8,128)(2,1)}) custom-call(s32[8,128]{1,0:T(8,128)S(1)} %get-tuple-element.127.limits_ref, f32[32,8,128]{2,1,0:T(8,128)S(1)} %get-tuple-element.128.member_ref, f32[32,8,128]{2,1,0:T(8,128)S(1)} %all-to-all-done.3.gathered_ref, f32[8,128]{1,0:T(8,128)S(1)} %get-tuple-element.163.moments_ref, ...), custom_call_target="tpu_custom_call" | custom-call | flops 1811939328 | tf_op jit(solution)/shard_map/weight_grad/pallas_call | solution.py:701
  105.8 5.7 %backward.3 = (f32[32,8,128]{2,1,0:T(8,128)}, f32[448,512]{1,0:T(8,128)S(1)}, bf16[448,512]{1,0:T(8,128)(2,1)S(1)}, f32[8,128]{1,0:T(8,128)S(1)}, bf16[768,128]{...) custom-call(s32[8,128]{1,0:T(8,128)S(1)} %get-tuple-element.127.limits_ref, ...), custom_call_target="tpu_custom_call" | custom-call | flops 2113929216 | tf_op jit(solution)/shard_map/backward/pallas_call | solution.py:701
  112.5 5.0 %all-to-all-start.5 = ((f32[32,8,128]{2,1,0:T(8,128)}), f32[32,8,128]{2,1,0:T(8,128)S(1)}, u32[]{:S(2)}, u32[]{:S(2)}) async-start(f32[32,8,128]{2,1,0:T(8,128)} %get-tuple-element.194), calls=%async_computation.5 | async-start | bytes 262144 | tf_op jit(solution)/shard_map/all_to_all | solution.py:747
  117.5 5.4 %weight_grad.4 = (f32[4,576,128]{2,1,0:T(8,128)}, bf16[4,576,128]{2,1,0:T(8,128)(2,1)}) custom-call(s32[8,128]{1,0:T(8,128)S(1)} %get-tuple-element.127.limits_ref, f32[32,8,128]{2,1,0:T(8,128)S(1)} %get-tuple-element.128.member_ref, f32[32,8,128]{2,1,0:T(8,128)S(1)} %all-to-all-done.4.gathered_ref, ...), custom_call_target="tpu_custom_call" | custom-call | flops 1811939328 | tf_op jit(solution)/shard_map/weight_grad/pallas_call | solution.py:701
  122.9 2.5 %all-to-all-done.5.gathered_ref = f32[32,8,128]{2,1,0:T(8,128)S(1)} async-done(((f32[32,8,128]{2,1,0:T(8,128)}), f32[32,8,128]{2,1,0:T(8,128)S(1)}, u32[]{:S(2)}, u32[]{:S(2)}) %all-to-all-start.5) | async-done | bytes 131104 | tf_op jit(solution)/shard_map/all_to_all | solution.py:747
  128.0 2.3 %halve.4 = (f32[2,576,128]{2,1,0:T(8,128)}, bf16[2,576,128]{2,1,0:T(8,128)(2,1)}) custom-call(f32[4,576,128]{2,1,0:T(8,128)} %get-tuple-element.218.keep_hbm, bf16[4,576,128]{2,1,0:T(8,128)(2,1)} %copy-done.16), custom_call_target="tpu_custom_call" | custom-call | tf_op jit(solution)/shard_map/halve/pallas_call | solution.py:701
  131.1 2.9 %collective-permute-done.22.rest_2_ = bf16[768,128]{1,0:T(8,128)(2,1)S(1)} collective-permute-done((bf16[768,128]{1,0:T(8,128)(2,1)S(1)}, bf16[768,128]{1,0:T(8,128)(2,1)S(1)}, u32[]{:S(2)}, u32[]{:S(2)}) %collective-permute-start.22) | collective-permute-done | bytes 196640 | tf_op jit(solution)/shard_map/ppermute | solution.py:751
  133.9 3.3 %collective-permute-done.23.rest_3_ = bf16[768,128]{1,0:T(8,128)(2,1)S(1)} collective-permute-done((bf16[768,128]{1,0:T(8,128)(2,1)S(1)}, bf16[768,128]{1,0:T(8,128)(2,1)S(1)}, u32[]{:S(2)}, u32[]{:S(2)}) %collective-permute-start.23) | collective-permute-done | bytes 196640 | tf_op jit(solution)/shard_map/ppermute | solution.py:751
  137.9 5.1 %weight_grad.5 = bf16[8,576,128]{2,1,0:T(8,128)(2,1)} custom-call(s32[8,128]{1,0:T(8,128)S(1)} %get-tuple-element.127.limits_ref, f32[32,8,128]{2,1,0:T(8,128)S(1)} %get-tuple-element.128.member_ref, f32[32,8,128]{2,1,0:T(8,128)S(1)} %all-to-all-done.5.gathered_ref, f32[8,128]{1,0:T(8,128)S(1)} %copy-done.11, f32[3,2,512]{2,1,0:T(2,128)S(1)} %bitcast.40, ...), custom_call_target="tpu_custom_call" | custom-call | flops 1811939328 | tf_op jit(solution)/shard_map/weight_grad/pallas_call | solution.py:701
  143.0 3.6 %all-to-all-start.6 = ((bf16[8,576,128]{2,1,0:T(8,128)(2,1)}), bf16[8,576,128]{2,1,0:T(8,128)(2,1)S(1)}, u32[]{:S(2)}, u32[]{:S(2)}) async-start(bf16[8,576,128]{2,1,0:T(8,128)(2,1)} %weight_grad.5), calls=%async_computation.6 | async-start | bytes 2359296 | tf_op jit(solution)/shard_map/all_to_all | solution.py:924
  146.6 2.3 %halve.5 = (f32[2,576,128]{2,1,0:T(8,128)}, bf16[2,576,128]{2,1,0:T(8,128)(2,1)}) custom-call(f32[4,576,128]{2,1,0:T(8,128)} %get-tuple-element.222.keep_hbm, bf16[4,576,128]{2,1,0:T(8,128)(2,1)} %copy-done.17), custom_call_target="tpu_custom_call" | custom-call | tf_op jit(solution)/shard_map/halve/pallas_call | solution.py:701
  149.0 2.0 collective-permute-start.26
  152.0 2.0 halve.7
  154.0 2.5 %collective-permute-start.28 = (bf16[1,576,128]{2,1,0:T(8,128)(2,1)}, bf16[1,576,128]{2,1,0:T(8,128)(2,1)S(1)}, u32[]{:S(2)}, u32[]{:S(2)}) collective-permute-start(bf16[1,576,128]{2,1,0:T(8,128)(2,1)} %get-tuple-element.231), channel_id=1, source_target_pairs={{0,16},{4,20},{8,24},{12,28},{16,0},{20,4},{24,8},{28,12},{1,17},{... | collective-permute-start | bytes 442376 | tf_op jit(solution)/shard_map/ppermute | solution.py:867
  156.4 18.1 %collective-permute-done.26.received_hbm = bf16[2,576,128]{2,1,0:T(8,128)(2,1)S(1)} collective-permute-done((bf16[2,576,128]{2,1,0:T(8,128)(2,1)}, bf16[2,576,128]{2,1,0:T(8,128)(2,1)S(1)}, u32[]{:S(2)}, u32[]{:S(2)}) %collective-permute-start.26) | collective-permute-done | bytes 294944 | tf_op jit(solution)/shard_map/ppermute | solution.py:867
  175.2 1.9 halve.6
  177.2 3.6 %collective-permute-start.27 = (bf16[1,576,128]{2,1,0:T(8,128)(2,1)}, bf16[1,576,128]{2,1,0:T(8,128)(2,1)S(1)}, u32[]{:S(2)}, u32[]{:S(2)}) collective-permute-start(bf16[1,576,128]{2,1,0:T(8,128)(2,1)} %get-tuple-element.227), channel_id=1, source_target_pairs={{0,16},{4,20},{8,24},{12,28},{16,0},{20,4},{24,8},{28,12},{1,17},{... | collective-permute-start | bytes 442376 | tf_op jit(solution)/shard_map/ppermute | solution.py:867
  180.8 4.2 %last.1 = (bf16[384,512]{1,0:T(8,128)(2,1)}, f32[8,128]{1,0:T(8,128)S(1)}, bf16[384,128]{1,0:T(8,128)(2,1)}) custom-call(s32[8,128]{1,0:T(8,128)S(1)} %get-tuple-element.127.limits_ref, f32[32,8,128]{2,1,0:T(8,128)S(1)} %get-tuple-element.128.member_ref, f32[32,8,128]{2,1,0:T(8,128)S(1)} %all-to-all-done.5.gathered_ref, f32[448,512]{1,0:T(8,128)S(1)} %copy-done.3, ...), custom_call_target="tpu_custom_call" | custom-call | flops 1811939328 | tf_op jit(solution)/shard_map/last/pallas_call | solution.py:701
  185.9 2.9 %collective-permute-done.27.last1_hbm = bf16[1,576,128]{2,1,0:T(8,128)(2,1)S(1)} collective-permute-done((bf16[1,576,128]{2,1,0:T(8,128)(2,1)}, bf16[1,576,128]{2,1,0:T(8,128)(2,1)S(1)}, u32[]{:S(2)}, u32[]{:S(2)}) %collective-permute-start.27) | collective-permute-done | bytes 147488 | tf_op jit(solution)/shard_map/ppermute | solution.py:867
  189.5 2.0 squares.1
  191.5 2.9 %all-to-all-start.7 = ((f32[32,1,128]{2,1,0:T(1,128)}), f32[32,1,128]{2,1,0:T(1,128)S(1)}, u32[]{:S(2)}, u32[]{:S(2)}) async-start(f32[32,1,128]{2,1,0:T(1,128)} %get-tuple-element.235), calls=%async_computation.7 | async-start | bytes 32768 | tf_op jit(solution)/shard_map/all_to_all | solution.py:942
  195.0 6.4 %all-to-all-done.7.every_ref = f32[32,1,128]{2,1,0:T(1,128)S(1)} async-done(((f32[32,1,128]{2,1,0:T(1,128)}), f32[32,1,128]{2,1,0:T(1,128)S(1)}, u32[]{:S(2)}, u32[]{:S(2)}) %all-to-all-start.7) | async-done | bytes 16416 | tf_op jit(solution)/shard_map/all_to_all | solution.py:942
  201.4 2.9 %adam.1 = (f32[1,128]{1,0:T(1,128)}, f32[3,576,128]{2,1,0:T(8,128)}, f32[3,576,128]{2,1,0:T(8,128)}, f32[3,576,128]{2,1,0:T(8,128)}, f32[3,2,512]{2,1,0:T(2,128)...) custom-call(f32[32,1,128]{2,1,0:T(1,128)S(1)} %all-to-all-done.7.every_ref, s32[1]{0:T(128)S(6)} %copy.24.step_ref, ...), custom_call_target="tpu_custom_call" | custom-call | tf_op jit(solution)/shard_map/adam/pallas_call | solution.py:701
  (120 shorter events, 23.2 us)
Async XLA Ops:
  2.0 9.2 %collective-permute-start = (bf16[224,512]{1,0:T(8,128)(2,1)S(1)}, bf16[224,512]{1,0:T(8,128)(2,1)S(1)}, u32[]{:S(2)}, u32[]{:S(2)}) collective-permute-start(bf16[224,512]{1,0:T(8,128)(2,1)S(1)} %get-tuple-element.129), channel_id=1, source_target_pairs={{0,1},{1,2},{2,3},{4,5},{5,6},{6,7},{8,9},{9,10},{10,11},{12,13},{... | collective-permute-start | bytes 688136 | tf_op jit(solution)/shard_map/ppermute | solution.py:764
  4.3 6.9 %collective-permute-start.1 = (bf16[224,512]{1,0:T(8,128)(2,1)S(1)}, bf16[224,512]{1,0:T(8,128)(2,1)S(1)}, u32[]{:S(2)}, u32[]{:S(2)}) collective-permute-start(bf16[224,512]{1,0:T(8,128)(2,1)S(1)} %get-tuple-element.131), channel_id=1, source_target_pairs={{1,0},{2,1},{3,2},{5,4},{6,5},{7,6},{9,8},{10,9},{11,10},{13,12},{... | collective-permute-start | bytes 688136 | tf_op jit(solution)/shard_map/ppermute | solution.py:765
  11.2 23.0 %copy-start.4 = (f32[2,3,512]{2,0,1:T(2,128)S(1)}, f32[2,3,512]{2,0,1:T(2,128)}, u32[]{:S(2)}) copy-start(f32[2,3,512]{2,0,1:T(2,128)} %param.16) | copy-start | bytes 36868
  16.8 17.4 %all-to-all-start = ((f32[32,8,128]{2,1,0:T(8,128)}), f32[32,8,128]{2,1,0:T(8,128)S(1)}, u32[]{:S(2)}, u32[]{:S(2)}) async-start(f32[32,8,128]{2,1,0:T(8,128)} %get-tuple-element.137), calls=%async_computation | async-start | bytes 262144 | tf_op jit(solution)/shard_map/all_to_all | solution.py:747
  26.0 14.6 %collective-permute-start.5 = (bf16[384,512]{1,0:T(8,128)(2,1)}, bf16[384,512]{1,0:T(8,128)(2,1)}, u32[]{:S(2)}, u32[]{:S(2)}) collective-permute-start(bf16[384,512]{1,0:T(8,128)(2,1)} %get-tuple-element.214.rest_4_), channel_id=1, source_target_pairs={{0,1},{1,0},{2,3},{3,2},{4,5},{5,4},{6,7},{7,6},{8,9},{9,8},{10,11... | collective-permute-start | bytes 1179656 | tf_op jit(solution)/shard_map/ppermute | solution.py:755
  26.3 14.3 %collective-permute-start.6 = (bf16[384,512]{1,0:T(8,128)(2,1)}, bf16[384,512]{1,0:T(8,128)(2,1)}, u32[]{:S(2)}, u32[]{:S(2)}) collective-permute-start(bf16[384,512]{1,0:T(8,128)(2,1)} %get-tuple-element.214.rest_4_), channel_id=1, source_target_pairs={{0,2},{1,3},{2,0},{3,1},{4,6},{5,7},{6,4},{7,5},{8,10},{9,11},{10,... | collective-permute-start | bytes 1179656 | tf_op jit(solution)/shard_map/ppermute | solution.py:755
  29.1 10.7 %collective-permute-start.2 = (bf16[160,128]{1,0:T(8,128)(2,1)}, bf16[160,128]{1,0:T(8,128)(2,1)}, u32[]{:S(2)}, u32[]{:S(2)}) collective-permute-start(bf16[160,128]{1,0:T(8,128)(2,1)} %get-tuple-element.142), channel_id=1, source_target_pairs={{0,1},{1,0},{2,3},{3,2},{4,5},{5,4},{6,7},{7,6},{8,9},{9,8},{10,11... | collective-permute-start | bytes 122888 | tf_op jit(solution)/shard_map/ppermute | solution.py:751
  29.2 11.2 %collective-permute-start.3 = (bf16[160,128]{1,0:T(8,128)(2,1)}, bf16[160,128]{1,0:T(8,128)(2,1)}, u32[]{:S(2)}, u32[]{:S(2)}) collective-permute-start(bf16[160,128]{1,0:T(8,128)(2,1)} %get-tuple-element.143), channel_id=1, source_target_pairs={{0,2},{1,3},{2,0},{3,1},{4,6},{5,7},{6,4},{7,5},{8,10},{9,11},{10,... | collective-permute-start | bytes 122888 | tf_op jit(solution)/shard_map/ppermute | solution.py:751
  29.6 11.0 %collective-permute-start.4 = (bf16[160,128]{1,0:T(8,128)(2,1)}, bf16[160,128]{1,0:T(8,128)(2,1)}, u32[]{:S(2)}, u32[]{:S(2)}) collective-permute-start(bf16[160,128]{1,0:T(8,128)(2,1)} %get-tuple-element.144), channel_id=1, source_target_pairs={{0,3},{1,2},{2,1},{3,0},{4,7},{5,6},{6,5},{7,4},{8,11},{9,10},{10,... | collective-permute-start | bytes 122888 | tf_op jit(solution)/shard_map/ppermute | solution.py:751
  40.6 13.0 %all-to-all-start.1 = ((f32[32,8,128]{2,1,0:T(8,128)}), f32[32,8,128]{2,1,0:T(8,128)S(1)}, u32[]{:S(2)}, u32[]{:S(2)}) async-start(f32[32,8,128]{2,1,0:T(8,128)} %copy-done.9), calls=%async_computation.1 | async-start | bytes 262144 | tf_op jit(solution)/shard_map/all_to_all | solution.py:747
  45.3 12.9 %collective-permute-start.7 = (bf16[384,512]{1,0:T(8,128)(2,1)}, bf16[384,512]{1,0:T(8,128)(2,1)S(1)}, u32[]{:S(2)}, u32[]{:S(2)}) collective-permute-start(bf16[384,512]{1,0:T(8,128)(2,1)} %get-tuple-element.199.rest_4_), channel_id=1, source_target_pairs={{0,1},{1,0},{2,3},{3,2},{4,5},{5,4},{6,7},{7,6},{8,9},{9,8},{10,11... | collective-permute-start | bytes 1179656 | tf_op jit(solution)/shard_map/ppermute | solution.py:755
  45.6 12.8 %collective-permute-start.8 = (bf16[384,512]{1,0:T(8,128)(2,1)}, bf16[384,512]{1,0:T(8,128)(2,1)}, u32[]{:S(2)}, u32[]{:S(2)}) collective-permute-start(bf16[384,512]{1,0:T(8,128)(2,1)} %get-tuple-element.199.rest_4_), channel_id=1, source_target_pairs={{0,2},{1,3},{2,0},{3,1},{4,6},{5,7},{6,4},{7,5},{8,10},{9,11},{10,... | collective-permute-start | bytes 1179656 | tf_op jit(solution)/shard_map/ppermute | solution.py:755
  48.4 26.0 %collective-permute-start.9 = (bf16[384,512]{1,0:T(8,128)(2,1)}, bf16[384,512]{1,0:T(8,128)(2,1)S(1)}, u32[]{:S(2)}, u32[]{:S(2)}) collective-permute-start(bf16[384,512]{1,0:T(8,128)(2,1)} %collective-permute-done.6.rest_6_), channel_id=1, source_target_pairs={{0,1},{1,0},{2,3},{3,2},{4,5},{5,4},{6,7},{7,6},{8,9},{9,8},{10,11... | collective-permute-start | bytes 1179656 | tf_op jit(solution)/shard_map/ppermute | solution.py:755
  57.6 16.9 %collective-permute-start.10 = (bf16[384,512]{1,0:T(8,128)(2,1)}, bf16[384,512]{1,0:T(8,128)(2,1)}, u32[]{:S(2)}, u32[]{:S(2)}) collective-permute-start(bf16[384,512]{1,0:T(8,128)(2,1)} %get-tuple-element.179.rest_4_), channel_id=1, source_target_pairs={{0,1},{1,0},{2,3},{3,2},{4,5},{5,4},{6,7},{7,6},{8,9},{9,8},{10,11... | collective-permute-start | bytes 1179656 | tf_op jit(solution)/shard_map/ppermute | solution.py:755
  57.8 16.6 %collective-permute-start.11 = (bf16[384,512]{1,0:T(8,128)(2,1)}, bf16[384,512]{1,0:T(8,128)(2,1)}, u32[]{:S(2)}, u32[]{:S(2)}) collective-permute-start(bf16[384,512]{1,0:T(8,128)(2,1)} %get-tuple-element.179.rest_4_), channel_id=1, source_target_pairs={{0,2},{1,3},{2,0},{3,1},{4,6},{5,7},{6,4},{7,5},{8,10},{9,11},{10,... | collective-permute-start | bytes 1179656 | tf_op jit(solution)/shard_map/ppermute | solution.py:755
  58.2 21.1 %copy-start.23 = (bf16[384,512]{1,0:T(8,128)(2,1)}, bf16[384,512]{1,0:T(8,128)(2,1)S(1)}, u32[]{:S(2)}) copy-start(bf16[384,512]{1,0:T(8,128)(2,1)S(1)} %collective-permute-done.7.rest_5_) | copy-start | bytes 1179652
  74.4 10.9 %copy-start.5 = (bf16[576,512]{1,0:T(8,128)(2,1)}, bf16[576,512]{1,0:T(8,128)(2,1)S(1)}, u32[]{:S(2)}) copy-start(bf16[576,512]{1,0:T(8,128)(2,1)S(1)} %get-tuple-element.162.normed_ref) | copy-start | bytes 1769476
  74.4 10.8 %copy-start.22 = (bf16[384,512]{1,0:T(8,128)(2,1)}, bf16[384,512]{1,0:T(8,128)(2,1)S(1)}, u32[]{:S(2)}) copy-start(bf16[384,512]{1,0:T(8,128)(2,1)S(1)} %collective-permute-done.9.rest_7_) | copy-start | bytes 1179652
  74.4 10.8 %all-to-all-start.3 = ((f32[32,8,128]{2,1,0:T(8,128)}), f32[32,8,128]{2,1,0:T(8,128)S(1)}, u32[]{:S(2)}, u32[]{:S(2)}) async-start(f32[32,8,128]{2,1,0:T(8,128)} %get-tuple-element.160), calls=%async_computation.3 | async-start | bytes 262144 | tf_op jit(solution)/shard_map/all_to_all | solution.py:747
  77.2 15.9 %collective-permute-start.12 = (bf16[384,512]{1,0:T(8,128)(2,1)}, bf16[384,512]{1,0:T(8,128)(2,1)}, u32[]{:S(2)}, u32[]{:S(2)}) collective-permute-start(bf16[384,512]{1,0:T(8,128)(2,1)} %collective-permute-done.8.rest_6_), channel_id=1, source_target_pairs={{0,1},{1,0},{2,3},{3,2},{4,5},{5,4},{6,7},{7,6},{8,9},{9,8},{10,11... | collective-permute-start | bytes 1179656 | tf_op jit(solution)/shard_map/ppermute | solution.py:755
  77.3 15.8 %collective-permute-start.14 = (bf16[864,128]{1,0:T(8,128)(2,1)}, bf16[864,128]{1,0:T(8,128)(2,1)}, u32[]{:S(2)}, u32[]{:S(2)}) collective-permute-start(bf16[864,128]{1,0:T(8,128)(2,1)} %get-tuple-element.171), channel_id=1, source_target_pairs={{0,1},{1,0},{2,3},{3,2},{4,5},{5,4},{6,7},{7,6},{8,9},{9,8},{10,11... | collective-permute-start | bytes 663560 | tf_op jit(solution)/shard_map/ppermute | solution.py:751
  77.8 15.3 %collective-permute-start.15 = (bf16[864,128]{1,0:T(8,128)(2,1)}, bf16[864,128]{1,0:T(8,128)(2,1)}, u32[]{:S(2)}, u32[]{:S(2)}) collective-permute-start(bf16[864,128]{1,0:T(8,128)(2,1)} %get-tuple-element.172), channel_id=1, source_target_pairs={{0,2},{1,3},{2,0},{3,1},{4,6},{5,7},{6,4},{7,5},{8,10},{9,11},{10,... | collective-permute-start | bytes 663560 | tf_op jit(solution)/shard_map/ppermute | solution.py:751
  79.3 13.8 %collective-permute-start.16 = (bf16[864,128]{1,0:T(8,128)(2,1)}, bf16[864,128]{1,0:T(8,128)(2,1)}, u32[]{:S(2)}, u32[]{:S(2)}) collective-permute-start(bf16[864,128]{1,0:T(8,128)(2,1)} %get-tuple-element.173), channel_id=1, source_target_pairs={{0,3},{1,2},{2,1},{3,0},{4,7},{5,6},{6,5},{7,4},{8,11},{9,10},{10,... | collective-permute-start | bytes 663560 | tf_op jit(solution)/shard_map/ppermute | solution.py:751
  79.3 13.8 %collective-permute-start.13 = (bf16[384,512]{1,0:T(8,128)(2,1)}, bf16[384,512]{1,0:T(8,128)(2,1)}, u32[]{:S(2)}, u32[]{:S(2)}) collective-permute-start(bf16[384,512]{1,0:T(8,128)(2,1)} %collective-permute-done.11.rest_6_), channel_id=1, source_target_pairs={{0,1},{1,0},{2,3},{3,2},{4,5},{5,4},{6,7},{7,6},{8,9},{9,8},{10,11... | collective-permute-start | bytes 1179656 | tf_op jit(solution)/shard_map/ppermute | solution.py:755
  93.1 10.8 %all-to-all-start.4 = ((f32[32,8,128]{2,1,0:T(8,128)}), f32[32,8,128]{2,1,0:T(8,128)S(1)}, u32[]{:S(2)}, u32[]{:S(2)}) async-start(f32[32,8,128]{2,1,0:T(8,128)} %get-tuple-element.174), calls=%async_computation.4 | async-start | bytes 262144 | tf_op jit(solution)/shard_map/all_to_all | solution.py:747
  95.7 16.8 %collective-permute-start.17 = (bf16[768,128]{1,0:T(8,128)(2,1)}, bf16[768,128]{1,0:T(8,128)(2,1)S(1)}, u32[]{:S(2)}, u32[]{:S(2)}) collective-permute-start(bf16[768,128]{1,0:T(8,128)(2,1)} %get-tuple-element.191), channel_id=1, source_target_pairs={{0,1},{1,0},{2,3},{3,2},{4,5},{5,4},{6,7},{7,6},{8,9},{9,8},{10,11... | collective-permute-start | bytes 589832 | tf_op jit(solution)/shard_map/ppermute | solution.py:751
  95.9 16.6 %collective-permute-start.18 = (bf16[768,128]{1,0:T(8,128)(2,1)}, bf16[768,128]{1,0:T(8,128)(2,1)S(1)}, u32[]{:S(2)}, u32[]{:S(2)}) collective-permute-start(bf16[768,128]{1,0:T(8,128)(2,1)} %get-tuple-element.192), channel_id=1, source_target_pairs={{0,2},{1,3},{2,0},{3,1},{4,6},{5,7},{6,4},{7,5},{8,10},{9,11},{10,... | collective-permute-start | bytes 589832 | tf_op jit(solution)/shard_map/ppermute | solution.py:751
  97.6 8.2 %copy-start.8 = (bf16[512,512]{1,0:T(8,128)(2,1)S(1)}, bf16[512,512]{1,0:T(8,128)(2,1)}, u32[]{:S(2)}) copy-start(bf16[512,512]{1,0:T(8,128)(2,1)} %copy-done.7) | copy-start | bytes 1572868
  97.6 8.2 %copy-start.11 = (f32[8,128]{1,0:T(8,128)S(1)}, f32[8,128]{1,0:T(8,128)}, u32[]{:S(2)}) copy-start(f32[8,128]{1,0:T(8,128)} %copy-done.10) | copy-start | bytes 12292
  97.6 14.9 %collective-permute-start.19 = (bf16[768,128]{1,0:T(8,128)(2,1)}, bf16[768,128]{1,0:T(8,128)(2,1)S(1)}, u32[]{:S(2)}, u32[]{:S(2)}) collective-permute-start(bf16[768,128]{1,0:T(8,128)(2,1)} %get-tuple-element.193), channel_id=1, source_target_pairs={{0,3},{1,2},{2,1},{3,0},{4,7},{5,6},{6,5},{7,4},{8,11},{9,10},{10,... | collective-permute-start | bytes 589832 | tf_op jit(solution)/shard_map/ppermute | solution.py:751
  103.9 21.6 %collective-permute-start.20 = (bf16[4,576,128]{2,1,0:T(8,128)(2,1)}, bf16[4,576,128]{2,1,0:T(8,128)(2,1)S(1)}, u32[]{:S(2)}, u32[]{:S(2)}) collective-permute-start(bf16[4,576,128]{2,1,0:T(8,128)(2,1)} %get-tuple-element.203), channel_id=1, source_target_pairs={{0,4},{4,0},{8,12},{12,8},{16,20},{20,16},{24,28},{28,24},{1,5},{5... | collective-permute-start | bytes 1769480 | tf_op jit(solution)/shard_map/ppermute | solution.py:867
  112.5 13.0 %all-to-all-start.5 = ((f32[32,8,128]{2,1,0:T(8,128)}), f32[32,8,128]{2,1,0:T(8,128)S(1)}, u32[]{:S(2)}, u32[]{:S(2)}) async-start(f32[32,8,128]{2,1,0:T(8,128)} %get-tuple-element.194), calls=%async_computation.5 | async-start | bytes 262144 | tf_op jit(solution)/shard_map/all_to_all | solution.py:747
  117.5 8.6 %copy-start.26 = (bf16[768,128]{1,0:T(8,128)(2,1)S(1)}, bf16[768,128]{1,0:T(8,128)(2,1)}, u32[]{:S(2)}) copy-start(bf16[768,128]{1,0:T(8,128)(2,1)} %get-tuple-element.211) | copy-start | bytes 589828
  117.5 8.6 %copy-start.25 = (bf16[768,128]{1,0:T(8,128)(2,1)S(1)}, bf16[768,128]{1,0:T(8,128)(2,1)}, u32[]{:S(2)}) copy-start(bf16[768,128]{1,0:T(8,128)(2,1)} %get-tuple-element.212) | copy-start | bytes 589828
  117.5 9.5 %copy-start.24 = (bf16[768,128]{1,0:T(8,128)(2,1)S(1)}, bf16[768,128]{1,0:T(8,128)(2,1)}, u32[]{:S(2)}) copy-start(bf16[768,128]{1,0:T(8,128)(2,1)} %get-tuple-element.213) | copy-start | bytes 589828
  125.5 17.5 %collective-permute-start.24 = (bf16[4,576,128]{2,1,0:T(8,128)(2,1)}, bf16[4,576,128]{2,1,0:T(8,128)(2,1)S(1)}, u32[]{:S(2)}, u32[]{:S(2)}) collective-permute-start(bf16[4,576,128]{2,1,0:T(8,128)(2,1)} %get-tuple-element.217), channel_id=1, source_target_pairs={{0,4},{4,0},{8,12},{12,8},{16,20},{20,16},{24,28},{28,24},{1,5},{5... | collective-permute-start | bytes 1769480 | tf_op jit(solution)/shard_map/ppermute | solution.py:867
  126.1 4.9 %collective-permute-start.21 = (bf16[768,128]{1,0:T(8,128)(2,1)S(1)}, bf16[768,128]{1,0:T(8,128)(2,1)S(1)}, u32[]{:S(2)}, u32[]{:S(2)}) collective-permute-start(bf16[768,128]{1,0:T(8,128)(2,1)S(1)} %copy-done.26), channel_id=1, source_target_pairs={{0,1},{1,0},{2,3},{3,2},{4,5},{5,4},{6,7},{7,6},{8,9},{9,8},{10,11... | collective-permute-start | bytes 589832 | tf_op jit(solution)/shard_map/ppermute | solution.py:751
  126.2 7.8 %collective-permute-start.22 = (bf16[768,128]{1,0:T(8,128)(2,1)S(1)}, bf16[768,128]{1,0:T(8,128)(2,1)S(1)}, u32[]{:S(2)}, u32[]{:S(2)}) collective-permute-start(bf16[768,128]{1,0:T(8,128)(2,1)S(1)} %copy-done.25), channel_id=1, source_target_pairs={{0,2},{1,3},{2,0},{3,1},{4,6},{5,7},{6,4},{7,5},{8,10},{9,11},{10,... | collective-permute-start | bytes 589832 | tf_op jit(solution)/shard_map/ppermute | solution.py:751
  127.0 10.2 %collective-permute-start.23 = (bf16[768,128]{1,0:T(8,128)(2,1)S(1)}, bf16[768,128]{1,0:T(8,128)(2,1)S(1)}, u32[]{:S(2)}, u32[]{:S(2)}) collective-permute-start(bf16[768,128]{1,0:T(8,128)(2,1)S(1)} %copy-done.24), channel_id=1, source_target_pairs={{0,3},{1,2},{2,1},{3,0},{4,7},{5,6},{6,5},{7,4},{8,11},{9,10},{10,... | collective-permute-start | bytes 589832 | tf_op jit(solution)/shard_map/ppermute | solution.py:751
  130.3 12.6 %collective-permute-start.25 = (bf16[2,576,128]{2,1,0:T(8,128)(2,1)}, bf16[2,576,128]{2,1,0:T(8,128)(2,1)S(1)}, u32[]{:S(2)}, u32[]{:S(2)}) collective-permute-start(bf16[2,576,128]{2,1,0:T(8,128)(2,1)} %get-tuple-element.220), channel_id=1, source_target_pairs={{0,8},{4,12},{8,0},{12,4},{16,24},{20,28},{24,16},{28,20},{1,9},{5... | collective-permute-start | bytes 884744 | tf_op jit(solution)/shard_map/ppermute | solution.py:867
  143.0 45.8 %all-to-all-start.6 = ((bf16[8,576,128]{2,1,0:T(8,128)(2,1)}), bf16[8,576,128]{2,1,0:T(8,128)(2,1)S(1)}, u32[]{:S(2)}, u32[]{:S(2)}) async-start(bf16[8,576,128]{2,1,0:T(8,128)(2,1)} %weight_grad.5), calls=%async_computation.6 | async-start | bytes 2359296 | tf_op jit(solution)/shard_map/all_to_all | solution.py:924
  148.9 31.8 %copy-start.3 = (f32[448,512]{1,0:T(8,128)S(1)}, f32[448,512]{1,0:T(8,128)}, u32[]{:S(2)}) copy-start(f32[448,512]{1,0:T(8,128)} %copy-done.2) | copy-start | bytes 2752516
  149.0 25.5 %collective-permute-start.26 = (bf16[2,576,128]{2,1,0:T(8,128)(2,1)}, bf16[2,576,128]{2,1,0:T(8,128)(2,1)S(1)}, u32[]{:S(2)}, u32[]{:S(2)}) collective-permute-start(bf16[2,576,128]{2,1,0:T(8,128)(2,1)} %get-tuple-element.225), channel_id=1, source_target_pairs={{0,8},{4,12},{8,0},{12,4},{16,24},{20,28},{24,16},{28,20},{1,9},{5... | collective-permute-start | bytes 884744 | tf_op jit(solution)/shard_map/ppermute | solution.py:867
  154.0 32.0 %collective-permute-start.28 = (bf16[1,576,128]{2,1,0:T(8,128)(2,1)}, bf16[1,576,128]{2,1,0:T(8,128)(2,1)S(1)}, u32[]{:S(2)}, u32[]{:S(2)}) collective-permute-start(bf16[1,576,128]{2,1,0:T(8,128)(2,1)} %get-tuple-element.231), channel_id=1, source_target_pairs={{0,16},{4,20},{8,24},{12,28},{16,0},{20,4},{24,8},{28,12},{1,17},{... | collective-permute-start | bytes 442376 | tf_op jit(solution)/shard_map/ppermute | solution.py:867
  177.2 11.6 %collective-permute-start.27 = (bf16[1,576,128]{2,1,0:T(8,128)(2,1)}, bf16[1,576,128]{2,1,0:T(8,128)(2,1)S(1)}, u32[]{:S(2)}, u32[]{:S(2)}) collective-permute-start(bf16[1,576,128]{2,1,0:T(8,128)(2,1)} %get-tuple-element.227), channel_id=1, source_target_pairs={{0,16},{4,20},{8,24},{12,28},{16,0},{20,4},{24,8},{28,12},{1,17},{... | collective-permute-start | bytes 442376 | tf_op jit(solution)/shard_map/ppermute | solution.py:867
  184.9 16.5 %copy-start.12 = (f32[2,3,512]{2,0,1:T(2,128)S(1)}, f32[2,3,512]{2,0,1:T(2,128)}, u32[]{:S(2)}) copy-start(f32[2,3,512]{2,0,1:T(2,128)} %param.26) | copy-start | bytes 36868
  184.9 16.5 %copy-start.13 = (f32[2,3,512]{2,0,1:T(2,128)S(1)}, f32[2,3,512]{2,0,1:T(2,128)}, u32[]{:S(2)}) copy-start(f32[2,3,512]{2,0,1:T(2,128)} %param.27) | copy-start | bytes 36868
  191.5 10.0 %all-to-all-start.7 = ((f32[32,1,128]{2,1,0:T(1,128)}), f32[32,1,128]{2,1,0:T(1,128)S(1)}, u32[]{:S(2)}, u32[]{:S(2)}) async-start(f32[32,1,128]{2,1,0:T(1,128)} %get-tuple-element.235), calls=%async_computation.7 | async-start | bytes 32768 | tf_op jit(solution)/shard_map/all_to_all | solution.py:942
  (21 other events, 58.0 us)

commit v4 on v3

--- a/solution.py
+++ b/solution.py
@@ -238,21 +238,21 @@
     ])
 
 
-def kernel_edges(sz, x_hbm, index_hbm, low_ref, high_ref, x_ref, index_ref, sems):
+def kernel_edges(sz, x_hbm, index_hbm, near_ref, far_ref, x_ref, index_ref, sems):
     copies = Copies(sems)
     edge = HALO * sz.width
     few = sz.width
-    lines = index_hbm.shape[0]
-    first = copies.start(index_hbm.at[pl.ds(lines - few, few)], index_ref.at[0])
-    second = copies.start(index_hbm.at[pl.ds(0, few)], index_ref.at[1])
-    rest = [
-        copies.start(x_hbm.at[pl.ds(sz.pixels - edge, edge)], low_ref.at[pl.ds(0, edge)]),
-        copies.start(x_hbm.at[pl.ds(0, edge)], high_ref.at[pl.ds(0, edge)]),
-        copies.start(x_hbm, x_ref),
-    ]
-    wait(first, second)
-    low_ref[edge : edge + few, :] = index_ref[0].astype(BF16)
-    high_ref[edge : edge + few, :] = index_ref[1].astype(BF16)
+    odd = lax.axis_index("rows") % 2
+    last = index_hbm.shape[0] - few
+    loads = []
+    rest = []
+    for k, (first, target) in enumerate(((1 - odd, near_ref), (odd, far_ref))):
+        loads.append(copies.start(line_share(index_hbm, first * last, few, few), index_ref.at[k]))
+        rest.append(copies.start(line_share(x_hbm, first * (sz.pixels - edge), edge, edge), target.at[pl.ds(0, edge)]))
+    rest.append(copies.start(x_hbm, x_ref))
+    wait(*loads)
+    near_ref[edge : edge + few, :] = index_ref[0].astype(BF16)
+    far_ref[edge : edge + few, :] = index_ref[1].astype(BF16)
     wait(*rest)
 
 
@@ -282,20 +282,23 @@
     )
 
 
-def kernel_first(sz, limits_ref, up_ref, x_ref, down_ref, head_ref, weights_hbm, stats_ref, conv_ref, act_hbm, x3_ref,
+def kernel_first(sz, limits_ref, near_ref, x_ref, far_ref, head_ref, weights_hbm, stats_ref, conv_ref, act_hbm, x3_ref,
                  buffer_ref, sems):
     copies = Copies(sems)
     weights = Weights(copies, head_ref, weights_hbm, buffer_ref, 0)
     masks = Masks(sz, limits_ref)
     stats = Stats(sz)
 
+    odd = lax.axis_index("rows") % 2 == 1
+
     def prepare(row):
         if row < HALO:
-            value = up_ref[line(sz, row), :]
+            value = jnp.where(odd, near_ref[line(sz, row), :], far_ref[line(sz, row), :])
         elif row < HALO + sz.rows:
             value = x_ref[line(sz, row - HALO), :]
         else:
-            value = down_ref[line(sz, row - HALO - sz.rows), :]
+            below = line(sz, row - HALO - sz.rows)
+            value = jnp.where(odd, far_ref[below, :], near_ref[below, :])
         put_shifted(sz, masks, x3_ref, row, value.astype(F32))
 
     def work(first, last):
@@ -350,11 +353,11 @@
     wait(*outs)
 
 
-def kernel_pool(sz, limits_ref, member_ref, gathered_ref, before_ref, norm_ref, index_hbm, up_hbm, down_hbm, *rest):
+def kernel_pool(sz, limits_ref, member_ref, gathered_ref, before_ref, norm_ref, index_hbm, near_hbm, far_hbm, *rest):
     cotangents, rest = rest[: sz.bands], rest[sz.bands :]
     (stats_ref, grad_ref, normed_ref, moments_ref), rest = rest[:4], rest[4:]
     shares, rest = rest[: sz.bands], rest[sz.bands :]
-    (index_ref, up_ref, down_ref, cotangent_ref, spread_ref, act_ref, pooled_ref, grad16_ref, normed16_ref, sems) = rest
+    (index_ref, near_ref, far_ref, cotangent_ref, spread_ref, act_ref, pooled_ref, grad16_ref, normed16_ref, sems) = rest
     c, w = sz.channels, sz.width
     half = w // 2
     windows = sz.rows // 2
@@ -362,8 +365,8 @@
     copies = Copies(sems)
     inputs = [
         copies.start(index_hbm, index_ref),
-        copies.start(up_hbm.at[pl.ds(edge, w)], up_ref),
-        copies.start(down_hbm.at[pl.ds(edge, w)], down_ref),
+        copies.start(near_hbm.at[pl.ds(edge, w)], near_ref),
+        copies.start(far_hbm.at[pl.ds(edge, w)], far_ref),
     ]
     inputs += [
         copies.start(
@@ -404,14 +407,16 @@
             result = jnp.where(index == corner, taken, result)
         pooled_ref[p * half : (p + 1) * half, :] = result.astype(BF16)
     outs += send_shares(sz, copies, pooled_ref, shares, 0)
+    odd = lax.axis_index("rows") % 2 == 1
     for p in range(windows + 4):
         if p < 2:
-            index = up_ref[p * half : (p + 1) * half, :].astype(jnp.int32)
+            place = slice(p * half, (p + 1) * half)
+            index = jnp.where(odd, near_ref[place, :].astype(jnp.int32), far_ref[place, :].astype(jnp.int32))
         elif p < windows + 2:
             index = index_ref[(p - 2) * half : (p - 1) * half, :]
         else:
-            first = (p - windows - 2) * half
-            index = down_ref[first : first + half, :].astype(jnp.int32)
+            place = slice((p - windows - 2) * half, (p - windows - 1) * half)
+            index = jnp.where(odd, far_ref[place, :].astype(jnp.int32), near_ref[place, :].astype(jnp.int32))
         given = cotangent_ref[p * half : (p + 1) * half, :].astype(F32)
         for corner in range(4):
             start = (2 * p + corner // 2) * w + corner % 2
@@ -529,11 +534,7 @@
     pixels = sz.height * w
     given, rest = rest[:bands], rest[bands:]
     acts, rest = rest[:bands], rest[bands:]
-    if layer == 0:
-        out_ref, grad_ref, normed_ref, act_ref, x9_ref, sems = rest
-    else:
-        (keep_hbm, send_hbm, grad_ref, normed_ref, act_ref, x9_ref, keep_ref, send_ref, term_ref,
-         sems) = rest
+    keep_hbm, send_hbm, grad_ref, normed_ref, act_ref, x9_ref, keep_ref, send_ref, term_ref, sems = rest
     copies = Copies(sems)
     inputs = []
     for n in range(bands):
@@ -577,15 +578,14 @@
     term = lax.dot_general(
         act_ref[...], x9_ref[...], (((0,), (0,)), ((), ())), preferred_element_type=F32
     )
+    term_ref[...] = term
     if layer == 0:
-        for tap in range(9):
-            part = term[:, tap * q : (tap + 1) * q].astype(BF16)
-            for m in range(sz.maps):
-                out_ref[m, tap * share : (tap + 1) * share, :] = part[m * share : (m + 1) * share, :]
-        return
-    term_ref[...] = term
-    for position, relative in enumerate(halving_order(sz.maps)):
-        lines = pl.ds(pl.multiple_of((own ^ relative) * share, share), share)
+        others = [2 * place + (own & 1) for place in range(sz.maps // 2)]
+        order = others + [other ^ 1 for other in others]
+    else:
+        order = [own ^ relative for relative in halving_order(sz.maps)]
+    for position, other in enumerate(order):
+        lines = pl.ds(pl.multiple_of(other * share, share), share)
         for tap in range(9):
             place = slice(tap * share, (tap + 1) * share)
             part = term_ref[lines, tap * q : (tap + 1) * q]
@@ -599,6 +599,17 @@
 def halving_order(maps):
     bits = maps.bit_length() - 1
     return [sum(((place >> (bits - 1 - k)) & 1) << k for k in range(bits)) for place in range(maps)]
+
+
+def kernel_add(keep_hbm, received_hbm, out_ref, keep_ref, received_ref, sems):
+    copies = Copies(sems)
+    loads = [
+        (copies.start(keep_hbm.at[k], keep_ref.at[k]), copies.start(received_hbm.at[k], received_ref.at[k]))
+        for k in range(keep_ref.shape[0])
+    ]
+    for k, load in enumerate(loads):
+        wait(*load)
+        out_ref[k] = (keep_ref[k] + received_ref[k].astype(F32)).astype(BF16)
 
 
 def kernel_halve(keep_hbm, received_hbm, next_keep_hbm, next_send_hbm, keep_ref, received_ref, send_ref, sems):
@@ -632,7 +643,7 @@
         norm_grad_ref[layer, 0:1, :] = gain_row
         norm_grad_ref[layer, 1:2, :] = shift_row
     value = received_ref[0].astype(F32)
-    for m in range(1, sz.maps):
+    for m in range(1, received_ref.shape[0]):
         value = value + received_ref[m].astype(F32)
     shard_ref[0] = value
     total = jnp.sum(value * value, axis=0, keepdims=True)
@@ -715,8 +726,6 @@
     w, c, q = sz.width, sz.channels, sz.quarter
     half = w // 2
     n_maps, bands = sz.maps, sz.bands
-    forward = [(i, i + 1) for i in range(bands - 1)]
-    backward = [(i + 1, i) for i in range(bands - 1)]
     x = block_input.reshape(sz.pixels, c)
     index = pool_index.reshape(sz.pixels // 4, c)
     norms, norm_first, norm_second = (v.transpose(1, 0, 2) for v in (norm_params, norm_moment1, norm_moment2))
@@ -756,13 +765,13 @@
 
     tie = lax.optimization_barrier
 
-    low, high, near = call(
+    to_near, to_far, own_x = call(
         functools.partial(kernel_edges, sz), "edges",
         [shape((edge + 2 * half, c), BF16)] * 2 + [pixel_shape(sz.rows, BF16)], [x, index],
         [pltpu.VMEM((2, 2 * half, c), jnp.int32)], hbm_ins=(0, 1), sems=5,
     )
-    up = lax.ppermute(low, "rows", forward)
-    down = lax.ppermute(high, "rows", backward)
+    far = lax.ppermute(to_far, "rows", [(i + 1 - k, i + k) for i in range(1, bands - 1, 2) for k in (0, 1)])
+    near = swap(to_near, 1)
 
     limits, member = call(
         functools.partial(kernel_places, sz), "places", [shape((8, 128), jnp.int32), stats_shape],
@@ -775,7 +784,7 @@
     rows = sz.rows + 2 * HALO
     stats, conv, kept = call(
         functools.partial(kernel_first, sz), "first",
-        [stats_shape, pixel_shape(rows - 2, F32), pixel_shape(sz.rows, BF16)], [limits, up, near, down, conv_weights[0, :HEAD], conv_weights],
+        [stats_shape, pixel_shape(rows - 2, F32), pixel_shape(sz.rows, BF16)], [limits, near, own_x, far, conv_weights[0, :HEAD], conv_weights],
         [pixel_space(rows, BF16, 3), weight_space], conv_flops(rows - 2), hbm_ins=(5,), hbm_outs=(2,), sems=4,
     )
     def head(layer, weights):
@@ -804,11 +813,11 @@
         moments.append(moment)
         saves.append(saved)
         if layer == 1:
-            stats, weights, *rest = tie((stats, conv_weights, *cots, *acts[0]))
-            cots, acts[0] = rest[:bands], rest[bands:]
+            stats, weights, *acts[0] = tie((stats, conv_weights, *acts[0]))
             gathered = spread(stats)
         else:
-            stats, *acts[1] = tie((stats, *acts[1]))
+            stats, *rest = tie((stats, *cots, *acts[1]))
+            cots, acts[1] = rest[:bands], rest[bands:]
             gathered = spread(stats)
         acts[layer - 1].append(swap(acts[layer - 1][2], 1))
         acts.append([act, swap(act, 1), swap(act, 2)])
@@ -818,7 +827,7 @@
         functools.partial(kernel_pool, sz), "pool",
         [stats_shape, pixel_shape(rows, F32), pixel_shape(rows, BF16), tile_shape]
         + share_shapes(lines + 2 * sz.pixels),
-        consts + [gathered, conv, norms, index, up, down] + cots,
+        consts + [gathered, conv, norms, index, near, far] + cots,
         [
             pltpu.VMEM((lines, c), jnp.int32), pltpu.VMEM((2 * half, c), BF16), pltpu.VMEM((2 * half, c), BF16),
             pltpu.VMEM((cot_lines, c), BF16),
@@ -851,16 +860,13 @@
             pltpu.VMEM((sz.height * w, c), BF16),
             pltpu.VMEM((sz.height * w, 9 * q), BF16),
         ]
-        if layer == 0:
-            outs = [part_shape(n_maps, BF16)]
-        else:
-            outs = [part_shape(n_maps // 2, dtype) for dtype in (F32, BF16)]
-            scratch += [part_space(n_maps // 2, dtype) for dtype in (F32, BF16)]
-            scratch.append(pltpu.VMEM((c, 9 * q), F32))
+        outs = [part_shape(n_maps // 2, dtype) for dtype in (F32, BF16)]
+        scratch += [part_space(n_maps // 2, dtype) for dtype in (F32, BF16)]
+        scratch.append(pltpu.VMEM((c, 9 * q), F32))
         return call(
             functools.partial(kernel_weight_grad, sz, layer, first), "weight_grad", outs,
             consts + [gathered, moments[layer], norms] + given + acts[layer], scratch, conv_flops(sz.rows),
-            hbm_ins=range(5, 5 + 2 * bands), hbm_outs=() if layer == 0 else (0, 1), sems=3 * bands + 2,
+            hbm_ins=range(5, 5 + 2 * bands), hbm_outs=(0, 1), sems=3 * bands + 2,
         )
 
     def step_of(send, k):
@@ -919,11 +925,23 @@
             keep2, send2 = halved(keep2, arrived2)
 
     arrived2 = step_of(send2, 1)
-    (partial,) = weight_grad(0, gathered, exchanged, (0, sz.pixels))
-    partial, arrived1, arrived2 = tie((partial, arrived1, arrived2))
-    received = lax.all_to_all(partial, "maps", 0, 0, tiled=True)
-    shards[2] = halve(keep2, arrived2, 1)
-    shards[1] = halve(keep1, arrived1, 0)
+    keep0, send0 = weight_grad(0, gathered, exchanged, (0, sz.pixels))
+    send0, arrived2 = tie((send0, arrived2))
+    arrived0 = step_of(send0, 0)
+    keep1, send1 = halved(keep1, arrived1)
+    keep2, send2 = halved(keep2, arrived2)
+    arrived1 = step_of(send1, 1)
+    arrived2 = step_of(send2, 2)
+    arrived0, arrived1, arrived2 = tie((arrived0, arrived1, arrived2))
+    half_maps = n_maps // 2
+    (partial,) = call(
+        kernel_add, "add", [part_shape(half_maps, BF16)], [keep0, arrived0],
+        [part_space(half_maps, dtype) for dtype in (F32, BF16)], hbm_ins=(0, 1), sems=2 * half_maps,
+    )
+    alike = [[m for m in range(n_maps) if m & 1 == bit] for bit in (0, 1)]
+    received = lax.all_to_all(partial, "maps", 0, 0, tiled=True, axis_index_groups=alike)
+    shards[2] = halve(keep2, arrived2, 2)
+    shards[1] = halve(keep1, arrived1, 1)
     input_grad, totals[0], pooled = call(
         functools.partial(kernel_last, sz), "last",
         [pixel_shape(sz.rows, BF16), tile_shape, shape((sz.height // 2 * half, q), BF16)],

time: 206 us -> 202 us (0.981)
  waiting for transfers between devices: 51.6 us -> 42.1 us
  local copies, waits for them, and re-layouts: 14 us -> 17.4 us
  Pallas kernels: 64.3 us -> 66.9 us
    ppermute x12, waiting for transfers between devices: 6.98 us -> 0.03 us  [trade(): lax.ppermute(shares[n], 'rows', [(i, i ^ n) for i in range(bands)])]
    unnamed x66 -> x72, local copies, waits for them, and re-layouts: 7.47 us -> 10.8 us
    ppermute x2 -> x1, starting transfers between devices: 3.66 us -> 0.66 us  [local(): lax.ppermute(to_far, 'rows', [(i + 1 - k, i + k) for i in range(1, bands...]
    pallas_call x19 -> x20, Pallas kernels: 64.3 us -> 66.9 us  [call(): pl.pallas_call(kernel, out_shape=tuple((space(out.shape, out.dtype) for s...]
    ppermute x6 -> x7, waiting for transfers between devices: 21.9 us -> 19.6 us  [step_of(): return lax.ppermute(send, 'maps', [(m, m ^ 1 << k) for m in range(n_maps)])]
    ppermute x9 -> x10, starting transfers between devices: 5.5 us -> 6.4 us  [swap(): return lax.ppermute(act, 'rows', [(i, i ^ n) for i in range(bands)])]
    ppermute x6 -> x7, starting transfers between devices: 10.2 us -> 10.5 us  [step_of(): return lax.ppermute(send, 'maps', [(m, m ^ 1 << k) for m in range(n_maps)])]
  transfers between devices with their start and end apart: 36 -> 37, of which waited for: 14 -> 12; matrix products, arithmetic and copies ran while one was open for 4% -> 4% of each run, Pallas kernels for 26% -> 26%
where the time goes in v4:
time: 202 us; the launch traced here: 201 us
  Pallas kernels  66.9 us (33%)
  starting transfers between devices  57.2 us (28%)
  waiting for transfers between devices  42.1 us (21%)
  local copies, waits for them, and re-layouts  17.4 us (9%)
  blocking collectives  13.3 us (7%)
  between operations  2.07 us (1%)
    pallas_call x20, Pallas kernels, call(): pl.pallas_call(kernel, out_shape=tuple((space(out.shape, out.dtype) for s...  66.9 us
    all_to_all x5, starting transfers between devices, spread(): return lax.all_to_all(stats, AXES, 0, 0, tiled=True)  23.2 us
    ppermute x7, waiting for transfers between devices, step_of(): return lax.ppermute(send, 'maps', [(m, m ^ 1 << k) for m in range(n_maps)])  19.6 us
    all_to_all x5, waiting for transfers between devices, spread(): return lax.all_to_all(stats, AXES, 0, 0, tiled=True)  14 us
    all_to_all x1, blocking collectives, spread(): return lax.all_to_all(stats, AXES, 0, 0, tiled=True)  13.3 us
    unnamed x72, local copies, waits for them, and re-layouts  10.8 us
    ppermute x7, starting transfers between devices, step_of(): return lax.ppermute(send, 'maps', [(m, m ^ 1 << k) for m in range(n_maps)])  10.5 us
    ppermute x12, starting transfers between devices, trade(): lax.ppermute(shares[n], 'rows', [(i, i ^ n) for i in range(bands)])  7.88 us
  transfers between devices with their start and end apart: 37, of which 12 were waited for; matrix products, arithmetic and copies ran while one was open for 4% of the time, Pallas kernels for 26%

profile of v4, /device:TPU:0, one launch (start us, length us, event | category | flops | bytes accessed | tf_op | source)
XLA Modules:
  0.0 200.6 jit_solution(15708299587831919584)
XLA Ops:
  0.7 1.3 edges.1
  7.6 1.1 slice_bitcast_fusion.5.head_ref
  8.7 5.3 %first.1 = (f32[32,8,128]{2,1,0:T(8,128)}, f32[704,512]{1,0:T(8,128)S(1)}, bf16[384,512]{1,0:T(8,128)(2,1)}) custom-call(s32[8,128]{1,0:T(8,128)S(1)} %get-tuple-element.131.limits_ref, bf16[224,512]{1,0:T(8,128)(2,1)S(1)} %collective-permute-done.near_ref.near_hbm, bf16[384,512]{1,0:T(8,128)(2,1)S(1)} %get-tuple-element.134.x_ref, ...), custom_call_target="tpu_custom_call" | custom-call | flops 3321888768 | tf_op jit(solution)/shard_map/first/pallas_call | solution.py:712
  14.1 8.7 %all-to-all-start = ((f32[32,8,128]{2,1,0:T(8,128)}), f32[32,8,128]{2,1,0:T(8,128)S(1)}, u32[]{:S(2)}, u32[]{:S(2)}) async-start(f32[32,8,128]{2,1,0:T(8,128)} %get-tuple-element.141), calls=%async_computation | async-start | bytes 262144 | tf_op jit(solution)/shard_map/all_to_all | solution.py:756
  23.1 1.7 collective-permute-start.3
  24.8 1.1 slice_bitcast_fusion.4.head_ref
  25.9 5.2 %all-to-all-done.gathered_ref = f32[32,8,128]{2,1,0:T(8,128)S(1)} async-done(((f32[32,8,128]{2,1,0:T(8,128)}), f32[32,8,128]{2,1,0:T(8,128)S(1)}, u32[]{:S(2)}, u32[]{:S(2)}) %all-to-all-start) | async-done | bytes 131104 | tf_op jit(solution)/shard_map/all_to_all | solution.py:756
  31.0 4.3 %forward.2 = (f32[32,8,128]{2,1,0:T(8,128)S(1)}, f32[640,512]{1,0:T(8,128)S(1)}, f32[8,128]{1,0:T(8,128)S(1)}, bf16[384,512]{1,0:T(8,128)(2,1)}, f32[448,512]{1,0:T(8,128)}) custom-call(s32[8,128]{1,0:T(8,128)S(1)} %get-tuple-element.131.limits_ref, f32[32,8,128]{2,1,0:T(8,128)S(1)} %get-tuple-element.132.member_ref, ...), custom_call_target="tpu_custom_call" | custom-call | flops 3019898880 | tf_op jit(solution)/shard_map/forward/pallas_call | solution.py:712
  36.6 4.2 %all-to-all-start.1 = ((f32[32,8,128]{2,1,0:T(8,128)}), f32[32,8,128]{2,1,0:T(8,128)S(1)}, u32[]{:S(2)}, u32[]{:S(2)}) async-start(f32[32,8,128]{2,1,0:T(8,128)} %copy-done.9), calls=%async_computation.1 | async-start | bytes 262144 | tf_op jit(solution)/shard_map/all_to_all | solution.py:756
  41.1 1.7 collective-permute-start.5
  43.2 1.7 collective-permute-start.8
  46.0 3.0 %all-to-all-done.1.gathered_ref = f32[32,8,128]{2,1,0:T(8,128)S(1)} async-done(((f32[32,8,128]{2,1,0:T(8,128)}), f32[32,8,128]{2,1,0:T(8,128)S(1)}, u32[]{:S(2)}, u32[]{:S(2)}) %all-to-all-start.1) | async-done | bytes 131104 | tf_op jit(solution)/shard_map/all_to_all | solution.py:756
  49.0 4.0 %forward.3 = (f32[32,8,128]{2,1,0:T(8,128)S(1)}, f32[576,512]{1,0:T(8,128)S(1)}, f32[8,128]{1,0:T(8,128)S(1)}, bf16[384,512]{1,0:T(8,128)(2,1)}, f32[512,512]{1,0:T(8,128)}) custom-call(s32[8,128]{1,0:T(8,128)S(1)} %get-tuple-element.131.limits_ref, f32[32,8,128]{2,1,0:T(8,128)S(1)} %get-tuple-element.132.member_ref, ...), custom_call_target="tpu_custom_call" | custom-call | flops 2717908992 | tf_op jit(solution)/shard_map/forward/pallas_call | solution.py:712
  54.1 1.9 collective-permute-done.8.rest_6_
  56.0 13.3 %all_to_all.40.gathered_ref = f32[32,8,128]{2,1,0:T(8,128)S(1)} all-to-all(f32[32,8,128]{2,1,0:T(8,128)S(1)} %get-tuple-element.155), channel_id=1, replica_groups=mesh['maps'=8,'rows'=4] {'maps','rows'}, dimensions={0} | all-to-all | bytes 262144 | tf_op jit(solution)/shard_map/all_to_all | solution.py:756
  69.3 2.9 %pool.1 = (f32[32,8,128]{2,1,0:T(8,128)}, f32[576,512]{1,0:T(8,128)S(1)}, bf16[576,512]{1,0:T(8,128)(2,1)S(1)}, f32[8,128]{1,0:T(8,128)S(1)}, bf16[864,128]{1,0:...) custom-call(s32[8,128]{1,0:T(8,128)S(1)} %get-tuple-element.131.limits_ref, ...), custom_call_target="tpu_custom_call" | custom-call | flops 603979776 | tf_op jit(solution)/shard_map/pool/pallas_call | solution.py:712
  73.1 2.8 %all-to-all-start.3 = ((f32[32,8,128]{2,1,0:T(8,128)}), f32[32,8,128]{2,1,0:T(8,128)S(1)}, u32[]{:S(2)}, u32[]{:S(2)}) async-start(f32[32,8,128]{2,1,0:T(8,128)} %get-tuple-element.164), calls=%async_computation.3 | async-start | bytes 262144 | tf_op jit(solution)/shard_map/all_to_all | solution.py:756
  76.4 1.5 collective-permute-start.15
  78.6 1.1 slice_bitcast_fusion.2.head_ref
  79.7 4.3 %all-to-all-done.3.gathered_ref = f32[32,8,128]{2,1,0:T(8,128)S(1)} async-done(((f32[32,8,128]{2,1,0:T(8,128)}), f32[32,8,128]{2,1,0:T(8,128)S(1)}, u32[]{:S(2)}, u32[]{:S(2)}) %all-to-all-start.3) | async-done | bytes 131104 | tf_op jit(solution)/shard_map/all_to_all | solution.py:756
  85.7 5.9 %backward.2 = (f32[32,8,128]{2,1,0:T(8,128)}, f32[512,512]{1,0:T(8,128)S(1)}, bf16[512,512]{1,0:T(8,128)(2,1)S(1)}, f32[8,128]{1,0:T(8,128)S(1)}, bf16[768,128]{...) custom-call(s32[8,128]{1,0:T(8,128)S(1)} %get-tuple-element.131.limits_ref, ...), custom_call_target="tpu_custom_call" | custom-call | flops 2415919104 | tf_op jit(solution)/shard_map/backward/pallas_call | solution.py:712
  92.5 2.6 %all-to-all-start.4 = ((f32[32,8,128]{2,1,0:T(8,128)}), f32[32,8,128]{2,1,0:T(8,128)S(1)}, u32[]{:S(2)}, u32[]{:S(2)}) async-start(f32[32,8,128]{2,1,0:T(8,128)} %get-tuple-element.178), calls=%async_computation.4 | async-start | bytes 262144 | tf_op jit(solution)/shard_map/all_to_all | solution.py:756
  95.2 1.7 collective-permute-start.18
  97.0 5.3 %weight_grad.3 = (f32[4,576,128]{2,1,0:T(8,128)}, bf16[4,576,128]{2,1,0:T(8,128)(2,1)}) custom-call(s32[8,128]{1,0:T(8,128)S(1)} %get-tuple-element.131.limits_ref, f32[32,8,128]{2,1,0:T(8,128)S(1)} %get-tuple-element.132.member_ref, f32[32,8,128]{2,1,0:T(8,128)S(1)} %all-to-all-done.3.gathered_ref, f32[8,128]{1,0:T(8,128)S(1)} %get-tuple-element.167.moments_ref, ...), custom_call_target="tpu_custom_call" | custom-call | flops 1811939328 | tf_op jit(solution)/shard_map/weight_grad/pallas_call | solution.py:712
  104.1 1.1 slice_bitcast_fusion.1.head_ref
  106.2 5.7 %backward.3 = (f32[32,8,128]{2,1,0:T(8,128)}, f32[448,512]{1,0:T(8,128)S(1)}, bf16[448,512]{1,0:T(8,128)(2,1)S(1)}, f32[8,128]{1,0:T(8,128)S(1)}, bf16[768,128]{...) custom-call(s32[8,128]{1,0:T(8,128)S(1)} %get-tuple-element.131.limits_ref, ...), custom_call_target="tpu_custom_call" | custom-call | flops 2113929216 | tf_op jit(solution)/shard_map/backward/pallas_call | solution.py:712
  112.7 5.0 %all-to-all-start.5 = ((f32[32,8,128]{2,1,0:T(8,128)}), f32[32,8,128]{2,1,0:T(8,128)S(1)}, u32[]{:S(2)}, u32[]{:S(2)}) async-start(f32[32,8,128]{2,1,0:T(8,128)} %get-tuple-element.198), calls=%async_computation.5 | async-start | bytes 262144 | tf_op jit(solution)/shard_map/all_to_all | solution.py:756
  117.8 1.7 collective-permute-start.22
  119.6 5.3 %weight_grad.4 = (f32[4,576,128]{2,1,0:T(8,128)}, bf16[4,576,128]{2,1,0:T(8,128)(2,1)}) custom-call(s32[8,128]{1,0:T(8,128)S(1)} %get-tuple-element.131.limits_ref, f32[32,8,128]{2,1,0:T(8,128)S(1)} %get-tuple-element.132.member_ref, f32[32,8,128]{2,1,0:T(8,128)S(1)} %all-to-all-done.4.gathered_ref, f32[8,128]{1,0:T(8,128)S(1)} %copy-done.12, ...), custom_call_target="tpu_custom_call" | custom-call | flops 1811939328 | tf_op jit(solution)/shard_map/weight_grad/pallas_call | solution.py:712
  126.6 2.3 %halve.4 = (f32[2,576,128]{2,1,0:T(8,128)}, bf16[2,576,128]{2,1,0:T(8,128)(2,1)}) custom-call(f32[4,576,128]{2,1,0:T(8,128)} %get-tuple-element.223.keep_hbm, bf16[4,576,128]{2,1,0:T(8,128)(2,1)} %collective-permute-done.20.received_hbm), custom_call_target="tpu_custom_call" | custom-call | tf_op jit(solution)/shard_map/halve/pallas_call | solution.py:712
  128.9 1.5 collective-permute-start.24
  131.3 5.6 %weight_grad.5 = (f32[4,576,128]{2,1,0:T(8,128)}, bf16[4,576,128]{2,1,0:T(8,128)(2,1)}) custom-call(s32[8,128]{1,0:T(8,128)S(1)} %get-tuple-element.131.limits_ref, f32[32,8,128]{2,1,0:T(8,128)S(1)} %get-tuple-element.132.member_ref, f32[32,8,128]{2,1,0:T(8,128)S(1)} %all-to-all-done.5.gathered_ref, f32[8,128]{1,0:T(8,128)S(1)} %copy-done.14, ...), custom_call_target="tpu_custom_call" | custom-call | flops 1811939328 | tf_op jit(solution)/shard_map/weight_grad/pallas_call | solution.py:712
  136.9 1.4 collective-permute-done.24.received_hbm
  139.2 2.9 %collective-permute-done.26.received_hbm = bf16[4,576,128]{2,1,0:T(8,128)(2,1)S(1)} collective-permute-done((bf16[4,576,128]{2,1,0:T(8,128)(2,1)}, bf16[4,576,128]{2,1,0:T(8,128)(2,1)S(1)}, u32[]{:S(2)}, u32[]{:S(2)}) %collective-permute-start.26) | collective-permute-done | bytes 589856 | tf_op jit(solution)/shard_map/ppermute | solution.py:873
  142.9 2.3 %halve.5 = (f32[2,576,128]{2,1,0:T(8,128)}, bf16[2,576,128]{2,1,0:T(8,128)(2,1)}) custom-call(f32[4,576,128]{2,1,0:T(8,128)} %get-tuple-element.227.keep_hbm, bf16[4,576,128]{2,1,0:T(8,128)(2,1)} %copy-done.19), custom_call_target="tpu_custom_call" | custom-call | tf_op jit(solution)/shard_map/halve/pallas_call | solution.py:712
  146.2 1.9 halve.6
  148.1 2.5 %collective-permute-start.28 = (bf16[1,576,128]{2,1,0:T(8,128)(2,1)}, bf16[1,576,128]{2,1,0:T(8,128)(2,1)S(1)}, u32[]{:S(2)}, u32[]{:S(2)}) collective-permute-start(bf16[1,576,128]{2,1,0:T(8,128)(2,1)} %get-tuple-element.232), channel_id=1, source_target_pairs={{0,16},{4,20},{8,24},{12,28},{16,0},{20,4},{24,8},{28,12},{1,17},{... | collective-permute-start | bytes 442376 | tf_op jit(solution)/shard_map/ppermute | solution.py:873
  150.6 5.3 %collective-permute-done.28.last2_hbm = bf16[1,576,128]{2,1,0:T(8,128)(2,1)S(1)} collective-permute-done((bf16[1,576,128]{2,1,0:T(8,128)(2,1)}, bf16[1,576,128]{2,1,0:T(8,128)(2,1)S(1)}, u32[]{:S(2)}, u32[]{:S(2)}) %collective-permute-start.28) | collective-permute-done | bytes 147488 | tf_op jit(solution)/shard_map/ppermute | solution.py:873
  157.1 2.3 %add.3 = bf16[4,576,128]{2,1,0:T(8,128)(2,1)} custom-call(f32[4,576,128]{2,1,0:T(8,128)} %get-tuple-element.221.keep_hbm, bf16[4,576,128]{2,1,0:T(8,128)(2,1)} %copy-done.20), custom_call_target="tpu_custom_call" | custom-call | tf_op jit(solution)/shard_map/add/pallas_call | solution.py:712
  159.5 4.6 %all-to-all-start.6 = ((bf16[4,576,128]{2,1,0:T(8,128)(2,1)}), bf16[4,576,128]{2,1,0:T(8,128)(2,1)S(1)}, u32[]{:S(2)}, u32[]{:S(2)}) async-start(bf16[4,576,128]{2,1,0:T(8,128)(2,1)} %add.3), calls=%async_computation.6 | async-start | bytes 1179648 | tf_op jit(solution)/shard_map/all_to_all | solution.py:942
  165.2 2.0 halve.7
  167.1 3.0 %collective-permute-start.29 = (bf16[1,576,128]{2,1,0:T(8,128)(2,1)}, bf16[1,576,128]{2,1,0:T(8,128)(2,1)S(1)}, u32[]{:S(2)}, u32[]{:S(2)}) collective-permute-start(bf16[1,576,128]{2,1,0:T(8,128)(2,1)} %get-tuple-element.237), channel_id=1, source_target_pairs={{0,16},{4,20},{8,24},{12,28},{16,0},{20,4},{24,8},{28,12},{1,17},{... | collective-permute-start | bytes 442376 | tf_op jit(solution)/shard_map/ppermute | solution.py:873
  170.1 4.2 %last.1 = (bf16[384,512]{1,0:T(8,128)(2,1)}, f32[8,128]{1,0:T(8,128)S(1)}, bf16[384,128]{1,0:T(8,128)(2,1)}) custom-call(s32[8,128]{1,0:T(8,128)S(1)} %get-tuple-element.131.limits_ref, f32[32,8,128]{2,1,0:T(8,128)S(1)} %get-tuple-element.132.member_ref, f32[32,8,128]{2,1,0:T(8,128)S(1)} %all-to-all-done.5.gathered_ref, ...), custom_call_target="tpu_custom_call" | custom-call | flops 1811939328 | tf_op jit(solution)/shard_map/last/pallas_call | solution.py:712
  174.3 9.7 %collective-permute-done.29.last1_hbm = bf16[1,576,128]{2,1,0:T(8,128)(2,1)S(1)} collective-permute-done((bf16[1,576,128]{2,1,0:T(8,128)(2,1)}, bf16[1,576,128]{2,1,0:T(8,128)(2,1)S(1)}, u32[]{:S(2)}, u32[]{:S(2)}) %collective-permute-start.29) | collective-permute-done | bytes 147488 | tf_op jit(solution)/shard_map/ppermute | solution.py:873
  184.6 2.0 squares.1
  186.6 3.9 %all-to-all-start.7 = ((f32[32,1,128]{2,1,0:T(1,128)}), f32[32,1,128]{2,1,0:T(1,128)S(1)}, u32[]{:S(2)}, u32[]{:S(2)}) async-start(f32[32,1,128]{2,1,0:T(1,128)} %get-tuple-element.243), calls=%async_computation.7 | async-start | bytes 32768 | tf_op jit(solution)/shard_map/all_to_all | solution.py:960
  191.1 6.4 %all-to-all-done.7.every_ref = f32[32,1,128]{2,1,0:T(1,128)S(1)} async-done(((f32[32,1,128]{2,1,0:T(1,128)}), f32[32,1,128]{2,1,0:T(1,128)S(1)}, u32[]{:S(2)}, u32[]{:S(2)}) %all-to-all-start.7) | async-done | bytes 16416 | tf_op jit(solution)/shard_map/all_to_all | solution.py:960
  197.6 2.9 %adam.1 = (f32[1,128]{1,0:T(1,128)}, f32[3,576,128]{2,1,0:T(8,128)}, f32[3,576,128]{2,1,0:T(8,128)}, f32[3,576,128]{2,1,0:T(8,128)}, f32[3,2,512]{2,1,0:T(2,128)...) custom-call(f32[32,1,128]{2,1,0:T(1,128)S(1)} %all-to-all-done.7.every_ref, s32[1]{0:T(128)S(6)} %copy.24.step_ref, ...), custom_call_target="tpu_custom_call" | custom-call | tf_op jit(solution)/shard_map/adam/pallas_call | solution.py:712
  (129 shorter events, 26.7 us)
Async XLA Ops:
  0.6 30.4 %copy-start.2 = (f32[2,3,512]{2,0,1:T(2,128)S(1)}, f32[2,3,512]{2,0,1:T(2,128)}, u32[]{:S(2)}) copy-start(f32[2,3,512]{2,0,1:T(2,128)} %param.16) | copy-start | bytes 36868
  2.0 6.7 %collective-permute-start = (bf16[224,512]{1,0:T(8,128)(2,1)S(1)}, bf16[224,512]{1,0:T(8,128)(2,1)S(1)}, u32[]{:S(2)}, u32[]{:S(2)}) collective-permute-start(bf16[224,512]{1,0:T(8,128)(2,1)S(1)} %get-tuple-element.133), channel_id=1, source_target_pairs={{0,1},{1,0},{2,3},{3,2},{4,5},{5,4},{6,7},{7,6},{8,9},{9,8},{10,11... | collective-permute-start | bytes 688136 | tf_op jit(solution)/shard_map/ppermute | solution.py:764
  2.5 6.2 %collective-permute-start.1 = (bf16[224,512]{1,0:T(8,128)(2,1)S(1)}, bf16[224,512]{1,0:T(8,128)(2,1)S(1)}, u32[]{:S(2)}, u32[]{:S(2)}) collective-permute-start(bf16[224,512]{1,0:T(8,128)(2,1)S(1)} %get-tuple-element.135), channel_id=1, source_target_pairs={{2,1},{1,2},{6,5},{5,6},{10,9},{9,10},{14,13},{13,14},{18,17},{17,... | collective-permute-start | bytes 688136 | tf_op jit(solution)/shard_map/ppermute | solution.py:773
  14.1 17.0 %all-to-all-start = ((f32[32,8,128]{2,1,0:T(8,128)}), f32[32,8,128]{2,1,0:T(8,128)S(1)}, u32[]{:S(2)}, u32[]{:S(2)}) async-start(f32[32,8,128]{2,1,0:T(8,128)} %get-tuple-element.141), calls=%async_computation | async-start | bytes 262144 | tf_op jit(solution)/shard_map/all_to_all | solution.py:756
  22.8 13.1 %collective-permute-start.2 = (bf16[384,512]{1,0:T(8,128)(2,1)}, bf16[384,512]{1,0:T(8,128)(2,1)}, u32[]{:S(2)}, u32[]{:S(2)}) collective-permute-start(bf16[384,512]{1,0:T(8,128)(2,1)} %get-tuple-element.218.rest_4_), channel_id=1, source_target_pairs={{0,1},{1,0},{2,3},{3,2},{4,5},{5,4},{6,7},{7,6},{8,9},{9,8},{10,11... | collective-permute-start | bytes 1179656 | tf_op jit(solution)/shard_map/ppermute | solution.py:764
  23.1 12.8 %collective-permute-start.3 = (bf16[384,512]{1,0:T(8,128)(2,1)}, bf16[384,512]{1,0:T(8,128)(2,1)}, u32[]{:S(2)}, u32[]{:S(2)}) collective-permute-start(bf16[384,512]{1,0:T(8,128)(2,1)} %get-tuple-element.218.rest_4_), channel_id=1, source_target_pairs={{0,2},{1,3},{2,0},{3,1},{4,6},{5,7},{6,4},{7,5},{8,10},{9,11},{10,... | collective-permute-start | bytes 1179656 | tf_op jit(solution)/shard_map/ppermute | solution.py:764
  36.6 12.4 %all-to-all-start.1 = ((f32[32,8,128]{2,1,0:T(8,128)}), f32[32,8,128]{2,1,0:T(8,128)S(1)}, u32[]{:S(2)}, u32[]{:S(2)}) async-start(f32[32,8,128]{2,1,0:T(8,128)} %copy-done.9), calls=%async_computation.1 | async-start | bytes 262144 | tf_op jit(solution)/shard_map/all_to_all | solution.py:756
  40.8 12.2 %collective-permute-start.4 = (bf16[160,128]{1,0:T(8,128)(2,1)}, bf16[160,128]{1,0:T(8,128)(2,1)S(1)}, u32[]{:S(2)}, u32[]{:S(2)}) collective-permute-start(bf16[160,128]{1,0:T(8,128)(2,1)} %get-tuple-element.151), channel_id=1, source_target_pairs={{0,1},{1,0},{2,3},{3,2},{4,5},{5,4},{6,7},{7,6},{8,9},{9,8},{10,11... | collective-permute-start | bytes 122888 | tf_op jit(solution)/shard_map/ppermute | solution.py:760
  41.1 12.2 %collective-permute-start.5 = (bf16[160,128]{1,0:T(8,128)(2,1)}, bf16[160,128]{1,0:T(8,128)(2,1)S(1)}, u32[]{:S(2)}, u32[]{:S(2)}) collective-permute-start(bf16[160,128]{1,0:T(8,128)(2,1)} %get-tuple-element.152), channel_id=1, source_target_pairs={{0,2},{1,3},{2,0},{3,1},{4,6},{5,7},{6,4},{7,5},{8,10},{9,11},{10,... | collective-permute-start | bytes 122888 | tf_op jit(solution)/shard_map/ppermute | solution.py:760
  42.8 10.8 %collective-permute-start.6 = (bf16[160,128]{1,0:T(8,128)(2,1)}, bf16[160,128]{1,0:T(8,128)(2,1)S(1)}, u32[]{:S(2)}, u32[]{:S(2)}) collective-permute-start(bf16[160,128]{1,0:T(8,128)(2,1)} %get-tuple-element.153), channel_id=1, source_target_pairs={{0,3},{1,2},{2,1},{3,0},{4,7},{5,6},{6,5},{7,4},{8,11},{9,10},{10,... | collective-permute-start | bytes 122888 | tf_op jit(solution)/shard_map/ppermute | solution.py:760
  42.8 11.3 %collective-permute-start.7 = (bf16[384,512]{1,0:T(8,128)(2,1)}, bf16[384,512]{1,0:T(8,128)(2,1)S(1)}, u32[]{:S(2)}, u32[]{:S(2)}) collective-permute-start(bf16[384,512]{1,0:T(8,128)(2,1)} %get-tuple-element.203.rest_4_), channel_id=1, source_target_pairs={{0,1},{1,0},{2,3},{3,2},{4,5},{5,4},{6,7},{7,6},{8,9},{9,8},{10,11... | collective-permute-start | bytes 1179656 | tf_op jit(solution)/shard_map/ppermute | solution.py:764
  43.2 12.7 %collective-permute-start.8 = (bf16[384,512]{1,0:T(8,128)(2,1)}, bf16[384,512]{1,0:T(8,128)(2,1)}, u32[]{:S(2)}, u32[]{:S(2)}) collective-permute-start(bf16[384,512]{1,0:T(8,128)(2,1)} %get-tuple-element.203.rest_4_), channel_id=1, source_target_pairs={{0,2},{1,3},{2,0},{3,1},{4,6},{5,7},{6,4},{7,5},{8,10},{9,11},{10,... | collective-permute-start | bytes 1179656 | tf_op jit(solution)/shard_map/ppermute | solution.py:764
  53.0 19.3 %copy-start.10 = (f32[8,128]{1,0:T(8,128)}, f32[8,128]{1,0:T(8,128)S(1)}, u32[]{:S(2)}) copy-start(f32[8,128]{1,0:T(8,128)S(1)} %get-tuple-element.170.moments_below_ref.moments_ref) | copy-start | bytes 12292
  53.0 16.3 %copy-start.26 = (bf16[160,128]{1,0:T(8,128)(2,1)}, bf16[160,128]{1,0:T(8,128)(2,1)S(1)}, u32[]{:S(2)}) copy-start(bf16[160,128]{1,0:T(8,128)(2,1)S(1)} %collective-permute-done.4.rest_1_) | copy-start | bytes 122884
  53.0 19.3 %collective-permute-start.9 = (bf16[384,512]{1,0:T(8,128)(2,1)}, bf16[384,512]{1,0:T(8,128)(2,1)S(1)}, u32[]{:S(2)}, u32[]{:S(2)}) collective-permute-start(bf16[384,512]{1,0:T(8,128)(2,1)} %collective-permute-done.3.rest_6_), channel_id=1, source_target_pairs={{0,1},{1,0},{2,3},{3,2},{4,5},{5,4},{6,7},{7,6},{8,9},{9,8},{10,11... | collective-permute-start | bytes 1179656 | tf_op jit(solution)/shard_map/ppermute | solution.py:764
  53.3 16.0 %copy-start.27 = (bf16[160,128]{1,0:T(8,128)(2,1)}, bf16[160,128]{1,0:T(8,128)(2,1)S(1)}, u32[]{:S(2)}) copy-start(bf16[160,128]{1,0:T(8,128)(2,1)S(1)} %collective-permute-done.5.rest_2_) | copy-start | bytes 122884
  53.3 19.0 %collective-permute-start.10 = (bf16[384,512]{1,0:T(8,128)(2,1)}, bf16[384,512]{1,0:T(8,128)(2,1)S(1)}, u32[]{:S(2)}, u32[]{:S(2)}) collective-permute-start(bf16[384,512]{1,0:T(8,128)(2,1)} %get-tuple-element.183.rest_4_), channel_id=1, source_target_pairs={{0,1},{1,0},{2,3},{3,2},{4,5},{5,4},{6,7},{7,6},{8,9},{9,8},{10,11... | collective-permute-start | bytes 1179656 | tf_op jit(solution)/shard_map/ppermute | solution.py:764
  53.6 15.7 %copy-start.28 = (bf16[160,128]{1,0:T(8,128)(2,1)}, bf16[160,128]{1,0:T(8,128)(2,1)S(1)}, u32[]{:S(2)}) copy-start(bf16[160,128]{1,0:T(8,128)(2,1)S(1)} %collective-permute-done.6.rest_3_) | copy-start | bytes 122884
  53.6 18.7 %collective-permute-start.11 = (bf16[384,512]{1,0:T(8,128)(2,1)}, bf16[384,512]{1,0:T(8,128)(2,1)S(1)}, u32[]{:S(2)}, u32[]{:S(2)}) collective-permute-start(bf16[384,512]{1,0:T(8,128)(2,1)} %get-tuple-element.183.rest_4_), channel_id=1, source_target_pairs={{0,2},{1,3},{2,0},{3,1},{4,6},{5,7},{6,4},{7,5},{8,10},{9,11},{10,... | collective-permute-start | bytes 1179656 | tf_op jit(solution)/shard_map/ppermute | solution.py:764
  69.3 35.8 %copy-start.14 = (f32[8,128]{1,0:T(8,128)S(1)}, f32[8,128]{1,0:T(8,128)}, u32[]{:S(2)}) copy-start(f32[8,128]{1,0:T(8,128)} %copy-done.13) | copy-start | bytes 12292
  72.3 32.8 %copy-start.12 = (f32[8,128]{1,0:T(8,128)S(1)}, f32[8,128]{1,0:T(8,128)}, u32[]{:S(2)}) copy-start(f32[8,128]{1,0:T(8,128)} %copy-done.10) | copy-start | bytes 12292
  73.1 10.8 %all-to-all-start.3 = ((f32[32,8,128]{2,1,0:T(8,128)}), f32[32,8,128]{2,1,0:T(8,128)S(1)}, u32[]{:S(2)}, u32[]{:S(2)}) async-start(f32[32,8,128]{2,1,0:T(8,128)} %get-tuple-element.164), calls=%async_computation.3 | async-start | bytes 262144 | tf_op jit(solution)/shard_map/all_to_all | solution.py:756
  75.9 16.6 %collective-permute-start.12 = (bf16[384,512]{1,0:T(8,128)(2,1)}, bf16[384,512]{1,0:T(8,128)(2,1)}, u32[]{:S(2)}, u32[]{:S(2)}) collective-permute-start(bf16[384,512]{1,0:T(8,128)(2,1)} %collective-permute-done.8.rest_6_), channel_id=1, source_target_pairs={{0,1},{1,0},{2,3},{3,2},{4,5},{5,4},{6,7},{7,6},{8,9},{9,8},{10,11... | collective-permute-start | bytes 1179656 | tf_op jit(solution)/shard_map/ppermute | solution.py:764
  75.9 16.5 %collective-permute-start.14 = (bf16[864,128]{1,0:T(8,128)(2,1)}, bf16[864,128]{1,0:T(8,128)(2,1)S(1)}, u32[]{:S(2)}, u32[]{:S(2)}) collective-permute-start(bf16[864,128]{1,0:T(8,128)(2,1)} %get-tuple-element.175), channel_id=1, source_target_pairs={{0,1},{1,0},{2,3},{3,2},{4,5},{5,4},{6,7},{7,6},{8,9},{9,8},{10,11... | collective-permute-start | bytes 663560 | tf_op jit(solution)/shard_map/ppermute | solution.py:760
  76.4 16.0 %collective-permute-start.15 = (bf16[864,128]{1,0:T(8,128)(2,1)}, bf16[864,128]{1,0:T(8,128)(2,1)}, u32[]{:S(2)}, u32[]{:S(2)}) collective-permute-start(bf16[864,128]{1,0:T(8,128)(2,1)} %get-tuple-element.176), channel_id=1, source_target_pairs={{0,2},{1,3},{2,0},{3,1},{4,6},{5,7},{6,4},{7,5},{8,10},{9,11},{10,... | collective-permute-start | bytes 663560 | tf_op jit(solution)/shard_map/ppermute | solution.py:760
  77.9 14.5 %collective-permute-start.16 = (bf16[864,128]{1,0:T(8,128)(2,1)}, bf16[864,128]{1,0:T(8,128)(2,1)}, u32[]{:S(2)}, u32[]{:S(2)}) collective-permute-start(bf16[864,128]{1,0:T(8,128)(2,1)} %get-tuple-element.177), channel_id=1, source_target_pairs={{0,3},{1,2},{2,1},{3,0},{4,7},{5,6},{6,5},{7,4},{8,11},{9,10},{10,... | collective-permute-start | bytes 663560 | tf_op jit(solution)/shard_map/ppermute | solution.py:760
  77.9 14.5 %collective-permute-start.13 = (bf16[384,512]{1,0:T(8,128)(2,1)}, bf16[384,512]{1,0:T(8,128)(2,1)}, u32[]{:S(2)}, u32[]{:S(2)}) collective-permute-start(bf16[384,512]{1,0:T(8,128)(2,1)} %copy-done.32), channel_id=1, source_target_pairs={{0,1},{1,0},{2,3},{3,2},{4,5},{5,4},{6,7},{7,6},{8,9},{9,8},{10,11... | collective-permute-start | bytes 1179656 | tf_op jit(solution)/shard_map/ppermute | solution.py:764
  92.5 10.8 %all-to-all-start.4 = ((f32[32,8,128]{2,1,0:T(8,128)}), f32[32,8,128]{2,1,0:T(8,128)S(1)}, u32[]{:S(2)}, u32[]{:S(2)}) async-start(f32[32,8,128]{2,1,0:T(8,128)} %get-tuple-element.178), calls=%async_computation.4 | async-start | bytes 262144 | tf_op jit(solution)/shard_map/all_to_all | solution.py:756
  95.1 17.6 %collective-permute-start.17 = (bf16[768,128]{1,0:T(8,128)(2,1)}, bf16[768,128]{1,0:T(8,128)(2,1)}, u32[]{:S(2)}, u32[]{:S(2)}) collective-permute-start(bf16[768,128]{1,0:T(8,128)(2,1)} %get-tuple-element.195), channel_id=1, source_target_pairs={{0,1},{1,0},{2,3},{3,2},{4,5},{5,4},{6,7},{7,6},{8,9},{9,8},{10,11... | collective-permute-start | bytes 589832 | tf_op jit(solution)/shard_map/ppermute | solution.py:760
  95.2 17.5 %collective-permute-start.18 = (bf16[768,128]{1,0:T(8,128)(2,1)}, bf16[768,128]{1,0:T(8,128)(2,1)}, u32[]{:S(2)}, u32[]{:S(2)}) collective-permute-start(bf16[768,128]{1,0:T(8,128)(2,1)} %get-tuple-element.196), channel_id=1, source_target_pairs={{0,2},{1,3},{2,0},{3,1},{4,6},{5,7},{6,4},{7,5},{8,10},{9,11},{10,... | collective-permute-start | bytes 589832 | tf_op jit(solution)/shard_map/ppermute | solution.py:760
  96.9 15.8 %collective-permute-start.19 = (bf16[768,128]{1,0:T(8,128)(2,1)}, bf16[768,128]{1,0:T(8,128)(2,1)}, u32[]{:S(2)}, u32[]{:S(2)}) collective-permute-start(bf16[768,128]{1,0:T(8,128)(2,1)} %get-tuple-element.197), channel_id=1, source_target_pairs={{0,3},{1,2},{2,1},{3,0},{4,7},{5,6},{6,5},{7,4},{8,11},{9,10},{10,... | collective-permute-start | bytes 589832 | tf_op jit(solution)/shard_map/ppermute | solution.py:760
  103.3 22.4 %collective-permute-start.20 = (bf16[4,576,128]{2,1,0:T(8,128)(2,1)}, bf16[4,576,128]{2,1,0:T(8,128)(2,1)}, u32[]{:S(2)}, u32[]{:S(2)}) collective-permute-start(bf16[4,576,128]{2,1,0:T(8,128)(2,1)} %get-tuple-element.207), channel_id=1, source_target_pairs={{0,4},{4,0},{8,12},{12,8},{16,20},{20,16},{24,28},{28,24},{1,5},{5... | collective-permute-start | bytes 1769480 | tf_op jit(solution)/shard_map/ppermute | solution.py:873
  112.7 57.4 %copy-start.8 = (bf16[448,512]{1,0:T(8,128)(2,1)S(1)}, bf16[448,512]{1,0:T(8,128)(2,1)}, u32[]{:S(2)}) copy-start(bf16[448,512]{1,0:T(8,128)(2,1)} %copy-done.7) | copy-start | bytes 1376260
  112.7 13.0 %all-to-all-start.5 = ((f32[32,8,128]{2,1,0:T(8,128)}), f32[32,8,128]{2,1,0:T(8,128)S(1)}, u32[]{:S(2)}, u32[]{:S(2)}) async-start(f32[32,8,128]{2,1,0:T(8,128)} %get-tuple-element.198), calls=%async_computation.5 | async-start | bytes 262144 | tf_op jit(solution)/shard_map/all_to_all | solution.py:756
  117.7 12.8 %collective-permute-start.21 = (bf16[768,128]{1,0:T(8,128)(2,1)}, bf16[768,128]{1,0:T(8,128)(2,1)S(1)}, u32[]{:S(2)}, u32[]{:S(2)}) collective-permute-start(bf16[768,128]{1,0:T(8,128)(2,1)} %get-tuple-element.215), channel_id=1, source_target_pairs={{0,1},{1,0},{2,3},{3,2},{4,5},{5,4},{6,7},{7,6},{8,9},{9,8},{10,11... | collective-permute-start | bytes 589832 | tf_op jit(solution)/shard_map/ppermute | solution.py:760
  117.8 12.7 %collective-permute-start.22 = (bf16[768,128]{1,0:T(8,128)(2,1)}, bf16[768,128]{1,0:T(8,128)(2,1)S(1)}, u32[]{:S(2)}, u32[]{:S(2)}) collective-permute-start(bf16[768,128]{1,0:T(8,128)(2,1)} %get-tuple-element.216), channel_id=1, source_target_pairs={{0,2},{1,3},{2,0},{3,1},{4,6},{5,7},{6,4},{7,5},{8,10},{9,11},{10,... | collective-permute-start | bytes 589832 | tf_op jit(solution)/shard_map/ppermute | solution.py:760
  119.5 11.0 %collective-permute-start.23 = (bf16[768,128]{1,0:T(8,128)(2,1)}, bf16[768,128]{1,0:T(8,128)(2,1)S(1)}, u32[]{:S(2)}, u32[]{:S(2)}) collective-permute-start(bf16[768,128]{1,0:T(8,128)(2,1)} %get-tuple-element.217), channel_id=1, source_target_pairs={{0,3},{1,2},{2,1},{3,0},{4,7},{5,6},{6,5},{7,4},{8,11},{9,10},{10,... | collective-permute-start | bytes 589832 | tf_op jit(solution)/shard_map/ppermute | solution.py:760
  125.7 16.4 %collective-permute-start.26 = (bf16[4,576,128]{2,1,0:T(8,128)(2,1)}, bf16[4,576,128]{2,1,0:T(8,128)(2,1)S(1)}, u32[]{:S(2)}, u32[]{:S(2)}) collective-permute-start(bf16[4,576,128]{2,1,0:T(8,128)(2,1)} %get-tuple-element.228), channel_id=1, source_target_pairs={{0,4},{4,0},{8,12},{12,8},{16,20},{20,16},{24,28},{28,24},{1,5},{5... | collective-permute-start | bytes 1769480 | tf_op jit(solution)/shard_map/ppermute | solution.py:873
  128.9 9.4 %collective-permute-start.24 = (bf16[2,576,128]{2,1,0:T(8,128)(2,1)}, bf16[2,576,128]{2,1,0:T(8,128)(2,1)S(1)}, u32[]{:S(2)}, u32[]{:S(2)}) collective-permute-start(bf16[2,576,128]{2,1,0:T(8,128)(2,1)} %get-tuple-element.225), channel_id=1, source_target_pairs={{0,8},{4,12},{8,0},{12,4},{16,24},{20,28},{24,16},{28,20},{1,9},{5... | collective-permute-start | bytes 884744 | tf_op jit(solution)/shard_map/ppermute | solution.py:873
  136.9 60.7 %copy-start.15 = (f32[2,3,512]{2,0,1:T(2,128)S(1)}, f32[2,3,512]{2,0,1:T(2,128)}, u32[]{:S(2)}) copy-start(f32[2,3,512]{2,0,1:T(2,128)} %param.26) | copy-start | bytes 36868
  136.9 60.7 %copy-start.16 = (f32[2,3,512]{2,0,1:T(2,128)S(1)}, f32[2,3,512]{2,0,1:T(2,128)}, u32[]{:S(2)}) copy-start(f32[2,3,512]{2,0,1:T(2,128)} %param.27) | copy-start | bytes 36868
  138.3 18.0 %collective-permute-start.25 = (bf16[4,576,128]{2,1,0:T(8,128)(2,1)}, bf16[4,576,128]{2,1,0:T(8,128)(2,1)S(1)}, u32[]{:S(2)}, u32[]{:S(2)}) collective-permute-start(bf16[4,576,128]{2,1,0:T(8,128)(2,1)} %get-tuple-element.226), channel_id=1, source_target_pairs={{0,4},{4,0},{8,12},{12,8},{16,20},{20,16},{24,28},{28,24},{1,5},{5... | collective-permute-start | bytes 1769480 | tf_op jit(solution)/shard_map/ppermute | solution.py:873
  145.2 11.0 %collective-permute-start.27 = (bf16[2,576,128]{2,1,0:T(8,128)(2,1)}, bf16[2,576,128]{2,1,0:T(8,128)(2,1)S(1)}, u32[]{:S(2)}, u32[]{:S(2)}) collective-permute-start(bf16[2,576,128]{2,1,0:T(8,128)(2,1)} %get-tuple-element.229), channel_id=1, source_target_pairs={{0,8},{4,12},{8,0},{12,4},{16,24},{20,28},{24,16},{28,20},{1,9},{5... | collective-permute-start | bytes 884744 | tf_op jit(solution)/shard_map/ppermute | solution.py:873
  148.1 7.8 %collective-permute-start.28 = (bf16[1,576,128]{2,1,0:T(8,128)(2,1)}, bf16[1,576,128]{2,1,0:T(8,128)(2,1)S(1)}, u32[]{:S(2)}, u32[]{:S(2)}) collective-permute-start(bf16[1,576,128]{2,1,0:T(8,128)(2,1)} %get-tuple-element.232), channel_id=1, source_target_pairs={{0,16},{4,20},{8,24},{12,28},{16,0},{20,4},{24,8},{28,12},{1,17},{... | collective-permute-start | bytes 442376 | tf_op jit(solution)/shard_map/ppermute | solution.py:873
  155.9 28.1 %copy-start.24 = (bf16[1,576,128]{2,1,0:T(8,128)(2,1)}, bf16[1,576,128]{2,1,0:T(8,128)(2,1)S(1)}, u32[]{:S(2)}) copy-start(bf16[1,576,128]{2,1,0:T(8,128)(2,1)S(1)} %collective-permute-done.28.last2_hbm) | copy-start | bytes 442372
  159.5 24.5 %all-to-all-start.6 = ((bf16[4,576,128]{2,1,0:T(8,128)(2,1)}), bf16[4,576,128]{2,1,0:T(8,128)(2,1)S(1)}, u32[]{:S(2)}, u32[]{:S(2)}) async-start(bf16[4,576,128]{2,1,0:T(8,128)(2,1)} %add.3), calls=%async_computation.6 | async-start | bytes 1179648 | tf_op jit(solution)/shard_map/all_to_all | solution.py:942
  167.1 16.8 %collective-permute-start.29 = (bf16[1,576,128]{2,1,0:T(8,128)(2,1)}, bf16[1,576,128]{2,1,0:T(8,128)(2,1)S(1)}, u32[]{:S(2)}, u32[]{:S(2)}) collective-permute-start(bf16[1,576,128]{2,1,0:T(8,128)(2,1)} %get-tuple-element.237), channel_id=1, source_target_pairs={{0,16},{4,20},{8,24},{12,28},{16,0},{20,4},{24,8},{28,12},{1,17},{... | collective-permute-start | bytes 442376 | tf_op jit(solution)/shard_map/ppermute | solution.py:873
  186.6 11.0 %all-to-all-start.7 = ((f32[32,1,128]{2,1,0:T(1,128)}), f32[32,1,128]{2,1,0:T(1,128)S(1)}, u32[]{:S(2)}, u32[]{:S(2)}) async-start(f32[32,1,128]{2,1,0:T(1,128)} %get-tuple-element.243), calls=%async_computation.7 | async-start | bytes 32768 | tf_op jit(solution)/shard_map/all_to_all | solution.py:960
  (25 other events, 106.5 us)

commit v5 on v4

--- a/solution.py
+++ b/solution.py
@@ -534,7 +534,8 @@
     pixels = sz.height * w
     given, rest = rest[:bands], rest[bands:]
     acts, rest = rest[:bands], rest[bands:]
-    keep_hbm, send_hbm, grad_ref, normed_ref, act_ref, x9_ref, keep_ref, send_ref, term_ref, sems = rest
+    keep_hbm, send_hbm, grad_ref, normed_ref, act_ref, x9_ref, term_ref, *spaces, sems = rest
+    keep_ref, send_ref = spaces or (keep_hbm, send_hbm)
     copies = Copies(sems)
     inputs = []
     for n in range(bands):
@@ -593,7 +594,8 @@
                 keep_ref[position, place, :] = part
             else:
                 send_ref[position - sz.maps // 2, place, :] = part.astype(BF16)
-    wait(copies.start(keep_ref, keep_hbm), copies.start(send_ref, send_hbm))
+    if spaces:
+        wait(copies.start(keep_ref, keep_hbm), copies.start(send_ref, send_hbm))
 
 
 def halving_order(maps):
@@ -601,31 +603,22 @@
     return [sum(((place >> (bits - 1 - k)) & 1) << k for k in range(bits)) for place in range(maps)]
 
 
-def kernel_add(keep_hbm, received_hbm, out_ref, keep_ref, received_ref, sems):
-    copies = Copies(sems)
-    loads = [
-        (copies.start(keep_hbm.at[k], keep_ref.at[k]), copies.start(received_hbm.at[k], received_ref.at[k]))
-        for k in range(keep_ref.shape[0])
-    ]
+def kernel_add(keep_hbm, received_ref, out_ref, keep_ref, sems):
+    copies = Copies(sems)
+    loads = [copies.start(keep_hbm.at[k], keep_ref.at[k]) for k in range(keep_ref.shape[0])]
     for k, load in enumerate(loads):
-        wait(*load)
+        wait(load)
         out_ref[k] = (keep_ref[k] + received_ref[k].astype(F32)).astype(BF16)
 
 
-def kernel_halve(keep_hbm, received_hbm, next_keep_hbm, next_send_hbm, keep_ref, received_ref, send_ref, sems):
+def kernel_halve(keep_hbm, received_ref, next_keep_hbm, next_send_hbm, keep_ref, send_ref, sems):
     half = next_keep_hbm.shape[0]
     copies = Copies(sems)
-    loads = [
-        [
-            copies.start(source.at[part], target.at[part])
-            for source, target in ((keep_hbm, keep_ref), (received_hbm, received_ref))
-        ]
-        for part in (pl.ds(half, half), pl.ds(0, half))
-    ]
-    wait(*loads[0])
+    loads = [copies.start(keep_hbm.at[part], keep_ref.at[part]) for part in (pl.ds(half, half), pl.ds(0, half))]
+    wait(loads[0])
     send_ref[...] = (keep_ref[half:] + received_ref[half:].astype(F32)).astype(BF16)
     first = copies.start(send_ref, next_send_hbm)
-    wait(*loads[1])
+    wait(loads[1])
     keep_ref[:half] += received_ref[:half].astype(F32)
     wait(first, copies.start(keep_ref.at[pl.ds(0, half)], next_keep_hbm))
 
@@ -861,12 +854,13 @@
             pltpu.VMEM((sz.height * w, 9 * q), BF16),
         ]
         outs = [part_shape(n_maps // 2, dtype) for dtype in (F32, BF16)]
-        scratch += [part_space(n_maps // 2, dtype) for dtype in (F32, BF16)]
         scratch.append(pltpu.VMEM((c, 9 * q), F32))
+        if layer > 0:
+            scratch += [part_space(n_maps // 2, dtype) for dtype in (F32, BF16)]
         return call(
             functools.partial(kernel_weight_grad, sz, layer, first), "weight_grad", outs,
             consts + [gathered, moments[layer], norms] + given + acts[layer], scratch, conv_flops(sz.rows),
-            hbm_ins=range(5, 5 + 2 * bands), hbm_outs=(0, 1), sems=3 * bands + 2,
+            hbm_ins=range(5, 5 + 2 * bands), hbm_outs=() if layer == 0 else (0, 1), sems=3 * bands + 2,
         )
 
     def step_of(send, k):
@@ -876,8 +870,8 @@
         size = keep.shape[0] // 2
         return call(
             kernel_halve, "halve", [part_shape(size, dtype) for dtype in (F32, BF16)], [keep, received],
-            [part_space(2 * size, F32), part_space(2 * size, BF16), part_space(size, BF16)],
-            hbm_ins=(0, 1), hbm_outs=(0, 1), sems=6,
+            [part_space(2 * size, F32), part_space(size, BF16)],
+            hbm_ins=(0,), hbm_outs=(0, 1), sems=4,
         )
 
     def halve(keep, received, k):
@@ -936,7 +930,7 @@
     half_maps = n_maps // 2
     (partial,) = call(
         kernel_add, "add", [part_shape(half_maps, BF16)], [keep0, arrived0],
-        [part_space(half_maps, dtype) for dtype in (F32, BF16)], hbm_ins=(0, 1), sems=2 * half_maps,
+        [part_space(half_maps, F32)], hbm_ins=(0,), sems=half_maps,
     )
     alike = [[m for m in range(n_maps) if m & 1 == bit] for bit in (0, 1)]
     received = lax.all_to_all(partial, "maps", 0, 0, tiled=True, axis_index_groups=alike)

time: 202 us -> 200 us (0.990)
    unnamed x72 -> x62, local copies, waits for them, and re-layouts: 10.8 us -> 9.99 us
  transfers between devices with their start and end apart: 37 -> 37, of which waited for: 12 -> 13; matrix products, arithmetic and copies ran while one was open for 4% -> 4% of each run, Pallas kernels for 26% -> 26%
where the time goes in v5:
time: 200 us; the launch traced here: 199 us
  Pallas kernels  64.9 us (32%)
  starting transfers between devices  57.2 us (29%)
  waiting for transfers between devices  43.3 us (22%)
  local copies, waits for them, and re-layouts  16.5 us (8%)
  blocking collectives  13.3 us (7%)
  between operations  2.03 us (1%)
    pallas_call x20, Pallas kernels, call(): pl.pallas_call(kernel, out_shape=tuple((space(out.shape, out.dtype) for s...  64.9 us
    all_to_all x5, starting transfers between devices, spread(): return lax.all_to_all(stats, AXES, 0, 0, tiled=True)  23.2 us
    ppermute x7, waiting for transfers between devices, step_of(): return lax.ppermute(send, 'maps', [(m, m ^ 1 << k) for m in range(n_maps)])  20.7 us
    all_to_all x5, waiting for transfers between devices, spread(): return lax.all_to_all(stats, AXES, 0, 0, tiled=True)  14 us
    all_to_all x1, blocking collectives, spread(): return lax.all_to_all(stats, AXES, 0, 0, tiled=True)  13.3 us
    ppermute x7, starting transfers between devices, step_of(): return lax.ppermute(send, 'maps', [(m, m ^ 1 << k) for m in range(n_maps)])  10.5 us
    unnamed x62, local copies, waits for them, and re-layouts  9.99 us
    ppermute x12, starting transfers between devices, trade(): lax.ppermute(shares[n], 'rows', [(i, i ^ n) for i in range(bands)])  7.88 us
  transfers between devices with their start and end apart: 37, of which 13 were waited for; matrix products, arithmetic and copies ran while one was open for 4% of the time, Pallas kernels for 26%

profile of v5, /device:TPU:0, one launch (start us, length us, event | category | flops | bytes accessed | tf_op | source)
XLA Modules:
  0.0 198.9 jit_solution(16941728059960458836)
XLA Ops:
  0.7 1.3 edges.1
  7.6 1.1 slice_bitcast_fusion.5.head_ref
  8.7 5.3 %first.1 = (f32[32,8,128]{2,1,0:T(8,128)}, f32[704,512]{1,0:T(8,128)S(1)}, bf16[384,512]{1,0:T(8,128)(2,1)}) custom-call(s32[8,128]{1,0:T(8,128)S(1)} %get-tuple-element.131.limits_ref, bf16[224,512]{1,0:T(8,128)(2,1)S(1)} %collective-permute-done.near_ref.near_hbm, bf16[384,512]{1,0:T(8,128)(2,1)S(1)} %get-tuple-element.134.x_ref, ...), custom_call_target="tpu_custom_call" | custom-call | flops 3321888768 | tf_op jit(solution)/shard_map/first/pallas_call | solution.py:705
  14.1 8.7 %all-to-all-start = ((f32[32,8,128]{2,1,0:T(8,128)}), f32[32,8,128]{2,1,0:T(8,128)S(1)}, u32[]{:S(2)}, u32[]{:S(2)}) async-start(f32[32,8,128]{2,1,0:T(8,128)} %get-tuple-element.141), calls=%async_computation | async-start | bytes 262144 | tf_op jit(solution)/shard_map/all_to_all | solution.py:749
  23.1 1.7 collective-permute-start.3
  24.8 1.1 slice_bitcast_fusion.4.head_ref
  25.9 5.2 %all-to-all-done.gathered_ref = f32[32,8,128]{2,1,0:T(8,128)S(1)} async-done(((f32[32,8,128]{2,1,0:T(8,128)}), f32[32,8,128]{2,1,0:T(8,128)S(1)}, u32[]{:S(2)}, u32[]{:S(2)}) %all-to-all-start) | async-done | bytes 131104 | tf_op jit(solution)/shard_map/all_to_all | solution.py:749
  31.0 4.3 %forward.2 = (f32[32,8,128]{2,1,0:T(8,128)S(1)}, f32[640,512]{1,0:T(8,128)S(1)}, f32[8,128]{1,0:T(8,128)S(1)}, bf16[384,512]{1,0:T(8,128)(2,1)}, f32[448,512]{1,0:T(8,128)}) custom-call(s32[8,128]{1,0:T(8,128)S(1)} %get-tuple-element.131.limits_ref, f32[32,8,128]{2,1,0:T(8,128)S(1)} %get-tuple-element.132.member_ref, ...), custom_call_target="tpu_custom_call" | custom-call | flops 3019898880 | tf_op jit(solution)/shard_map/forward/pallas_call | solution.py:705
  36.6 4.2 %all-to-all-start.1 = ((f32[32,8,128]{2,1,0:T(8,128)}), f32[32,8,128]{2,1,0:T(8,128)S(1)}, u32[]{:S(2)}, u32[]{:S(2)}) async-start(f32[32,8,128]{2,1,0:T(8,128)} %copy-done.10), calls=%async_computation.1 | async-start | bytes 262144 | tf_op jit(solution)/shard_map/all_to_all | solution.py:749
  41.1 1.7 collective-permute-start.5
  43.2 1.7 collective-permute-start.8
  44.9 1.1 slice_bitcast_fusion.3.head_ref
  46.0 3.0 %all-to-all-done.1.gathered_ref = f32[32,8,128]{2,1,0:T(8,128)S(1)} async-done(((f32[32,8,128]{2,1,0:T(8,128)}), f32[32,8,128]{2,1,0:T(8,128)S(1)}, u32[]{:S(2)}, u32[]{:S(2)}) %all-to-all-start.1) | async-done | bytes 131104 | tf_op jit(solution)/shard_map/all_to_all | solution.py:749
  49.0 4.0 %forward.3 = (f32[32,8,128]{2,1,0:T(8,128)S(1)}, f32[576,512]{1,0:T(8,128)S(1)}, f32[8,128]{1,0:T(8,128)S(1)}, bf16[384,512]{1,0:T(8,128)(2,1)}, f32[512,512]{1,0:T(8,128)}) custom-call(s32[8,128]{1,0:T(8,128)S(1)} %get-tuple-element.131.limits_ref, f32[32,8,128]{2,1,0:T(8,128)S(1)} %get-tuple-element.132.member_ref, ...), custom_call_target="tpu_custom_call" | custom-call | flops 2717908992 | tf_op jit(solution)/shard_map/forward/pallas_call | solution.py:705
  54.1 1.9 collective-permute-done.8.rest_6_
  56.0 13.3 %all_to_all.40.gathered_ref = f32[32,8,128]{2,1,0:T(8,128)S(1)} all-to-all(f32[32,8,128]{2,1,0:T(8,128)S(1)} %get-tuple-element.155), channel_id=1, replica_groups=mesh['maps'=8,'rows'=4] {'maps','rows'}, dimensions={0} | all-to-all | bytes 262144 | tf_op jit(solution)/shard_map/all_to_all | solution.py:749
  69.3 2.9 %pool.1 = (f32[32,8,128]{2,1,0:T(8,128)}, f32[576,512]{1,0:T(8,128)S(1)}, bf16[576,512]{1,0:T(8,128)(2,1)S(1)}, f32[8,128]{1,0:T(8,128)S(1)}, bf16[864,128]{1,0:...) custom-call(s32[8,128]{1,0:T(8,128)S(1)} %get-tuple-element.131.limits_ref, ...), custom_call_target="tpu_custom_call" | custom-call | flops 603979776 | tf_op jit(solution)/shard_map/pool/pallas_call | solution.py:705
  73.1 2.7 %all-to-all-start.3 = ((f32[32,8,128]{2,1,0:T(8,128)}), f32[32,8,128]{2,1,0:T(8,128)S(1)}, u32[]{:S(2)}, u32[]{:S(2)}) async-start(f32[32,8,128]{2,1,0:T(8,128)} %get-tuple-element.164), calls=%async_computation.3 | async-start | bytes 262144 | tf_op jit(solution)/shard_map/all_to_all | solution.py:749
  76.4 1.5 collective-permute-start.15
  78.6 1.1 slice_bitcast_fusion.2.head_ref
  79.7 4.3 %all-to-all-done.3.gathered_ref = f32[32,8,128]{2,1,0:T(8,128)S(1)} async-done(((f32[32,8,128]{2,1,0:T(8,128)}), f32[32,8,128]{2,1,0:T(8,128)S(1)}, u32[]{:S(2)}, u32[]{:S(2)}) %all-to-all-start.3) | async-done | bytes 131104 | tf_op jit(solution)/shard_map/all_to_all | solution.py:749
  85.7 6.0 %backward.2 = (f32[32,8,128]{2,1,0:T(8,128)}, f32[512,512]{1,0:T(8,128)S(1)}, bf16[512,512]{1,0:T(8,128)(2,1)S(1)}, f32[8,128]{1,0:T(8,128)S(1)}, bf16[768,128]{...) custom-call(s32[8,128]{1,0:T(8,128)S(1)} %get-tuple-element.131.limits_ref, ...), custom_call_target="tpu_custom_call" | custom-call | flops 2415919104 | tf_op jit(solution)/shard_map/backward/pallas_call | solution.py:705
  92.5 2.6 %all-to-all-start.4 = ((f32[32,8,128]{2,1,0:T(8,128)}), f32[32,8,128]{2,1,0:T(8,128)S(1)}, u32[]{:S(2)}, u32[]{:S(2)}) async-start(f32[32,8,128]{2,1,0:T(8,128)} %get-tuple-element.178), calls=%async_computation.4 | async-start | bytes 262144 | tf_op jit(solution)/shard_map/all_to_all | solution.py:749
  95.3 1.7 collective-permute-start.18
  97.1 5.3 %weight_grad.3 = (f32[4,576,128]{2,1,0:T(8,128)}, bf16[4,576,128]{2,1,0:T(8,128)(2,1)}) custom-call(s32[8,128]{1,0:T(8,128)S(1)} %get-tuple-element.131.limits_ref, f32[32,8,128]{2,1,0:T(8,128)S(1)} %get-tuple-element.132.member_ref, f32[32,8,128]{2,1,0:T(8,128)S(1)} %all-to-all-done.3.gathered_ref, f32[8,128]{1,0:T(8,128)S(1)} %get-tuple-element.167.moments_ref, ...), custom_call_target="tpu_custom_call" | custom-call | flops 1811939328 | tf_op jit(solution)/shard_map/weight_grad/pallas_call | solution.py:705
  106.3 5.7 %backward.3 = (f32[32,8,128]{2,1,0:T(8,128)}, f32[448,512]{1,0:T(8,128)S(1)}, bf16[448,512]{1,0:T(8,128)(2,1)S(1)}, f32[8,128]{1,0:T(8,128)S(1)}, bf16[768,128]{...) custom-call(s32[8,128]{1,0:T(8,128)S(1)} %get-tuple-element.131.limits_ref, ...), custom_call_target="tpu_custom_call" | custom-call | flops 2113929216 | tf_op jit(solution)/shard_map/backward/pallas_call | solution.py:705
  112.7 5.0 %all-to-all-start.5 = ((f32[32,8,128]{2,1,0:T(8,128)}), f32[32,8,128]{2,1,0:T(8,128)S(1)}, u32[]{:S(2)}, u32[]{:S(2)}) async-start(f32[32,8,128]{2,1,0:T(8,128)} %get-tuple-element.198), calls=%async_computation.5 | async-start | bytes 262144 | tf_op jit(solution)/shard_map/all_to_all | solution.py:749
  117.8 1.7 collective-permute-start.22
  119.6 5.3 %weight_grad.4 = (f32[4,576,128]{2,1,0:T(8,128)}, bf16[4,576,128]{2,1,0:T(8,128)(2,1)}) custom-call(s32[8,128]{1,0:T(8,128)S(1)} %get-tuple-element.131.limits_ref, f32[32,8,128]{2,1,0:T(8,128)S(1)} %get-tuple-element.132.member_ref, f32[32,8,128]{2,1,0:T(8,128)S(1)} %all-to-all-done.4.gathered_ref, f32[8,128]{1,0:T(8,128)S(1)} %copy-done.13, ...), custom_call_target="tpu_custom_call" | custom-call | flops 1811939328 | tf_op jit(solution)/shard_map/weight_grad/pallas_call | solution.py:705
  126.6 2.1 %halve.4 = (f32[2,576,128]{2,1,0:T(8,128)}, bf16[2,576,128]{2,1,0:T(8,128)(2,1)}) custom-call(f32[4,576,128]{2,1,0:T(8,128)} %get-tuple-element.223.keep_hbm, bf16[4,576,128]{2,1,0:T(8,128)(2,1)S(1)} %collective-permute-done.20.received_ref), custom_call_target="tpu_custom_call" | custom-call | tf_op jit(solution)/shard_map/halve/pallas_call | solution.py:705
  128.8 1.5 collective-permute-start.24
  131.0 4.4 %weight_grad.5 = (f32[4,576,128]{2,1,0:T(8,128)S(1)}, bf16[4,576,128]{2,1,0:T(8,128)(2,1)S(1)}) custom-call(s32[8,128]{1,0:T(8,128)S(1)} %get-tuple-element.131.limits_ref, f32[32,8,128]{2,1,0:T(8,128)S(1)} %get-tuple-element.132.member_ref, f32[32,8,128]{2,1,0:T(8,128)S(1)} %all-to-all-done.5.gathered_ref, f32[8,128]{1,0:T(8,128)S(1)} %copy-done.15, ...), custom_call_target="tpu_custom_call" | custom-call | flops 1811939328 | tf_op jit(solution)/shard_map/weight_grad/pallas_call | solution.py:705
  136.4 1.7 collective-permute-done.24.received_ref
  139.0 3.1 %collective-permute-done.26.received_ref = bf16[4,576,128]{2,1,0:T(8,128)(2,1)S(1)} collective-permute-done((bf16[4,576,128]{2,1,0:T(8,128)(2,1)}, bf16[4,576,128]{2,1,0:T(8,128)(2,1)S(1)}, u32[]{:S(2)}, u32[]{:S(2)}) %collective-permute-start.26) | collective-permute-done | bytes 589856 | tf_op jit(solution)/shard_map/ppermute | solution.py:867
  142.1 2.1 %halve.5 = (f32[2,576,128]{2,1,0:T(8,128)}, bf16[2,576,128]{2,1,0:T(8,128)(2,1)}) custom-call(f32[4,576,128]{2,1,0:T(8,128)} %get-tuple-element.227.keep_hbm, bf16[4,576,128]{2,1,0:T(8,128)(2,1)S(1)} %collective-permute-done.26.received_ref), custom_call_target="tpu_custom_call" | custom-call | tf_op jit(solution)/shard_map/halve/pallas_call | solution.py:705
  145.2 1.8 halve.6
  147.0 2.5 %collective-permute-start.28 = (bf16[1,576,128]{2,1,0:T(8,128)(2,1)}, bf16[1,576,128]{2,1,0:T(8,128)(2,1)S(1)}, u32[]{:S(2)}, u32[]{:S(2)}) collective-permute-start(bf16[1,576,128]{2,1,0:T(8,128)(2,1)} %get-tuple-element.232), channel_id=1, source_target_pairs={{0,16},{4,20},{8,24},{12,28},{16,0},{20,4},{24,8},{28,12},{1,17},{... | collective-permute-start | bytes 442376 | tf_op jit(solution)/shard_map/ppermute | solution.py:867
  149.5 5.1 %collective-permute-done.28.last2_hbm = bf16[1,576,128]{2,1,0:T(8,128)(2,1)S(1)} collective-permute-done((bf16[1,576,128]{2,1,0:T(8,128)(2,1)}, bf16[1,576,128]{2,1,0:T(8,128)(2,1)S(1)}, u32[]{:S(2)}, u32[]{:S(2)}) %collective-permute-start.28) | collective-permute-done | bytes 147488 | tf_op jit(solution)/shard_map/ppermute | solution.py:867
  155.3 2.1 %add.3 = bf16[4,576,128]{2,1,0:T(8,128)(2,1)} custom-call(f32[4,576,128]{2,1,0:T(8,128)} %copy-done, bf16[4,576,128]{2,1,0:T(8,128)(2,1)S(1)} %collective-permute-done.25.received_ref), custom_call_target="tpu_custom_call" | custom-call | tf_op jit(solution)/shard_map/add/pallas_call | solution.py:705
  157.4 4.5 %all-to-all-start.6 = ((bf16[4,576,128]{2,1,0:T(8,128)(2,1)}), bf16[4,576,128]{2,1,0:T(8,128)(2,1)S(1)}, u32[]{:S(2)}, u32[]{:S(2)}) async-start(bf16[4,576,128]{2,1,0:T(8,128)(2,1)} %add.3), calls=%async_computation.6 | async-start | bytes 1179648 | tf_op jit(solution)/shard_map/all_to_all | solution.py:936
  163.0 1.8 halve.7
  164.8 3.0 %collective-permute-start.29 = (bf16[1,576,128]{2,1,0:T(8,128)(2,1)}, bf16[1,576,128]{2,1,0:T(8,128)(2,1)S(1)}, u32[]{:S(2)}, u32[]{:S(2)}) collective-permute-start(bf16[1,576,128]{2,1,0:T(8,128)(2,1)} %get-tuple-element.237), channel_id=1, source_target_pairs={{0,16},{4,20},{8,24},{12,28},{16,0},{20,4},{24,8},{28,12},{1,17},{... | collective-permute-start | bytes 442376 | tf_op jit(solution)/shard_map/ppermute | solution.py:867
  167.8 4.2 %last.1 = (bf16[384,512]{1,0:T(8,128)(2,1)}, f32[8,128]{1,0:T(8,128)S(1)}, bf16[384,128]{1,0:T(8,128)(2,1)}) custom-call(s32[8,128]{1,0:T(8,128)S(1)} %get-tuple-element.131.limits_ref, f32[32,8,128]{2,1,0:T(8,128)S(1)} %get-tuple-element.132.member_ref, f32[32,8,128]{2,1,0:T(8,128)S(1)} %all-to-all-done.5.gathered_ref, ...), custom_call_target="tpu_custom_call" | custom-call | flops 1811939328 | tf_op jit(solution)/shard_map/last/pallas_call | solution.py:705
  172.0 10.2 %collective-permute-done.29.last1_hbm = bf16[1,576,128]{2,1,0:T(8,128)(2,1)S(1)} collective-permute-done((bf16[1,576,128]{2,1,0:T(8,128)(2,1)}, bf16[1,576,128]{2,1,0:T(8,128)(2,1)S(1)}, u32[]{:S(2)}, u32[]{:S(2)}) %collective-permute-start.29) | collective-permute-done | bytes 147488 | tf_op jit(solution)/shard_map/ppermute | solution.py:867
  182.8 2.0 squares.1
  184.8 4.0 %all-to-all-start.7 = ((f32[32,1,128]{2,1,0:T(1,128)}), f32[32,1,128]{2,1,0:T(1,128)S(1)}, u32[]{:S(2)}, u32[]{:S(2)}) async-start(f32[32,1,128]{2,1,0:T(1,128)} %get-tuple-element.243), calls=%async_computation.7 | async-start | bytes 32768 | tf_op jit(solution)/shard_map/all_to_all | solution.py:954
  189.4 6.4 %all-to-all-done.7.every_ref = f32[32,1,128]{2,1,0:T(1,128)S(1)} async-done(((f32[32,1,128]{2,1,0:T(1,128)}), f32[32,1,128]{2,1,0:T(1,128)S(1)}, u32[]{:S(2)}, u32[]{:S(2)}) %all-to-all-start.7) | async-done | bytes 16416 | tf_op jit(solution)/shard_map/all_to_all | solution.py:954
  195.8 2.9 %adam.1 = (f32[1,128]{1,0:T(1,128)}, f32[3,576,128]{2,1,0:T(8,128)}, f32[3,576,128]{2,1,0:T(8,128)}, f32[3,576,128]{2,1,0:T(8,128)}, f32[3,2,512]{2,1,0:T(2,128)...) custom-call(f32[32,1,128]{2,1,0:T(1,128)S(1)} %all-to-all-done.7.every_ref, s32[1]{0:T(128)S(6)} %copy.24.step_ref, ...), custom_call_target="tpu_custom_call" | custom-call | tf_op jit(solution)/shard_map/adam/pallas_call | solution.py:705
  (119 shorter events, 26.3 us)
Async XLA Ops:
  0.6 30.4 %copy-start.3 = (f32[2,3,512]{2,0,1:T(2,128)S(1)}, f32[2,3,512]{2,0,1:T(2,128)}, u32[]{:S(2)}) copy-start(f32[2,3,512]{2,0,1:T(2,128)} %param.16) | copy-start | bytes 36868
  2.0 6.7 %collective-permute-start = (bf16[224,512]{1,0:T(8,128)(2,1)S(1)}, bf16[224,512]{1,0:T(8,128)(2,1)S(1)}, u32[]{:S(2)}, u32[]{:S(2)}) collective-permute-start(bf16[224,512]{1,0:T(8,128)(2,1)S(1)} %get-tuple-element.133), channel_id=1, source_target_pairs={{0,1},{1,0},{2,3},{3,2},{4,5},{5,4},{6,7},{7,6},{8,9},{9,8},{10,11... | collective-permute-start | bytes 688136 | tf_op jit(solution)/shard_map/ppermute | solution.py:757
  2.5 6.2 %collective-permute-start.1 = (bf16[224,512]{1,0:T(8,128)(2,1)S(1)}, bf16[224,512]{1,0:T(8,128)(2,1)S(1)}, u32[]{:S(2)}, u32[]{:S(2)}) collective-permute-start(bf16[224,512]{1,0:T(8,128)(2,1)S(1)} %get-tuple-element.135), channel_id=1, source_target_pairs={{2,1},{1,2},{6,5},{5,6},{10,9},{9,10},{14,13},{13,14},{18,17},{17,... | collective-permute-start | bytes 688136 | tf_op jit(solution)/shard_map/ppermute | solution.py:766
  14.1 17.0 %all-to-all-start = ((f32[32,8,128]{2,1,0:T(8,128)}), f32[32,8,128]{2,1,0:T(8,128)S(1)}, u32[]{:S(2)}, u32[]{:S(2)}) async-start(f32[32,8,128]{2,1,0:T(8,128)} %get-tuple-element.141), calls=%async_computation | async-start | bytes 262144 | tf_op jit(solution)/shard_map/all_to_all | solution.py:749
  22.8 13.1 %collective-permute-start.2 = (bf16[384,512]{1,0:T(8,128)(2,1)}, bf16[384,512]{1,0:T(8,128)(2,1)}, u32[]{:S(2)}, u32[]{:S(2)}) collective-permute-start(bf16[384,512]{1,0:T(8,128)(2,1)} %get-tuple-element.218.rest_4_), channel_id=1, source_target_pairs={{0,1},{1,0},{2,3},{3,2},{4,5},{5,4},{6,7},{7,6},{8,9},{9,8},{10,11... | collective-permute-start | bytes 1179656 | tf_op jit(solution)/shard_map/ppermute | solution.py:757
  23.1 12.8 %collective-permute-start.3 = (bf16[384,512]{1,0:T(8,128)(2,1)}, bf16[384,512]{1,0:T(8,128)(2,1)}, u32[]{:S(2)}, u32[]{:S(2)}) collective-permute-start(bf16[384,512]{1,0:T(8,128)(2,1)} %get-tuple-element.218.rest_4_), channel_id=1, source_target_pairs={{0,2},{1,3},{2,0},{3,1},{4,6},{5,7},{6,4},{7,5},{8,10},{9,11},{10,... | collective-permute-start | bytes 1179656 | tf_op jit(solution)/shard_map/ppermute | solution.py:757
  36.6 12.4 %all-to-all-start.1 = ((f32[32,8,128]{2,1,0:T(8,128)}), f32[32,8,128]{2,1,0:T(8,128)S(1)}, u32[]{:S(2)}, u32[]{:S(2)}) async-start(f32[32,8,128]{2,1,0:T(8,128)} %copy-done.10), calls=%async_computation.1 | async-start | bytes 262144 | tf_op jit(solution)/shard_map/all_to_all | solution.py:749
  40.8 12.2 %collective-permute-start.4 = (bf16[160,128]{1,0:T(8,128)(2,1)}, bf16[160,128]{1,0:T(8,128)(2,1)S(1)}, u32[]{:S(2)}, u32[]{:S(2)}) collective-permute-start(bf16[160,128]{1,0:T(8,128)(2,1)} %get-tuple-element.151), channel_id=1, source_target_pairs={{0,1},{1,0},{2,3},{3,2},{4,5},{5,4},{6,7},{7,6},{8,9},{9,8},{10,11... | collective-permute-start | bytes 122888 | tf_op jit(solution)/shard_map/ppermute | solution.py:753
  41.1 12.2 %collective-permute-start.5 = (bf16[160,128]{1,0:T(8,128)(2,1)}, bf16[160,128]{1,0:T(8,128)(2,1)S(1)}, u32[]{:S(2)}, u32[]{:S(2)}) collective-permute-start(bf16[160,128]{1,0:T(8,128)(2,1)} %get-tuple-element.152), channel_id=1, source_target_pairs={{0,2},{1,3},{2,0},{3,1},{4,6},{5,7},{6,4},{7,5},{8,10},{9,11},{10,... | collective-permute-start | bytes 122888 | tf_op jit(solution)/shard_map/ppermute | solution.py:753
  42.8 10.8 %collective-permute-start.6 = (bf16[160,128]{1,0:T(8,128)(2,1)}, bf16[160,128]{1,0:T(8,128)(2,1)S(1)}, u32[]{:S(2)}, u32[]{:S(2)}) collective-permute-start(bf16[160,128]{1,0:T(8,128)(2,1)} %get-tuple-element.153), channel_id=1, source_target_pairs={{0,3},{1,2},{2,1},{3,0},{4,7},{5,6},{6,5},{7,4},{8,11},{9,10},{10,... | collective-permute-start | bytes 122888 | tf_op jit(solution)/shard_map/ppermute | solution.py:753
  42.8 11.3 %collective-permute-start.7 = (bf16[384,512]{1,0:T(8,128)(2,1)}, bf16[384,512]{1,0:T(8,128)(2,1)S(1)}, u32[]{:S(2)}, u32[]{:S(2)}) collective-permute-start(bf16[384,512]{1,0:T(8,128)(2,1)} %get-tuple-element.203.rest_4_), channel_id=1, source_target_pairs={{0,1},{1,0},{2,3},{3,2},{4,5},{5,4},{6,7},{7,6},{8,9},{9,8},{10,11... | collective-permute-start | bytes 1179656 | tf_op jit(solution)/shard_map/ppermute | solution.py:757
  43.2 12.7 %collective-permute-start.8 = (bf16[384,512]{1,0:T(8,128)(2,1)}, bf16[384,512]{1,0:T(8,128)(2,1)}, u32[]{:S(2)}, u32[]{:S(2)}) collective-permute-start(bf16[384,512]{1,0:T(8,128)(2,1)} %get-tuple-element.203.rest_4_), channel_id=1, source_target_pairs={{0,2},{1,3},{2,0},{3,1},{4,6},{5,7},{6,4},{7,5},{8,10},{9,11},{10,... | collective-permute-start | bytes 1179656 | tf_op jit(solution)/shard_map/ppermute | solution.py:757
  53.0 19.2 %copy-start.11 = (f32[8,128]{1,0:T(8,128)}, f32[8,128]{1,0:T(8,128)S(1)}, u32[]{:S(2)}) copy-start(f32[8,128]{1,0:T(8,128)S(1)} %get-tuple-element.170.moments_below_ref.moments_ref) | copy-start | bytes 12292
  53.0 16.3 %copy-start.23 = (bf16[160,128]{1,0:T(8,128)(2,1)}, bf16[160,128]{1,0:T(8,128)(2,1)S(1)}, u32[]{:S(2)}) copy-start(bf16[160,128]{1,0:T(8,128)(2,1)S(1)} %collective-permute-done.4.rest_1_) | copy-start | bytes 122884
  53.0 19.2 %collective-permute-start.9 = (bf16[384,512]{1,0:T(8,128)(2,1)}, bf16[384,512]{1,0:T(8,128)(2,1)S(1)}, u32[]{:S(2)}, u32[]{:S(2)}) collective-permute-start(bf16[384,512]{1,0:T(8,128)(2,1)} %collective-permute-done.3.rest_6_), channel_id=1, source_target_pairs={{0,1},{1,0},{2,3},{3,2},{4,5},{5,4},{6,7},{7,6},{8,9},{9,8},{10,11... | collective-permute-start | bytes 1179656 | tf_op jit(solution)/shard_map/ppermute | solution.py:757
  53.3 16.0 %copy-start.24 = (bf16[160,128]{1,0:T(8,128)(2,1)}, bf16[160,128]{1,0:T(8,128)(2,1)S(1)}, u32[]{:S(2)}) copy-start(bf16[160,128]{1,0:T(8,128)(2,1)S(1)} %collective-permute-done.5.rest_2_) | copy-start | bytes 122884
  53.3 19.0 %collective-permute-start.10 = (bf16[384,512]{1,0:T(8,128)(2,1)}, bf16[384,512]{1,0:T(8,128)(2,1)S(1)}, u32[]{:S(2)}, u32[]{:S(2)}) collective-permute-start(bf16[384,512]{1,0:T(8,128)(2,1)} %get-tuple-element.183.rest_4_), channel_id=1, source_target_pairs={{0,1},{1,0},{2,3},{3,2},{4,5},{5,4},{6,7},{7,6},{8,9},{9,8},{10,11... | collective-permute-start | bytes 1179656 | tf_op jit(solution)/shard_map/ppermute | solution.py:757
  53.6 15.7 %copy-start.25 = (bf16[160,128]{1,0:T(8,128)(2,1)}, bf16[160,128]{1,0:T(8,128)(2,1)S(1)}, u32[]{:S(2)}) copy-start(bf16[160,128]{1,0:T(8,128)(2,1)S(1)} %collective-permute-done.6.rest_3_) | copy-start | bytes 122884
  53.6 18.7 %collective-permute-start.11 = (bf16[384,512]{1,0:T(8,128)(2,1)}, bf16[384,512]{1,0:T(8,128)(2,1)S(1)}, u32[]{:S(2)}, u32[]{:S(2)}) collective-permute-start(bf16[384,512]{1,0:T(8,128)(2,1)} %get-tuple-element.183.rest_4_), channel_id=1, source_target_pairs={{0,2},{1,3},{2,0},{3,1},{4,6},{5,7},{6,4},{7,5},{8,10},{9,11},{10,... | collective-permute-start | bytes 1179656 | tf_op jit(solution)/shard_map/ppermute | solution.py:757
  69.3 35.9 %copy-start.15 = (f32[8,128]{1,0:T(8,128)S(1)}, f32[8,128]{1,0:T(8,128)}, u32[]{:S(2)}) copy-start(f32[8,128]{1,0:T(8,128)} %copy-done.14) | copy-start | bytes 12292
  72.3 32.9 %copy-start.13 = (f32[8,128]{1,0:T(8,128)S(1)}, f32[8,128]{1,0:T(8,128)}, u32[]{:S(2)}) copy-start(f32[8,128]{1,0:T(8,128)} %copy-done.11) | copy-start | bytes 12292
  73.1 10.8 %all-to-all-start.3 = ((f32[32,8,128]{2,1,0:T(8,128)}), f32[32,8,128]{2,1,0:T(8,128)S(1)}, u32[]{:S(2)}, u32[]{:S(2)}) async-start(f32[32,8,128]{2,1,0:T(8,128)} %get-tuple-element.164), calls=%async_computation.3 | async-start | bytes 262144 | tf_op jit(solution)/shard_map/all_to_all | solution.py:749
  75.9 16.6 %collective-permute-start.12 = (bf16[384,512]{1,0:T(8,128)(2,1)}, bf16[384,512]{1,0:T(8,128)(2,1)}, u32[]{:S(2)}, u32[]{:S(2)}) collective-permute-start(bf16[384,512]{1,0:T(8,128)(2,1)} %collective-permute-done.8.rest_6_), channel_id=1, source_target_pairs={{0,1},{1,0},{2,3},{3,2},{4,5},{5,4},{6,7},{7,6},{8,9},{9,8},{10,11... | collective-permute-start | bytes 1179656 | tf_op jit(solution)/shard_map/ppermute | solution.py:757
  76.0 16.5 %collective-permute-start.14 = (bf16[864,128]{1,0:T(8,128)(2,1)}, bf16[864,128]{1,0:T(8,128)(2,1)S(1)}, u32[]{:S(2)}, u32[]{:S(2)}) collective-permute-start(bf16[864,128]{1,0:T(8,128)(2,1)} %get-tuple-element.175), channel_id=1, source_target_pairs={{0,1},{1,0},{2,3},{3,2},{4,5},{5,4},{6,7},{7,6},{8,9},{9,8},{10,11... | collective-permute-start | bytes 663560 | tf_op jit(solution)/shard_map/ppermute | solution.py:753
  76.4 16.0 %collective-permute-start.15 = (bf16[864,128]{1,0:T(8,128)(2,1)}, bf16[864,128]{1,0:T(8,128)(2,1)}, u32[]{:S(2)}, u32[]{:S(2)}) collective-permute-start(bf16[864,128]{1,0:T(8,128)(2,1)} %get-tuple-element.176), channel_id=1, source_target_pairs={{0,2},{1,3},{2,0},{3,1},{4,6},{5,7},{6,4},{7,5},{8,10},{9,11},{10,... | collective-permute-start | bytes 663560 | tf_op jit(solution)/shard_map/ppermute | solution.py:753
  77.9 14.6 %collective-permute-start.16 = (bf16[864,128]{1,0:T(8,128)(2,1)}, bf16[864,128]{1,0:T(8,128)(2,1)}, u32[]{:S(2)}, u32[]{:S(2)}) collective-permute-start(bf16[864,128]{1,0:T(8,128)(2,1)} %get-tuple-element.177), channel_id=1, source_target_pairs={{0,3},{1,2},{2,1},{3,0},{4,7},{5,6},{6,5},{7,4},{8,11},{9,10},{10,... | collective-permute-start | bytes 663560 | tf_op jit(solution)/shard_map/ppermute | solution.py:753
  77.9 14.6 %collective-permute-start.13 = (bf16[384,512]{1,0:T(8,128)(2,1)}, bf16[384,512]{1,0:T(8,128)(2,1)}, u32[]{:S(2)}, u32[]{:S(2)}) collective-permute-start(bf16[384,512]{1,0:T(8,128)(2,1)} %copy-done.29), channel_id=1, source_target_pairs={{0,1},{1,0},{2,3},{3,2},{4,5},{5,4},{6,7},{7,6},{8,9},{9,8},{10,11... | collective-permute-start | bytes 1179656 | tf_op jit(solution)/shard_map/ppermute | solution.py:757
  92.5 10.8 %all-to-all-start.4 = ((f32[32,8,128]{2,1,0:T(8,128)}), f32[32,8,128]{2,1,0:T(8,128)S(1)}, u32[]{:S(2)}, u32[]{:S(2)}) async-start(f32[32,8,128]{2,1,0:T(8,128)} %get-tuple-element.178), calls=%async_computation.4 | async-start | bytes 262144 | tf_op jit(solution)/shard_map/all_to_all | solution.py:749
  95.1 17.6 %collective-permute-start.17 = (bf16[768,128]{1,0:T(8,128)(2,1)}, bf16[768,128]{1,0:T(8,128)(2,1)}, u32[]{:S(2)}, u32[]{:S(2)}) collective-permute-start(bf16[768,128]{1,0:T(8,128)(2,1)} %get-tuple-element.195), channel_id=1, source_target_pairs={{0,1},{1,0},{2,3},{3,2},{4,5},{5,4},{6,7},{7,6},{8,9},{9,8},{10,11... | collective-permute-start | bytes 589832 | tf_op jit(solution)/shard_map/ppermute | solution.py:753
  95.3 17.4 %collective-permute-start.18 = (bf16[768,128]{1,0:T(8,128)(2,1)}, bf16[768,128]{1,0:T(8,128)(2,1)}, u32[]{:S(2)}, u32[]{:S(2)}) collective-permute-start(bf16[768,128]{1,0:T(8,128)(2,1)} %get-tuple-element.196), channel_id=1, source_target_pairs={{0,2},{1,3},{2,0},{3,1},{4,6},{5,7},{6,4},{7,5},{8,10},{9,11},{10,... | collective-permute-start | bytes 589832 | tf_op jit(solution)/shard_map/ppermute | solution.py:753
  97.0 15.8 %collective-permute-start.19 = (bf16[768,128]{1,0:T(8,128)(2,1)}, bf16[768,128]{1,0:T(8,128)(2,1)}, u32[]{:S(2)}, u32[]{:S(2)}) collective-permute-start(bf16[768,128]{1,0:T(8,128)(2,1)} %get-tuple-element.197), channel_id=1, source_target_pairs={{0,3},{1,2},{2,1},{3,0},{4,7},{5,6},{6,5},{7,4},{8,11},{9,10},{10,... | collective-permute-start | bytes 589832 | tf_op jit(solution)/shard_map/ppermute | solution.py:753
  103.3 22.4 %collective-permute-start.20 = (bf16[4,576,128]{2,1,0:T(8,128)(2,1)}, bf16[4,576,128]{2,1,0:T(8,128)(2,1)S(1)}, u32[]{:S(2)}, u32[]{:S(2)}) collective-permute-start(bf16[4,576,128]{2,1,0:T(8,128)(2,1)} %get-tuple-element.207), channel_id=1, source_target_pairs={{0,4},{4,0},{8,12},{12,8},{16,20},{20,16},{24,28},{28,24},{1,5},{5... | collective-permute-start | bytes 1769480 | tf_op jit(solution)/shard_map/ppermute | solution.py:867
  112.7 55.1 %copy-start.9 = (bf16[448,512]{1,0:T(8,128)(2,1)S(1)}, bf16[448,512]{1,0:T(8,128)(2,1)}, u32[]{:S(2)}) copy-start(bf16[448,512]{1,0:T(8,128)(2,1)} %copy-done.8) | copy-start | bytes 1376260
  112.7 13.0 %all-to-all-start.5 = ((f32[32,8,128]{2,1,0:T(8,128)}), f32[32,8,128]{2,1,0:T(8,128)S(1)}, u32[]{:S(2)}, u32[]{:S(2)}) async-start(f32[32,8,128]{2,1,0:T(8,128)} %get-tuple-element.198), calls=%async_computation.5 | async-start | bytes 262144 | tf_op jit(solution)/shard_map/all_to_all | solution.py:749
  117.7 12.6 %collective-permute-start.21 = (bf16[768,128]{1,0:T(8,128)(2,1)}, bf16[768,128]{1,0:T(8,128)(2,1)S(1)}, u32[]{:S(2)}, u32[]{:S(2)}) collective-permute-start(bf16[768,128]{1,0:T(8,128)(2,1)} %get-tuple-element.215), channel_id=1, source_target_pairs={{0,1},{1,0},{2,3},{3,2},{4,5},{5,4},{6,7},{7,6},{8,9},{9,8},{10,11... | collective-permute-start | bytes 589832 | tf_op jit(solution)/shard_map/ppermute | solution.py:753
  117.8 12.5 %collective-permute-start.22 = (bf16[768,128]{1,0:T(8,128)(2,1)}, bf16[768,128]{1,0:T(8,128)(2,1)}, u32[]{:S(2)}, u32[]{:S(2)}) collective-permute-start(bf16[768,128]{1,0:T(8,128)(2,1)} %get-tuple-element.216), channel_id=1, source_target_pairs={{0,2},{1,3},{2,0},{3,1},{4,6},{5,7},{6,4},{7,5},{8,10},{9,11},{10,... | collective-permute-start | bytes 589832 | tf_op jit(solution)/shard_map/ppermute | solution.py:753
  119.5 10.9 %collective-permute-start.23 = (bf16[768,128]{1,0:T(8,128)(2,1)}, bf16[768,128]{1,0:T(8,128)(2,1)}, u32[]{:S(2)}, u32[]{:S(2)}) collective-permute-start(bf16[768,128]{1,0:T(8,128)(2,1)} %get-tuple-element.217), channel_id=1, source_target_pairs={{0,3},{1,2},{2,1},{3,0},{4,7},{5,6},{6,5},{7,4},{8,11},{9,10},{10,... | collective-permute-start | bytes 589832 | tf_op jit(solution)/shard_map/ppermute | solution.py:753
  125.7 16.4 %collective-permute-start.26 = (bf16[4,576,128]{2,1,0:T(8,128)(2,1)}, bf16[4,576,128]{2,1,0:T(8,128)(2,1)S(1)}, u32[]{:S(2)}, u32[]{:S(2)}) collective-permute-start(bf16[4,576,128]{2,1,0:T(8,128)(2,1)} %get-tuple-element.228), channel_id=1, source_target_pairs={{0,4},{4,0},{8,12},{12,8},{16,20},{20,16},{24,28},{28,24},{1,5},{5... | collective-permute-start | bytes 1769480 | tf_op jit(solution)/shard_map/ppermute | solution.py:867
  128.8 9.4 %collective-permute-start.24 = (bf16[2,576,128]{2,1,0:T(8,128)(2,1)}, bf16[2,576,128]{2,1,0:T(8,128)(2,1)S(1)}, u32[]{:S(2)}, u32[]{:S(2)}) collective-permute-start(bf16[2,576,128]{2,1,0:T(8,128)(2,1)} %get-tuple-element.225), channel_id=1, source_target_pairs={{0,8},{4,12},{8,0},{12,4},{16,24},{20,28},{24,16},{28,20},{1,9},{5... | collective-permute-start | bytes 884744 | tf_op jit(solution)/shard_map/ppermute | solution.py:867
  136.4 59.4 %copy-start.16 = (f32[2,3,512]{2,0,1:T(2,128)S(1)}, f32[2,3,512]{2,0,1:T(2,128)}, u32[]{:S(2)}) copy-start(f32[2,3,512]{2,0,1:T(2,128)} %param.26) | copy-start | bytes 36868
  136.4 59.4 %copy-start.17 = (f32[2,3,512]{2,0,1:T(2,128)S(1)}, f32[2,3,512]{2,0,1:T(2,128)}, u32[]{:S(2)}) copy-start(f32[2,3,512]{2,0,1:T(2,128)} %param.27) | copy-start | bytes 36868
  138.1 17.1 %collective-permute-start.25 = (bf16[4,576,128]{2,1,0:T(8,128)(2,1)S(1)}, bf16[4,576,128]{2,1,0:T(8,128)(2,1)S(1)}, u32[]{:S(2)}, u32[]{:S(2)}) collective-permute-start(bf16[4,576,128]{2,1,0:T(8,128)(2,1)S(1)} %get-tuple-element.226), channel_id=1, source_target_pairs={{0,4},{4,0},{8,12},{12,8},{16,20},{20,16},{24,28},{28,24},{1,5},{5... | collective-permute-start | bytes 1769480 | tf_op jit(solution)/shard_map/ppermute | solution.py:867
  144.2 11.0 %collective-permute-start.27 = (bf16[2,576,128]{2,1,0:T(8,128)(2,1)}, bf16[2,576,128]{2,1,0:T(8,128)(2,1)S(1)}, u32[]{:S(2)}, u32[]{:S(2)}) collective-permute-start(bf16[2,576,128]{2,1,0:T(8,128)(2,1)} %get-tuple-element.229), channel_id=1, source_target_pairs={{0,8},{4,12},{8,0},{12,4},{16,24},{20,28},{24,16},{28,20},{1,9},{5... | collective-permute-start | bytes 884744 | tf_op jit(solution)/shard_map/ppermute | solution.py:867
  147.0 7.6 %collective-permute-start.28 = (bf16[1,576,128]{2,1,0:T(8,128)(2,1)}, bf16[1,576,128]{2,1,0:T(8,128)(2,1)S(1)}, u32[]{:S(2)}, u32[]{:S(2)}) collective-permute-start(bf16[1,576,128]{2,1,0:T(8,128)(2,1)} %get-tuple-element.232), channel_id=1, source_target_pairs={{0,16},{4,20},{8,24},{12,28},{16,0},{20,4},{24,8},{28,12},{1,17},{... | collective-permute-start | bytes 442376 | tf_op jit(solution)/shard_map/ppermute | solution.py:867
  154.6 27.5 %copy-start.21 = (bf16[1,576,128]{2,1,0:T(8,128)(2,1)}, bf16[1,576,128]{2,1,0:T(8,128)(2,1)S(1)}, u32[]{:S(2)}) copy-start(bf16[1,576,128]{2,1,0:T(8,128)(2,1)S(1)} %collective-permute-done.28.last2_hbm) | copy-start | bytes 442372
  157.4 24.8 %all-to-all-start.6 = ((bf16[4,576,128]{2,1,0:T(8,128)(2,1)}), bf16[4,576,128]{2,1,0:T(8,128)(2,1)S(1)}, u32[]{:S(2)}, u32[]{:S(2)}) async-start(bf16[4,576,128]{2,1,0:T(8,128)(2,1)} %add.3), calls=%async_computation.6 | async-start | bytes 1179648 | tf_op jit(solution)/shard_map/all_to_all | solution.py:936
  164.8 17.3 %collective-permute-start.29 = (bf16[1,576,128]{2,1,0:T(8,128)(2,1)}, bf16[1,576,128]{2,1,0:T(8,128)(2,1)S(1)}, u32[]{:S(2)}, u32[]{:S(2)}) collective-permute-start(bf16[1,576,128]{2,1,0:T(8,128)(2,1)} %get-tuple-element.237), channel_id=1, source_target_pairs={{0,16},{4,20},{8,24},{12,28},{16,0},{20,4},{24,8},{28,12},{1,17},{... | collective-permute-start | bytes 442376 | tf_op jit(solution)/shard_map/ppermute | solution.py:867
  184.8 11.0 %all-to-all-start.7 = ((f32[32,1,128]{2,1,0:T(1,128)}), f32[32,1,128]{2,1,0:T(1,128)S(1)}, u32[]{:S(2)}, u32[]{:S(2)}) async-start(f32[32,1,128]{2,1,0:T(1,128)} %get-tuple-element.243), calls=%async_computation.7 | async-start | bytes 32768 | tf_op jit(solution)/shard_map/all_to_all | solution.py:954
  (20 other events, 87.7 us)

commit v6 on v5

--- a/solution.py
+++ b/solution.py
@@ -809,10 +809,10 @@
             stats, weights, *acts[0] = tie((stats, conv_weights, *acts[0]))
             gathered = spread(stats)
         else:
-            stats, *rest = tie((stats, *cots, *acts[1]))
-            cots, acts[1] = rest[:bands], rest[bands:]
+            stats, *cots = tie((stats, *cots))
             gathered = spread(stats)
-        acts[layer - 1].append(swap(acts[layer - 1][2], 1))
+        if layer == 1:
+            acts[0].append(swap(acts[0][2], 1))
         acts.append([act, swap(act, 1), swap(act, 2)])
 
     rows = sz.rows + 2 * (HALO - 3)
@@ -830,7 +830,9 @@
         conv_flops(4), hbm_ins=range(5, 8 + bands), hbm_outs=range(4, 4 + bands), sems=3 + 4 * bands,
     )
     moments.append(moment)
-    stats, weights, acts[0][3], *acts[2] = tie((stats, conv_weights, acts[0][3], *acts[2]))
+    stats, weights, acts[0][3], *rest = tie((stats, conv_weights, acts[0][3], *acts[1], *acts[2]))
+    acts[1], acts[2] = rest[:3], rest[3:]
+    acts[1].append(swap(acts[1][2], 1))
     gathered = spread(stats)
     exchanged = trade(shares)
     acts[2].append(swap(acts[2][2], 1))

time: 200 us -> 198 us (0.990)
    unnamed x62 -> x58, local copies, waits for them, and re-layouts: 9.99 us -> 9.22 us
  transfers between devices with their start and end apart: 37 -> 37, of which waited for: 13 -> 12; matrix products, arithmetic and copies ran while one was open for 4% -> 4% of each run, Pallas kernels for 26% -> 26%
where the time goes in v6:
time: 198 us; the launch traced here: 196 us
  Pallas kernels  64.9 us (33%)
  starting transfers between devices  57.9 us (29%)
  waiting for transfers between devices  41.6 us (21%)
  local copies, waits for them, and re-layouts  15.8 us (8%)
  blocking collectives  12.5 us (6%)
  between operations  2.02 us (1%)
    pallas_call x20, Pallas kernels, call(): pl.pallas_call(kernel, out_shape=tuple((space(out.shape, out.dtype) for s...  64.9 us
    all_to_all x5, starting transfers between devices, spread(): return lax.all_to_all(stats, AXES, 0, 0, tiled=True)  24.3 us
    ppermute x7, waiting for transfers between devices, step_of(): return lax.ppermute(send, 'maps', [(m, m ^ 1 << k) for m in range(n_maps)])  20.7 us
    all_to_all x5, waiting for transfers between devices, spread(): return lax.all_to_all(stats, AXES, 0, 0, tiled=True)  14.3 us
    all_to_all x1, blocking collectives, spread(): return lax.all_to_all(stats, AXES, 0, 0, tiled=True)  12.5 us
    ppermute x7, starting transfers between devices, step_of(): return lax.ppermute(send, 'maps', [(m, m ^ 1 << k) for m in range(n_maps)])  10.5 us
    unnamed x58, local copies, waits for them, and re-layouts  9.22 us
    ppermute x12, starting transfers between devices, trade(): lax.ppermute(shares[n], 'rows', [(i, i ^ n) for i in range(bands)])  7.84 us
  transfers between devices with their start and end apart: 37, of which 12 were waited for; matrix products, arithmetic and copies ran while one was open for 4% of the time, Pallas kernels for 26%

profile of v6, /device:TPU:0, one launch (start us, length us, event | category | flops | bytes accessed | tf_op | source)
XLA Modules:
  0.0 196.5 jit_solution(5004451819170956467)
XLA Ops:
  0.7 1.3 edges.1
  7.6 1.1 slice_bitcast_fusion.5.head_ref
  8.7 5.3 %first.1 = (f32[32,8,128]{2,1,0:T(8,128)}, f32[704,512]{1,0:T(8,128)S(1)}, bf16[384,512]{1,0:T(8,128)(2,1)}) custom-call(s32[8,128]{1,0:T(8,128)S(1)} %get-tuple-element.131.limits_ref, bf16[224,512]{1,0:T(8,128)(2,1)S(1)} %collective-permute-done.near_ref.near_hbm, bf16[384,512]{1,0:T(8,128)(2,1)S(1)} %get-tuple-element.134.x_ref, ...), custom_call_target="tpu_custom_call" | custom-call | flops 3321888768 | tf_op jit(solution)/shard_map/first/pallas_call | solution.py:705
  14.1 8.7 %all-to-all-start = ((f32[32,8,128]{2,1,0:T(8,128)}), f32[32,8,128]{2,1,0:T(8,128)S(1)}, u32[]{:S(2)}, u32[]{:S(2)}) async-start(f32[32,8,128]{2,1,0:T(8,128)} %get-tuple-element.141), calls=%async_computation | async-start | bytes 262144 | tf_op jit(solution)/shard_map/all_to_all | solution.py:749
  23.1 1.7 collective-permute-start.3
  24.8 1.1 slice_bitcast_fusion.4.head_ref
  25.9 5.2 %all-to-all-done.gathered_ref = f32[32,8,128]{2,1,0:T(8,128)S(1)} async-done(((f32[32,8,128]{2,1,0:T(8,128)}), f32[32,8,128]{2,1,0:T(8,128)S(1)}, u32[]{:S(2)}, u32[]{:S(2)}) %all-to-all-start) | async-done | bytes 131104 | tf_op jit(solution)/shard_map/all_to_all | solution.py:749
  31.0 4.3 %forward.2 = (f32[32,8,128]{2,1,0:T(8,128)S(1)}, f32[640,512]{1,0:T(8,128)S(1)}, f32[8,128]{1,0:T(8,128)S(1)}, bf16[384,512]{1,0:T(8,128)(2,1)}, f32[448,512]{1,0:T(8,128)}) custom-call(s32[8,128]{1,0:T(8,128)S(1)} %get-tuple-element.131.limits_ref, f32[32,8,128]{2,1,0:T(8,128)S(1)} %get-tuple-element.132.member_ref, ...), custom_call_target="tpu_custom_call" | custom-call | flops 3019898880 | tf_op jit(solution)/shard_map/forward/pallas_call | solution.py:705
  36.5 4.2 %all-to-all-start.1 = ((f32[32,8,128]{2,1,0:T(8,128)}), f32[32,8,128]{2,1,0:T(8,128)S(1)}, u32[]{:S(2)}, u32[]{:S(2)}) async-start(f32[32,8,128]{2,1,0:T(8,128)} %copy-done.10), calls=%async_computation.1 | async-start | bytes 262144 | tf_op jit(solution)/shard_map/all_to_all | solution.py:749
  41.1 1.7 collective-permute-start.5
  43.2 1.7 collective-permute-start.9
  44.9 1.1 slice_bitcast_fusion.3.head_ref
  46.0 3.0 %all-to-all-done.1.gathered_ref = f32[32,8,128]{2,1,0:T(8,128)S(1)} async-done(((f32[32,8,128]{2,1,0:T(8,128)}), f32[32,8,128]{2,1,0:T(8,128)S(1)}, u32[]{:S(2)}, u32[]{:S(2)}) %all-to-all-start.1) | async-done | bytes 131104 | tf_op jit(solution)/shard_map/all_to_all | solution.py:749
  49.0 4.0 %forward.3 = (f32[32,8,128]{2,1,0:T(8,128)S(1)}, f32[576,512]{1,0:T(8,128)S(1)}, f32[8,128]{1,0:T(8,128)S(1)}, bf16[384,512]{1,0:T(8,128)(2,1)}, f32[512,512]{1,0:T(8,128)}) custom-call(s32[8,128]{1,0:T(8,128)S(1)} %get-tuple-element.131.limits_ref, f32[32,8,128]{2,1,0:T(8,128)S(1)} %get-tuple-element.132.member_ref, ...), custom_call_target="tpu_custom_call" | custom-call | flops 2717908992 | tf_op jit(solution)/shard_map/forward/pallas_call | solution.py:705
  54.1 12.5 %all_to_all.40.gathered_ref = f32[32,8,128]{2,1,0:T(8,128)S(1)} all-to-all(f32[32,8,128]{2,1,0:T(8,128)S(1)} %get-tuple-element.154), channel_id=1, replica_groups=mesh['maps'=8,'rows'=4] {'maps','rows'}, dimensions={0} | all-to-all | bytes 262144 | tf_op jit(solution)/shard_map/all_to_all | solution.py:749
  66.6 2.9 %pool.1 = (f32[32,8,128]{2,1,0:T(8,128)}, f32[576,512]{1,0:T(8,128)S(1)}, bf16[576,512]{1,0:T(8,128)(2,1)S(1)}, f32[8,128]{1,0:T(8,128)S(1)}, bf16[864,128]{1,0:...) custom-call(s32[8,128]{1,0:T(8,128)S(1)} %get-tuple-element.131.limits_ref, ...), custom_call_target="tpu_custom_call" | custom-call | flops 603979776 | tf_op jit(solution)/shard_map/pool/pallas_call | solution.py:705
  69.6 3.8 %all-to-all-start.3 = ((f32[32,8,128]{2,1,0:T(8,128)}), f32[32,8,128]{2,1,0:T(8,128)S(1)}, u32[]{:S(2)}, u32[]{:S(2)}) async-start(f32[32,8,128]{2,1,0:T(8,128)} %get-tuple-element.164), calls=%async_computation.3 | async-start | bytes 262144 | tf_op jit(solution)/shard_map/all_to_all | solution.py:749
  73.5 1.7 collective-permute-start.15
  75.8 1.1 slice_bitcast_fusion.2.head_ref
  76.9 4.5 %all-to-all-done.3.gathered_ref = f32[32,8,128]{2,1,0:T(8,128)S(1)} async-done(((f32[32,8,128]{2,1,0:T(8,128)}), f32[32,8,128]{2,1,0:T(8,128)S(1)}, u32[]{:S(2)}, u32[]{:S(2)}) %all-to-all-start.3) | async-done | bytes 131104 | tf_op jit(solution)/shard_map/all_to_all | solution.py:749
  83.2 6.0 %backward.2 = (f32[32,8,128]{2,1,0:T(8,128)}, f32[512,512]{1,0:T(8,128)S(1)}, bf16[512,512]{1,0:T(8,128)(2,1)S(1)}, f32[8,128]{1,0:T(8,128)S(1)}, bf16[768,128]{...) custom-call(s32[8,128]{1,0:T(8,128)S(1)} %get-tuple-element.131.limits_ref, ...), custom_call_target="tpu_custom_call" | custom-call | flops 2415919104 | tf_op jit(solution)/shard_map/backward/pallas_call | solution.py:705
  90.0 2.6 %all-to-all-start.4 = ((f32[32,8,128]{2,1,0:T(8,128)}), f32[32,8,128]{2,1,0:T(8,128)S(1)}, u32[]{:S(2)}, u32[]{:S(2)}) async-start(f32[32,8,128]{2,1,0:T(8,128)} %get-tuple-element.178), calls=%async_computation.4 | async-start | bytes 262144 | tf_op jit(solution)/shard_map/all_to_all | solution.py:749
  92.8 1.7 collective-permute-start.18
  94.6 5.3 %weight_grad.3 = (f32[4,576,128]{2,1,0:T(8,128)}, bf16[4,576,128]{2,1,0:T(8,128)(2,1)}) custom-call(s32[8,128]{1,0:T(8,128)S(1)} %get-tuple-element.131.limits_ref, f32[32,8,128]{2,1,0:T(8,128)S(1)} %get-tuple-element.132.member_ref, f32[32,8,128]{2,1,0:T(8,128)S(1)} %all-to-all-done.3.gathered_ref, f32[8,128]{1,0:T(8,128)S(1)} %get-tuple-element.167.moments_ref, ...), custom_call_target="tpu_custom_call" | custom-call | flops 1811939328 | tf_op jit(solution)/shard_map/weight_grad/pallas_call | solution.py:705
  101.6 1.1 slice_bitcast_fusion.1.head_ref
  103.8 5.7 %backward.3 = (f32[32,8,128]{2,1,0:T(8,128)}, f32[448,512]{1,0:T(8,128)S(1)}, bf16[448,512]{1,0:T(8,128)(2,1)S(1)}, f32[8,128]{1,0:T(8,128)S(1)}, bf16[768,128]{...) custom-call(s32[8,128]{1,0:T(8,128)S(1)} %get-tuple-element.131.limits_ref, ...), custom_call_target="tpu_custom_call" | custom-call | flops 2113929216 | tf_op jit(solution)/shard_map/backward/pallas_call | solution.py:705
  110.3 5.0 %all-to-all-start.5 = ((f32[32,8,128]{2,1,0:T(8,128)}), f32[32,8,128]{2,1,0:T(8,128)S(1)}, u32[]{:S(2)}, u32[]{:S(2)}) async-start(f32[32,8,128]{2,1,0:T(8,128)} %get-tuple-element.198), calls=%async_computation.5 | async-start | bytes 262144 | tf_op jit(solution)/shard_map/all_to_all | solution.py:749
  115.4 1.7 collective-permute-start.22
  117.2 5.3 %weight_grad.4 = (f32[4,576,128]{2,1,0:T(8,128)}, bf16[4,576,128]{2,1,0:T(8,128)(2,1)}) custom-call(s32[8,128]{1,0:T(8,128)S(1)} %get-tuple-element.131.limits_ref, f32[32,8,128]{2,1,0:T(8,128)S(1)} %get-tuple-element.132.member_ref, f32[32,8,128]{2,1,0:T(8,128)S(1)} %all-to-all-done.4.gathered_ref, f32[8,128]{1,0:T(8,128)S(1)} %copy-done.13, ...), custom_call_target="tpu_custom_call" | custom-call | flops 1811939328 | tf_op jit(solution)/shard_map/weight_grad/pallas_call | solution.py:705
  124.2 2.1 %halve.4 = (f32[2,576,128]{2,1,0:T(8,128)}, bf16[2,576,128]{2,1,0:T(8,128)(2,1)}) custom-call(f32[4,576,128]{2,1,0:T(8,128)} %get-tuple-element.223.keep_hbm, bf16[4,576,128]{2,1,0:T(8,128)(2,1)S(1)} %collective-permute-done.20.received_ref), custom_call_target="tpu_custom_call" | custom-call | tf_op jit(solution)/shard_map/halve/pallas_call | solution.py:705
  126.3 1.5 collective-permute-start.24
  128.5 4.4 %weight_grad.5 = (f32[4,576,128]{2,1,0:T(8,128)S(1)}, bf16[4,576,128]{2,1,0:T(8,128)(2,1)S(1)}) custom-call(s32[8,128]{1,0:T(8,128)S(1)} %get-tuple-element.131.limits_ref, f32[32,8,128]{2,1,0:T(8,128)S(1)} %get-tuple-element.132.member_ref, f32[32,8,128]{2,1,0:T(8,128)S(1)} %all-to-all-done.5.gathered_ref, f32[8,128]{1,0:T(8,128)S(1)} %copy-done.15, ...), custom_call_target="tpu_custom_call" | custom-call | flops 1811939328 | tf_op jit(solution)/shard_map/weight_grad/pallas_call | solution.py:705
  134.0 1.7 collective-permute-done.24.received_ref
  136.6 3.1 %collective-permute-done.26.received_ref = bf16[4,576,128]{2,1,0:T(8,128)(2,1)S(1)} collective-permute-done((bf16[4,576,128]{2,1,0:T(8,128)(2,1)}, bf16[4,576,128]{2,1,0:T(8,128)(2,1)S(1)}, u32[]{:S(2)}, u32[]{:S(2)}) %collective-permute-start.26) | collective-permute-done | bytes 589856 | tf_op jit(solution)/shard_map/ppermute | solution.py:869
  139.6 2.1 %halve.5 = (f32[2,576,128]{2,1,0:T(8,128)}, bf16[2,576,128]{2,1,0:T(8,128)(2,1)}) custom-call(f32[4,576,128]{2,1,0:T(8,128)} %get-tuple-element.227.keep_hbm, bf16[4,576,128]{2,1,0:T(8,128)(2,1)S(1)} %collective-permute-done.26.received_ref), custom_call_target="tpu_custom_call" | custom-call | tf_op jit(solution)/shard_map/halve/pallas_call | solution.py:705
  142.7 1.8 halve.6
  144.6 2.5 %collective-permute-start.28 = (bf16[1,576,128]{2,1,0:T(8,128)(2,1)}, bf16[1,576,128]{2,1,0:T(8,128)(2,1)S(1)}, u32[]{:S(2)}, u32[]{:S(2)}) collective-permute-start(bf16[1,576,128]{2,1,0:T(8,128)(2,1)} %get-tuple-element.232), channel_id=1, source_target_pairs={{0,16},{4,20},{8,24},{12,28},{16,0},{20,4},{24,8},{28,12},{1,17},{... | collective-permute-start | bytes 442376 | tf_op jit(solution)/shard_map/ppermute | solution.py:869
  147.0 5.2 %collective-permute-done.28.last2_hbm = bf16[1,576,128]{2,1,0:T(8,128)(2,1)S(1)} collective-permute-done((bf16[1,576,128]{2,1,0:T(8,128)(2,1)}, bf16[1,576,128]{2,1,0:T(8,128)(2,1)S(1)}, u32[]{:S(2)}, u32[]{:S(2)}) %collective-permute-start.28) | collective-permute-done | bytes 147488 | tf_op jit(solution)/shard_map/ppermute | solution.py:869
  152.8 2.1 %add.3 = bf16[4,576,128]{2,1,0:T(8,128)(2,1)} custom-call(f32[4,576,128]{2,1,0:T(8,128)} %copy-done, bf16[4,576,128]{2,1,0:T(8,128)(2,1)S(1)} %collective-permute-done.25.received_ref), custom_call_target="tpu_custom_call" | custom-call | tf_op jit(solution)/shard_map/add/pallas_call | solution.py:705
  154.9 4.5 %all-to-all-start.6 = ((bf16[4,576,128]{2,1,0:T(8,128)(2,1)}), bf16[4,576,128]{2,1,0:T(8,128)(2,1)S(1)}, u32[]{:S(2)}, u32[]{:S(2)}) async-start(bf16[4,576,128]{2,1,0:T(8,128)(2,1)} %add.3), calls=%async_computation.6 | async-start | bytes 1179648 | tf_op jit(solution)/shard_map/all_to_all | solution.py:938
  160.5 1.8 halve.7
  162.4 3.0 %collective-permute-start.29 = (bf16[1,576,128]{2,1,0:T(8,128)(2,1)}, bf16[1,576,128]{2,1,0:T(8,128)(2,1)S(1)}, u32[]{:S(2)}, u32[]{:S(2)}) collective-permute-start(bf16[1,576,128]{2,1,0:T(8,128)(2,1)} %get-tuple-element.237), channel_id=1, source_target_pairs={{0,16},{4,20},{8,24},{12,28},{16,0},{20,4},{24,8},{28,12},{1,17},{... | collective-permute-start | bytes 442376 | tf_op jit(solution)/shard_map/ppermute | solution.py:869
  165.4 4.2 %last.1 = (bf16[384,512]{1,0:T(8,128)(2,1)}, f32[8,128]{1,0:T(8,128)S(1)}, bf16[384,128]{1,0:T(8,128)(2,1)}) custom-call(s32[8,128]{1,0:T(8,128)S(1)} %get-tuple-element.131.limits_ref, f32[32,8,128]{2,1,0:T(8,128)S(1)} %get-tuple-element.132.member_ref, f32[32,8,128]{2,1,0:T(8,128)S(1)} %all-to-all-done.5.gathered_ref, ...), custom_call_target="tpu_custom_call" | custom-call | flops 1811939328 | tf_op jit(solution)/shard_map/last/pallas_call | solution.py:705
  169.5 10.2 %collective-permute-done.29.last1_hbm = bf16[1,576,128]{2,1,0:T(8,128)(2,1)S(1)} collective-permute-done((bf16[1,576,128]{2,1,0:T(8,128)(2,1)}, bf16[1,576,128]{2,1,0:T(8,128)(2,1)S(1)}, u32[]{:S(2)}, u32[]{:S(2)}) %collective-permute-start.29) | collective-permute-done | bytes 147488 | tf_op jit(solution)/shard_map/ppermute | solution.py:869
  180.4 2.0 %squares.1 = (f32[32,1,128]{2,1,0:T(1,128)}, f32[3,576,128]{2,1,0:T(8,128)S(1)}, f32[3,2,512]{2,1,0:T(2,128)S(1)}) custom-call(bf16[4,576,128]{2,1,0:T(8,128)(2,1)S(1)} %all-to-all-done.6.received_ref, f32[1,576,128]{2,1,0:T(8,128)} %get-tuple-element.236.keep1_hbm, bf16[1,576,128]{2,1,0:T(8,128)(2,1)} %copy-done.22, ...), custom_call_target="tpu_custom_call" | custom-call | tf_op jit(solution)/shard_map/squares/pallas_call | solution.py:705
  182.3 4.0 %all-to-all-start.7 = ((f32[32,1,128]{2,1,0:T(1,128)}), f32[32,1,128]{2,1,0:T(1,128)S(1)}, u32[]{:S(2)}, u32[]{:S(2)}) async-start(f32[32,1,128]{2,1,0:T(1,128)} %get-tuple-element.243), calls=%async_computation.7 | async-start | bytes 32768 | tf_op jit(solution)/shard_map/all_to_all | solution.py:956
  187.0 6.4 %all-to-all-done.7.every_ref = f32[32,1,128]{2,1,0:T(1,128)S(1)} async-done(((f32[32,1,128]{2,1,0:T(1,128)}), f32[32,1,128]{2,1,0:T(1,128)S(1)}, u32[]{:S(2)}, u32[]{:S(2)}) %all-to-all-start.7) | async-done | bytes 16416 | tf_op jit(solution)/shard_map/all_to_all | solution.py:956
  193.4 2.9 %adam.1 = (f32[1,128]{1,0:T(1,128)}, f32[3,576,128]{2,1,0:T(8,128)}, f32[3,576,128]{2,1,0:T(8,128)}, f32[3,576,128]{2,1,0:T(8,128)}, f32[3,2,512]{2,1,0:T(2,128)...) custom-call(f32[32,1,128]{2,1,0:T(1,128)S(1)} %all-to-all-done.7.every_ref, s32[1]{0:T(128)S(6)} %copy.24.step_ref, ...), custom_call_target="tpu_custom_call" | custom-call | tf_op jit(solution)/shard_map/adam/pallas_call | solution.py:705
  (115 shorter events, 23.9 us)
Async XLA Ops:
  0.6 30.4 %copy-start.3 = (f32[2,3,512]{2,0,1:T(2,128)S(1)}, f32[2,3,512]{2,0,1:T(2,128)}, u32[]{:S(2)}) copy-start(f32[2,3,512]{2,0,1:T(2,128)} %param.16) | copy-start | bytes 36868
  2.0 6.7 %collective-permute-start = (bf16[224,512]{1,0:T(8,128)(2,1)S(1)}, bf16[224,512]{1,0:T(8,128)(2,1)S(1)}, u32[]{:S(2)}, u32[]{:S(2)}) collective-permute-start(bf16[224,512]{1,0:T(8,128)(2,1)S(1)} %get-tuple-element.133), channel_id=1, source_target_pairs={{0,1},{1,0},{2,3},{3,2},{4,5},{5,4},{6,7},{7,6},{8,9},{9,8},{10,11... | collective-permute-start | bytes 688136 | tf_op jit(solution)/shard_map/ppermute | solution.py:757
  2.5 6.2 %collective-permute-start.1 = (bf16[224,512]{1,0:T(8,128)(2,1)S(1)}, bf16[224,512]{1,0:T(8,128)(2,1)S(1)}, u32[]{:S(2)}, u32[]{:S(2)}) collective-permute-start(bf16[224,512]{1,0:T(8,128)(2,1)S(1)} %get-tuple-element.135), channel_id=1, source_target_pairs={{2,1},{1,2},{6,5},{5,6},{10,9},{9,10},{14,13},{13,14},{18,17},{17,... | collective-permute-start | bytes 688136 | tf_op jit(solution)/shard_map/ppermute | solution.py:766
  8.7 14.4 %copy-start.1 = (bf16[224,512]{1,0:T(8,128)(2,1)}, bf16[224,512]{1,0:T(8,128)(2,1)S(1)}, u32[]{:S(2)}) copy-start(bf16[224,512]{1,0:T(8,128)(2,1)S(1)} %collective-permute-done.near_ref.near_hbm) | copy-start | bytes 688132
  8.7 14.4 %copy-start.2 = (bf16[224,512]{1,0:T(8,128)(2,1)}, bf16[224,512]{1,0:T(8,128)(2,1)S(1)}, u32[]{:S(2)}) copy-start(bf16[224,512]{1,0:T(8,128)(2,1)S(1)} %collective-permute-done.1.far_ref.far_hbm) | copy-start | bytes 688132
  14.1 17.0 %all-to-all-start = ((f32[32,8,128]{2,1,0:T(8,128)}), f32[32,8,128]{2,1,0:T(8,128)S(1)}, u32[]{:S(2)}, u32[]{:S(2)}) async-start(f32[32,8,128]{2,1,0:T(8,128)} %get-tuple-element.141), calls=%async_computation | async-start | bytes 262144 | tf_op jit(solution)/shard_map/all_to_all | solution.py:749
  22.8 13.1 %collective-permute-start.2 = (bf16[384,512]{1,0:T(8,128)(2,1)}, bf16[384,512]{1,0:T(8,128)(2,1)}, u32[]{:S(2)}, u32[]{:S(2)}) collective-permute-start(bf16[384,512]{1,0:T(8,128)(2,1)} %get-tuple-element.218.rest_4_), channel_id=1, source_target_pairs={{0,1},{1,0},{2,3},{3,2},{4,5},{5,4},{6,7},{7,6},{8,9},{9,8},{10,11... | collective-permute-start | bytes 1179656 | tf_op jit(solution)/shard_map/ppermute | solution.py:757
  23.1 12.8 %collective-permute-start.3 = (bf16[384,512]{1,0:T(8,128)(2,1)}, bf16[384,512]{1,0:T(8,128)(2,1)}, u32[]{:S(2)}, u32[]{:S(2)}) collective-permute-start(bf16[384,512]{1,0:T(8,128)(2,1)} %get-tuple-element.218.rest_4_), channel_id=1, source_target_pairs={{0,2},{1,3},{2,0},{3,1},{4,6},{5,7},{6,4},{7,5},{8,10},{9,11},{10,... | collective-permute-start | bytes 1179656 | tf_op jit(solution)/shard_map/ppermute | solution.py:757
  36.5 12.5 %all-to-all-start.1 = ((f32[32,8,128]{2,1,0:T(8,128)}), f32[32,8,128]{2,1,0:T(8,128)S(1)}, u32[]{:S(2)}, u32[]{:S(2)}) async-start(f32[32,8,128]{2,1,0:T(8,128)} %copy-done.10), calls=%async_computation.1 | async-start | bytes 262144 | tf_op jit(solution)/shard_map/all_to_all | solution.py:749
  40.8 12.2 %collective-permute-start.4 = (bf16[160,128]{1,0:T(8,128)(2,1)}, bf16[160,128]{1,0:T(8,128)(2,1)S(1)}, u32[]{:S(2)}, u32[]{:S(2)}) collective-permute-start(bf16[160,128]{1,0:T(8,128)(2,1)} %get-tuple-element.151), channel_id=1, source_target_pairs={{0,1},{1,0},{2,3},{3,2},{4,5},{5,4},{6,7},{7,6},{8,9},{9,8},{10,11... | collective-permute-start | bytes 122888 | tf_op jit(solution)/shard_map/ppermute | solution.py:753
  41.1 12.2 %collective-permute-start.5 = (bf16[160,128]{1,0:T(8,128)(2,1)}, bf16[160,128]{1,0:T(8,128)(2,1)S(1)}, u32[]{:S(2)}, u32[]{:S(2)}) collective-permute-start(bf16[160,128]{1,0:T(8,128)(2,1)} %get-tuple-element.152), channel_id=1, source_target_pairs={{0,2},{1,3},{2,0},{3,1},{4,6},{5,7},{6,4},{7,5},{8,10},{9,11},{10,... | collective-permute-start | bytes 122888 | tf_op jit(solution)/shard_map/ppermute | solution.py:753
  42.8 10.8 %collective-permute-start.6 = (bf16[160,128]{1,0:T(8,128)(2,1)}, bf16[160,128]{1,0:T(8,128)(2,1)S(1)}, u32[]{:S(2)}, u32[]{:S(2)}) collective-permute-start(bf16[160,128]{1,0:T(8,128)(2,1)} %get-tuple-element.153), channel_id=1, source_target_pairs={{0,3},{1,2},{2,1},{3,0},{4,7},{5,6},{6,5},{7,4},{8,11},{9,10},{10,... | collective-permute-start | bytes 122888 | tf_op jit(solution)/shard_map/ppermute | solution.py:753
  42.8 26.8 %collective-permute-start.8 = (bf16[384,512]{1,0:T(8,128)(2,1)}, bf16[384,512]{1,0:T(8,128)(2,1)}, u32[]{:S(2)}, u32[]{:S(2)}) collective-permute-start(bf16[384,512]{1,0:T(8,128)(2,1)} %get-tuple-element.203.rest_4_), channel_id=1, source_target_pairs={{0,1},{1,0},{2,3},{3,2},{4,5},{5,4},{6,7},{7,6},{8,9},{9,8},{10,11... | collective-permute-start | bytes 1179656 | tf_op jit(solution)/shard_map/ppermute | solution.py:757
  43.2 26.3 %collective-permute-start.9 = (bf16[384,512]{1,0:T(8,128)(2,1)}, bf16[384,512]{1,0:T(8,128)(2,1)}, u32[]{:S(2)}, u32[]{:S(2)}) collective-permute-start(bf16[384,512]{1,0:T(8,128)(2,1)} %get-tuple-element.203.rest_4_), channel_id=1, source_target_pairs={{0,2},{1,3},{2,0},{3,1},{4,6},{5,7},{6,4},{7,5},{8,10},{9,11},{10,... | collective-permute-start | bytes 1179656 | tf_op jit(solution)/shard_map/ppermute | solution.py:757
  53.0 16.5 %copy-start.11 = (f32[8,128]{1,0:T(8,128)}, f32[8,128]{1,0:T(8,128)S(1)}, u32[]{:S(2)}) copy-start(f32[8,128]{1,0:T(8,128)S(1)} %get-tuple-element.170.moments_below_ref.moments_ref) | copy-start | bytes 12292
  53.0 13.6 %copy-start.23 = (bf16[160,128]{1,0:T(8,128)(2,1)}, bf16[160,128]{1,0:T(8,128)(2,1)S(1)}, u32[]{:S(2)}) copy-start(bf16[160,128]{1,0:T(8,128)(2,1)S(1)} %collective-permute-done.4.rest_1_) | copy-start | bytes 122884
  53.0 16.5 %collective-permute-start.7 = (bf16[384,512]{1,0:T(8,128)(2,1)}, bf16[384,512]{1,0:T(8,128)(2,1)S(1)}, u32[]{:S(2)}, u32[]{:S(2)}) collective-permute-start(bf16[384,512]{1,0:T(8,128)(2,1)} %collective-permute-done.3.rest_6_), channel_id=1, source_target_pairs={{0,1},{1,0},{2,3},{3,2},{4,5},{5,4},{6,7},{7,6},{8,9},{9,8},{10,11... | collective-permute-start | bytes 1179656 | tf_op jit(solution)/shard_map/ppermute | solution.py:757
  53.3 16.3 %collective-permute-start.10 = (bf16[384,512]{1,0:T(8,128)(2,1)}, bf16[384,512]{1,0:T(8,128)(2,1)S(1)}, u32[]{:S(2)}, u32[]{:S(2)}) collective-permute-start(bf16[384,512]{1,0:T(8,128)(2,1)} %get-tuple-element.183.rest_4_), channel_id=1, source_target_pairs={{0,1},{1,0},{2,3},{3,2},{4,5},{5,4},{6,7},{7,6},{8,9},{9,8},{10,11... | collective-permute-start | bytes 1179656 | tf_op jit(solution)/shard_map/ppermute | solution.py:757
  53.6 16.0 %collective-permute-start.11 = (bf16[384,512]{1,0:T(8,128)(2,1)}, bf16[384,512]{1,0:T(8,128)(2,1)}, u32[]{:S(2)}, u32[]{:S(2)}) collective-permute-start(bf16[384,512]{1,0:T(8,128)(2,1)} %get-tuple-element.183.rest_4_), channel_id=1, source_target_pairs={{0,2},{1,3},{2,0},{3,1},{4,6},{5,7},{6,4},{7,5},{8,10},{9,11},{10,... | collective-permute-start | bytes 1179656 | tf_op jit(solution)/shard_map/ppermute | solution.py:757
  66.6 36.1 %copy-start.15 = (f32[8,128]{1,0:T(8,128)S(1)}, f32[8,128]{1,0:T(8,128)}, u32[]{:S(2)}) copy-start(f32[8,128]{1,0:T(8,128)} %copy-done.14) | copy-start | bytes 12292
  69.5 33.2 %copy-start.13 = (f32[8,128]{1,0:T(8,128)S(1)}, f32[8,128]{1,0:T(8,128)}, u32[]{:S(2)}) copy-start(f32[8,128]{1,0:T(8,128)} %copy-done.11) | copy-start | bytes 12292
  69.6 11.8 %all-to-all-start.3 = ((f32[32,8,128]{2,1,0:T(8,128)}), f32[32,8,128]{2,1,0:T(8,128)S(1)}, u32[]{:S(2)}, u32[]{:S(2)}) async-start(f32[32,8,128]{2,1,0:T(8,128)} %get-tuple-element.164), calls=%async_computation.3 | async-start | bytes 262144 | tf_op jit(solution)/shard_map/all_to_all | solution.py:749
  73.4 16.6 %collective-permute-start.14 = (bf16[864,128]{1,0:T(8,128)(2,1)}, bf16[864,128]{1,0:T(8,128)(2,1)S(1)}, u32[]{:S(2)}, u32[]{:S(2)}) collective-permute-start(bf16[864,128]{1,0:T(8,128)(2,1)} %get-tuple-element.175), channel_id=1, source_target_pairs={{0,1},{1,0},{2,3},{3,2},{4,5},{5,4},{6,7},{7,6},{8,9},{9,8},{10,11... | collective-permute-start | bytes 663560 | tf_op jit(solution)/shard_map/ppermute | solution.py:753
  73.5 16.5 %collective-permute-start.15 = (bf16[864,128]{1,0:T(8,128)(2,1)}, bf16[864,128]{1,0:T(8,128)(2,1)}, u32[]{:S(2)}, u32[]{:S(2)}) collective-permute-start(bf16[864,128]{1,0:T(8,128)(2,1)} %get-tuple-element.176), channel_id=1, source_target_pairs={{0,2},{1,3},{2,0},{3,1},{4,6},{5,7},{6,4},{7,5},{8,10},{9,11},{10,... | collective-permute-start | bytes 663560 | tf_op jit(solution)/shard_map/ppermute | solution.py:753
  75.2 14.8 %collective-permute-start.16 = (bf16[864,128]{1,0:T(8,128)(2,1)}, bf16[864,128]{1,0:T(8,128)(2,1)}, u32[]{:S(2)}, u32[]{:S(2)}) collective-permute-start(bf16[864,128]{1,0:T(8,128)(2,1)} %get-tuple-element.177), channel_id=1, source_target_pairs={{0,3},{1,2},{2,1},{3,0},{4,7},{5,6},{6,5},{7,4},{8,11},{9,10},{10,... | collective-permute-start | bytes 663560 | tf_op jit(solution)/shard_map/ppermute | solution.py:753
  75.3 14.7 %collective-permute-start.12 = (bf16[384,512]{1,0:T(8,128)(2,1)}, bf16[384,512]{1,0:T(8,128)(2,1)}, u32[]{:S(2)}, u32[]{:S(2)}) collective-permute-start(bf16[384,512]{1,0:T(8,128)(2,1)} %collective-permute-done.9.rest_6_), channel_id=1, source_target_pairs={{0,1},{1,0},{2,3},{3,2},{4,5},{5,4},{6,7},{7,6},{8,9},{9,8},{10,11... | collective-permute-start | bytes 1179656 | tf_op jit(solution)/shard_map/ppermute | solution.py:757
  75.7 14.4 %collective-permute-start.13 = (bf16[384,512]{1,0:T(8,128)(2,1)}, bf16[384,512]{1,0:T(8,128)(2,1)}, u32[]{:S(2)}, u32[]{:S(2)}) collective-permute-start(bf16[384,512]{1,0:T(8,128)(2,1)} %collective-permute-done.11.rest_6_), channel_id=1, source_target_pairs={{0,1},{1,0},{2,3},{3,2},{4,5},{5,4},{6,7},{7,6},{8,9},{9,8},{10,11... | collective-permute-start | bytes 1179656 | tf_op jit(solution)/shard_map/ppermute | solution.py:757
  90.0 10.8 %all-to-all-start.4 = ((f32[32,8,128]{2,1,0:T(8,128)}), f32[32,8,128]{2,1,0:T(8,128)S(1)}, u32[]{:S(2)}, u32[]{:S(2)}) async-start(f32[32,8,128]{2,1,0:T(8,128)} %get-tuple-element.178), calls=%async_computation.4 | async-start | bytes 262144 | tf_op jit(solution)/shard_map/all_to_all | solution.py:749
  92.6 17.6 %collective-permute-start.17 = (bf16[768,128]{1,0:T(8,128)(2,1)}, bf16[768,128]{1,0:T(8,128)(2,1)}, u32[]{:S(2)}, u32[]{:S(2)}) collective-permute-start(bf16[768,128]{1,0:T(8,128)(2,1)} %get-tuple-element.195), channel_id=1, source_target_pairs={{0,1},{1,0},{2,3},{3,2},{4,5},{5,4},{6,7},{7,6},{8,9},{9,8},{10,11... | collective-permute-start | bytes 589832 | tf_op jit(solution)/shard_map/ppermute | solution.py:753
  92.8 17.5 %collective-permute-start.18 = (bf16[768,128]{1,0:T(8,128)(2,1)}, bf16[768,128]{1,0:T(8,128)(2,1)}, u32[]{:S(2)}, u32[]{:S(2)}) collective-permute-start(bf16[768,128]{1,0:T(8,128)(2,1)} %get-tuple-element.196), channel_id=1, source_target_pairs={{0,2},{1,3},{2,0},{3,1},{4,6},{5,7},{6,4},{7,5},{8,10},{9,11},{10,... | collective-permute-start | bytes 589832 | tf_op jit(solution)/shard_map/ppermute | solution.py:753
  94.5 15.8 %collective-permute-start.19 = (bf16[768,128]{1,0:T(8,128)(2,1)}, bf16[768,128]{1,0:T(8,128)(2,1)}, u32[]{:S(2)}, u32[]{:S(2)}) collective-permute-start(bf16[768,128]{1,0:T(8,128)(2,1)} %get-tuple-element.197), channel_id=1, source_target_pairs={{0,3},{1,2},{2,1},{3,0},{4,7},{5,6},{6,5},{7,4},{8,11},{9,10},{10,... | collective-permute-start | bytes 589832 | tf_op jit(solution)/shard_map/ppermute | solution.py:753
  100.9 22.4 %collective-permute-start.20 = (bf16[4,576,128]{2,1,0:T(8,128)(2,1)}, bf16[4,576,128]{2,1,0:T(8,128)(2,1)S(1)}, u32[]{:S(2)}, u32[]{:S(2)}) collective-permute-start(bf16[4,576,128]{2,1,0:T(8,128)(2,1)} %get-tuple-element.207), channel_id=1, source_target_pairs={{0,4},{4,0},{8,12},{12,8},{16,20},{20,16},{24,28},{28,24},{1,5},{5... | collective-permute-start | bytes 1769480 | tf_op jit(solution)/shard_map/ppermute | solution.py:869
  110.3 55.1 %copy-start.9 = (bf16[448,512]{1,0:T(8,128)(2,1)S(1)}, bf16[448,512]{1,0:T(8,128)(2,1)}, u32[]{:S(2)}) copy-start(bf16[448,512]{1,0:T(8,128)(2,1)} %copy-done.8) | copy-start | bytes 1376260
  110.3 13.0 %all-to-all-start.5 = ((f32[32,8,128]{2,1,0:T(8,128)}), f32[32,8,128]{2,1,0:T(8,128)S(1)}, u32[]{:S(2)}, u32[]{:S(2)}) async-start(f32[32,8,128]{2,1,0:T(8,128)} %get-tuple-element.198), calls=%async_computation.5 | async-start | bytes 262144 | tf_op jit(solution)/shard_map/all_to_all | solution.py:749
  115.3 12.6 %collective-permute-start.21 = (bf16[768,128]{1,0:T(8,128)(2,1)}, bf16[768,128]{1,0:T(8,128)(2,1)S(1)}, u32[]{:S(2)}, u32[]{:S(2)}) collective-permute-start(bf16[768,128]{1,0:T(8,128)(2,1)} %get-tuple-element.215), channel_id=1, source_target_pairs={{0,1},{1,0},{2,3},{3,2},{4,5},{5,4},{6,7},{7,6},{8,9},{9,8},{10,11... | collective-permute-start | bytes 589832 | tf_op jit(solution)/shard_map/ppermute | solution.py:753
  115.4 12.5 %collective-permute-start.22 = (bf16[768,128]{1,0:T(8,128)(2,1)}, bf16[768,128]{1,0:T(8,128)(2,1)}, u32[]{:S(2)}, u32[]{:S(2)}) collective-permute-start(bf16[768,128]{1,0:T(8,128)(2,1)} %get-tuple-element.216), channel_id=1, source_target_pairs={{0,2},{1,3},{2,0},{3,1},{4,6},{5,7},{6,4},{7,5},{8,10},{9,11},{10,... | collective-permute-start | bytes 589832 | tf_op jit(solution)/shard_map/ppermute | solution.py:753
  117.0 10.9 %collective-permute-start.23 = (bf16[768,128]{1,0:T(8,128)(2,1)}, bf16[768,128]{1,0:T(8,128)(2,1)}, u32[]{:S(2)}, u32[]{:S(2)}) collective-permute-start(bf16[768,128]{1,0:T(8,128)(2,1)} %get-tuple-element.217), channel_id=1, source_target_pairs={{0,3},{1,2},{2,1},{3,0},{4,7},{5,6},{6,5},{7,4},{8,11},{9,10},{10,... | collective-permute-start | bytes 589832 | tf_op jit(solution)/shard_map/ppermute | solution.py:753
  123.3 16.4 %collective-permute-start.26 = (bf16[4,576,128]{2,1,0:T(8,128)(2,1)}, bf16[4,576,128]{2,1,0:T(8,128)(2,1)S(1)}, u32[]{:S(2)}, u32[]{:S(2)}) collective-permute-start(bf16[4,576,128]{2,1,0:T(8,128)(2,1)} %get-tuple-element.228), channel_id=1, source_target_pairs={{0,4},{4,0},{8,12},{12,8},{16,20},{20,16},{24,28},{28,24},{1,5},{5... | collective-permute-start | bytes 1769480 | tf_op jit(solution)/shard_map/ppermute | solution.py:869
  126.3 9.4 %collective-permute-start.24 = (bf16[2,576,128]{2,1,0:T(8,128)(2,1)}, bf16[2,576,128]{2,1,0:T(8,128)(2,1)S(1)}, u32[]{:S(2)}, u32[]{:S(2)}) collective-permute-start(bf16[2,576,128]{2,1,0:T(8,128)(2,1)} %get-tuple-element.225), channel_id=1, source_target_pairs={{0,8},{4,12},{8,0},{12,4},{16,24},{20,28},{24,16},{28,20},{1,9},{5... | collective-permute-start | bytes 884744 | tf_op jit(solution)/shard_map/ppermute | solution.py:869
  134.0 59.4 %copy-start.16 = (f32[2,3,512]{2,0,1:T(2,128)S(1)}, f32[2,3,512]{2,0,1:T(2,128)}, u32[]{:S(2)}) copy-start(f32[2,3,512]{2,0,1:T(2,128)} %param.26) | copy-start | bytes 36868
  134.0 59.4 %copy-start.17 = (f32[2,3,512]{2,0,1:T(2,128)S(1)}, f32[2,3,512]{2,0,1:T(2,128)}, u32[]{:S(2)}) copy-start(f32[2,3,512]{2,0,1:T(2,128)} %param.27) | copy-start | bytes 36868
  135.7 17.1 %collective-permute-start.25 = (bf16[4,576,128]{2,1,0:T(8,128)(2,1)S(1)}, bf16[4,576,128]{2,1,0:T(8,128)(2,1)S(1)}, u32[]{:S(2)}, u32[]{:S(2)}) collective-permute-start(bf16[4,576,128]{2,1,0:T(8,128)(2,1)S(1)} %get-tuple-element.226), channel_id=1, source_target_pairs={{0,4},{4,0},{8,12},{12,8},{16,20},{20,16},{24,28},{28,24},{1,5},{5... | collective-permute-start | bytes 1769480 | tf_op jit(solution)/shard_map/ppermute | solution.py:869
  141.8 11.0 %collective-permute-start.27 = (bf16[2,576,128]{2,1,0:T(8,128)(2,1)}, bf16[2,576,128]{2,1,0:T(8,128)(2,1)S(1)}, u32[]{:S(2)}, u32[]{:S(2)}) collective-permute-start(bf16[2,576,128]{2,1,0:T(8,128)(2,1)} %get-tuple-element.229), channel_id=1, source_target_pairs={{0,8},{4,12},{8,0},{12,4},{16,24},{20,28},{24,16},{28,20},{1,9},{5... | collective-permute-start | bytes 884744 | tf_op jit(solution)/shard_map/ppermute | solution.py:869
  144.6 7.6 %collective-permute-start.28 = (bf16[1,576,128]{2,1,0:T(8,128)(2,1)}, bf16[1,576,128]{2,1,0:T(8,128)(2,1)S(1)}, u32[]{:S(2)}, u32[]{:S(2)}) collective-permute-start(bf16[1,576,128]{2,1,0:T(8,128)(2,1)} %get-tuple-element.232), channel_id=1, source_target_pairs={{0,16},{4,20},{8,24},{12,28},{16,0},{20,4},{24,8},{28,12},{1,17},{... | collective-permute-start | bytes 442376 | tf_op jit(solution)/shard_map/ppermute | solution.py:869
  152.2 27.5 %copy-start.21 = (bf16[1,576,128]{2,1,0:T(8,128)(2,1)}, bf16[1,576,128]{2,1,0:T(8,128)(2,1)S(1)}, u32[]{:S(2)}) copy-start(bf16[1,576,128]{2,1,0:T(8,128)(2,1)S(1)} %collective-permute-done.28.last2_hbm) | copy-start | bytes 442372
  154.9 24.8 %all-to-all-start.6 = ((bf16[4,576,128]{2,1,0:T(8,128)(2,1)}), bf16[4,576,128]{2,1,0:T(8,128)(2,1)S(1)}, u32[]{:S(2)}, u32[]{:S(2)}) async-start(bf16[4,576,128]{2,1,0:T(8,128)(2,1)} %add.3), calls=%async_computation.6 | async-start | bytes 1179648 | tf_op jit(solution)/shard_map/all_to_all | solution.py:938
  162.4 17.3 %collective-permute-start.29 = (bf16[1,576,128]{2,1,0:T(8,128)(2,1)}, bf16[1,576,128]{2,1,0:T(8,128)(2,1)S(1)}, u32[]{:S(2)}, u32[]{:S(2)}) collective-permute-start(bf16[1,576,128]{2,1,0:T(8,128)(2,1)} %get-tuple-element.237), channel_id=1, source_target_pairs={{0,16},{4,20},{8,24},{12,28},{16,0},{20,4},{24,8},{28,12},{1,17},{... | collective-permute-start | bytes 442376 | tf_op jit(solution)/shard_map/ppermute | solution.py:869
  182.3 11.0 %all-to-all-start.7 = ((f32[32,1,128]{2,1,0:T(1,128)}), f32[32,1,128]{2,1,0:T(1,128)S(1)}, u32[]{:S(2)}, u32[]{:S(2)}) async-start(f32[32,1,128]{2,1,0:T(1,128)} %get-tuple-element.243), calls=%async_computation.7 | async-start | bytes 32768 | tf_op jit(solution)/shard_map/all_to_all | solution.py:956
  (18 other events, 70.0 us)

commit v7 on v6

--- a/solution.py
+++ b/solution.py
@@ -648,7 +648,7 @@
     squares_ref[...] = jnp.broadcast_to(total[None], squares_ref.shape)
 
 
-def kernel_adam(sz, rate, every_ref, step_ref, shard_ref, master_hbm, first_hbm, second_hbm, norm_grad_ref, norm_ref,
+def kernel_adam(sz, rate, every_ref, step_ref, shard_ref, master_hbm, first_old_ref, second_old_ref, norm_grad_ref, norm_ref,
                 norm_first_ref, norm_second_ref, total_hbm, first_out_hbm, second_out_hbm, master_out_hbm,
                 norm_first_hbm, norm_second_hbm, norm_hbm,
                 total_ref, master_ref, first_ref, second_ref, small_ref, sems):
@@ -656,7 +656,7 @@
     loads = [
         [
             copies.start(source.at[layer], target.at[layer])
-            for source, target in ((master_hbm, master_ref), (first_hbm, first_ref), (second_hbm, second_ref))
+            for source, target in ((master_hbm, master_ref),)
         ]
         for layer in range(3)
     ]
@@ -672,7 +672,7 @@
     for layer in range(3):
         wait(*loads[layer])
         first_ref[layer], second_ref[layer], master_ref[layer] = adam(
-            master_ref[layer], shard_ref[layer], first_ref[layer], second_ref[layer], rate, weight_decay,
+            master_ref[layer], shard_ref[layer], first_old_ref[layer], second_old_ref[layer], rate, weight_decay,
             scale, first_fix, second_fix,
         )
         for source, target in (
@@ -922,8 +922,8 @@
 
     arrived2 = step_of(send2, 1)
     keep0, send0 = weight_grad(0, gathered, exchanged, (0, sz.pixels))
-    send0, arrived2 = tie((send0, arrived2))
     arrived0 = step_of(send0, 0)
+    arrived1, arrived2 = tie((arrived1, arrived2))
     keep1, send1 = halved(keep1, arrived1)
     keep2, send2 = halved(keep2, arrived2)
     arrived1 = step_of(send1, 1)
@@ -962,7 +962,7 @@
         + [v.reshape(3, share, q) for v in (conv_master, conv_moment1, conv_moment2)]
         + [norm_grad, norms, norm_first, norm_second],
         [pltpu.VMEM((1, 128), F32)] + [part_space(3, F32)] * 3 + [pltpu.VMEM((3, 3, 2, c), F32)],
-        hbm_ins=(3, 4, 5), hbm_outs=range(7), smem_ins=(1,), sems=22,
+        hbm_ins=(3,), hbm_outs=range(7), smem_ins=(1,), sems=16,
     )
     return (
         pooled.reshape(1, sz.height // 2, half, q),

time: 198 us -> 203 us (1.025)
  local copies, waits for them, and re-layouts: 15.8 us -> 24.2 us
  waiting for transfers between devices: 41.6 us -> 38.7 us
    unnamed x58 -> x90, local copies, waits for them, and re-layouts: 9.22 us -> 17.6 us
    ppermute x7, waiting for transfers between devices: 20.7 us -> 17.8 us  [step_of(): return lax.ppermute(send, 'maps', [(m, m ^ 1 << k) for m in range(n_maps)])]
  transfers between devices with their start and end apart: 37 -> 37, of which waited for: 12 -> 12; matrix products, arithmetic and copies ran while one was open for 4% -> 4% of each run, Pallas kernels for 26% -> 25%
where the time goes in v7:
time: 203 us; the launch traced here: 201 us
  Pallas kernels  64 us (32%)
  starting transfers between devices  58.1 us (29%)
  waiting for transfers between devices  38.7 us (19%)
  local copies, waits for them, and re-layouts  24.2 us (12%)
  blocking collectives  12.5 us (6%)
  between operations  2.1 us (1%)
    pallas_call x20, Pallas kernels, call(): pl.pallas_call(kernel, out_shape=tuple((space(out.shape, out.dtype) for s...  64 us
    all_to_all x5, starting transfers between devices, spread(): return lax.all_to_all(stats, AXES, 0, 0, tiled=True)  24.2 us
    ppermute x7, waiting for transfers between devices, step_of(): return lax.ppermute(send, 'maps', [(m, m ^ 1 << k) for m in range(n_maps)])  17.8 us
    unnamed x90, local copies, waits for them, and re-layouts  17.6 us
    all_to_all x5, waiting for transfers between devices, spread(): return lax.all_to_all(stats, AXES, 0, 0, tiled=True)  14.3 us
    all_to_all x1, blocking collectives, spread(): return lax.all_to_all(stats, AXES, 0, 0, tiled=True)  12.5 us
    ppermute x7, starting transfers between devices, step_of(): return lax.ppermute(send, 'maps', [(m, m ^ 1 << k) for m in range(n_maps)])  11 us
    ppermute x12, starting transfers between devices, trade(): lax.ppermute(shares[n], 'rows', [(i, i ^ n) for i in range(bands)])  7.84 us
  transfers between devices with their start and end apart: 37, of which 12 were waited for; matrix products, arithmetic and copies ran while one was open for 4% of the time, Pallas kernels for 25%

profile of v7, /device:TPU:0, one launch (start us, length us, event | category | flops | bytes accessed | tf_op | source)
XLA Modules:
  0.0 201.2 jit_solution(11842871450938811056)
XLA Ops:
  0.7 1.3 edges.1
  7.6 1.1 slice_bitcast_fusion.5.head_ref
  8.7 5.3 %first.1 = (f32[32,8,128]{2,1,0:T(8,128)}, f32[704,512]{1,0:T(8,128)S(1)}, bf16[384,512]{1,0:T(8,128)(2,1)}) custom-call(s32[8,128]{1,0:T(8,128)S(1)} %get-tuple-element.131.limits_ref, bf16[224,512]{1,0:T(8,128)(2,1)S(1)} %collective-permute-done.near_ref.near_hbm, bf16[384,512]{1,0:T(8,128)(2,1)S(1)} %get-tuple-element.134.x_ref, ...), custom_call_target="tpu_custom_call" | custom-call | flops 3321888768 | tf_op jit(solution)/shard_map/first/pallas_call | solution.py:705
  14.1 8.7 %all-to-all-start = ((f32[32,8,128]{2,1,0:T(8,128)}), f32[32,8,128]{2,1,0:T(8,128)S(1)}, u32[]{:S(2)}, u32[]{:S(2)}) async-start(f32[32,8,128]{2,1,0:T(8,128)} %get-tuple-element.141), calls=%async_computation | async-start | bytes 262144 | tf_op jit(solution)/shard_map/all_to_all | solution.py:749
  23.1 1.7 collective-permute-start.3
  24.8 1.1 slice_bitcast_fusion.4.head_ref
  25.9 5.2 %all-to-all-done.gathered_ref = f32[32,8,128]{2,1,0:T(8,128)S(1)} async-done(((f32[32,8,128]{2,1,0:T(8,128)}), f32[32,8,128]{2,1,0:T(8,128)S(1)}, u32[]{:S(2)}, u32[]{:S(2)}) %all-to-all-start) | async-done | bytes 131104 | tf_op jit(solution)/shard_map/all_to_all | solution.py:749
  31.0 4.3 %forward.2 = (f32[32,8,128]{2,1,0:T(8,128)S(1)}, f32[640,512]{1,0:T(8,128)S(1)}, f32[8,128]{1,0:T(8,128)S(1)}, bf16[384,512]{1,0:T(8,128)(2,1)}, f32[448,512]{1,0:T(8,128)}) custom-call(s32[8,128]{1,0:T(8,128)S(1)} %get-tuple-element.131.limits_ref, f32[32,8,128]{2,1,0:T(8,128)S(1)} %get-tuple-element.132.member_ref, ...), custom_call_target="tpu_custom_call" | custom-call | flops 3019898880 | tf_op jit(solution)/shard_map/forward/pallas_call | solution.py:705
  36.6 4.2 %all-to-all-start.1 = ((f32[32,8,128]{2,1,0:T(8,128)}), f32[32,8,128]{2,1,0:T(8,128)S(1)}, u32[]{:S(2)}, u32[]{:S(2)}) async-start(f32[32,8,128]{2,1,0:T(8,128)} %copy-done.15), calls=%async_computation.1 | async-start | bytes 262144 | tf_op jit(solution)/shard_map/all_to_all | solution.py:749
  41.1 1.7 collective-permute-start.5
  43.2 1.7 collective-permute-start.9
  44.9 1.1 slice_bitcast_fusion.3.head_ref
  46.0 3.0 %all-to-all-done.1.gathered_ref = f32[32,8,128]{2,1,0:T(8,128)S(1)} async-done(((f32[32,8,128]{2,1,0:T(8,128)}), f32[32,8,128]{2,1,0:T(8,128)S(1)}, u32[]{:S(2)}, u32[]{:S(2)}) %all-to-all-start.1) | async-done | bytes 131104 | tf_op jit(solution)/shard_map/all_to_all | solution.py:749
  49.0 4.0 %forward.3 = (f32[32,8,128]{2,1,0:T(8,128)S(1)}, f32[576,512]{1,0:T(8,128)S(1)}, f32[8,128]{1,0:T(8,128)S(1)}, bf16[384,512]{1,0:T(8,128)(2,1)}, f32[512,512]{1,0:T(8,128)}) custom-call(s32[8,128]{1,0:T(8,128)S(1)} %get-tuple-element.131.limits_ref, f32[32,8,128]{2,1,0:T(8,128)S(1)} %get-tuple-element.132.member_ref, ...), custom_call_target="tpu_custom_call" | custom-call | flops 2717908992 | tf_op jit(solution)/shard_map/forward/pallas_call | solution.py:705
  54.1 12.5 %all_to_all.40.gathered_ref = f32[32,8,128]{2,1,0:T(8,128)S(1)} all-to-all(f32[32,8,128]{2,1,0:T(8,128)S(1)} %get-tuple-element.154), channel_id=1, replica_groups=mesh['maps'=8,'rows'=4] {'maps','rows'}, dimensions={0} | all-to-all | bytes 262144 | tf_op jit(solution)/shard_map/all_to_all | solution.py:749
  66.6 2.9 %pool.1 = (f32[32,8,128]{2,1,0:T(8,128)}, f32[576,512]{1,0:T(8,128)S(1)}, bf16[576,512]{1,0:T(8,128)(2,1)S(1)}, f32[8,128]{1,0:T(8,128)S(1)}, bf16[864,128]{1,0:...) custom-call(s32[8,128]{1,0:T(8,128)S(1)} %get-tuple-element.131.limits_ref, ...), custom_call_target="tpu_custom_call" | custom-call | flops 603979776 | tf_op jit(solution)/shard_map/pool/pallas_call | solution.py:705
  70.4 3.7 %all-to-all-start.3 = ((f32[32,8,128]{2,1,0:T(8,128)}), f32[32,8,128]{2,1,0:T(8,128)S(1)}, u32[]{:S(2)}, u32[]{:S(2)}) async-start(f32[32,8,128]{2,1,0:T(8,128)} %get-tuple-element.164), calls=%async_computation.3 | async-start | bytes 262144 | tf_op jit(solution)/shard_map/all_to_all | solution.py:749
  74.3 1.7 collective-permute-start.15
  76.6 1.1 slice_bitcast_fusion.2.head_ref
  77.7 4.5 %all-to-all-done.3.gathered_ref = f32[32,8,128]{2,1,0:T(8,128)S(1)} async-done(((f32[32,8,128]{2,1,0:T(8,128)}), f32[32,8,128]{2,1,0:T(8,128)S(1)}, u32[]{:S(2)}, u32[]{:S(2)}) %all-to-all-start.3) | async-done | bytes 131104 | tf_op jit(solution)/shard_map/all_to_all | solution.py:749
  83.9 5.9 %backward.2 = (f32[32,8,128]{2,1,0:T(8,128)}, f32[512,512]{1,0:T(8,128)S(1)}, bf16[512,512]{1,0:T(8,128)(2,1)S(1)}, f32[8,128]{1,0:T(8,128)S(1)}, bf16[768,128]{...) custom-call(s32[8,128]{1,0:T(8,128)S(1)} %get-tuple-element.131.limits_ref, ...), custom_call_target="tpu_custom_call" | custom-call | flops 2415919104 | tf_op jit(solution)/shard_map/backward/pallas_call | solution.py:705
  90.7 2.6 %all-to-all-start.4 = ((f32[32,8,128]{2,1,0:T(8,128)}), f32[32,8,128]{2,1,0:T(8,128)S(1)}, u32[]{:S(2)}, u32[]{:S(2)}) async-start(f32[32,8,128]{2,1,0:T(8,128)} %get-tuple-element.178), calls=%async_computation.4 | async-start | bytes 262144 | tf_op jit(solution)/shard_map/all_to_all | solution.py:749
  93.5 1.7 collective-permute-start.18
  95.3 5.3 %weight_grad.3 = (f32[4,576,128]{2,1,0:T(8,128)}, bf16[4,576,128]{2,1,0:T(8,128)(2,1)}) custom-call(s32[8,128]{1,0:T(8,128)S(1)} %get-tuple-element.131.limits_ref, f32[32,8,128]{2,1,0:T(8,128)S(1)} %get-tuple-element.132.member_ref, f32[32,8,128]{2,1,0:T(8,128)S(1)} %all-to-all-done.3.gathered_ref, f32[8,128]{1,0:T(8,128)S(1)} %get-tuple-element.167.moments_ref, ...), custom_call_target="tpu_custom_call" | custom-call | flops 1811939328 | tf_op jit(solution)/shard_map/weight_grad/pallas_call | solution.py:705
  102.3 1.1 slice_bitcast_fusion.1.head_ref
  104.5 5.0 %backward.3 = (f32[32,8,128]{2,1,0:T(8,128)S(1)}, f32[448,512]{1,0:T(8,128)S(1)}, bf16[448,512]{1,0:T(8,128)(2,1)S(1)}, f32[8,128]{1,0:T(8,128)S(1)}, bf16[768,1...) custom-call(s32[8,128]{1,0:T(8,128)S(1)} %get-tuple-element.131.limits_ref, ...), custom_call_target="tpu_custom_call" | custom-call | flops 2113929216 | tf_op jit(solution)/shard_map/backward/pallas_call | solution.py:705
  110.9 5.0 %all-to-all-start.5 = ((f32[32,8,128]{2,1,0:T(8,128)}), f32[32,8,128]{2,1,0:T(8,128)S(1)}, u32[]{:S(2)}, u32[]{:S(2)}) async-start(f32[32,8,128]{2,1,0:T(8,128)} %copy-done.14), calls=%async_computation.5 | async-start | bytes 262144 | tf_op jit(solution)/shard_map/all_to_all | solution.py:749
  116.0 1.7 collective-permute-start.22
  117.9 5.3 %weight_grad.4 = (f32[4,576,128]{2,1,0:T(8,128)}, bf16[4,576,128]{2,1,0:T(8,128)(2,1)}) custom-call(s32[8,128]{1,0:T(8,128)S(1)} %get-tuple-element.131.limits_ref, f32[32,8,128]{2,1,0:T(8,128)S(1)} %get-tuple-element.132.member_ref, f32[32,8,128]{2,1,0:T(8,128)S(1)} %all-to-all-done.4.gathered_ref, f32[8,128]{1,0:T(8,128)S(1)} %copy-done.19, ...), custom_call_target="tpu_custom_call" | custom-call | flops 1811939328 | tf_op jit(solution)/shard_map/weight_grad/pallas_call | solution.py:705
  124.8 2.1 %halve.4 = (f32[2,576,128]{2,1,0:T(8,128)}, bf16[2,576,128]{2,1,0:T(8,128)(2,1)}) custom-call(f32[4,576,128]{2,1,0:T(8,128)} %get-tuple-element.225.keep_hbm, bf16[4,576,128]{2,1,0:T(8,128)(2,1)S(1)} %collective-permute-done.20.received_ref), custom_call_target="tpu_custom_call" | custom-call | tf_op jit(solution)/shard_map/halve/pallas_call | solution.py:705
  127.0 1.5 collective-permute-start.26
  129.4 4.4 %weight_grad.5 = (f32[4,576,128]{2,1,0:T(8,128)S(1)}, bf16[4,576,128]{2,1,0:T(8,128)(2,1)S(1)}) custom-call(s32[8,128]{1,0:T(8,128)S(1)} %get-tuple-element.131.limits_ref, f32[32,8,128]{2,1,0:T(8,128)S(1)} %get-tuple-element.132.member_ref, f32[32,8,128]{2,1,0:T(8,128)S(1)} %all-to-all-done.5.gathered_ref, f32[8,128]{1,0:T(8,128)S(1)} %copy-done.22, ...), custom_call_target="tpu_custom_call" | custom-call | flops 1811939328 | tf_op jit(solution)/shard_map/weight_grad/pallas_call | solution.py:705
  134.8 1.3 collective-permute-start.24
  136.3 4.0 %collective-permute-done.25.received_ref = bf16[4,576,128]{2,1,0:T(8,128)(2,1)S(1)} collective-permute-done((bf16[4,576,128]{2,1,0:T(8,128)(2,1)}, bf16[4,576,128]{2,1,0:T(8,128)(2,1)S(1)}, u32[]{:S(2)}, u32[]{:S(2)}) %collective-permute-start.25) | collective-permute-done | bytes 589856 | tf_op jit(solution)/shard_map/ppermute | solution.py:869
  140.3 2.2 %halve.5 = (f32[2,576,128]{2,1,0:T(8,128)}, bf16[2,576,128]{2,1,0:T(8,128)(2,1)}) custom-call(f32[4,576,128]{2,1,0:T(8,128)} %get-tuple-element.223.keep_hbm, bf16[4,576,128]{2,1,0:T(8,128)(2,1)S(1)} %collective-permute-done.25.received_ref), custom_call_target="tpu_custom_call" | custom-call | tf_op jit(solution)/shard_map/halve/pallas_call | solution.py:705
  143.4 1.8 halve.6
  145.2 2.5 %collective-permute-start.28 = (bf16[1,576,128]{2,1,0:T(8,128)(2,1)}, bf16[1,576,128]{2,1,0:T(8,128)(2,1)S(1)}, u32[]{:S(2)}, u32[]{:S(2)}) collective-permute-start(bf16[1,576,128]{2,1,0:T(8,128)(2,1)} %get-tuple-element.232), channel_id=1, source_target_pairs={{0,16},{4,20},{8,24},{12,28},{16,0},{20,4},{24,8},{28,12},{1,17},{... | collective-permute-start | bytes 442376 | tf_op jit(solution)/shard_map/ppermute | solution.py:869
  147.7 4.5 %collective-permute-done.24.received_ref = bf16[4,576,128]{2,1,0:T(8,128)(2,1)S(1)} collective-permute-done((bf16[4,576,128]{2,1,0:T(8,128)(2,1)S(1)}, bf16[4,576,128]{2,1,0:T(8,128)(2,1)S(1)}, u32[]{:S(2)}, u32[]{:S(2)}) %collective-permute-start.24) | collective-permute-done | bytes 589856 | tf_op jit(solution)/shard_map/ppermute | solution.py:869
  154.2 2.1 %add.3 = bf16[4,576,128]{2,1,0:T(8,128)(2,1)} custom-call(f32[4,576,128]{2,1,0:T(8,128)} %copy-done, bf16[4,576,128]{2,1,0:T(8,128)(2,1)S(1)} %collective-permute-done.24.received_ref), custom_call_target="tpu_custom_call" | custom-call | tf_op jit(solution)/shard_map/add/pallas_call | solution.py:705
  156.3 4.5 %all-to-all-start.6 = ((bf16[4,576,128]{2,1,0:T(8,128)(2,1)}), bf16[4,576,128]{2,1,0:T(8,128)(2,1)S(1)}, u32[]{:S(2)}, u32[]{:S(2)}) async-start(bf16[4,576,128]{2,1,0:T(8,128)(2,1)} %add.3), calls=%async_computation.6 | async-start | bytes 1179648 | tf_op jit(solution)/shard_map/all_to_all | solution.py:938
  162.9 1.8 halve.7
  164.7 3.0 %collective-permute-start.29 = (bf16[1,576,128]{2,1,0:T(8,128)(2,1)}, bf16[1,576,128]{2,1,0:T(8,128)(2,1)}, u32[]{:S(2)}, u32[]{:S(2)}) collective-permute-start(bf16[1,576,128]{2,1,0:T(8,128)(2,1)} %get-tuple-element.237), channel_id=1, source_target_pairs={{0,16},{4,20},{8,24},{12,28},{16,0},{20,4},{24,8},{28,12},{1,17},{... | collective-permute-start | bytes 442376 | tf_op jit(solution)/shard_map/ppermute | solution.py:869
  169.4 4.2 %last.1 = (bf16[384,512]{1,0:T(8,128)(2,1)}, f32[8,128]{1,0:T(8,128)S(1)}, bf16[384,128]{1,0:T(8,128)(2,1)}) custom-call(s32[8,128]{1,0:T(8,128)S(1)} %get-tuple-element.131.limits_ref, f32[32,8,128]{2,1,0:T(8,128)S(1)} %get-tuple-element.132.member_ref, f32[32,8,128]{2,1,0:T(8,128)S(1)} %all-to-all-done.5.gathered_ref, ...), custom_call_target="tpu_custom_call" | custom-call | flops 1811939328 | tf_op jit(solution)/shard_map/last/pallas_call | solution.py:705
  174.2 7.9 %collective-permute-done.29.last1_hbm = bf16[1,576,128]{2,1,0:T(8,128)(2,1)} collective-permute-done((bf16[1,576,128]{2,1,0:T(8,128)(2,1)}, bf16[1,576,128]{2,1,0:T(8,128)(2,1)}, u32[]{:S(2)}, u32[]{:S(2)}) %collective-permute-start.29) | collective-permute-done | bytes 147488 | tf_op jit(solution)/shard_map/ppermute | solution.py:869
  184.2 2.0 squares.1
  186.2 3.7 %all-to-all-start.7 = ((f32[32,1,128]{2,1,0:T(1,128)}), f32[32,1,128]{2,1,0:T(1,128)S(1)}, u32[]{:S(2)}, u32[]{:S(2)}) async-start(f32[32,1,128]{2,1,0:T(1,128)} %get-tuple-element.243), calls=%async_computation.7 | async-start | bytes 32768 | tf_op jit(solution)/shard_map/all_to_all | solution.py:956
  190.5 6.4 %all-to-all-done.7.every_ref = f32[32,1,128]{2,1,0:T(1,128)S(1)} async-done(((f32[32,1,128]{2,1,0:T(1,128)}), f32[32,1,128]{2,1,0:T(1,128)S(1)}, u32[]{:S(2)}, u32[]{:S(2)}) %all-to-all-start.7) | async-done | bytes 16416 | tf_op jit(solution)/shard_map/all_to_all | solution.py:956
  198.4 2.7 %adam.1 = (f32[1,128]{1,0:T(1,128)}, f32[3,576,128]{2,1,0:T(8,128)}, f32[3,576,128]{2,1,0:T(8,128)}, f32[3,576,128]{2,1,0:T(8,128)}, f32[3,2,512]{2,1,0:T(2,128)...) custom-call(f32[32,1,128]{2,1,0:T(1,128)S(1)} %all-to-all-done.7.every_ref, s32[1]{0:T(128)S(6)} %copy.24.step_ref, ...), custom_call_target="tpu_custom_call" | custom-call | tf_op jit(solution)/shard_map/adam/pallas_call | solution.py:705
  (147 shorter events, 32.2 us)
Async XLA Ops:
  0.6 30.4 %copy-start.5 = (f32[2,3,512]{2,0,1:T(2,128)S(1)}, f32[2,3,512]{2,0,1:T(2,128)}, u32[]{:S(2)}) copy-start(f32[2,3,512]{2,0,1:T(2,128)} %param.16) | copy-start | bytes 36868
  2.0 6.7 %collective-permute-start = (bf16[224,512]{1,0:T(8,128)(2,1)S(1)}, bf16[224,512]{1,0:T(8,128)(2,1)S(1)}, u32[]{:S(2)}, u32[]{:S(2)}) collective-permute-start(bf16[224,512]{1,0:T(8,128)(2,1)S(1)} %get-tuple-element.133), channel_id=1, source_target_pairs={{0,1},{1,0},{2,3},{3,2},{4,5},{5,4},{6,7},{7,6},{8,9},{9,8},{10,11... | collective-permute-start | bytes 688136 | tf_op jit(solution)/shard_map/ppermute | solution.py:757
  2.5 6.2 %collective-permute-start.1 = (bf16[224,512]{1,0:T(8,128)(2,1)S(1)}, bf16[224,512]{1,0:T(8,128)(2,1)S(1)}, u32[]{:S(2)}, u32[]{:S(2)}) collective-permute-start(bf16[224,512]{1,0:T(8,128)(2,1)S(1)} %get-tuple-element.135), channel_id=1, source_target_pairs={{2,1},{1,2},{6,5},{5,6},{10,9},{9,10},{14,13},{13,14},{18,17},{17,... | collective-permute-start | bytes 688136 | tf_op jit(solution)/shard_map/ppermute | solution.py:766
  8.7 14.4 %copy-start.1 = (bf16[224,512]{1,0:T(8,128)(2,1)}, bf16[224,512]{1,0:T(8,128)(2,1)S(1)}, u32[]{:S(2)}) copy-start(bf16[224,512]{1,0:T(8,128)(2,1)S(1)} %collective-permute-done.near_ref.near_hbm) | copy-start | bytes 688132
  14.1 17.0 %all-to-all-start = ((f32[32,8,128]{2,1,0:T(8,128)}), f32[32,8,128]{2,1,0:T(8,128)S(1)}, u32[]{:S(2)}, u32[]{:S(2)}) async-start(f32[32,8,128]{2,1,0:T(8,128)} %get-tuple-element.141), calls=%async_computation | async-start | bytes 262144 | tf_op jit(solution)/shard_map/all_to_all | solution.py:749
  22.8 13.1 %collective-permute-start.2 = (bf16[384,512]{1,0:T(8,128)(2,1)}, bf16[384,512]{1,0:T(8,128)(2,1)}, u32[]{:S(2)}, u32[]{:S(2)}) collective-permute-start(bf16[384,512]{1,0:T(8,128)(2,1)} %get-tuple-element.218.rest_4_), channel_id=1, source_target_pairs={{0,1},{1,0},{2,3},{3,2},{4,5},{5,4},{6,7},{7,6},{8,9},{9,8},{10,11... | collective-permute-start | bytes 1179656 | tf_op jit(solution)/shard_map/ppermute | solution.py:757
  23.1 12.8 %collective-permute-start.3 = (bf16[384,512]{1,0:T(8,128)(2,1)}, bf16[384,512]{1,0:T(8,128)(2,1)}, u32[]{:S(2)}, u32[]{:S(2)}) collective-permute-start(bf16[384,512]{1,0:T(8,128)(2,1)} %get-tuple-element.218.rest_4_), channel_id=1, source_target_pairs={{0,2},{1,3},{2,0},{3,1},{4,6},{5,7},{6,4},{7,5},{8,10},{9,11},{10,... | collective-permute-start | bytes 1179656 | tf_op jit(solution)/shard_map/ppermute | solution.py:757
  36.6 12.4 %all-to-all-start.1 = ((f32[32,8,128]{2,1,0:T(8,128)}), f32[32,8,128]{2,1,0:T(8,128)S(1)}, u32[]{:S(2)}, u32[]{:S(2)}) async-start(f32[32,8,128]{2,1,0:T(8,128)} %copy-done.15), calls=%async_computation.1 | async-start | bytes 262144 | tf_op jit(solution)/shard_map/all_to_all | solution.py:749
  40.8 12.2 %collective-permute-start.4 = (bf16[160,128]{1,0:T(8,128)(2,1)}, bf16[160,128]{1,0:T(8,128)(2,1)S(1)}, u32[]{:S(2)}, u32[]{:S(2)}) collective-permute-start(bf16[160,128]{1,0:T(8,128)(2,1)} %get-tuple-element.151), channel_id=1, source_target_pairs={{0,1},{1,0},{2,3},{3,2},{4,5},{5,4},{6,7},{7,6},{8,9},{9,8},{10,11... | collective-permute-start | bytes 122888 | tf_op jit(solution)/shard_map/ppermute | solution.py:753
  41.1 12.2 %collective-permute-start.5 = (bf16[160,128]{1,0:T(8,128)(2,1)}, bf16[160,128]{1,0:T(8,128)(2,1)S(1)}, u32[]{:S(2)}, u32[]{:S(2)}) collective-permute-start(bf16[160,128]{1,0:T(8,128)(2,1)} %get-tuple-element.152), channel_id=1, source_target_pairs={{0,2},{1,3},{2,0},{3,1},{4,6},{5,7},{6,4},{7,5},{8,10},{9,11},{10,... | collective-permute-start | bytes 122888 | tf_op jit(solution)/shard_map/ppermute | solution.py:753
  42.8 10.8 %collective-permute-start.6 = (bf16[160,128]{1,0:T(8,128)(2,1)}, bf16[160,128]{1,0:T(8,128)(2,1)S(1)}, u32[]{:S(2)}, u32[]{:S(2)}) collective-permute-start(bf16[160,128]{1,0:T(8,128)(2,1)} %get-tuple-element.153), channel_id=1, source_target_pairs={{0,3},{1,2},{2,1},{3,0},{4,7},{5,6},{6,5},{7,4},{8,11},{9,10},{10,... | collective-permute-start | bytes 122888 | tf_op jit(solution)/shard_map/ppermute | solution.py:753
  42.8 26.8 %collective-permute-start.8 = (bf16[384,512]{1,0:T(8,128)(2,1)}, bf16[384,512]{1,0:T(8,128)(2,1)}, u32[]{:S(2)}, u32[]{:S(2)}) collective-permute-start(bf16[384,512]{1,0:T(8,128)(2,1)} %get-tuple-element.203.rest_4_), channel_id=1, source_target_pairs={{0,1},{1,0},{2,3},{3,2},{4,5},{5,4},{6,7},{7,6},{8,9},{9,8},{10,11... | collective-permute-start | bytes 1179656 | tf_op jit(solution)/shard_map/ppermute | solution.py:757
  43.2 26.3 %collective-permute-start.9 = (bf16[384,512]{1,0:T(8,128)(2,1)}, bf16[384,512]{1,0:T(8,128)(2,1)}, u32[]{:S(2)}, u32[]{:S(2)}) collective-permute-start(bf16[384,512]{1,0:T(8,128)(2,1)} %get-tuple-element.203.rest_4_), channel_id=1, source_target_pairs={{0,2},{1,3},{2,0},{3,1},{4,6},{5,7},{6,4},{7,5},{8,10},{9,11},{10,... | collective-permute-start | bytes 1179656 | tf_op jit(solution)/shard_map/ppermute | solution.py:757
  53.0 16.5 %copy-start.16 = (f32[8,128]{1,0:T(8,128)}, f32[8,128]{1,0:T(8,128)S(1)}, u32[]{:S(2)}) copy-start(f32[8,128]{1,0:T(8,128)S(1)} %get-tuple-element.170.moments_below_ref.moments_ref) | copy-start | bytes 12292
  53.0 16.5 %collective-permute-start.7 = (bf16[384,512]{1,0:T(8,128)(2,1)}, bf16[384,512]{1,0:T(8,128)(2,1)S(1)}, u32[]{:S(2)}, u32[]{:S(2)}) collective-permute-start(bf16[384,512]{1,0:T(8,128)(2,1)} %collective-permute-done.3.rest_6_), channel_id=1, source_target_pairs={{0,1},{1,0},{2,3},{3,2},{4,5},{5,4},{6,7},{7,6},{8,9},{9,8},{10,11... | collective-permute-start | bytes 1179656 | tf_op jit(solution)/shard_map/ppermute | solution.py:757
  53.3 16.3 %collective-permute-start.10 = (bf16[384,512]{1,0:T(8,128)(2,1)}, bf16[384,512]{1,0:T(8,128)(2,1)S(1)}, u32[]{:S(2)}, u32[]{:S(2)}) collective-permute-start(bf16[384,512]{1,0:T(8,128)(2,1)} %get-tuple-element.183.rest_4_), channel_id=1, source_target_pairs={{0,1},{1,0},{2,3},{3,2},{4,5},{5,4},{6,7},{7,6},{8,9},{9,8},{10,11... | collective-permute-start | bytes 1179656 | tf_op jit(solution)/shard_map/ppermute | solution.py:757
  53.6 16.0 %collective-permute-start.11 = (bf16[384,512]{1,0:T(8,128)(2,1)}, bf16[384,512]{1,0:T(8,128)(2,1)S(1)}, u32[]{:S(2)}, u32[]{:S(2)}) collective-permute-start(bf16[384,512]{1,0:T(8,128)(2,1)} %get-tuple-element.183.rest_4_), channel_id=1, source_target_pairs={{0,2},{1,3},{2,0},{3,1},{4,6},{5,7},{6,4},{7,5},{8,10},{9,11},{10,... | collective-permute-start | bytes 1179656 | tf_op jit(solution)/shard_map/ppermute | solution.py:757
  66.6 36.8 %copy-start.21 = (f32[8,128]{1,0:T(8,128)S(1)}, f32[8,128]{1,0:T(8,128)}, u32[]{:S(2)}) copy-start(f32[8,128]{1,0:T(8,128)} %copy-done.20) | copy-start | bytes 12292
  69.6 33.9 %copy-start.18 = (f32[8,128]{1,0:T(8,128)S(1)}, f32[8,128]{1,0:T(8,128)}, u32[]{:S(2)}) copy-start(f32[8,128]{1,0:T(8,128)} %copy-done.16) | copy-start | bytes 12292
  70.4 11.8 %all-to-all-start.3 = ((f32[32,8,128]{2,1,0:T(8,128)}), f32[32,8,128]{2,1,0:T(8,128)S(1)}, u32[]{:S(2)}, u32[]{:S(2)}) async-start(f32[32,8,128]{2,1,0:T(8,128)} %get-tuple-element.164), calls=%async_computation.3 | async-start | bytes 262144 | tf_op jit(solution)/shard_map/all_to_all | solution.py:749
  74.1 16.6 %collective-permute-start.14 = (bf16[864,128]{1,0:T(8,128)(2,1)}, bf16[864,128]{1,0:T(8,128)(2,1)S(1)}, u32[]{:S(2)}, u32[]{:S(2)}) collective-permute-start(bf16[864,128]{1,0:T(8,128)(2,1)} %get-tuple-element.175), channel_id=1, source_target_pairs={{0,1},{1,0},{2,3},{3,2},{4,5},{5,4},{6,7},{7,6},{8,9},{9,8},{10,11... | collective-permute-start | bytes 663560 | tf_op jit(solution)/shard_map/ppermute | solution.py:753
  74.3 16.4 %collective-permute-start.15 = (bf16[864,128]{1,0:T(8,128)(2,1)}, bf16[864,128]{1,0:T(8,128)(2,1)}, u32[]{:S(2)}, u32[]{:S(2)}) collective-permute-start(bf16[864,128]{1,0:T(8,128)(2,1)} %get-tuple-element.176), channel_id=1, source_target_pairs={{0,2},{1,3},{2,0},{3,1},{4,6},{5,7},{6,4},{7,5},{8,10},{9,11},{10,... | collective-permute-start | bytes 663560 | tf_op jit(solution)/shard_map/ppermute | solution.py:753
  76.0 14.7 %collective-permute-start.16 = (bf16[864,128]{1,0:T(8,128)(2,1)}, bf16[864,128]{1,0:T(8,128)(2,1)}, u32[]{:S(2)}, u32[]{:S(2)}) collective-permute-start(bf16[864,128]{1,0:T(8,128)(2,1)} %get-tuple-element.177), channel_id=1, source_target_pairs={{0,3},{1,2},{2,1},{3,0},{4,7},{5,6},{6,5},{7,4},{8,11},{9,10},{10,... | collective-permute-start | bytes 663560 | tf_op jit(solution)/shard_map/ppermute | solution.py:753
  76.1 14.6 %collective-permute-start.12 = (bf16[384,512]{1,0:T(8,128)(2,1)}, bf16[384,512]{1,0:T(8,128)(2,1)}, u32[]{:S(2)}, u32[]{:S(2)}) collective-permute-start(bf16[384,512]{1,0:T(8,128)(2,1)} %collective-permute-done.9.rest_6_), channel_id=1, source_target_pairs={{0,1},{1,0},{2,3},{3,2},{4,5},{5,4},{6,7},{7,6},{8,9},{9,8},{10,11... | collective-permute-start | bytes 1179656 | tf_op jit(solution)/shard_map/ppermute | solution.py:757
  76.4 14.3 %collective-permute-start.13 = (bf16[384,512]{1,0:T(8,128)(2,1)}, bf16[384,512]{1,0:T(8,128)(2,1)}, u32[]{:S(2)}, u32[]{:S(2)}) collective-permute-start(bf16[384,512]{1,0:T(8,128)(2,1)} %copy-done.41), channel_id=1, source_target_pairs={{0,1},{1,0},{2,3},{3,2},{4,5},{5,4},{6,7},{7,6},{8,9},{9,8},{10,11... | collective-permute-start | bytes 1179656 | tf_op jit(solution)/shard_map/ppermute | solution.py:757
  90.7 20.3 %copy-start.26 = (f32[8,128]{1,0:T(8,128)}, f32[8,128]{1,0:T(8,128)S(1)}, u32[]{:S(2)}) copy-start(f32[8,128]{1,0:T(8,128)S(1)} %get-tuple-element.240.totals2_ref) | copy-start | bytes 12292
  90.7 27.2 %copy-start.19 = (f32[8,128]{1,0:T(8,128)S(1)}, f32[8,128]{1,0:T(8,128)}, u32[]{:S(2)}) copy-start(f32[8,128]{1,0:T(8,128)} %copy-done.16) | copy-start | bytes 12292
  90.7 10.8 %all-to-all-start.4 = ((f32[32,8,128]{2,1,0:T(8,128)}), f32[32,8,128]{2,1,0:T(8,128)S(1)}, u32[]{:S(2)}, u32[]{:S(2)}) async-start(f32[32,8,128]{2,1,0:T(8,128)} %get-tuple-element.178), calls=%async_computation.4 | async-start | bytes 262144 | tf_op jit(solution)/shard_map/all_to_all | solution.py:749
  93.3 17.0 %collective-permute-start.17 = (bf16[768,128]{1,0:T(8,128)(2,1)}, bf16[768,128]{1,0:T(8,128)(2,1)}, u32[]{:S(2)}, u32[]{:S(2)}) collective-permute-start(bf16[768,128]{1,0:T(8,128)(2,1)} %get-tuple-element.195), channel_id=1, source_target_pairs={{0,1},{1,0},{2,3},{3,2},{4,5},{5,4},{6,7},{7,6},{8,9},{9,8},{10,11... | collective-permute-start | bytes 589832 | tf_op jit(solution)/shard_map/ppermute | solution.py:753
  93.5 16.8 %collective-permute-start.18 = (bf16[768,128]{1,0:T(8,128)(2,1)}, bf16[768,128]{1,0:T(8,128)(2,1)}, u32[]{:S(2)}, u32[]{:S(2)}) collective-permute-start(bf16[768,128]{1,0:T(8,128)(2,1)} %get-tuple-element.196), channel_id=1, source_target_pairs={{0,2},{1,3},{2,0},{3,1},{4,6},{5,7},{6,4},{7,5},{8,10},{9,11},{10,... | collective-permute-start | bytes 589832 | tf_op jit(solution)/shard_map/ppermute | solution.py:753
  95.2 15.1 %collective-permute-start.19 = (bf16[768,128]{1,0:T(8,128)(2,1)}, bf16[768,128]{1,0:T(8,128)(2,1)}, u32[]{:S(2)}, u32[]{:S(2)}) collective-permute-start(bf16[768,128]{1,0:T(8,128)(2,1)} %get-tuple-element.197), channel_id=1, source_target_pairs={{0,3},{1,2},{2,1},{3,0},{4,7},{5,6},{6,5},{7,4},{8,11},{9,10},{10,... | collective-permute-start | bytes 589832 | tf_op jit(solution)/shard_map/ppermute | solution.py:753
  100.6 28.7 %copy-start.22 = (f32[8,128]{1,0:T(8,128)S(1)}, f32[8,128]{1,0:T(8,128)}, u32[]{:S(2)}) copy-start(f32[8,128]{1,0:T(8,128)} %copy-done.20) | copy-start | bytes 12292
  101.6 22.4 %collective-permute-start.20 = (bf16[4,576,128]{2,1,0:T(8,128)(2,1)}, bf16[4,576,128]{2,1,0:T(8,128)(2,1)S(1)}, u32[]{:S(2)}, u32[]{:S(2)}) collective-permute-start(bf16[4,576,128]{2,1,0:T(8,128)(2,1)} %get-tuple-element.207), channel_id=1, source_target_pairs={{0,4},{4,0},{8,12},{12,8},{16,20},{20,16},{24,28},{28,24},{1,5},{5... | collective-permute-start | bytes 1769480 | tf_op jit(solution)/shard_map/ppermute | solution.py:869
  110.3 18.3 %copy-start.28 = (f32[8,128]{1,0:T(8,128)}, f32[8,128]{1,0:T(8,128)S(1)}, u32[]{:S(2)}) copy-start(f32[8,128]{1,0:T(8,128)S(1)} %get-tuple-element.241.totals1_ref) | copy-start | bytes 12292
  110.9 13.0 %all-to-all-start.5 = ((f32[32,8,128]{2,1,0:T(8,128)}), f32[32,8,128]{2,1,0:T(8,128)S(1)}, u32[]{:S(2)}, u32[]{:S(2)}) async-start(f32[32,8,128]{2,1,0:T(8,128)} %copy-done.14), calls=%async_computation.5 | async-start | bytes 262144 | tf_op jit(solution)/shard_map/all_to_all | solution.py:749
  115.9 12.6 %collective-permute-start.21 = (bf16[768,128]{1,0:T(8,128)(2,1)}, bf16[768,128]{1,0:T(8,128)(2,1)S(1)}, u32[]{:S(2)}, u32[]{:S(2)}) collective-permute-start(bf16[768,128]{1,0:T(8,128)(2,1)} %get-tuple-element.215), channel_id=1, source_target_pairs={{0,1},{1,0},{2,3},{3,2},{4,5},{5,4},{6,7},{7,6},{8,9},{9,8},{10,11... | collective-permute-start | bytes 589832 | tf_op jit(solution)/shard_map/ppermute | solution.py:753
  116.0 12.5 %collective-permute-start.22 = (bf16[768,128]{1,0:T(8,128)(2,1)}, bf16[768,128]{1,0:T(8,128)(2,1)S(1)}, u32[]{:S(2)}, u32[]{:S(2)}) collective-permute-start(bf16[768,128]{1,0:T(8,128)(2,1)} %get-tuple-element.216), channel_id=1, source_target_pairs={{0,2},{1,3},{2,0},{3,1},{4,6},{5,7},{6,4},{7,5},{8,10},{9,11},{10,... | collective-permute-start | bytes 589832 | tf_op jit(solution)/shard_map/ppermute | solution.py:753
  117.7 10.8 %collective-permute-start.23 = (bf16[768,128]{1,0:T(8,128)(2,1)}, bf16[768,128]{1,0:T(8,128)(2,1)S(1)}, u32[]{:S(2)}, u32[]{:S(2)}) collective-permute-start(bf16[768,128]{1,0:T(8,128)(2,1)} %get-tuple-element.217), channel_id=1, source_target_pairs={{0,3},{1,2},{2,1},{3,0},{4,7},{5,6},{6,5},{7,4},{8,11},{9,10},{10,... | collective-permute-start | bytes 589832 | tf_op jit(solution)/shard_map/ppermute | solution.py:753
  123.9 16.4 %collective-permute-start.25 = (bf16[4,576,128]{2,1,0:T(8,128)(2,1)}, bf16[4,576,128]{2,1,0:T(8,128)(2,1)S(1)}, u32[]{:S(2)}, u32[]{:S(2)}) collective-permute-start(bf16[4,576,128]{2,1,0:T(8,128)(2,1)} %get-tuple-element.224), channel_id=1, source_target_pairs={{0,4},{4,0},{8,12},{12,8},{16,20},{20,16},{24,28},{28,24},{1,5},{5... | collective-permute-start | bytes 1769480 | tf_op jit(solution)/shard_map/ppermute | solution.py:869
  127.0 9.4 %collective-permute-start.26 = (bf16[2,576,128]{2,1,0:T(8,128)(2,1)}, bf16[2,576,128]{2,1,0:T(8,128)(2,1)S(1)}, u32[]{:S(2)}, u32[]{:S(2)}) collective-permute-start(bf16[2,576,128]{2,1,0:T(8,128)(2,1)} %get-tuple-element.227), channel_id=1, source_target_pairs={{0,8},{4,12},{8,0},{12,4},{16,24},{20,28},{24,16},{28,20},{1,9},{5... | collective-permute-start | bytes 884744 | tf_op jit(solution)/shard_map/ppermute | solution.py:869
  134.8 62.1 %copy-start.3 = (f32[3,9,64,128]{3,2,1,0:T(8,128)S(1)}, f32[3,9,64,128]{3,2,1,0:T(8,128)}, u32[]{:S(2)}) copy-start(f32[3,9,64,128]{3,2,1,0:T(8,128)} %param.24) | copy-start | bytes 2654212
  134.8 62.1 %copy-start.4 = (f32[3,9,64,128]{3,2,1,0:T(8,128)S(1)}, f32[3,9,64,128]{3,2,1,0:T(8,128)}, u32[]{:S(2)}) copy-start(f32[3,9,64,128]{3,2,1,0:T(8,128)} %param.25) | copy-start | bytes 2654212
  134.8 17.4 %collective-permute-start.24 = (bf16[4,576,128]{2,1,0:T(8,128)(2,1)S(1)}, bf16[4,576,128]{2,1,0:T(8,128)(2,1)S(1)}, u32[]{:S(2)}, u32[]{:S(2)}) collective-permute-start(bf16[4,576,128]{2,1,0:T(8,128)(2,1)S(1)} %get-tuple-element.222), channel_id=1, source_target_pairs={{0,4},{4,0},{8,12},{12,8},{16,20},{20,16},{24,28},{28,24},{1,5},{5... | collective-permute-start | bytes 1769480 | tf_op jit(solution)/shard_map/ppermute | solution.py:869
  142.5 11.0 %collective-permute-start.27 = (bf16[2,576,128]{2,1,0:T(8,128)(2,1)}, bf16[2,576,128]{2,1,0:T(8,128)(2,1)S(1)}, u32[]{:S(2)}, u32[]{:S(2)}) collective-permute-start(bf16[2,576,128]{2,1,0:T(8,128)(2,1)} %get-tuple-element.229), channel_id=1, source_target_pairs={{0,8},{4,12},{8,0},{12,4},{16,24},{20,28},{24,16},{28,20},{1,9},{5... | collective-permute-start | bytes 884744 | tf_op jit(solution)/shard_map/ppermute | solution.py:869
  145.2 7.6 %collective-permute-start.28 = (bf16[1,576,128]{2,1,0:T(8,128)(2,1)}, bf16[1,576,128]{2,1,0:T(8,128)(2,1)S(1)}, u32[]{:S(2)}, u32[]{:S(2)}) collective-permute-start(bf16[1,576,128]{2,1,0:T(8,128)(2,1)} %get-tuple-element.232), channel_id=1, source_target_pairs={{0,16},{4,20},{8,24},{12,28},{16,0},{20,4},{24,8},{28,12},{1,17},{... | collective-permute-start | bytes 442376 | tf_op jit(solution)/shard_map/ppermute | solution.py:869
  156.3 25.8 %all-to-all-start.6 = ((bf16[4,576,128]{2,1,0:T(8,128)(2,1)}), bf16[4,576,128]{2,1,0:T(8,128)(2,1)S(1)}, u32[]{:S(2)}, u32[]{:S(2)}) async-start(bf16[4,576,128]{2,1,0:T(8,128)(2,1)} %add.3), calls=%async_computation.6 | async-start | bytes 1179648 | tf_op jit(solution)/shard_map/all_to_all | solution.py:938
  164.7 17.4 %collective-permute-start.29 = (bf16[1,576,128]{2,1,0:T(8,128)(2,1)}, bf16[1,576,128]{2,1,0:T(8,128)(2,1)}, u32[]{:S(2)}, u32[]{:S(2)}) collective-permute-start(bf16[1,576,128]{2,1,0:T(8,128)(2,1)} %get-tuple-element.237), channel_id=1, source_target_pairs={{0,16},{4,20},{8,24},{12,28},{16,0},{20,4},{24,8},{28,12},{1,17},{... | collective-permute-start | bytes 442376 | tf_op jit(solution)/shard_map/ppermute | solution.py:869
  186.2 10.7 %all-to-all-start.7 = ((f32[32,1,128]{2,1,0:T(1,128)}), f32[32,1,128]{2,1,0:T(1,128)S(1)}, u32[]{:S(2)}, u32[]{:S(2)}) async-start(f32[32,1,128]{2,1,0:T(1,128)} %get-tuple-element.243), calls=%async_computation.7 | async-start | bytes 32768 | tf_op jit(solution)/shard_map/all_to_all | solution.py:956
  (34 other events, 110.6 us)
